TPU v7x, 512 devices: a whole 4x8x8 slice. The times are simulated.
512 devices in a mesh: section: 2 (over core), dp: 16 (over z_hi, y), vocab: 16 (over x, z_lo).
Axes of the slice: x: 4, y: 8, z: 8 (z_hi: 2, z_lo: 4; z = z_hi * 4 + z_lo), core: 2. Of those that a mesh axis runs over, the one named last changes fastest.
Arguments:
- hidden: bfloat16 [2048, 3072], P('dp', 'section'), may hold values from -2400 to 2400
- head: bfloat16 [3072, 65536], P(('section', 'dp'), 'vocab'), may hold values from -0.109375 to 0.109375
- codes: int32 [2048, 65536], P('dp', 'vocab'), may hold values from -127 to 127
- exponents: int32 [2048, 512], P('dp', 'vocab'), may hold values from -5 to -3
- loss_weight: float32 [2048], P('dp'), may hold values from 0.5 to 4
Outputs:
- kl_loss: float32 [2048], P('dp')
- hidden_grad: bfloat16 [2048, 3072], P('dp', ('section', 'vocab'))
All inputs are finite; a program needn't handle non-finite values.
Results may differ from a plain program's by a relative error of at most 0.0046.
Values may be sent and summed in bfloat16 or wider, within the bound.
No kernel may reach another device: no remote copies, remote signals or barrier semaphores. Data moves between devices by JAX's collectives and lax.ppermute only.
A program may use at most 64 MiB of HBM per device.

v0:
```python
import jax
import jax.numpy as jnp
from jax import lax
from jax.sharding import PartitionSpec as P

GROUP = 128
TEMP = 2


def dequantize(codes, exponents):
    row_count = codes.shape[0]
    groups = exponents.shape[1]
    scale = jnp.exp2(exponents.astype(jnp.float32))
    return (
        codes.astype(jnp.float32).reshape(row_count, groups, GROUP) * scale[:, :, None]
    ).reshape(row_count, groups * GROUP)


def local_sums(scaled_s, scaled_t, highest):
    t_exp = jnp.exp(scaled_t)
    return (
        jnp.sum(jnp.exp(scaled_s - highest[:, None]), axis=1),
        jnp.sum(t_exp, axis=1),
        jnp.sum(t_exp * (scaled_t - scaled_s), axis=1),
    )


def finish_rows(scaled_s, scaled_t, highest, totals, loss_weight):
    s_sum, t_sum, cross = totals
    student_lse = highest + jnp.log(s_sum)
    teacher_lse = jnp.log(t_sum)
    kl_loss = TEMP * TEMP * (cross / t_sum - teacher_lse + student_lse)
    logit_grad = (
        loss_weight[:, None]
        * TEMP
        * (jnp.exp(scaled_s - student_lse[:, None]) - jnp.exp(scaled_t - teacher_lse[:, None]))
    ).astype(jnp.bfloat16)
    return (kl_loss, logit_grad)


def grad_terms(logit_grad, weights):
    return lax.dot_general(
        logit_grad, weights, (((1,), (1,)), ((), ())), preferred_element_type=jnp.float32
    )


def on_device(hidden, head, codes, exponents, loss_weight):
    weights = lax.all_gather(head, "dp", axis=0, tiled=True)
    partial_logits = jnp.dot(hidden, weights, preferred_element_type=jnp.float32)
    logits = lax.psum(partial_logits, "section")
    scaled_s = logits / TEMP
    scaled_t = dequantize(codes, exponents) / TEMP
    highest = lax.pmax(jnp.max(scaled_s, axis=1), "vocab")
    totals = lax.psum(local_sums(scaled_s, scaled_t, highest), "vocab")
    kl_loss, logit_grad = finish_rows(scaled_s, scaled_t, highest, totals, loss_weight)
    hidden_grad = lax.psum_scatter(
        grad_terms(logit_grad, weights), "vocab", scatter_dimension=1, tiled=True
    )
    return (kl_loss, hidden_grad.astype(jnp.bfloat16))


def solution(mesh):
    in_specs = (
        P("dp", "section"),
        P(("section", "dp"), "vocab"),
        P("dp", "vocab"),
        P("dp", "vocab"),
        P("dp"),
    )
    out_specs = (P("dp"), P("dp", ("section", "vocab")))
    return jax.shard_map(
        on_device, mesh=mesh, in_specs=in_specs, out_specs=out_specs, check_vma=False
    )
```

profile of v0, /device:TPU:8, one launch (start us, length us, event | category | flops | bytes accessed | tf_op | source)
XLA Modules:
  0.0 513.5 jit_solution(12973126701796538241)
XLA Ops:
  7.2 0.0 copy-start
  7.2 0.0 all-gather.2.cloned.1.call-start
  7.2 0.7 all-gather.2.cloned.1.call-update
  7.9 0.0 all-reduce.3.cloned.1.call-start
  8.0 271.9 %all-gather.2.cloned.1.call-done = bf16[1536,4096]{1,0:T(8,128)(2,1)} async-done(((bf16[96,4096]{1,0:T(8,128)(2,1)}), bf16[1536,4096]{1,0:T(8,128)(2,1)}) %all-gather.2.cloned.1.call-update) | async-done | bytes 12582928 | tf_op jit(solution)/shard_map/all_gather | solution.py:48
  279.9 0.0 copy-done
  279.9 7.7 %fusion.8 = f32[128,4096]{1,0:T(8,128)} fusion(bf16[128,1536]{1,0:T(8,128)(2,1)S(1)} %copy-done, bf16[1536,4096]{1,0:T(8,128)(2,1)} %all-gather.2.cloned.1.call-done), kind=kOutput, calls=%fused_computation.17 | convolution fusion | flops 1610612736 | bytes 15073280 | tf_op jit(solution)/shard_map/dot_general | solution.py:49
  287.6 0.0 copy-start.3
  287.6 0.0 copy-start.4
  287.7 0.0 all-reduce.3.cloned.1.call-update
  287.7 0.0 reduce-scatter.2.cloned.1.call-start
  287.7 0.6 copy-done.3
  288.4 0.1 copy.7
  288.5 0.0 copy-done.4
  288.5 32.3 %all-reduce.3.cloned.1.call-done = f32[128,4096]{1,0:T(8,128)} async-done(((f32[128,4096]{1,0:T(8,128)}), f32[128,4096]{1,0:T(8,128)}) %all-reduce.3.cloned.1.call-update) | async-done | bytes 2097168 | tf_op jit(solution)/shard_map/psum | solution.py:50
  320.8 0.0 copy-start.1
  320.8 0.6 mul.35
  321.4 0.0 copy-start.2
  321.4 1.0 copy-done.1
  322.4 3.6 exponential_reduce_fusion.1
  326.1 0.0 copy-done.2
  326.1 43.9 %pmax.7 = f32[128]{0:T(128)S(1)} all-reduce(f32[128]{0:T(128)S(1)} %get-tuple-element.4), channel_id=1, replica_groups=mesh['section'=2,'dp'=16,'vocab'=16] {'vocab'}, use_global_device_ids=true, to_apply=%region_6.0 | all-reduce | flops 128 | bytes 1024 | tf_op jit(solution)/shard_map/pmax | solution.py:53
  370.0 0.5 exponential_reduce_fusion
  370.5 38.0 %all-reduce = (f32[128]{0:T(128)S(1)}, f32[128]{0:T(128)S(1)}, f32[128]{0:T(128)S(1)}) all-reduce(f32[128]{0:T(128)S(1)} %exponential_reduce_fusion, f32[128]{0:T(128)S(1)} %get-tuple-element.3, f32[128]{0:T(128)S(1)} %get-tuple-element.2), channel_id=1, replica_groups=mesh['section'=2,'dp'=16,'vocab'=16] {'vocab'}, use_global_device_ids=true, to_apply=%region_8.0 | all-reduce | flops 384 | bytes 3072 | tf_op jit(solution)/shard_map/psum | solution.py:54
  408.5 0.5 add_multiply_fusion
  409.0 11.0 %fusion.1 = f32[128,1536]{0,1:T(8,128)} fusion(bf16[1536,4096]{1,0:T(8,128)(2,1)} %all-gather.2.cloned.1.call-done, f32[128,4096]{1,0:T(8,128)S(1)} %copy-done.1, f32[128]{0:T(128)S(1)} %get-tuple-element.10, f32[128]{0:T(128)S(1)} %get-tuple-element.9, f32[128]{0:T(128)S(1)} %broadcast_multiply_fusion, f32[16,8,32,128]{3,2,1,0:T(8,128)} %bitcast.16, ...), kind=kOutput, calls=%fused_computation.7 | convolution fusion | flops 1615331328 | bytes 19662336 | tf_op jit(solution)/shard_map/dot_general | solution.py:42
  419.9 0.0 reduce-scatter.2.cloned.1.call-update
  420.0 85.6 %reduce-scatter.2.cloned.1.call-done = f32[128,96]{0,1:T(8,128)} async-done(((f32[128,1536]{0,1:T(8,128)}), f32[128,96]{0,1:T(8,128)}) %reduce-scatter.2.cloned.1.call-update) | async-done | bytes 49168 | tf_op jit(solution)/shard_map/reduce_scatter | solution.py:56
  505.6 1.4 convert_element_type.15
  (2 shorter events, 0.0 us)
Async XLA Ops:
  7.2 272.7 %copy-start = (bf16[128,1536]{1,0:T(8,128)(2,1)S(1)}, bf16[128,1536]{1,0:T(8,128)(2,1)}, u32[]{:S(2)}) copy-start(bf16[128,1536]{1,0:T(8,128)(2,1)} %param.5) | copy-start | bytes 1179652
  7.2 272.7 %all-gather.2.cloned.1.call-start = ((), (), s32[]{:S(2)}) async-start(), calls=%async_computation.1 | async-start | bytes 13369344 | tf_op jit(solution)/shard_map/all_gather | solution.py:48
  7.9 312.9 %all-reduce.3.cloned.1.call-start = ((), (), s32[]{:S(2)}) async-start(), calls=%async_computation.2 | async-start | bytes 4194304 | tf_op jit(solution)/shard_map/psum | solution.py:50
  287.6 0.7 copy-start.3
  287.6 0.8 copy-start.4
  287.7 217.9 %reduce-scatter.2.cloned.1.call-start = ((), (), s32[]{:S(2)}) async-start(), calls=%async_computation.3 | async-start | bytes 835584 | tf_op jit(solution)/shard_map/reduce_scatter | solution.py:56
  320.8 1.6 copy-start.1
  321.4 4.6 copy-start.2
Sparse Core Ops, SparseCore 0:
  11.2 268.6 all-gather.1
  287.8 32.9 all-reduce.2
  420.1 85.4 reduce-scatter.1
where the time goes:
time: 514 us
  waiting for transfers between devices  391 us (76%)
  blocking collectives  81.9 us (16%)
  matrix products  18.7 us (4%)
  between operations  13.8 us (3%)
  other arithmetic  6.07 us (1%)
    all_gather x1, waiting for transfers between devices, on_device(): weights = lax.all_gather(head, 'dp', axis=0, tiled=True)  272 us
    reduce_scatter x1, waiting for transfers between devices, on_device(): lax.psum_scatter(grad_terms(logit_grad, weights), 'vocab', scatter_dimens...  85.6 us
    pmax x1, blocking collectives, on_device(): highest = lax.pmax(jnp.max(scaled_s, axis=1), 'vocab')  43.9 us
    psum x1, blocking collectives, on_device(): totals = lax.psum(local_sums(scaled_s, scaled_t, highest), 'vocab')  38 us
    psum x1, waiting for transfers between devices, on_device(): logits = lax.psum(partial_logits, 'section')  32.3 us
    dot_general x1, matrix products, grad_terms(): lax.dot_general(logit_grad, weights, (((1,), (1,)), ((), ())), preferred_...  11 us
  transfers between devices with their start and end apart: 3, of which 3 were waited for; matrix products, arithmetic and copies ran while one was open for 0% of the time, Pallas kernels for 0%

commit v1 on v0

v1 whole, which is shorter than its diff:
```python
import jax
import jax.numpy as jnp
from jax import lax
from jax.sharding import PartitionSpec as P

GROUP = 128
TEMP = 2
NY = 8
NZH = 2
NQ = 16


def flip(x, ds, dz):
    n = NZH * NY
    perm = []
    for s in range(2):
        for zh in range(NZH):
            for y in range(NY):
                perm.append((s * n + zh * NY + y, (s ^ ds) * n + (zh ^ dz) * NY + y))
    return lax.ppermute(x, ("section", "dp"), perm)


def along_y(x, step):
    perm = [(zh * NY + y, zh * NY + (y + step) % NY) for zh in range(NZH) for y in range(NY)]
    return lax.ppermute(x, "dp", perm)


def same_y(per_section):
    n = NZH * NY * NQ
    groups = []
    for y in range(NY):
        rows = [
            [s * n + (zh * NY + y) * NQ + q for zh in range(NZH) for q in range(NQ)]
            for s in range(2)
        ]
        groups += rows if per_section else [rows[0] + rows[1]]
    return groups


def exchange(x, per_section):
    return lax.all_to_all(
        x,
        ("section", "dp", "vocab"),
        split_axis=0,
        concat_axis=0,
        axis_index_groups=same_y(per_section),
        tiled=True,
    )


def teacher_half(codes, exponents):
    rows, groups = exponents.shape
    scale = jnp.exp2(exponents.astype(jnp.float32)) / TEMP
    t = codes.astype(jnp.float32).reshape(rows, groups, GROUP) * scale[:, :, None]
    return t.reshape(rows, groups * GROUP).astype(jnp.bfloat16)


def after(x, *others):
    return lax.optimization_barrier((x,) + others)[0]


def ring(block):
    half = block.shape[0] // 2
    fwd, bwd = block, block
    parts = [(0, 0, block)]
    for step in range(1, NY // 2):
        fwd, bwd = along_y(fwd, 1), along_y(bwd, -1)
        parts.append((-step, 0, fwd))
        parts.append((step, 0, bwd))
    parts.append((NY // 2, 0, along_y(fwd[:half], 1)))
    parts.append((NY // 2, half, along_y(bwd[half:], -1)))
    return parts


def on_device(hidden, head, codes, exponents, loss_weight):
    s = lax.axis_index("section")
    dp = lax.axis_index("dp")
    zh, y = dp // NY, dp % NY
    rows, cols = head.shape
    width = cols // 4
    tok = hidden.shape[0]

    def columns(x, ds, dz):
        at = ((zh ^ dz) * 2 + (s ^ ds)) * width
        return lax.dynamic_slice_in_dim(x, at, width, axis=1)

    def both(mine, other):
        return jnp.where(
            zh == 0, jnp.concatenate([mine, other]), jnp.concatenate([other, mine])
        )

    near = jnp.concatenate([columns(head, 0, 0), flip(columns(head, 1, 0), 1, 0)], axis=0)
    near_parts = ring(near)
    away = lax.dynamic_slice_in_dim(head, (zh ^ 1) * 2 * width, 2 * width, axis=1)
    came = flip(away, 0, 1)
    came_mine = lax.dynamic_slice_in_dim(came, s * width, width, axis=1)
    came_send = lax.dynamic_slice_in_dim(came, (s ^ 1) * width, width, axis=1)
    far = jnp.concatenate([came_mine, flip(came_send, 1, 0)], axis=0)
    far_parts = ring(far)

    weights = jnp.zeros((2, NZH, NY, rows, width), head.dtype)
    for dz, parts in enumerate([near_parts, far_parts]):
        for dy, at, block in parts:
            block = block.reshape(-1, 1, 1, rows, width)
            weights = lax.dynamic_update_slice(
                weights, block, (at // rows, zh ^ dz, (y + dy) % NY, 0, 0)
            )
    weights = weights.reshape(2 * NZH * NY * rows, width)

    hidden = after(hidden, near_parts[1][2])
    h_sec = both(hidden, flip(hidden, 0, 1))
    h_all = jnp.concatenate([h_sec, flip(h_sec, 1, 0)], axis=1)
    teacher = teacher_half(codes, exponents)
    t_send = after(columns(teacher, 0, 1), near_parts[3][2])
    scaled_t = both(columns(teacher, 0, 0), flip(t_send, 0, 1)).astype(jnp.float32)
    weight = both(loss_weight, flip(after(loss_weight, near_parts[3][2]), 0, 1))

    logits = jnp.dot(h_all, weights, preferred_element_type=jnp.float32)
    scaled_s = logits / TEMP
    m = jnp.max(scaled_s, axis=1)
    t_exp = jnp.exp(scaled_t)
    stats = jnp.stack(
        [
            m,
            jnp.sum(jnp.exp(scaled_s - m[:, None]), axis=1),
            jnp.sum(t_exp, axis=1),
            jnp.sum(t_exp * (scaled_t - scaled_s), axis=1),
        ]
    )
    n = 2 * NZH * NQ
    stats = exchange(jnp.broadcast_to(stats[None], (n,) + stats.shape), False)
    top = jnp.max(stats[:, 0], axis=0)
    s_sum = jnp.sum(stats[:, 1] * jnp.exp(stats[:, 0] - top), axis=0)
    t_sum = jnp.sum(stats[:, 2], axis=0)
    cross = jnp.sum(stats[:, 3], axis=0)
    student_lse = top + jnp.log(s_sum)
    teacher_lse = jnp.log(t_sum)
    kl_loss = TEMP * TEMP * (cross / t_sum - teacher_lse + student_lse)
    kl_loss = lax.dynamic_slice_in_dim(kl_loss, zh * tok, tok)

    logit_grad = (
        weight[:, None]
        * TEMP
        * (jnp.exp(scaled_s - student_lse[:, None]) - jnp.exp(scaled_t - teacher_lse[:, None]))
    ).astype(jnp.bfloat16)

    g = lax.dot_general(
        weights, logit_grad, (((1,), (1,)), ((), ())), preferred_element_type=jnp.float32
    ).reshape(2, NQ, rows, 2 * tok)
    g = g[0] + flip(g[1].astype(jnp.bfloat16), 1, 0).astype(jnp.float32)
    g = g.astype(jnp.bfloat16)
    g = jnp.concatenate([g[:, :, :tok], g[:, :, tok:]])
    g = exchange(g, True)
    g = jnp.sum(g.astype(jnp.float32), axis=0)
    return (kl_loss, g.T.astype(jnp.bfloat16))


def solution(mesh):
    in_specs = (
        P("dp", "section"),
        P(("section", "dp"), "vocab"),
        P("dp", "vocab"),
        P("dp", "vocab"),
        P("dp"),
    )
    out_specs = (P("dp"), P("dp", ("section", "vocab")))
    return jax.shard_map(
        on_device, mesh=mesh, in_specs=in_specs, out_specs=out_specs, check_vma=False
    )
```

time: 514 us -> 182 us (0.35)
  the two profiles are of different devices: /device:TPU:8 before, /device:TPU:25 now
where the time goes in v1:
time: 182 us; the launch traced here: 179 us
  starting transfers between devices  113 us (62%)
  waiting for transfers between devices  43.9 us (24%)
  matrix products  7.08 us (4%)
  local copies, waits for them, and re-layouts  6.87 us (4%)
  other arithmetic  6.62 us (4%)
    ppermute x16, starting transfers between devices, along_y(): return lax.ppermute(x, 'dp', perm)  49.2 us
    ppermute x8, starting transfers between devices, flip(): return lax.ppermute(x, ('section', 'dp'), perm)  46.3 us
    all_to_all x2, waiting for transfers between devices, exchange(): lax.all_to_all(x, ('section', 'dp', 'vocab'), split_axis=0, concat_axis=0...  24 us
    all_to_all x2, starting transfers between devices, exchange(): lax.all_to_all(x, ('section', 'dp', 'vocab'), split_axis=0, concat_axis=0...  17.9 us
    ppermute x16, waiting for transfers between devices, along_y(): return lax.ppermute(x, 'dp', perm)  13.7 us
    ppermute x8, waiting for transfers between devices, flip(): return lax.ppermute(x, ('section', 'dp'), perm)  6.23 us
    dot_general x1, matrix products, on_device(): lax.dot_general(weights, logit_grad, (((1,), (1,)), ((), ())), preferred_...  5.08 us
  transfers between devices with their start and end apart: 26, of which 9 were waited for; matrix products, arithmetic and copies ran while one was open for 6% of the time, Pallas kernels for 0%

profile of v1, /device:TPU:25, one launch (start us, length us, event | category | flops | bytes accessed | tf_op | source)
XLA Modules:
  0.0 179.4 jit_solution(17686050402651518266)
XLA Ops:
  0.7 1.1 constant_dynamic-slice_fusion.6
  1.8 2.6 %collective-permute-start = (bf16[96,1024]{1,0:T(8,128)(2,1)S(1)}, bf16[96,1024]{1,0:T(8,128)(2,1)S(1)}, u32[]{:S(2)}, u32[]{:S(2)}) collective-permute-start(bf16[96,1024]{1,0:T(8,128)(2,1)S(1)} %get-tuple-element.21), channel_id=1, source_target_pairs={{0,256},{16,272},{32,288},{48,304},{64,320},{80,336},{96,352},{112... | collective-permute-start | bytes 589832 | tf_op jit(solution)/shard_map/ppermute | solution.py:20
  4.4 1.8 constant_dynamic-slice_fusion.4
  6.1 10.6 %collective-permute-start.11 = (bf16[96,2048]{1,0:T(8,128)(2,1)}, bf16[96,2048]{1,0:T(8,128)(2,1)S(1)}, u32[]{:S(2)}, u32[]{:S(2)}) collective-permute-start(bf16[96,2048]{1,0:T(8,128)(2,1)} %constant_dynamic-slice_fusion.4), channel_id=1, source_target_pairs={{0,128},{16,144},{32,160},{48,176},{64,192},{80,208},{96,224},{112... | collective-permute-start | bytes 1179656 | tf_op jit(solution)/shard_map/ppermute | solution.py:20
  16.8 0.7 exponential_multiply_fusion
  17.6 4.4 %collective-permute-start.1 = (bf16[192,1024]{1,0:T(8,128)(2,1)S(1)}, bf16[192,1024]{1,0:T(8,128)(2,1)S(1)}, u32[]{:S(2)}, u32[]{:S(2)}) collective-permute-start(bf16[192,1024]{1,0:T(8,128)(2,1)S(1)} %pad_maximum_fusion.1), channel_id=1, source_target_pairs={{0,16},{16,32},{32,48},{48,64},{64,80},{80,96},{96,112},{112,0},{1... | collective-permute-start | bytes 1179656 | tf_op jit(solution)/shard_map/ppermute | solution.py:25
  22.1 1.9 %collective-permute-start.4 = (bf16[192,1024]{1,0:T(8,128)(2,1)S(1)}, bf16[192,1024]{1,0:T(8,128)(2,1)S(1)}, u32[]{:S(2)}, u32[]{:S(2)}) collective-permute-start(bf16[192,1024]{1,0:T(8,128)(2,1)S(1)} %pad_maximum_fusion.1), channel_id=1, source_target_pairs={{0,112},{16,0},{32,16},{48,32},{64,48},{80,64},{96,80},{112,96},{1... | collective-permute-start | bytes 1179656 | tf_op jit(solution)/shard_map/ppermute | solution.py:25
  24.0 0.6 mul.79
  24.6 2.9 %fusion = bf16[128,4096]{1,0:T(8,128)(2,1)S(1)} fusion(f32[16,8,32,128]{3,2,1,0:T(8,128)S(1)} %bitcast.77, s32[128,4096]{1,0:T(8,128)} %param.7), kind=kLoop, calls=%fused_computation.1 | loop fusion | flops 1572864 | bytes 5242880 | tf_op jit(solution)/shard_map/convert_element_type | solution.py:55
  27.8 2.5 %collective-permute-start.12 = (bf16[96,1024]{1,0:T(8,128)(2,1)S(1)}, bf16[96,1024]{1,0:T(8,128)(2,1)S(1)}, u32[]{:S(2)}, u32[]{:S(2)}) collective-permute-start(bf16[96,1024]{1,0:T(8,128)(2,1)S(1)} %get-tuple-element.23), channel_id=1, source_target_pairs={{0,256},{16,272},{32,288},{48,304},{64,320},{80,336},{96,352},{112... | collective-permute-start | bytes 589832 | tf_op jit(solution)/shard_map/ppermute | solution.py:20
  30.3 14.4 %collective-permute-start.2 = (bf16[128,1536]{1,0:T(8,128)(2,1)S(1)}, bf16[128,1536]{1,0:T(8,128)(2,1)S(1)}, u32[]{:S(2)}, u32[]{:S(2)}) collective-permute-start(bf16[128,1536]{1,0:T(8,128)(2,1)S(1)} %copy-done.1), channel_id=1, source_target_pairs={{0,128},{16,144},{32,160},{48,176},{64,192},{80,208},{96,224},{112... | collective-permute-start | bytes 1179656 | tf_op jit(solution)/shard_map/ppermute | solution.py:20
  44.8 4.4 %collective-permute-start.5 = (bf16[192,1024]{1,0:T(8,128)(2,1)S(1)}, bf16[192,1024]{1,0:T(8,128)(2,1)S(1)}, u32[]{:S(2)}, u32[]{:S(2)}) collective-permute-start(bf16[192,1024]{1,0:T(8,128)(2,1)S(1)} %collective-permute-done.1), channel_id=1, source_target_pairs={{0,16},{16,32},{32,48},{48,64},{64,80},{80,96},{96,112},{112,0},{1... | collective-permute-start | bytes 1179656 | tf_op jit(solution)/shard_map/ppermute | solution.py:25
  49.2 1.9 %collective-permute-start.6 = (bf16[192,1024]{1,0:T(8,128)(2,1)S(1)}, bf16[192,1024]{1,0:T(8,128)(2,1)S(1)}, u32[]{:S(2)}, u32[]{:S(2)}) collective-permute-start(bf16[192,1024]{1,0:T(8,128)(2,1)S(1)} %collective-permute-done.4), channel_id=1, source_target_pairs={{0,112},{16,0},{32,16},{48,32},{64,48},{80,64},{96,80},{112,96},{1... | collective-permute-start | bytes 1179656 | tf_op jit(solution)/shard_map/ppermute | solution.py:25
  51.1 0.8 broadcast_in_dim.4
  52.0 4.6 %collective-permute-start.13 = (bf16[192,1024]{1,0:T(8,128)(2,1)S(1)}, bf16[192,1024]{1,0:T(8,128)(2,1)S(1)}, u32[]{:S(2)}, u32[]{:S(2)}) collective-permute-start(bf16[192,1024]{1,0:T(8,128)(2,1)S(1)} %pad_maximum_fusion.2), channel_id=1, source_target_pairs={{0,16},{16,32},{32,48},{48,64},{64,80},{80,96},{96,112},{112,0},{1... | collective-permute-start | bytes 1179656 | tf_op jit(solution)/shard_map/ppermute | solution.py:25
  56.6 1.9 %collective-permute-start.14 = (bf16[192,1024]{1,0:T(8,128)(2,1)S(1)}, bf16[192,1024]{1,0:T(8,128)(2,1)S(1)}, u32[]{:S(2)}, u32[]{:S(2)}) collective-permute-start(bf16[192,1024]{1,0:T(8,128)(2,1)S(1)} %pad_maximum_fusion.2), channel_id=1, source_target_pairs={{0,112},{16,0},{32,16},{48,32},{64,48},{80,64},{96,80},{112,96},{1... | collective-permute-start | bytes 1179656 | tf_op jit(solution)/shard_map/ppermute | solution.py:25
  58.6 4.6 %collective-permute-start.7 = (bf16[192,1024]{1,0:T(8,128)(2,1)S(1)}, bf16[192,1024]{1,0:T(8,128)(2,1)S(1)}, u32[]{:S(2)}, u32[]{:S(2)}) collective-permute-start(bf16[192,1024]{1,0:T(8,128)(2,1)S(1)} %collective-permute-done.5), channel_id=1, source_target_pairs={{0,16},{16,32},{32,48},{48,64},{64,80},{80,96},{96,112},{112,0},{1... | collective-permute-start | bytes 1179656 | tf_op jit(solution)/shard_map/ppermute | solution.py:25
  63.2 1.9 %collective-permute-start.8 = (bf16[192,1024]{1,0:T(8,128)(2,1)S(1)}, bf16[192,1024]{1,0:T(8,128)(2,1)S(1)}, u32[]{:S(2)}, u32[]{:S(2)}) collective-permute-start(bf16[192,1024]{1,0:T(8,128)(2,1)S(1)} %collective-permute-done.6), channel_id=1, source_target_pairs={{0,112},{16,0},{32,16},{48,32},{64,48},{80,64},{96,80},{112,96},{1... | collective-permute-start | bytes 1179656 | tf_op jit(solution)/shard_map/ppermute | solution.py:25
  65.3 3.6 %collective-permute-start.3 = (bf16[256,1536]{1,0:T(8,128)(2,1)S(1)}, bf16[256,1536]{1,0:T(8,128)(2,1)S(1)}, u32[]{:S(2)}, u32[]{:S(2)}) collective-permute-start(bf16[256,1536]{1,0:T(8,128)(2,1)S(1)} %maximum_select_fusion), channel_id=1, source_target_pairs={{0,256},{16,272},{32,288},{48,304},{64,320},{80,336},{96,352},{112... | collective-permute-start | bytes 2359304 | tf_op jit(solution)/shard_map/ppermute | solution.py:20
  68.9 4.9 %collective-permute-start.15 = (bf16[192,1024]{1,0:T(8,128)(2,1)S(1)}, bf16[192,1024]{1,0:T(8,128)(2,1)S(1)}, u32[]{:S(2)}, u32[]{:S(2)}) collective-permute-start(bf16[192,1024]{1,0:T(8,128)(2,1)S(1)} %collective-permute-done.13), channel_id=1, source_target_pairs={{0,16},{16,32},{32,48},{48,64},{64,80},{80,96},{96,112},{112,0},{1... | collective-permute-start | bytes 1179656 | tf_op jit(solution)/shard_map/ppermute | solution.py:25
  73.8 1.9 %collective-permute-start.16 = (bf16[192,1024]{1,0:T(8,128)(2,1)S(1)}, bf16[192,1024]{1,0:T(8,128)(2,1)S(1)}, u32[]{:S(2)}, u32[]{:S(2)}) collective-permute-start(bf16[192,1024]{1,0:T(8,128)(2,1)S(1)} %collective-permute-done.14), channel_id=1, source_target_pairs={{0,112},{16,0},{32,16},{48,32},{64,48},{80,64},{96,80},{112,96},{1... | collective-permute-start | bytes 1179656 | tf_op jit(solution)/shard_map/ppermute | solution.py:25
  75.9 3.2 %collective-permute-start.21 = (bf16[128,1024]{1,0:T(8,128)(2,1)S(1)}, bf16[128,1024]{1,0:T(8,128)(2,1)S(1)}, u32[]{:S(2)}, u32[]{:S(2)}) collective-permute-start(bf16[128,1024]{1,0:T(8,128)(2,1)S(1)} %get-tuple-element.6), channel_id=1, source_target_pairs={{0,128},{16,144},{32,160},{48,176},{64,192},{80,208},{96,224},{112... | collective-permute-start | bytes 786440 | tf_op jit(solution)/shard_map/ppermute | solution.py:20
  79.1 0.2 collective-permute-done.8
  79.3 4.3 %collective-permute-start.9 = (bf16[96,1024]{1,0:T(8,128)(2,1)S(1)}, bf16[96,1024]{1,0:T(8,128)(2,1)S(1)}, u32[]{:S(2)}, u32[]{:S(2)}) collective-permute-start(bf16[96,1024]{1,0:T(8,128)(2,1)S(1)} %slice.52), channel_id=1, source_target_pairs={{0,16},{16,32},{32,48},{48,64},{64,80},{80,96},{96,112},{112,0},{1... | collective-permute-start | bytes 589832 | tf_op jit(solution)/shard_map/ppermute | solution.py:25
  83.8 1.9 %collective-permute-start.10 = (bf16[96,1024]{1,0:T(8,128)(2,1)S(1)}, bf16[96,1024]{1,0:T(8,128)(2,1)S(1)}, u32[]{:S(2)}, u32[]{:S(2)}) collective-permute-start(bf16[96,1024]{1,0:T(8,128)(2,1)S(1)} %slice.53), channel_id=1, source_target_pairs={{0,112},{16,0},{32,16},{48,32},{64,48},{80,64},{96,80},{112,96},{1... | collective-permute-start | bytes 589832 | tf_op jit(solution)/shard_map/ppermute | solution.py:25
  85.7 2.4 %collective-permute-done.16 = bf16[192,1024]{1,0:T(8,128)(2,1)S(1)} collective-permute-done((bf16[192,1024]{1,0:T(8,128)(2,1)S(1)}, bf16[192,1024]{1,0:T(8,128)(2,1)S(1)}, u32[]{:S(2)}, u32[]{:S(2)}) %collective-permute-start.16) | collective-permute-done | bytes 393248 | tf_op jit(solution)/shard_map/ppermute | solution.py:25
  88.1 2.2 %collective-permute-start.17 = (bf16[192,1024]{1,0:T(8,128)(2,1)S(1)}, bf16[192,1024]{1,0:T(8,128)(2,1)S(1)}, u32[]{:S(2)}, u32[]{:S(2)}) collective-permute-start(bf16[192,1024]{1,0:T(8,128)(2,1)S(1)} %collective-permute-done.15), channel_id=1, source_target_pairs={{0,16},{16,32},{32,48},{48,64},{64,80},{80,96},{96,112},{112,0},{1... | collective-permute-start | bytes 1179656 | tf_op jit(solution)/shard_map/ppermute | solution.py:25
  90.3 3.1 %collective-permute-start.18 = (bf16[192,1024]{1,0:T(8,128)(2,1)S(1)}, bf16[192,1024]{1,0:T(8,128)(2,1)S(1)}, u32[]{:S(2)}, u32[]{:S(2)}) collective-permute-start(bf16[192,1024]{1,0:T(8,128)(2,1)S(1)} %collective-permute-done.16), channel_id=1, source_target_pairs={{0,112},{16,0},{32,16},{48,32},{64,48},{80,64},{96,80},{112,96},{1... | collective-permute-start | bytes 1179656 | tf_op jit(solution)/shard_map/ppermute | solution.py:25
  93.7 5.9 %collective-permute-done.17 = bf16[192,1024]{1,0:T(8,128)(2,1)S(1)} collective-permute-done((bf16[192,1024]{1,0:T(8,128)(2,1)S(1)}, bf16[192,1024]{1,0:T(8,128)(2,1)S(1)}, u32[]{:S(2)}, u32[]{:S(2)}) %collective-permute-start.17) | collective-permute-done | bytes 393248 | tf_op jit(solution)/shard_map/ppermute | solution.py:25
  99.7 3.0 %collective-permute-start.19 = (bf16[96,1024]{1,0:T(8,128)(2,1)S(1)}, bf16[96,1024]{1,0:T(8,128)(2,1)S(1)}, u32[]{:S(2)}, u32[]{:S(2)}) collective-permute-start(bf16[96,1024]{1,0:T(8,128)(2,1)S(1)} %slice.54), channel_id=1, source_target_pairs={{0,16},{16,32},{32,48},{48,64},{64,80},{80,96},{96,112},{112,0},{1... | collective-permute-start | bytes 589832 | tf_op jit(solution)/shard_map/ppermute | solution.py:25
  102.7 2.3 %collective-permute-start.20 = (bf16[96,1024]{1,0:T(8,128)(2,1)S(1)}, bf16[96,1024]{1,0:T(8,128)(2,1)S(1)}, u32[]{:S(2)}, u32[]{:S(2)}) collective-permute-start(bf16[96,1024]{1,0:T(8,128)(2,1)S(1)} %slice.55), channel_id=1, source_target_pairs={{0,112},{16,0},{32,16},{48,32},{64,48},{80,64},{96,80},{112,96},{1... | collective-permute-start | bytes 589832 | tf_op jit(solution)/shard_map/ppermute | solution.py:25
  105.1 1.0 collective-permute-done.19
  106.1 4.2 %collective-permute-done.20 = bf16[96,1024]{1,0:T(8,128)(2,1)S(1)} collective-permute-done((bf16[96,1024]{1,0:T(8,128)(2,1)S(1)}, bf16[96,1024]{1,0:T(8,128)(2,1)S(1)}, u32[]{:S(2)}, u32[]{:S(2)}) %collective-permute-start.20) | collective-permute-done | bytes 196640 | tf_op jit(solution)/shard_map/ppermute | solution.py:25
  110.4 2.0 %fusion.28 = (f32[256]{0:T(256)S(1)}, f32[256,1024]{1,0:T(8,128)S(1)}) fusion(bf16[3072,1024]{1,0:T(8,128)(2,1)S(1)} %bitcast.78, bf16[256,1536]{1,0:T(8,128)(2,1)S(1)} %collective-permute-done.3, bf16[256,1536]{1,0:T(8,128)(2,1)S(1)} %maximum_select_fusion), kind=kOutput, calls=%fused_computation.71 | convolution fusion | flops 1614282496 | bytes 8913920 | tf_op jit(solution)/shard_map/dot_general | solution.py:118
  112.4 0.6 exponential_reduce_fusion
  113.0 0.7 broadcast_in_dim.5
  113.7 12.5 %all-to-all-start = ((f32[64,4,256]{2,1,0:T(4,128)}), f32[64,4,256]{2,1,0:T(4,128)S(1)}, u32[]{:S(2)}, u32[]{:S(2)}) async-start(f32[64,4,256]{2,1,0:T(4,128)} %broadcast_in_dim.5), calls=%async_computation | async-start | bytes 524288 | tf_op jit(solution)/shard_map/all_to_all | solution.py:41
  126.3 7.3 %collective-permute-start.22 = (f32[128]{0:T(128)S(1)}, f32[128]{0:T(128)S(1)}, u32[]{:S(2)}, u32[]{:S(2)}) collective-permute-start(f32[128]{0:T(128)S(1)} %copy-done.2), channel_id=1, source_target_pairs={{0,128},{16,144},{32,160},{48,176},{64,192},{80,208},{96,224},{112... | collective-permute-start | bytes 1544 | tf_op jit(solution)/shard_map/ppermute | solution.py:20
  133.6 4.3 %collective-permute-done.22 = f32[128]{0:T(128)S(1)} collective-permute-done((f32[128]{0:T(128)S(1)}, f32[128]{0:T(128)S(1)}, u32[]{:S(2)}, u32[]{:S(2)}) %collective-permute-start.22) | collective-permute-done | bytes 544 | tf_op jit(solution)/shard_map/ppermute | solution.py:20
  137.8 1.7 all-to-all-done
  139.9 5.1 %fusion.15 = f32[3072,256]{1,0:T(8,128)S(1)} fusion(bf16[3072,1024]{1,0:T(8,128)(2,1)} %bitcast.79, f32[256,1024]{1,0:T(8,128)S(1)} %get-tuple-element.31, f32[256]{0:T(256)S(1)} %get-tuple-element.29, f32[256]{0:T(256)S(1)} %get-tuple-element.15, f32[256]{0:T(256)S(1)} %fusion.24, bf16[128,1024]{1,0:T(8,128)(2,1)S(1)} %collective-permute-done.21, ...), kind=kOutput, calls=%fused_computation.22 | convolution fusion | flops 1614544896 | bytes 11013121 | tf_op jit(solution)/shard_map/dot_general | solution.py:147
  145.0 2.1 %collective-permute-start.23 = (bf16[16,96,256]{2,1,0:T(8,128)(2,1)S(1)}, bf16[16,96,256]{2,1,0:T(8,128)(2,1)S(1)}, u32[]{:S(2)}, u32[]{:S(2)}) collective-permute-start(bf16[16,96,256]{2,1,0:T(8,128)(2,1)S(1)} %bitcast.87), channel_id=1, source_target_pairs={{0,256},{16,272},{32,288},{48,304},{64,320},{80,336},{96,352},{112... | collective-permute-start | bytes 2359304 | tf_op jit(solution)/shard_map/ppermute | solution.py:20
  147.3 1.9 %collective-permute-done.23 = bf16[16,96,256]{2,1,0:T(8,128)(2,1)S(1)} collective-permute-done((bf16[16,96,256]{2,1,0:T(8,128)(2,1)S(1)}, bf16[16,96,256]{2,1,0:T(8,128)(2,1)S(1)}, u32[]{:S(2)}, u32[]{:S(2)}) %collective-permute-start.23) | collective-permute-done | bytes 786464 | tf_op jit(solution)/shard_map/ppermute | solution.py:20
  149.6 1.0 pad_maximum_fusion
  150.6 5.3 %all-to-all-start.1 = ((bf16[32,96,128]{2,1,0:T(8,128)(2,1)}), bf16[32,96,128]{2,1,0:T(8,128)(2,1)S(1)}, u32[]{:S(2)}, u32[]{:S(2)}) async-start(bf16[32,96,128]{2,1,0:T(8,128)(2,1)} %pad_maximum_fusion), calls=%async_computation.1 | async-start | bytes 1572864 | tf_op jit(solution)/shard_map/all_to_all | solution.py:41
  155.9 0.6 dynamic_slice.31
  156.5 22.2 %all-to-all-done.1 = bf16[32,96,128]{2,1,0:T(8,128)(2,1)S(1)} async-done(((bf16[32,96,128]{2,1,0:T(8,128)(2,1)}), bf16[32,96,128]{2,1,0:T(8,128)(2,1)S(1)}, u32[]{:S(2)}, u32[]{:S(2)}) %all-to-all-start.1) | async-done | bytes 786464 | tf_op jit(solution)/shard_map/all_to_all | solution.py:41
  178.7 0.7 reduce_sum.72
  (60 shorter events, 2.1 us)
Async XLA Ops:
  0.6 29.7 %copy-start.1 = (bf16[128,1536]{1,0:T(8,128)(2,1)S(1)}, bf16[128,1536]{1,0:T(8,128)(2,1)}, u32[]{:S(2)}) copy-start(bf16[128,1536]{1,0:T(8,128)(2,1)} %param.5) | copy-start | bytes 1179652
  1.8 15.8 %collective-permute-start = (bf16[96,1024]{1,0:T(8,128)(2,1)S(1)}, bf16[96,1024]{1,0:T(8,128)(2,1)S(1)}, u32[]{:S(2)}, u32[]{:S(2)}) collective-permute-start(bf16[96,1024]{1,0:T(8,128)(2,1)S(1)} %get-tuple-element.21), channel_id=1, source_target_pairs={{0,256},{16,272},{32,288},{48,304},{64,320},{80,336},{96,352},{112... | collective-permute-start | bytes 589832 | tf_op jit(solution)/shard_map/ppermute | solution.py:20
  6.1 21.6 %collective-permute-start.11 = (bf16[96,2048]{1,0:T(8,128)(2,1)}, bf16[96,2048]{1,0:T(8,128)(2,1)S(1)}, u32[]{:S(2)}, u32[]{:S(2)}) collective-permute-start(bf16[96,2048]{1,0:T(8,128)(2,1)} %constant_dynamic-slice_fusion.4), channel_id=1, source_target_pairs={{0,128},{16,144},{32,160},{48,176},{64,192},{80,208},{96,224},{112... | collective-permute-start | bytes 1179656 | tf_op jit(solution)/shard_map/ppermute | solution.py:20
  17.6 12.7 %collective-permute-start.1 = (bf16[192,1024]{1,0:T(8,128)(2,1)S(1)}, bf16[192,1024]{1,0:T(8,128)(2,1)S(1)}, u32[]{:S(2)}, u32[]{:S(2)}) collective-permute-start(bf16[192,1024]{1,0:T(8,128)(2,1)S(1)} %pad_maximum_fusion.1), channel_id=1, source_target_pairs={{0,16},{16,32},{32,48},{48,64},{64,80},{80,96},{96,112},{112,0},{1... | collective-permute-start | bytes 1179656 | tf_op jit(solution)/shard_map/ppermute | solution.py:25
  22.1 27.1 %collective-permute-start.4 = (bf16[192,1024]{1,0:T(8,128)(2,1)S(1)}, bf16[192,1024]{1,0:T(8,128)(2,1)S(1)}, u32[]{:S(2)}, u32[]{:S(2)}) collective-permute-start(bf16[192,1024]{1,0:T(8,128)(2,1)S(1)} %pad_maximum_fusion.1), channel_id=1, source_target_pairs={{0,112},{16,0},{32,16},{48,32},{64,48},{80,64},{96,80},{112,96},{1... | collective-permute-start | bytes 1179656 | tf_op jit(solution)/shard_map/ppermute | solution.py:25
  27.8 24.2 %collective-permute-start.12 = (bf16[96,1024]{1,0:T(8,128)(2,1)S(1)}, bf16[96,1024]{1,0:T(8,128)(2,1)S(1)}, u32[]{:S(2)}, u32[]{:S(2)}) collective-permute-start(bf16[96,1024]{1,0:T(8,128)(2,1)S(1)} %get-tuple-element.23), channel_id=1, source_target_pairs={{0,256},{16,272},{32,288},{48,304},{64,320},{80,336},{96,352},{112... | collective-permute-start | bytes 589832 | tf_op jit(solution)/shard_map/ppermute | solution.py:20
  30.3 34.8 %collective-permute-start.2 = (bf16[128,1536]{1,0:T(8,128)(2,1)S(1)}, bf16[128,1536]{1,0:T(8,128)(2,1)S(1)}, u32[]{:S(2)}, u32[]{:S(2)}) collective-permute-start(bf16[128,1536]{1,0:T(8,128)(2,1)S(1)} %copy-done.1), channel_id=1, source_target_pairs={{0,128},{16,144},{32,160},{48,176},{64,192},{80,208},{96,224},{112... | collective-permute-start | bytes 1179656 | tf_op jit(solution)/shard_map/ppermute | solution.py:20
  44.8 13.9 %collective-permute-start.5 = (bf16[192,1024]{1,0:T(8,128)(2,1)S(1)}, bf16[192,1024]{1,0:T(8,128)(2,1)S(1)}, u32[]{:S(2)}, u32[]{:S(2)}) collective-permute-start(bf16[192,1024]{1,0:T(8,128)(2,1)S(1)} %collective-permute-done.1), channel_id=1, source_target_pairs={{0,16},{16,32},{32,48},{48,64},{64,80},{80,96},{96,112},{112,0},{1... | collective-permute-start | bytes 1179656 | tf_op jit(solution)/shard_map/ppermute | solution.py:25
  49.2 14.0 %collective-permute-start.6 = (bf16[192,1024]{1,0:T(8,128)(2,1)S(1)}, bf16[192,1024]{1,0:T(8,128)(2,1)S(1)}, u32[]{:S(2)}, u32[]{:S(2)}) collective-permute-start(bf16[192,1024]{1,0:T(8,128)(2,1)S(1)} %collective-permute-done.4), channel_id=1, source_target_pairs={{0,112},{16,0},{32,16},{48,32},{64,48},{80,64},{96,80},{112,96},{1... | collective-permute-start | bytes 1179656 | tf_op jit(solution)/shard_map/ppermute | solution.py:25
  52.0 16.9 %collective-permute-start.13 = (bf16[192,1024]{1,0:T(8,128)(2,1)S(1)}, bf16[192,1024]{1,0:T(8,128)(2,1)S(1)}, u32[]{:S(2)}, u32[]{:S(2)}) collective-permute-start(bf16[192,1024]{1,0:T(8,128)(2,1)S(1)} %pad_maximum_fusion.2), channel_id=1, source_target_pairs={{0,16},{16,32},{32,48},{48,64},{64,80},{80,96},{96,112},{112,0},{1... | collective-permute-start | bytes 1179656 | tf_op jit(solution)/shard_map/ppermute | solution.py:25
  56.6 17.2 %collective-permute-start.14 = (bf16[192,1024]{1,0:T(8,128)(2,1)S(1)}, bf16[192,1024]{1,0:T(8,128)(2,1)S(1)}, u32[]{:S(2)}, u32[]{:S(2)}) collective-permute-start(bf16[192,1024]{1,0:T(8,128)(2,1)S(1)} %pad_maximum_fusion.2), channel_id=1, source_target_pairs={{0,112},{16,0},{32,16},{48,32},{64,48},{80,64},{96,80},{112,96},{1... | collective-permute-start | bytes 1179656 | tf_op jit(solution)/shard_map/ppermute | solution.py:25
  58.6 17.2 %collective-permute-start.7 = (bf16[192,1024]{1,0:T(8,128)(2,1)S(1)}, bf16[192,1024]{1,0:T(8,128)(2,1)S(1)}, u32[]{:S(2)}, u32[]{:S(2)}) collective-permute-start(bf16[192,1024]{1,0:T(8,128)(2,1)S(1)} %collective-permute-done.5), channel_id=1, source_target_pairs={{0,16},{16,32},{32,48},{48,64},{64,80},{80,96},{96,112},{112,0},{1... | collective-permute-start | bytes 1179656 | tf_op jit(solution)/shard_map/ppermute | solution.py:25
  63.2 16.1 %collective-permute-start.8 = (bf16[192,1024]{1,0:T(8,128)(2,1)S(1)}, bf16[192,1024]{1,0:T(8,128)(2,1)S(1)}, u32[]{:S(2)}, u32[]{:S(2)}) collective-permute-start(bf16[192,1024]{1,0:T(8,128)(2,1)S(1)} %collective-permute-done.6), channel_id=1, source_target_pairs={{0,112},{16,0},{32,16},{48,32},{64,48},{80,64},{96,80},{112,96},{1... | collective-permute-start | bytes 1179656 | tf_op jit(solution)/shard_map/ppermute | solution.py:25
  65.3 45.0 %collective-permute-start.3 = (bf16[256,1536]{1,0:T(8,128)(2,1)S(1)}, bf16[256,1536]{1,0:T(8,128)(2,1)S(1)}, u32[]{:S(2)}, u32[]{:S(2)}) collective-permute-start(bf16[256,1536]{1,0:T(8,128)(2,1)S(1)} %maximum_select_fusion), channel_id=1, source_target_pairs={{0,256},{16,272},{32,288},{48,304},{64,320},{80,336},{96,352},{112... | collective-permute-start | bytes 2359304 | tf_op jit(solution)/shard_map/ppermute | solution.py:20
  68.9 14.8 %collective-permute-start.15 = (bf16[192,1024]{1,0:T(8,128)(2,1)S(1)}, bf16[192,1024]{1,0:T(8,128)(2,1)S(1)}, u32[]{:S(2)}, u32[]{:S(2)}) collective-permute-start(bf16[192,1024]{1,0:T(8,128)(2,1)S(1)} %collective-permute-done.13), channel_id=1, source_target_pairs={{0,16},{16,32},{32,48},{48,64},{64,80},{80,96},{96,112},{112,0},{1... | collective-permute-start | bytes 1179656 | tf_op jit(solution)/shard_map/ppermute | solution.py:25
  73.8 14.3 %collective-permute-start.16 = (bf16[192,1024]{1,0:T(8,128)(2,1)S(1)}, bf16[192,1024]{1,0:T(8,128)(2,1)S(1)}, u32[]{:S(2)}, u32[]{:S(2)}) collective-permute-start(bf16[192,1024]{1,0:T(8,128)(2,1)S(1)} %collective-permute-done.14), channel_id=1, source_target_pairs={{0,112},{16,0},{32,16},{48,32},{64,48},{80,64},{96,80},{112,96},{1... | collective-permute-start | bytes 1179656 | tf_op jit(solution)/shard_map/ppermute | solution.py:25
  75.9 36.5 %collective-permute-start.21 = (bf16[128,1024]{1,0:T(8,128)(2,1)S(1)}, bf16[128,1024]{1,0:T(8,128)(2,1)S(1)}, u32[]{:S(2)}, u32[]{:S(2)}) collective-permute-start(bf16[128,1024]{1,0:T(8,128)(2,1)S(1)} %get-tuple-element.6), channel_id=1, source_target_pairs={{0,128},{16,144},{32,160},{48,176},{64,192},{80,208},{96,224},{112... | collective-permute-start | bytes 786440 | tf_op jit(solution)/shard_map/ppermute | solution.py:20
  79.3 11.0 %collective-permute-start.9 = (bf16[96,1024]{1,0:T(8,128)(2,1)S(1)}, bf16[96,1024]{1,0:T(8,128)(2,1)S(1)}, u32[]{:S(2)}, u32[]{:S(2)}) collective-permute-start(bf16[96,1024]{1,0:T(8,128)(2,1)S(1)} %slice.52), channel_id=1, source_target_pairs={{0,16},{16,32},{32,48},{48,64},{64,80},{80,96},{96,112},{112,0},{1... | collective-permute-start | bytes 589832 | tf_op jit(solution)/shard_map/ppermute | solution.py:25
  83.8 9.6 %collective-permute-start.10 = (bf16[96,1024]{1,0:T(8,128)(2,1)S(1)}, bf16[96,1024]{1,0:T(8,128)(2,1)S(1)}, u32[]{:S(2)}, u32[]{:S(2)}) collective-permute-start(bf16[96,1024]{1,0:T(8,128)(2,1)S(1)} %slice.53), channel_id=1, source_target_pairs={{0,112},{16,0},{32,16},{48,32},{64,48},{80,64},{96,80},{112,96},{1... | collective-permute-start | bytes 589832 | tf_op jit(solution)/shard_map/ppermute | solution.py:25
  88.1 11.5 %collective-permute-start.17 = (bf16[192,1024]{1,0:T(8,128)(2,1)S(1)}, bf16[192,1024]{1,0:T(8,128)(2,1)S(1)}, u32[]{:S(2)}, u32[]{:S(2)}) collective-permute-start(bf16[192,1024]{1,0:T(8,128)(2,1)S(1)} %collective-permute-done.15), channel_id=1, source_target_pairs={{0,16},{16,32},{32,48},{48,64},{64,80},{80,96},{96,112},{112,0},{1... | collective-permute-start | bytes 1179656 | tf_op jit(solution)/shard_map/ppermute | solution.py:25
  90.3 12.3 %collective-permute-start.18 = (bf16[192,1024]{1,0:T(8,128)(2,1)S(1)}, bf16[192,1024]{1,0:T(8,128)(2,1)S(1)}, u32[]{:S(2)}, u32[]{:S(2)}) collective-permute-start(bf16[192,1024]{1,0:T(8,128)(2,1)S(1)} %collective-permute-done.16), channel_id=1, source_target_pairs={{0,112},{16,0},{32,16},{48,32},{64,48},{80,64},{96,80},{112,96},{1... | collective-permute-start | bytes 1179656 | tf_op jit(solution)/shard_map/ppermute | solution.py:25
  99.7 6.4 %collective-permute-start.19 = (bf16[96,1024]{1,0:T(8,128)(2,1)S(1)}, bf16[96,1024]{1,0:T(8,128)(2,1)S(1)}, u32[]{:S(2)}, u32[]{:S(2)}) collective-permute-start(bf16[96,1024]{1,0:T(8,128)(2,1)S(1)} %slice.54), channel_id=1, source_target_pairs={{0,16},{16,32},{32,48},{48,64},{64,80},{80,96},{96,112},{112,0},{1... | collective-permute-start | bytes 589832 | tf_op jit(solution)/shard_map/ppermute | solution.py:25
  102.7 7.6 %collective-permute-start.20 = (bf16[96,1024]{1,0:T(8,128)(2,1)S(1)}, bf16[96,1024]{1,0:T(8,128)(2,1)S(1)}, u32[]{:S(2)}, u32[]{:S(2)}) collective-permute-start(bf16[96,1024]{1,0:T(8,128)(2,1)S(1)} %slice.55), channel_id=1, source_target_pairs={{0,112},{16,0},{32,16},{48,32},{64,48},{80,64},{96,80},{112,96},{1... | collective-permute-start | bytes 589832 | tf_op jit(solution)/shard_map/ppermute | solution.py:25
  110.3 2.7 %copy-start = (bf16[2,2,8,96,1024]{4,3,2,1,0:T(8,128)(2,1)}, bf16[2,2,8,96,1024]{4,3,2,1,0:T(8,128)(2,1)S(1)}, u32[]{:S(2)}) copy-start(bf16[2,2,8,96,1024]{4,3,2,1,0:T(8,128)(2,1)S(1)} %bitcast_dynamic-update-slice_fusion) | copy-start | bytes 18874372
  110.3 15.9 %copy-start.2 = (f32[128]{0:T(128)S(1)}, f32[128]{0:T(128)}, u32[]{:S(2)}) copy-start(f32[128]{0:T(128)} %param.9) | copy-start | bytes 1540
  113.7 25.9 %all-to-all-start = ((f32[64,4,256]{2,1,0:T(4,128)}), f32[64,4,256]{2,1,0:T(4,128)S(1)}, u32[]{:S(2)}, u32[]{:S(2)}) async-start(f32[64,4,256]{2,1,0:T(4,128)} %broadcast_in_dim.5), calls=%async_computation | async-start | bytes 524288 | tf_op jit(solution)/shard_map/all_to_all | solution.py:41
  126.3 11.6 %collective-permute-start.22 = (f32[128]{0:T(128)S(1)}, f32[128]{0:T(128)S(1)}, u32[]{:S(2)}, u32[]{:S(2)}) collective-permute-start(f32[128]{0:T(128)S(1)} %copy-done.2), channel_id=1, source_target_pairs={{0,128},{16,144},{32,160},{48,176},{64,192},{80,208},{96,224},{112... | collective-permute-start | bytes 1544 | tf_op jit(solution)/shard_map/ppermute | solution.py:20
  145.0 4.2 %collective-permute-start.23 = (bf16[16,96,256]{2,1,0:T(8,128)(2,1)S(1)}, bf16[16,96,256]{2,1,0:T(8,128)(2,1)S(1)}, u32[]{:S(2)}, u32[]{:S(2)}) collective-permute-start(bf16[16,96,256]{2,1,0:T(8,128)(2,1)S(1)} %bitcast.87), channel_id=1, source_target_pairs={{0,256},{16,272},{32,288},{48,304},{64,320},{80,336},{96,352},{112... | collective-permute-start | bytes 2359304 | tf_op jit(solution)/shard_map/ppermute | solution.py:20
  150.6 28.1 %all-to-all-start.1 = ((bf16[32,96,128]{2,1,0:T(8,128)(2,1)}), bf16[32,96,128]{2,1,0:T(8,128)(2,1)S(1)}, u32[]{:S(2)}, u32[]{:S(2)}) async-start(bf16[32,96,128]{2,1,0:T(8,128)(2,1)} %pad_maximum_fusion), calls=%async_computation.1 | async-start | bytes 1572864 | tf_op jit(solution)/shard_map/all_to_all | solution.py:41

commit v2 on v1

v2 whole, which is shorter than its diff:
```python
import jax
import jax.numpy as jnp
from jax import lax
from jax.sharding import PartitionSpec as P

GROUP = 128
TEMP = 2
NY = 8
NZH = 2
NQ = 16
NZL = 4


def flip(x, ds, dz):
    n = NZH * NY
    perm = []
    for s in range(2):
        for zh in range(NZH):
            for y in range(NY):
                perm.append((s * n + zh * NY + y, (s ^ ds) * n + (zh ^ dz) * NY + y))
    return lax.ppermute(x, ("section", "dp"), perm)


def along_y(x, step):
    perm = [(zh * NY + y, zh * NY + (y + step) % NY) for zh in range(NZH) for y in range(NY)]
    return lax.ppermute(x, "dp", perm)


def exchange(x):
    n = NZH * NY * NQ
    groups = [
        [s * n + (zh * NY + y) * NQ + q for zh in range(NZH) for q in range(NQ)]
        for s in range(2)
        for y in range(NY)
    ]
    return lax.all_to_all(
        x,
        ("section", "dp", "vocab"),
        split_axis=0,
        concat_axis=0,
        axis_index_groups=groups,
        tiled=True,
    )


def teacher_half(codes, exponents):
    rows, groups = exponents.shape
    scale = jnp.exp2(exponents.astype(jnp.float32)) / TEMP
    t = codes.astype(jnp.float32).reshape(rows, groups, GROUP) * scale[:, :, None]
    return t.reshape(rows, groups * GROUP).astype(jnp.bfloat16)


def along_x(x, bit):
    return lax.ppermute(x, "vocab", [(q, q ^ (bit * NZL)) for q in range(NQ)])


def after(x, *others):
    return lax.optimization_barrier((x,) + others)[0]


def reach(block, first3=(), first4=()):
    half = block.shape[0] // 2
    parts, one, two = [(0, 0, block)], {}, {}
    for way in (1, -1):
        one[way] = along_y(block, way)
        parts.append((-way, 0, one[way]))
    for way in (1, -1):
        two[way] = along_y(block, 2 * way)
        parts.append((-2 * way, 0, two[way]))
    for way in (1, -1):
        parts.append((-3 * way, 0, along_y(after(one[way], *first3), 2 * way)))
    for way, at in ((1, 0), (-1, half)):
        send = after(two[way][at : at + half], *first4)
        parts.append((NY // 2, at, along_y(send, 2 * way)))
    return parts


def on_device(hidden, head, codes, exponents, loss_weight):
    s = lax.axis_index("section")
    dp = lax.axis_index("dp")
    zh, y = dp // NY, dp % NY
    x = lax.axis_index("vocab") // NZL
    rows, cols = head.shape
    width = cols // 4
    tok, feats = hidden.shape

    def columns(a, ds, dz):
        at = ((zh ^ dz) * 2 + (s ^ ds)) * width
        return lax.dynamic_slice_in_dim(a, at, width, axis=1)

    def both(mine, other, which, axis=0):
        return jnp.where(
            which == 0,
            jnp.concatenate([mine, other], axis),
            jnp.concatenate([other, mine], axis),
        )

    near = jnp.concatenate([columns(head, 0, 0), flip(columns(head, 1, 0), 1, 0)], axis=0)
    away = lax.dynamic_slice_in_dim(head, (zh ^ 1) * 2 * width, 2 * width, axis=1)
    came = flip(away, 0, 1)
    near_parts = reach(near)
    came = after(came, near_parts[3][2], near_parts[4][2])
    came_mine = lax.dynamic_slice_in_dim(came, s * width, width, axis=1)
    came_send = lax.dynamic_slice_in_dim(came, (s ^ 1) * width, width, axis=1)
    came_flip = flip(came_send, 1, 0)

    teacher = teacher_half(codes, exponents)
    part = feats // 4
    h_send = lax.dynamic_slice_in_dim(hidden, x * part, part, axis=1)
    sent = jnp.concatenate([columns(teacher, 0, 1), h_send], axis=1)
    got = flip(after(sent, came_flip), 0, 1)
    far_parts = reach(jnp.concatenate([came_mine, came_flip], axis=0), (got,))
    scaled_t = both(columns(teacher, 0, 0), got[:, :width], zh).astype(jnp.float32)

    weights = jnp.zeros((2, NZH, NY, rows, width), head.dtype)
    for dz, parts in enumerate([near_parts, far_parts]):
        for dy, at, block in parts:
            block = block.reshape(-1, 1, 1, rows, width)
            weights = lax.dynamic_update_slice(
                weights, block, (at // rows, zh ^ dz, (y + dy) % NY, 0, 0)
            )
    weights = weights.reshape(2 * NZH * NY * rows, width)

    h_other = after(got, *[block for _, _, block in far_parts[1:5]])[:, width:]
    h_other = both(h_other, along_x(h_other, 1), x % 2, axis=1)
    h_other = both(h_other, along_x(h_other, 2), x // 2, axis=1)
    h_sec = both(hidden, h_other, zh)
    h_all = jnp.concatenate([h_sec, flip(h_sec, 1, 0)], axis=1)

    logits = jnp.dot(h_all, weights, preferred_element_type=jnp.float32)
    scaled_s = logits / TEMP
    m = jnp.max(scaled_s, axis=1)
    t_exp = jnp.exp(scaled_t)
    stats = jnp.stack(
        [
            m,
            jnp.sum(jnp.exp(scaled_s - m[:, None]), axis=1),
            jnp.sum(t_exp, axis=1),
            jnp.sum(t_exp * (scaled_t - scaled_s), axis=1),
        ]
    ).reshape(8, tok)

    stats = jnp.stack([stats, flip(stats, 1, 0)])
    top = jnp.max(stats[:, 0:2], axis=0)
    s_sum = jnp.sum(stats[:, 2:4] * jnp.exp(stats[:, 0:2] - top), axis=0)
    rest = jnp.sum(stats[:, 4:8], axis=0)
    tiles = [
        jnp.concatenate([top, s_sum, rest[0:2], rest[2 + z : 3 + z], loss_weight[None]])
        for z in range(NZH)
    ]
    parts = jnp.broadcast_to(jnp.stack(tiles)[:, None], (NZH, NQ, 8, tok))
    parts = exchange(parts.reshape(NZH * NQ, 8, tok))
    top = jnp.max(parts[:, 0:2], axis=0)
    s_sum = jnp.sum(parts[:, 2:4] * jnp.exp(parts[:, 0:2] - top), axis=0)
    t_sum = jnp.sum(parts[:, 4:6], axis=0)
    cross = jnp.sum(parts[:, 6], axis=0)
    weight = jnp.concatenate([parts[0, 7], parts[NQ, 7]])
    student_lse = top + jnp.log(s_sum)
    teacher_lse = jnp.log(t_sum)

    def of_mine(a):
        return lax.dynamic_index_in_dim(a, zh, axis=0, keepdims=False)

    kl_loss = cross / of_mine(t_sum) - of_mine(teacher_lse) + of_mine(student_lse)
    kl_loss = TEMP * TEMP * kl_loss

    student_lse, teacher_lse = student_lse.reshape(2 * tok), teacher_lse.reshape(2 * tok)
    logit_grad = (
        weight[:, None]
        * TEMP
        * (jnp.exp(scaled_s - student_lse[:, None]) - jnp.exp(scaled_t - teacher_lse[:, None]))
    ).astype(jnp.bfloat16)

    g = lax.dot_general(
        weights, logit_grad, (((1,), (1,)), ((), ())), preferred_element_type=jnp.float32
    ).reshape(2, NQ, rows, 2 * tok)
    g = g[0] + flip(g[1].astype(jnp.bfloat16), 1, 0).astype(jnp.float32)
    g = g.astype(jnp.bfloat16).reshape(NQ, rows, 2, tok)
    g = g.transpose(2, 0, 1, 3).reshape(NZH * NQ, rows, tok)
    g = exchange(g)
    g = jnp.sum(g.astype(jnp.float32), axis=0)
    return (kl_loss, g.T.astype(jnp.bfloat16))


def solution(mesh):
    in_specs = (
        P("dp", "section"),
        P(("section", "dp"), "vocab"),
        P("dp", "vocab"),
        P("dp", "vocab"),
        P("dp"),
    )
    out_specs = (P("dp"), P("dp", ("section", "vocab")))
    return jax.shard_map(
        on_device, mesh=mesh, in_specs=in_specs, out_specs=out_specs, check_vma=False
    )
```

time: 182 us -> 215 us (1.18)
  the two profiles are of different devices: /device:TPU:25 before, /device:TPU:1 now
where the time goes in v2:
time: 215 us; the launch traced here: 214 us
  starting transfers between devices  118 us (55%)
  waiting for transfers between devices  58.3 us (27%)
  blocking collectives  16 us (7%)
  matrix products  7.08 us (3%)
  local copies, waits for them, and re-layouts  6.68 us (3%)
  other arithmetic  6.32 us (3%)
    ppermute x16, starting transfers between devices, along_y(): return lax.ppermute(x, 'dp', perm)  65.6 us
    ppermute x7, starting transfers between devices, flip(): return lax.ppermute(x, ('section', 'dp'), perm)  40.4 us
    all_to_all x1, waiting for transfers between devices, exchange(): lax.all_to_all(x, ('section', 'dp', 'vocab'), split_axis=0, concat_axis=0...  22.3 us
    ppermute x7, waiting for transfers between devices, flip(): return lax.ppermute(x, ('section', 'dp'), perm)  18 us
    all_to_all x1, blocking collectives, exchange(): lax.all_to_all(x, ('section', 'dp', 'vocab'), split_axis=0, concat_axis=0...  16 us
    ppermute x16, waiting for transfers between devices, along_y(): return lax.ppermute(x, 'dp', perm)  12.1 us
    ppermute x2, starting transfers between devices, along_x(): return lax.ppermute(x, 'vocab', [(q, q ^ bit * NZL) for q in range(NQ)])  7.77 us
    ppermute x2, waiting for transfers between devices, along_x(): return lax.ppermute(x, 'vocab', [(q, q ^ bit * NZL) for q in range(NQ)])  5.93 us
  transfers between devices with their start and end apart: 26, of which 10 were waited for; matrix products, arithmetic and copies ran while one was open for 4% of the time, Pallas kernels for 0%

profile of v2, /device:TPU:1, one launch (start us, length us, event | category | flops | bytes accessed | tf_op | source)
XLA Modules:
  0.0 213.7 jit_solution(1069876556220249929)
XLA Ops:
  0.7 1.1 constant_dynamic-slice_fusion.7
  1.8 8.8 %collective-permute-start.1 = (bf16[96,1024]{1,0:T(8,128)(2,1)S(1)}, bf16[96,1024]{1,0:T(8,128)(2,1)S(1)}, u32[]{:S(2)}, u32[]{:S(2)}) collective-permute-start(bf16[96,1024]{1,0:T(8,128)(2,1)S(1)} %get-tuple-element.20), channel_id=1, source_target_pairs={{0,256},{16,272},{32,288},{48,304},{64,320},{80,336},{96,352},{112... | collective-permute-start | bytes 589832 | tf_op jit(solution)/shard_map/ppermute | solution.py:21
  10.6 1.8 constant_dynamic-slice_fusion.8
  12.4 5.2 %collective-permute-start = (bf16[96,2048]{1,0:T(8,128)(2,1)}, bf16[96,2048]{1,0:T(8,128)(2,1)S(1)}, u32[]{:S(2)}, u32[]{:S(2)}) collective-permute-start(bf16[96,2048]{1,0:T(8,128)(2,1)} %constant_dynamic-slice_fusion.8), channel_id=1, source_target_pairs={{0,128},{16,144},{32,160},{48,176},{64,192},{80,208},{96,224},{112... | collective-permute-start | bytes 1179656 | tf_op jit(solution)/shard_map/ppermute | solution.py:21
  17.6 0.7 exponential_multiply_fusion
  18.4 0.6 mul.76
  19.1 2.9 %fusion = bf16[128,4096]{1,0:T(8,128)(2,1)S(1)} fusion(f32[16,8,32,128]{3,2,1,0:T(8,128)S(1)} %bitcast.103, s32[128,4096]{1,0:T(8,128)} %param.7), kind=kLoop, calls=%fused_computation.1 | loop fusion | flops 1572864 | bytes 5242880 | tf_op jit(solution)/shard_map/convert_element_type | solution.py:50
  22.1 3.2 %collective-permute-start.13 = (bf16[192,1024]{1,0:T(8,128)(2,1)S(1)}, bf16[192,1024]{1,0:T(8,128)(2,1)S(1)}, u32[]{:S(2)}, u32[]{:S(2)}) collective-permute-start(bf16[192,1024]{1,0:T(8,128)(2,1)S(1)} %pad_maximum_fusion), channel_id=1, source_target_pairs={{0,16},{16,32},{32,48},{48,64},{64,80},{80,96},{96,112},{112,0},{1... | collective-permute-start | bytes 1179656 | tf_op jit(solution)/shard_map/ppermute | solution.py:26
  25.3 3.8 %collective-permute-start.14 = (bf16[192,1024]{1,0:T(8,128)(2,1)S(1)}, bf16[192,1024]{1,0:T(8,128)(2,1)S(1)}, u32[]{:S(2)}, u32[]{:S(2)}) collective-permute-start(bf16[192,1024]{1,0:T(8,128)(2,1)S(1)} %pad_maximum_fusion), channel_id=1, source_target_pairs={{0,112},{16,0},{32,16},{48,32},{64,48},{80,64},{96,80},{112,96},{1... | collective-permute-start | bytes 1179656 | tf_op jit(solution)/shard_map/ppermute | solution.py:26
  29.1 2.5 %collective-permute-start.2 = (bf16[192,1024]{1,0:T(8,128)(2,1)S(1)}, bf16[192,1024]{1,0:T(8,128)(2,1)S(1)}, u32[]{:S(2)}, u32[]{:S(2)}) collective-permute-start(bf16[192,1024]{1,0:T(8,128)(2,1)S(1)} %pad_maximum_fusion), channel_id=1, source_target_pairs={{0,32},{16,48},{32,64},{48,80},{64,96},{80,112},{96,0},{112,16},{1... | collective-permute-start | bytes 1179656 | tf_op jit(solution)/shard_map/ppermute | solution.py:26
  31.6 4.9 %collective-permute-start.3 = (bf16[192,1024]{1,0:T(8,128)(2,1)S(1)}, bf16[192,1024]{1,0:T(8,128)(2,1)S(1)}, u32[]{:S(2)}, u32[]{:S(2)}) collective-permute-start(bf16[192,1024]{1,0:T(8,128)(2,1)S(1)} %pad_maximum_fusion), channel_id=1, source_target_pairs={{0,96},{16,112},{32,0},{48,16},{64,32},{80,48},{96,64},{112,80},{1... | collective-permute-start | bytes 1179656 | tf_op jit(solution)/shard_map/ppermute | solution.py:26
  36.9 0.8 broadcast_in_dim.6
  37.7 3.6 %collective-permute-start.15 = (bf16[192,1024]{1,0:T(8,128)(2,1)S(1)}, bf16[192,1024]{1,0:T(8,128)(2,1)S(1)}, u32[]{:S(2)}, u32[]{:S(2)}) collective-permute-start(bf16[192,1024]{1,0:T(8,128)(2,1)S(1)} %collective-permute-done.13), channel_id=1, source_target_pairs={{0,32},{16,48},{32,64},{48,80},{64,96},{80,112},{96,0},{112,16},{1... | collective-permute-start | bytes 1179656 | tf_op jit(solution)/shard_map/ppermute | solution.py:26
  41.4 3.7 %collective-permute-start.16 = (bf16[192,1024]{1,0:T(8,128)(2,1)S(1)}, bf16[192,1024]{1,0:T(8,128)(2,1)S(1)}, u32[]{:S(2)}, u32[]{:S(2)}) collective-permute-start(bf16[192,1024]{1,0:T(8,128)(2,1)S(1)} %collective-permute-done.14), channel_id=1, source_target_pairs={{0,96},{16,112},{32,0},{48,16},{64,32},{80,48},{96,64},{112,80},{1... | collective-permute-start | bytes 1179656 | tf_op jit(solution)/shard_map/ppermute | solution.py:26
  45.1 2.1 %collective-permute-done.2 = bf16[192,1024]{1,0:T(8,128)(2,1)S(1)} collective-permute-done((bf16[192,1024]{1,0:T(8,128)(2,1)S(1)}, bf16[192,1024]{1,0:T(8,128)(2,1)S(1)}, u32[]{:S(2)}, u32[]{:S(2)}) %collective-permute-start.2) | collective-permute-done | bytes 393248 | tf_op jit(solution)/shard_map/ppermute | solution.py:26
  47.3 2.4 %collective-permute-start.17 = (bf16[96,1024]{1,0:T(8,128)(2,1)S(1)}, bf16[96,1024]{1,0:T(8,128)(2,1)S(1)}, u32[]{:S(2)}, u32[]{:S(2)}) collective-permute-start(bf16[96,1024]{1,0:T(8,128)(2,1)S(1)} %slice.87), channel_id=1, source_target_pairs={{0,32},{16,48},{32,64},{48,80},{64,96},{80,112},{96,0},{112,16},{1... | collective-permute-start | bytes 589832 | tf_op jit(solution)/shard_map/ppermute | solution.py:26
  49.7 9.9 %collective-permute-done.3 = bf16[192,1024]{1,0:T(8,128)(2,1)S(1)} collective-permute-done((bf16[192,1024]{1,0:T(8,128)(2,1)S(1)}, bf16[192,1024]{1,0:T(8,128)(2,1)S(1)}, u32[]{:S(2)}, u32[]{:S(2)}) %collective-permute-start.3) | collective-permute-done | bytes 393248 | tf_op jit(solution)/shard_map/ppermute | solution.py:26
  59.6 6.4 %collective-permute-start.18 = (bf16[96,1024]{1,0:T(8,128)(2,1)S(1)}, bf16[96,1024]{1,0:T(8,128)(2,1)S(1)}, u32[]{:S(2)}, u32[]{:S(2)}) collective-permute-start(bf16[96,1024]{1,0:T(8,128)(2,1)S(1)} %slice.88), channel_id=1, source_target_pairs={{0,96},{16,112},{32,0},{48,16},{64,32},{80,48},{96,64},{112,80},{1... | collective-permute-start | bytes 589832 | tf_op jit(solution)/shard_map/ppermute | solution.py:26
  66.0 4.0 %collective-permute-start.4 = (bf16[96,1024]{1,0:T(8,128)(2,1)S(1)}, bf16[96,1024]{1,0:T(8,128)(2,1)S(1)}, u32[]{:S(2)}, u32[]{:S(2)}) collective-permute-start(bf16[96,1024]{1,0:T(8,128)(2,1)S(1)} %get-tuple-element.22), channel_id=1, source_target_pairs={{0,256},{16,272},{32,288},{48,304},{64,320},{80,336},{96,352},{112... | collective-permute-start | bytes 589832 | tf_op jit(solution)/shard_map/ppermute | solution.py:21
  70.3 0.9 collective-permute-done.4
  71.1 10.2 %collective-permute-start.6 = (bf16[192,1024]{1,0:T(8,128)(2,1)S(1)}, bf16[192,1024]{1,0:T(8,128)(2,1)S(1)}, u32[]{:S(2)}, u32[]{:S(2)}) collective-permute-start(bf16[192,1024]{1,0:T(8,128)(2,1)S(1)} %pad_maximum_fusion.1), channel_id=1, source_target_pairs={{0,16},{16,32},{32,48},{48,64},{64,80},{80,96},{96,112},{112,0},{1... | collective-permute-start | bytes 1179656 | tf_op jit(solution)/shard_map/ppermute | solution.py:26
  81.3 2.5 %collective-permute-start.7 = (bf16[192,1024]{1,0:T(8,128)(2,1)S(1)}, bf16[192,1024]{1,0:T(8,128)(2,1)S(1)}, u32[]{:S(2)}, u32[]{:S(2)}) collective-permute-start(bf16[192,1024]{1,0:T(8,128)(2,1)S(1)} %pad_maximum_fusion.1), channel_id=1, source_target_pairs={{0,112},{16,0},{32,16},{48,32},{64,48},{80,64},{96,80},{112,96},{1... | collective-permute-start | bytes 1179656 | tf_op jit(solution)/shard_map/ppermute | solution.py:26
  83.8 3.1 %collective-permute-start.8 = (bf16[192,1024]{1,0:T(8,128)(2,1)S(1)}, bf16[192,1024]{1,0:T(8,128)(2,1)S(1)}, u32[]{:S(2)}, u32[]{:S(2)}) collective-permute-start(bf16[192,1024]{1,0:T(8,128)(2,1)S(1)} %pad_maximum_fusion.1), channel_id=1, source_target_pairs={{0,32},{16,48},{32,64},{48,80},{64,96},{80,112},{96,0},{112,16},{1... | collective-permute-start | bytes 1179656 | tf_op jit(solution)/shard_map/ppermute | solution.py:26
  87.0 4.6 %collective-permute-start.9 = (bf16[192,1024]{1,0:T(8,128)(2,1)S(1)}, bf16[192,1024]{1,0:T(8,128)(2,1)S(1)}, u32[]{:S(2)}, u32[]{:S(2)}) collective-permute-start(bf16[192,1024]{1,0:T(8,128)(2,1)S(1)} %pad_maximum_fusion.1), channel_id=1, source_target_pairs={{0,96},{16,112},{32,0},{48,16},{64,32},{80,48},{96,64},{112,80},{1... | collective-permute-start | bytes 1179656 | tf_op jit(solution)/shard_map/ppermute | solution.py:26
  91.6 1.9 collective-permute-start.5
  93.6 13.0 %collective-permute-done.5 = bf16[128,1408]{1,0:T(8,128)(2,1)S(1)} collective-permute-done((bf16[128,1408]{1,0:T(8,128)(2,1)S(1)}, bf16[128,1408]{1,0:T(8,128)(2,1)S(1)}, u32[]{:S(2)}, u32[]{:S(2)}) %collective-permute-start.5) | collective-permute-done | bytes 360480 | tf_op jit(solution)/shard_map/ppermute | solution.py:21
  106.6 3.1 %collective-permute-start.19 = (bf16[192,1024]{1,0:T(8,128)(2,1)S(1)}, bf16[192,1024]{1,0:T(8,128)(2,1)S(1)}, u32[]{:S(2)}, u32[]{:S(2)}) collective-permute-start(bf16[192,1024]{1,0:T(8,128)(2,1)S(1)} %collective-permute-done.6), channel_id=1, source_target_pairs={{0,32},{16,48},{32,64},{48,80},{64,96},{80,112},{96,0},{112,16},{1... | collective-permute-start | bytes 1179656 | tf_op jit(solution)/shard_map/ppermute | solution.py:26
  109.7 4.3 %collective-permute-start.20 = (bf16[192,1024]{1,0:T(8,128)(2,1)S(1)}, bf16[192,1024]{1,0:T(8,128)(2,1)S(1)}, u32[]{:S(2)}, u32[]{:S(2)}) collective-permute-start(bf16[192,1024]{1,0:T(8,128)(2,1)S(1)} %collective-permute-done.7), channel_id=1, source_target_pairs={{0,96},{16,112},{32,0},{48,16},{64,32},{80,48},{96,64},{112,80},{1... | collective-permute-start | bytes 1179656 | tf_op jit(solution)/shard_map/ppermute | solution.py:26
  114.1 2.8 %collective-permute-start.21 = (bf16[96,1024]{1,0:T(8,128)(2,1)S(1)}, bf16[96,1024]{1,0:T(8,128)(2,1)S(1)}, u32[]{:S(2)}, u32[]{:S(2)}) collective-permute-start(bf16[96,1024]{1,0:T(8,128)(2,1)S(1)} %slice.89), channel_id=1, source_target_pairs={{0,32},{16,48},{32,64},{48,80},{64,96},{80,112},{96,0},{112,16},{1... | collective-permute-start | bytes 589832 | tf_op jit(solution)/shard_map/ppermute | solution.py:26
  116.9 4.6 %collective-permute-start.22 = (bf16[96,1024]{1,0:T(8,128)(2,1)S(1)}, bf16[96,1024]{1,0:T(8,128)(2,1)S(1)}, u32[]{:S(2)}, u32[]{:S(2)}) collective-permute-start(bf16[96,1024]{1,0:T(8,128)(2,1)S(1)} %slice.90), channel_id=1, source_target_pairs={{0,96},{16,112},{32,0},{48,16},{64,32},{80,48},{96,64},{112,80},{1... | collective-permute-start | bytes 589832 | tf_op jit(solution)/shard_map/ppermute | solution.py:26
  121.5 3.1 %collective-permute-start.10 = (bf16[128,384]{1,0:T(8,128)(2,1)S(1)}, bf16[128,384]{1,0:T(8,128)(2,1)S(1)}, u32[]{:S(2)}, u32[]{:S(2)}) collective-permute-start(bf16[128,384]{1,0:T(8,128)(2,1)S(1)} %slice.67), channel_id=1, source_target_pairs={{0,4},{1,5},{2,6},{3,7},{4,0},{5,1},{6,2},{7,3},{8,12},{9,13},{10,... | collective-permute-start | bytes 294920 | tf_op jit(solution)/shard_map/ppermute | solution.py:54
  124.7 2.5 %collective-permute-done.10 = bf16[128,384]{1,0:T(8,128)(2,1)S(1)} collective-permute-done((bf16[128,384]{1,0:T(8,128)(2,1)S(1)}, bf16[128,384]{1,0:T(8,128)(2,1)S(1)}, u32[]{:S(2)}, u32[]{:S(2)}) %collective-permute-start.10) | collective-permute-done | bytes 98336 | tf_op jit(solution)/shard_map/ppermute | solution.py:54
  127.3 4.7 %collective-permute-start.11 = (bf16[128,768]{1,0:T(8,128)(2,1)S(1)}, bf16[128,768]{1,0:T(8,128)(2,1)S(1)}, u32[]{:S(2)}, u32[]{:S(2)}) collective-permute-start(bf16[128,768]{1,0:T(8,128)(2,1)S(1)} %maximum_select_fusion.3), channel_id=1, source_target_pairs={{0,8},{1,9},{2,10},{3,11},{4,12},{5,13},{6,14},{7,15},{8,0},{9,1},... | collective-permute-start | bytes 589832 | tf_op jit(solution)/shard_map/ppermute | solution.py:54
  132.0 3.5 %collective-permute-done.11 = bf16[128,768]{1,0:T(8,128)(2,1)S(1)} collective-permute-done((bf16[128,768]{1,0:T(8,128)(2,1)S(1)}, bf16[128,768]{1,0:T(8,128)(2,1)S(1)}, u32[]{:S(2)}, u32[]{:S(2)}) %collective-permute-start.11) | collective-permute-done | bytes 196640 | tf_op jit(solution)/shard_map/ppermute | solution.py:54
  135.7 14.1 %collective-permute-start.12 = (bf16[256,1536]{1,0:T(8,128)(2,1)S(1)}, bf16[256,1536]{1,0:T(8,128)(2,1)S(1)}, u32[]{:S(2)}, u32[]{:S(2)}) collective-permute-start(bf16[256,1536]{1,0:T(8,128)(2,1)S(1)} %maximum_select_fusion), channel_id=1, source_target_pairs={{0,256},{16,272},{32,288},{48,304},{64,320},{80,336},{96,352},{112... | collective-permute-start | bytes 2359304 | tf_op jit(solution)/shard_map/ppermute | solution.py:21
  150.1 1.6 collective-permute-done.12
  151.7 2.0 fusion.32
  153.7 0.6 exponential_reduce_fusion
  154.3 2.3 %collective-permute-start.23 = (f32[8,128]{1,0:T(8,128)S(1)}, f32[8,128]{1,0:T(8,128)S(1)}, u32[]{:S(2)}, u32[]{:S(2)}) collective-permute-start(f32[8,128]{1,0:T(8,128)S(1)} %reshape.142), channel_id=1, source_target_pairs={{0,256},{16,272},{32,288},{48,304},{64,320},{80,336},{96,352},{112... | collective-permute-start | bytes 12296 | tf_op jit(solution)/shard_map/ppermute | solution.py:21
  156.6 0.8 collective-permute-done.23
  157.5 16.0 %all_to_all.10 = f32[32,8,128]{2,1,0:T(8,128)S(1)} all-to-all(f32[32,8,128]{2,1,0:T(8,128)S(1)} %bitcast.115), channel_id=1, replica_groups={{0,1,2,3,4,5,6,7,8,9,10,11,12,13,14,15,128,129,130,131,132,133,134,135,..., dimensions={0} | all-to-all | bytes 262144 | tf_op jit(solution)/shard_map/all_to_all | solution.py:36
  173.7 5.1 %fusion.15 = f32[3072,256]{1,0:T(8,128)S(1)} fusion(bf16[3072,1024]{1,0:T(8,128)(2,1)} %bitcast.105, f32[256,1024]{1,0:T(8,128)S(1)} %get-tuple-element.28, f32[256]{0:T(256)S(1)} %get-tuple-element.25, f32[256]{0:T(256)S(1)} %bitcast.134, f32[256]{0:T(256)S(1)} %maximum_multiply_fusion.1, bf16[128,1024]{1,0:T(8,128)(2,1)S(1)} %slice.91, ...), kind=kOutput, calls=%fused_computation.21 | convolution fusion | flops 1614544896 | bytes 11013121 | tf_op jit(solution)/shard_map/dot_general | solution.py:174
  178.9 4.0 %collective-permute-start.24 = (bf16[16,96,256]{2,1,0:T(8,128)(2,1)S(1)}, bf16[16,96,256]{2,1,0:T(8,128)(2,1)S(1)}, u32[]{:S(2)}, u32[]{:S(2)}) collective-permute-start(bf16[16,96,256]{2,1,0:T(8,128)(2,1)S(1)} %bitcast.114), channel_id=1, source_target_pairs={{0,256},{16,272},{32,288},{48,304},{64,320},{80,336},{96,352},{112... | collective-permute-start | bytes 2359304 | tf_op jit(solution)/shard_map/ppermute | solution.py:21
  183.0 1.8 collective-permute-done.24
  185.2 1.0 copy.68
  186.2 3.9 %all-to-all-start.1 = ((bf16[32,96,128]{2,1,0:T(8,128)(2,1)}), bf16[32,96,128]{2,1,0:T(8,128)(2,1)S(1)}, u32[]{:S(2)}, u32[]{:S(2)}) async-start(bf16[32,96,128]{2,1,0:T(8,128)(2,1)} %bitcast.52), calls=%async_computation.1 | async-start | bytes 1572864 | tf_op jit(solution)/shard_map/all_to_all | solution.py:36
  190.7 22.3 %all-to-all-done.1 = bf16[32,96,128]{2,1,0:T(8,128)(2,1)S(1)} async-done(((bf16[32,96,128]{2,1,0:T(8,128)(2,1)}), bf16[32,96,128]{2,1,0:T(8,128)(2,1)S(1)}, u32[]{:S(2)}, u32[]{:S(2)}) %all-to-all-start.1) | async-done | bytes 786464 | tf_op jit(solution)/shard_map/all_to_all | solution.py:36
  213.0 0.7 reduce_sum.92
  (79 shorter events, 2.8 us)
Async XLA Ops:
  0.6 35.9 %copy-start.1 = (bf16[128,1536]{1,0:T(8,128)(2,1)S(1)}, bf16[128,1536]{1,0:T(8,128)(2,1)}, u32[]{:S(2)}) copy-start(bf16[128,1536]{1,0:T(8,128)(2,1)} %param.5) | copy-start | bytes 1179652
  1.8 20.3 %collective-permute-start.1 = (bf16[96,1024]{1,0:T(8,128)(2,1)S(1)}, bf16[96,1024]{1,0:T(8,128)(2,1)S(1)}, u32[]{:S(2)}, u32[]{:S(2)}) collective-permute-start(bf16[96,1024]{1,0:T(8,128)(2,1)S(1)} %get-tuple-element.20), channel_id=1, source_target_pairs={{0,256},{16,272},{32,288},{48,304},{64,320},{80,336},{96,352},{112... | collective-permute-start | bytes 589832 | tf_op jit(solution)/shard_map/ppermute | solution.py:21
  12.4 53.6 %collective-permute-start = (bf16[96,2048]{1,0:T(8,128)(2,1)}, bf16[96,2048]{1,0:T(8,128)(2,1)S(1)}, u32[]{:S(2)}, u32[]{:S(2)}) collective-permute-start(bf16[96,2048]{1,0:T(8,128)(2,1)} %constant_dynamic-slice_fusion.8), channel_id=1, source_target_pairs={{0,128},{16,144},{32,160},{48,176},{64,192},{80,208},{96,224},{112... | collective-permute-start | bytes 1179656 | tf_op jit(solution)/shard_map/ppermute | solution.py:21
  22.1 15.6 %collective-permute-start.13 = (bf16[192,1024]{1,0:T(8,128)(2,1)S(1)}, bf16[192,1024]{1,0:T(8,128)(2,1)S(1)}, u32[]{:S(2)}, u32[]{:S(2)}) collective-permute-start(bf16[192,1024]{1,0:T(8,128)(2,1)S(1)} %pad_maximum_fusion), channel_id=1, source_target_pairs={{0,16},{16,32},{32,48},{48,64},{64,80},{80,96},{96,112},{112,0},{1... | collective-permute-start | bytes 1179656 | tf_op jit(solution)/shard_map/ppermute | solution.py:26
  25.3 16.1 %collective-permute-start.14 = (bf16[192,1024]{1,0:T(8,128)(2,1)S(1)}, bf16[192,1024]{1,0:T(8,128)(2,1)S(1)}, u32[]{:S(2)}, u32[]{:S(2)}) collective-permute-start(bf16[192,1024]{1,0:T(8,128)(2,1)S(1)} %pad_maximum_fusion), channel_id=1, source_target_pairs={{0,112},{16,0},{32,16},{48,32},{64,48},{80,64},{96,80},{112,96},{1... | collective-permute-start | bytes 1179656 | tf_op jit(solution)/shard_map/ppermute | solution.py:26
  29.1 18.1 %collective-permute-start.2 = (bf16[192,1024]{1,0:T(8,128)(2,1)S(1)}, bf16[192,1024]{1,0:T(8,128)(2,1)S(1)}, u32[]{:S(2)}, u32[]{:S(2)}) collective-permute-start(bf16[192,1024]{1,0:T(8,128)(2,1)S(1)} %pad_maximum_fusion), channel_id=1, source_target_pairs={{0,32},{16,48},{32,64},{48,80},{64,96},{80,112},{96,0},{112,16},{1... | collective-permute-start | bytes 1179656 | tf_op jit(solution)/shard_map/ppermute | solution.py:26
  31.6 28.0 %collective-permute-start.3 = (bf16[192,1024]{1,0:T(8,128)(2,1)S(1)}, bf16[192,1024]{1,0:T(8,128)(2,1)S(1)}, u32[]{:S(2)}, u32[]{:S(2)}) collective-permute-start(bf16[192,1024]{1,0:T(8,128)(2,1)S(1)} %pad_maximum_fusion), channel_id=1, source_target_pairs={{0,96},{16,112},{32,0},{48,16},{64,32},{80,48},{96,64},{112,80},{1... | collective-permute-start | bytes 1179656 | tf_op jit(solution)/shard_map/ppermute | solution.py:26
  37.7 43.6 %collective-permute-start.15 = (bf16[192,1024]{1,0:T(8,128)(2,1)S(1)}, bf16[192,1024]{1,0:T(8,128)(2,1)S(1)}, u32[]{:S(2)}, u32[]{:S(2)}) collective-permute-start(bf16[192,1024]{1,0:T(8,128)(2,1)S(1)} %collective-permute-done.13), channel_id=1, source_target_pairs={{0,32},{16,48},{32,64},{48,80},{64,96},{80,112},{96,0},{112,16},{1... | collective-permute-start | bytes 1179656 | tf_op jit(solution)/shard_map/ppermute | solution.py:26
  41.4 42.5 %collective-permute-start.16 = (bf16[192,1024]{1,0:T(8,128)(2,1)S(1)}, bf16[192,1024]{1,0:T(8,128)(2,1)S(1)}, u32[]{:S(2)}, u32[]{:S(2)}) collective-permute-start(bf16[192,1024]{1,0:T(8,128)(2,1)S(1)} %collective-permute-done.14), channel_id=1, source_target_pairs={{0,96},{16,112},{32,0},{48,16},{64,32},{80,48},{96,64},{112,80},{1... | collective-permute-start | bytes 1179656 | tf_op jit(solution)/shard_map/ppermute | solution.py:26
  47.3 39.7 %collective-permute-start.17 = (bf16[96,1024]{1,0:T(8,128)(2,1)S(1)}, bf16[96,1024]{1,0:T(8,128)(2,1)S(1)}, u32[]{:S(2)}, u32[]{:S(2)}) collective-permute-start(bf16[96,1024]{1,0:T(8,128)(2,1)S(1)} %slice.87), channel_id=1, source_target_pairs={{0,32},{16,48},{32,64},{48,80},{64,96},{80,112},{96,0},{112,16},{1... | collective-permute-start | bytes 589832 | tf_op jit(solution)/shard_map/ppermute | solution.py:26
  59.6 32.0 %collective-permute-start.18 = (bf16[96,1024]{1,0:T(8,128)(2,1)S(1)}, bf16[96,1024]{1,0:T(8,128)(2,1)S(1)}, u32[]{:S(2)}, u32[]{:S(2)}) collective-permute-start(bf16[96,1024]{1,0:T(8,128)(2,1)S(1)} %slice.88), channel_id=1, source_target_pairs={{0,96},{16,112},{32,0},{48,16},{64,32},{80,48},{96,64},{112,80},{1... | collective-permute-start | bytes 589832 | tf_op jit(solution)/shard_map/ppermute | solution.py:26
  66.0 5.1 %collective-permute-start.4 = (bf16[96,1024]{1,0:T(8,128)(2,1)S(1)}, bf16[96,1024]{1,0:T(8,128)(2,1)S(1)}, u32[]{:S(2)}, u32[]{:S(2)}) collective-permute-start(bf16[96,1024]{1,0:T(8,128)(2,1)S(1)} %get-tuple-element.22), channel_id=1, source_target_pairs={{0,256},{16,272},{32,288},{48,304},{64,320},{80,336},{96,352},{112... | collective-permute-start | bytes 589832 | tf_op jit(solution)/shard_map/ppermute | solution.py:21
  71.1 35.5 %collective-permute-start.6 = (bf16[192,1024]{1,0:T(8,128)(2,1)S(1)}, bf16[192,1024]{1,0:T(8,128)(2,1)S(1)}, u32[]{:S(2)}, u32[]{:S(2)}) collective-permute-start(bf16[192,1024]{1,0:T(8,128)(2,1)S(1)} %pad_maximum_fusion.1), channel_id=1, source_target_pairs={{0,16},{16,32},{32,48},{48,64},{64,80},{80,96},{96,112},{112,0},{1... | collective-permute-start | bytes 1179656 | tf_op jit(solution)/shard_map/ppermute | solution.py:26
  81.3 28.4 %collective-permute-start.7 = (bf16[192,1024]{1,0:T(8,128)(2,1)S(1)}, bf16[192,1024]{1,0:T(8,128)(2,1)S(1)}, u32[]{:S(2)}, u32[]{:S(2)}) collective-permute-start(bf16[192,1024]{1,0:T(8,128)(2,1)S(1)} %pad_maximum_fusion.1), channel_id=1, source_target_pairs={{0,112},{16,0},{32,16},{48,32},{64,48},{80,64},{96,80},{112,96},{1... | collective-permute-start | bytes 1179656 | tf_op jit(solution)/shard_map/ppermute | solution.py:26
  83.8 30.2 %collective-permute-start.8 = (bf16[192,1024]{1,0:T(8,128)(2,1)S(1)}, bf16[192,1024]{1,0:T(8,128)(2,1)S(1)}, u32[]{:S(2)}, u32[]{:S(2)}) collective-permute-start(bf16[192,1024]{1,0:T(8,128)(2,1)S(1)} %pad_maximum_fusion.1), channel_id=1, source_target_pairs={{0,32},{16,48},{32,64},{48,80},{64,96},{80,112},{96,0},{112,16},{1... | collective-permute-start | bytes 1179656 | tf_op jit(solution)/shard_map/ppermute | solution.py:26
  87.0 29.9 %collective-permute-start.9 = (bf16[192,1024]{1,0:T(8,128)(2,1)S(1)}, bf16[192,1024]{1,0:T(8,128)(2,1)S(1)}, u32[]{:S(2)}, u32[]{:S(2)}) collective-permute-start(bf16[192,1024]{1,0:T(8,128)(2,1)S(1)} %pad_maximum_fusion.1), channel_id=1, source_target_pairs={{0,96},{16,112},{32,0},{48,16},{64,32},{80,48},{96,64},{112,80},{1... | collective-permute-start | bytes 1179656 | tf_op jit(solution)/shard_map/ppermute | solution.py:26
  91.6 15.0 %collective-permute-start.5 = (bf16[128,1408]{1,0:T(8,128)(2,1)S(1)}, bf16[128,1408]{1,0:T(8,128)(2,1)S(1)}, u32[]{:S(2)}, u32[]{:S(2)}) collective-permute-start(bf16[128,1408]{1,0:T(8,128)(2,1)S(1)} %pad_maximum_fusion.2), channel_id=1, source_target_pairs={{0,128},{16,144},{32,160},{48,176},{64,192},{80,208},{96,224},{112... | collective-permute-start | bytes 1081352 | tf_op jit(solution)/shard_map/ppermute | solution.py:21
  106.6 43.3 %collective-permute-start.19 = (bf16[192,1024]{1,0:T(8,128)(2,1)S(1)}, bf16[192,1024]{1,0:T(8,128)(2,1)S(1)}, u32[]{:S(2)}, u32[]{:S(2)}) collective-permute-start(bf16[192,1024]{1,0:T(8,128)(2,1)S(1)} %collective-permute-done.6), channel_id=1, source_target_pairs={{0,32},{16,48},{32,64},{48,80},{64,96},{80,112},{96,0},{112,16},{1... | collective-permute-start | bytes 1179656 | tf_op jit(solution)/shard_map/ppermute | solution.py:26
  109.7 40.2 %collective-permute-start.20 = (bf16[192,1024]{1,0:T(8,128)(2,1)S(1)}, bf16[192,1024]{1,0:T(8,128)(2,1)S(1)}, u32[]{:S(2)}, u32[]{:S(2)}) collective-permute-start(bf16[192,1024]{1,0:T(8,128)(2,1)S(1)} %collective-permute-done.7), channel_id=1, source_target_pairs={{0,96},{16,112},{32,0},{48,16},{64,32},{80,48},{96,64},{112,80},{1... | collective-permute-start | bytes 1179656 | tf_op jit(solution)/shard_map/ppermute | solution.py:26
  114.1 35.9 %collective-permute-start.21 = (bf16[96,1024]{1,0:T(8,128)(2,1)S(1)}, bf16[96,1024]{1,0:T(8,128)(2,1)S(1)}, u32[]{:S(2)}, u32[]{:S(2)}) collective-permute-start(bf16[96,1024]{1,0:T(8,128)(2,1)S(1)} %slice.89), channel_id=1, source_target_pairs={{0,32},{16,48},{32,64},{48,80},{64,96},{80,112},{96,0},{112,16},{1... | collective-permute-start | bytes 589832 | tf_op jit(solution)/shard_map/ppermute | solution.py:26
  116.9 33.1 %collective-permute-start.22 = (bf16[96,1024]{1,0:T(8,128)(2,1)S(1)}, bf16[96,1024]{1,0:T(8,128)(2,1)S(1)}, u32[]{:S(2)}, u32[]{:S(2)}) collective-permute-start(bf16[96,1024]{1,0:T(8,128)(2,1)S(1)} %slice.90), channel_id=1, source_target_pairs={{0,96},{16,112},{32,0},{48,16},{64,32},{80,48},{96,64},{112,80},{1... | collective-permute-start | bytes 589832 | tf_op jit(solution)/shard_map/ppermute | solution.py:26
  121.5 5.7 %collective-permute-start.10 = (bf16[128,384]{1,0:T(8,128)(2,1)S(1)}, bf16[128,384]{1,0:T(8,128)(2,1)S(1)}, u32[]{:S(2)}, u32[]{:S(2)}) collective-permute-start(bf16[128,384]{1,0:T(8,128)(2,1)S(1)} %slice.67), channel_id=1, source_target_pairs={{0,4},{1,5},{2,6},{3,7},{4,0},{5,1},{6,2},{7,3},{8,12},{9,13},{10,... | collective-permute-start | bytes 294920 | tf_op jit(solution)/shard_map/ppermute | solution.py:54
  127.3 8.2 %collective-permute-start.11 = (bf16[128,768]{1,0:T(8,128)(2,1)S(1)}, bf16[128,768]{1,0:T(8,128)(2,1)S(1)}, u32[]{:S(2)}, u32[]{:S(2)}) collective-permute-start(bf16[128,768]{1,0:T(8,128)(2,1)S(1)} %maximum_select_fusion.3), channel_id=1, source_target_pairs={{0,8},{1,9},{2,10},{3,11},{4,12},{5,13},{6,14},{7,15},{8,0},{9,1},... | collective-permute-start | bytes 589832 | tf_op jit(solution)/shard_map/ppermute | solution.py:54
  135.7 16.0 %collective-permute-start.12 = (bf16[256,1536]{1,0:T(8,128)(2,1)S(1)}, bf16[256,1536]{1,0:T(8,128)(2,1)S(1)}, u32[]{:S(2)}, u32[]{:S(2)}) collective-permute-start(bf16[256,1536]{1,0:T(8,128)(2,1)S(1)} %maximum_select_fusion), channel_id=1, source_target_pairs={{0,256},{16,272},{32,288},{48,304},{64,320},{80,336},{96,352},{112... | collective-permute-start | bytes 2359304 | tf_op jit(solution)/shard_map/ppermute | solution.py:21
  150.1 4.2 %copy-start = (bf16[2,2,8,96,1024]{4,3,2,1,0:T(8,128)(2,1)}, bf16[2,2,8,96,1024]{4,3,2,1,0:T(8,128)(2,1)S(1)}, u32[]{:S(2)}) copy-start(bf16[2,2,8,96,1024]{4,3,2,1,0:T(8,128)(2,1)S(1)} %bitcast_dynamic-update-slice_fusion) | copy-start | bytes 18874372
  151.7 5.7 %copy-start.2 = (f32[128]{0:T(128)S(1)}, f32[128]{0:T(128)}, u32[]{:S(2)}) copy-start(f32[128]{0:T(128)} %param.9) | copy-start | bytes 1540
  154.3 3.1 %collective-permute-start.23 = (f32[8,128]{1,0:T(8,128)S(1)}, f32[8,128]{1,0:T(8,128)S(1)}, u32[]{:S(2)}, u32[]{:S(2)}) collective-permute-start(f32[8,128]{1,0:T(8,128)S(1)} %reshape.142), channel_id=1, source_target_pairs={{0,256},{16,272},{32,288},{48,304},{64,320},{80,336},{96,352},{112... | collective-permute-start | bytes 12296 | tf_op jit(solution)/shard_map/ppermute | solution.py:21
  178.9 5.9 %collective-permute-start.24 = (bf16[16,96,256]{2,1,0:T(8,128)(2,1)S(1)}, bf16[16,96,256]{2,1,0:T(8,128)(2,1)S(1)}, u32[]{:S(2)}, u32[]{:S(2)}) collective-permute-start(bf16[16,96,256]{2,1,0:T(8,128)(2,1)S(1)} %bitcast.114), channel_id=1, source_target_pairs={{0,256},{16,272},{32,288},{48,304},{64,320},{80,336},{96,352},{112... | collective-permute-start | bytes 2359304 | tf_op jit(solution)/shard_map/ppermute | solution.py:21
  186.2 26.8 %all-to-all-start.1 = ((bf16[32,96,128]{2,1,0:T(8,128)(2,1)}), bf16[32,96,128]{2,1,0:T(8,128)(2,1)S(1)}, u32[]{:S(2)}, u32[]{:S(2)}) async-start(bf16[32,96,128]{2,1,0:T(8,128)(2,1)} %bitcast.52), calls=%async_computation.1 | async-start | bytes 1572864 | tf_op jit(solution)/shard_map/all_to_all | solution.py:36

commit v3 on v1

--- a/solution.py
+++ b/solution.py
@@ -25,25 +25,19 @@
     return lax.ppermute(x, "dp", perm)
 
 
-def same_y(per_section):
+def exchange(x):
     n = NZH * NY * NQ
-    groups = []
-    for y in range(NY):
-        rows = [
-            [s * n + (zh * NY + y) * NQ + q for zh in range(NZH) for q in range(NQ)]
-            for s in range(2)
-        ]
-        groups += rows if per_section else [rows[0] + rows[1]]
-    return groups
-
-
-def exchange(x, per_section):
+    groups = [
+        [s * n + (zh * NY + y) * NQ + q for zh in range(NZH) for q in range(NQ)]
+        for s in range(2)
+        for y in range(NY)
+    ]
     return lax.all_to_all(
         x,
         ("section", "dp", "vocab"),
         split_axis=0,
         concat_axis=0,
-        axis_index_groups=same_y(per_section),
+        axis_index_groups=groups,
         tiled=True,
     )
 
@@ -113,7 +107,6 @@
     teacher = teacher_half(codes, exponents)
     t_send = after(columns(teacher, 0, 1), near_parts[3][2])
     scaled_t = both(columns(teacher, 0, 0), flip(t_send, 0, 1)).astype(jnp.float32)
-    weight = both(loss_weight, flip(after(loss_weight, near_parts[3][2]), 0, 1))
 
     logits = jnp.dot(h_all, weights, preferred_element_type=jnp.float32)
     scaled_s = logits / TEMP
@@ -126,18 +119,33 @@
             jnp.sum(t_exp, axis=1),
             jnp.sum(t_exp * (scaled_t - scaled_s), axis=1),
         ]
-    )
-    n = 2 * NZH * NQ
-    stats = exchange(jnp.broadcast_to(stats[None], (n,) + stats.shape), False)
-    top = jnp.max(stats[:, 0], axis=0)
-    s_sum = jnp.sum(stats[:, 1] * jnp.exp(stats[:, 0] - top), axis=0)
-    t_sum = jnp.sum(stats[:, 2], axis=0)
-    cross = jnp.sum(stats[:, 3], axis=0)
+    ).reshape(8, tok)
+
+    stats = jnp.stack([stats, flip(stats, 1, 0)])
+    top = jnp.max(stats[:, 0:2], axis=0)
+    s_sum = jnp.sum(stats[:, 2:4] * jnp.exp(stats[:, 0:2] - top), axis=0)
+    rest = jnp.sum(stats[:, 4:8], axis=0)
+    tiles = [
+        jnp.concatenate([top, s_sum, rest[0:2], rest[2 + z : 3 + z], loss_weight[None]])
+        for z in range(NZH)
+    ]
+    parts = jnp.broadcast_to(jnp.stack(tiles)[:, None], (NZH, NQ, 8, tok))
+    parts = exchange(parts.reshape(NZH * NQ, 8, tok))
+    top = jnp.max(parts[:, 0:2], axis=0)
+    s_sum = jnp.sum(parts[:, 2:4] * jnp.exp(parts[:, 0:2] - top), axis=0)
+    t_sum = jnp.sum(parts[:, 4:6], axis=0)
+    cross = jnp.sum(parts[:, 6], axis=0)
+    weight = jnp.concatenate([parts[0, 7], parts[NQ, 7]])
     student_lse = top + jnp.log(s_sum)
     teacher_lse = jnp.log(t_sum)
-    kl_loss = TEMP * TEMP * (cross / t_sum - teacher_lse + student_lse)
-    kl_loss = lax.dynamic_slice_in_dim(kl_loss, zh * tok, tok)
 
+    def of_mine(a):
+        return lax.dynamic_index_in_dim(a, zh, axis=0, keepdims=False)
+
+    kl_loss = cross / of_mine(t_sum) - of_mine(teacher_lse) + of_mine(student_lse)
+    kl_loss = TEMP * TEMP * kl_loss
+
+    student_lse, teacher_lse = student_lse.reshape(2 * tok), teacher_lse.reshape(2 * tok)
     logit_grad = (
         weight[:, None]
         * TEMP
@@ -148,9 +156,9 @@
         weights, logit_grad, (((1,), (1,)), ((), ())), preferred_element_type=jnp.float32
     ).reshape(2, NQ, rows, 2 * tok)
     g = g[0] + flip(g[1].astype(jnp.bfloat16), 1, 0).astype(jnp.float32)
-    g = g.astype(jnp.bfloat16)
-    g = jnp.concatenate([g[:, :, :tok], g[:, :, tok:]])
-    g = exchange(g, True)
+    g = g.astype(jnp.bfloat16).reshape(NQ, rows, 2, tok)
+    g = g.transpose(2, 0, 1, 3).reshape(NZH * NQ, rows, tok)
+    g = exchange(g)
     g = jnp.sum(g.astype(jnp.float32), axis=0)
     return (kl_loss, g.T.astype(jnp.bfloat16))
 

time: 182 us -> 180 us (0.989)
  blocking collectives: 0 us -> 17.8 us
  starting transfers between devices: 113 us -> 99.8 us
  waiting for transfers between devices: 43.9 us -> 38.6 us
    all_to_all x0 -> x1, blocking collectives: none -> 17.8 us  [exchange(): lax.all_to_all(x, ('section', 'dp', 'vocab'), split_axis=0, concat_axis=0...]
    all_to_all x2 -> x1, starting transfers between devices: 17.9 us -> 3.91 us  [exchange(): lax.all_to_all(x, ('section', 'dp', 'vocab'), split_axis=0, concat_axis=0...]
    ppermute x8, waiting for transfers between devices: 6.23 us -> 2.58 us  [flip(): return lax.ppermute(x, ('section', 'dp'), perm)]
    all_to_all x2 -> x1, waiting for transfers between devices: 24 us -> 22.3 us  [exchange(): lax.all_to_all(x, ('section', 'dp', 'vocab'), split_axis=0, concat_axis=0...]
  transfers between devices with their start and end apart: 26 -> 25, of which waited for: 9 -> 8; matrix products, arithmetic and copies ran while one was open for 6% -> 6% of each run, Pallas kernels for 0% -> 0%
where the time goes in v3:
time: 180 us; the launch traced here: 178 us
  starting transfers between devices  99.8 us (55%)
  waiting for transfers between devices  38.6 us (21%)
  blocking collectives  17.8 us (10%)
  matrix products  7.09 us (4%)
  local copies, waits for them, and re-layouts  6.64 us (4%)
  other arithmetic  6.14 us (3%)
    ppermute x16, starting transfers between devices, along_y(): return lax.ppermute(x, 'dp', perm)  49.2 us
    ppermute x8, starting transfers between devices, flip(): return lax.ppermute(x, ('section', 'dp'), perm)  46.6 us
    all_to_all x1, waiting for transfers between devices, exchange(): lax.all_to_all(x, ('section', 'dp', 'vocab'), split_axis=0, concat_axis=0...  22.3 us
    all_to_all x1, blocking collectives, exchange(): lax.all_to_all(x, ('section', 'dp', 'vocab'), split_axis=0, concat_axis=0...  17.8 us
    ppermute x16, waiting for transfers between devices, along_y(): return lax.ppermute(x, 'dp', perm)  13.7 us
    dot_general x1, matrix products, on_device(): lax.dot_general(weights, logit_grad, (((1,), (1,)), ((), ())), preferred_...  5.08 us
    all_to_all x1, starting transfers between devices, exchange(): lax.all_to_all(x, ('section', 'dp', 'vocab'), split_axis=0, concat_axis=0...  3.91 us
  transfers between devices with their start and end apart: 25, of which 8 were waited for; matrix products, arithmetic and copies ran while one was open for 6% of the time, Pallas kernels for 0%

profile of v3, /device:TPU:25, one launch (start us, length us, event | category | flops | bytes accessed | tf_op | source)
XLA Modules:
  0.0 177.6 jit_solution(17980615476409414473)
XLA Ops:
  0.7 1.1 constant_dynamic-slice_fusion.9
  1.8 2.6 %collective-permute-start = (bf16[96,1024]{1,0:T(8,128)(2,1)S(1)}, bf16[96,1024]{1,0:T(8,128)(2,1)S(1)}, u32[]{:S(2)}, u32[]{:S(2)}) collective-permute-start(bf16[96,1024]{1,0:T(8,128)(2,1)S(1)} %get-tuple-element.14), channel_id=1, source_target_pairs={{0,256},{16,272},{32,288},{48,304},{64,320},{80,336},{96,352},{112... | collective-permute-start | bytes 589832 | tf_op jit(solution)/shard_map/ppermute | solution.py:20
  4.4 1.8 constant_dynamic-slice_fusion.7
  6.1 10.6 %collective-permute-start.11 = (bf16[96,2048]{1,0:T(8,128)(2,1)}, bf16[96,2048]{1,0:T(8,128)(2,1)S(1)}, u32[]{:S(2)}, u32[]{:S(2)}) collective-permute-start(bf16[96,2048]{1,0:T(8,128)(2,1)} %constant_dynamic-slice_fusion.7), channel_id=1, source_target_pairs={{0,128},{16,144},{32,160},{48,176},{64,192},{80,208},{96,224},{112... | collective-permute-start | bytes 1179656 | tf_op jit(solution)/shard_map/ppermute | solution.py:20
  16.8 0.7 exponential_multiply_fusion
  17.6 4.4 %collective-permute-start.1 = (bf16[192,1024]{1,0:T(8,128)(2,1)S(1)}, bf16[192,1024]{1,0:T(8,128)(2,1)S(1)}, u32[]{:S(2)}, u32[]{:S(2)}) collective-permute-start(bf16[192,1024]{1,0:T(8,128)(2,1)S(1)} %pad_maximum_fusion), channel_id=1, source_target_pairs={{0,16},{16,32},{32,48},{48,64},{64,80},{80,96},{96,112},{112,0},{1... | collective-permute-start | bytes 1179656 | tf_op jit(solution)/shard_map/ppermute | solution.py:25
  22.1 1.9 %collective-permute-start.4 = (bf16[192,1024]{1,0:T(8,128)(2,1)S(1)}, bf16[192,1024]{1,0:T(8,128)(2,1)S(1)}, u32[]{:S(2)}, u32[]{:S(2)}) collective-permute-start(bf16[192,1024]{1,0:T(8,128)(2,1)S(1)} %pad_maximum_fusion), channel_id=1, source_target_pairs={{0,112},{16,0},{32,16},{48,32},{64,48},{80,64},{96,80},{112,96},{1... | collective-permute-start | bytes 1179656 | tf_op jit(solution)/shard_map/ppermute | solution.py:25
  24.0 0.6 mul.79
  24.6 2.9 %fusion = bf16[128,4096]{1,0:T(8,128)(2,1)S(1)} fusion(f32[16,8,32,128]{3,2,1,0:T(8,128)S(1)} %bitcast.103, s32[128,4096]{1,0:T(8,128)} %param.7), kind=kLoop, calls=%fused_computation.1 | loop fusion | flops 1572864 | bytes 5242880 | tf_op jit(solution)/shard_map/convert_element_type | solution.py:49
  27.8 2.5 %collective-permute-start.12 = (bf16[96,1024]{1,0:T(8,128)(2,1)S(1)}, bf16[96,1024]{1,0:T(8,128)(2,1)S(1)}, u32[]{:S(2)}, u32[]{:S(2)}) collective-permute-start(bf16[96,1024]{1,0:T(8,128)(2,1)S(1)} %get-tuple-element.16), channel_id=1, source_target_pairs={{0,256},{16,272},{32,288},{48,304},{64,320},{80,336},{96,352},{112... | collective-permute-start | bytes 589832 | tf_op jit(solution)/shard_map/ppermute | solution.py:20
  30.3 14.4 %collective-permute-start.2 = (bf16[128,1536]{1,0:T(8,128)(2,1)S(1)}, bf16[128,1536]{1,0:T(8,128)(2,1)S(1)}, u32[]{:S(2)}, u32[]{:S(2)}) collective-permute-start(bf16[128,1536]{1,0:T(8,128)(2,1)S(1)} %copy-done.1), channel_id=1, source_target_pairs={{0,128},{16,144},{32,160},{48,176},{64,192},{80,208},{96,224},{112... | collective-permute-start | bytes 1179656 | tf_op jit(solution)/shard_map/ppermute | solution.py:20
  44.8 4.4 %collective-permute-start.5 = (bf16[192,1024]{1,0:T(8,128)(2,1)S(1)}, bf16[192,1024]{1,0:T(8,128)(2,1)S(1)}, u32[]{:S(2)}, u32[]{:S(2)}) collective-permute-start(bf16[192,1024]{1,0:T(8,128)(2,1)S(1)} %collective-permute-done.1), channel_id=1, source_target_pairs={{0,16},{16,32},{32,48},{48,64},{64,80},{80,96},{96,112},{112,0},{1... | collective-permute-start | bytes 1179656 | tf_op jit(solution)/shard_map/ppermute | solution.py:25
  49.2 1.9 %collective-permute-start.6 = (bf16[192,1024]{1,0:T(8,128)(2,1)S(1)}, bf16[192,1024]{1,0:T(8,128)(2,1)S(1)}, u32[]{:S(2)}, u32[]{:S(2)}) collective-permute-start(bf16[192,1024]{1,0:T(8,128)(2,1)S(1)} %collective-permute-done.4), channel_id=1, source_target_pairs={{0,112},{16,0},{32,16},{48,32},{64,48},{80,64},{96,80},{112,96},{1... | collective-permute-start | bytes 1179656 | tf_op jit(solution)/shard_map/ppermute | solution.py:25
  51.1 0.8 broadcast_in_dim.6
  52.0 4.6 %collective-permute-start.13 = (bf16[192,1024]{1,0:T(8,128)(2,1)S(1)}, bf16[192,1024]{1,0:T(8,128)(2,1)S(1)}, u32[]{:S(2)}, u32[]{:S(2)}) collective-permute-start(bf16[192,1024]{1,0:T(8,128)(2,1)S(1)} %pad_maximum_fusion.1), channel_id=1, source_target_pairs={{0,16},{16,32},{32,48},{48,64},{64,80},{80,96},{96,112},{112,0},{1... | collective-permute-start | bytes 1179656 | tf_op jit(solution)/shard_map/ppermute | solution.py:25
  56.6 1.9 %collective-permute-start.14 = (bf16[192,1024]{1,0:T(8,128)(2,1)S(1)}, bf16[192,1024]{1,0:T(8,128)(2,1)S(1)}, u32[]{:S(2)}, u32[]{:S(2)}) collective-permute-start(bf16[192,1024]{1,0:T(8,128)(2,1)S(1)} %pad_maximum_fusion.1), channel_id=1, source_target_pairs={{0,112},{16,0},{32,16},{48,32},{64,48},{80,64},{96,80},{112,96},{1... | collective-permute-start | bytes 1179656 | tf_op jit(solution)/shard_map/ppermute | solution.py:25
  58.6 4.6 %collective-permute-start.7 = (bf16[192,1024]{1,0:T(8,128)(2,1)S(1)}, bf16[192,1024]{1,0:T(8,128)(2,1)S(1)}, u32[]{:S(2)}, u32[]{:S(2)}) collective-permute-start(bf16[192,1024]{1,0:T(8,128)(2,1)S(1)} %collective-permute-done.5), channel_id=1, source_target_pairs={{0,16},{16,32},{32,48},{48,64},{64,80},{80,96},{96,112},{112,0},{1... | collective-permute-start | bytes 1179656 | tf_op jit(solution)/shard_map/ppermute | solution.py:25
  63.2 1.9 %collective-permute-start.8 = (bf16[192,1024]{1,0:T(8,128)(2,1)S(1)}, bf16[192,1024]{1,0:T(8,128)(2,1)S(1)}, u32[]{:S(2)}, u32[]{:S(2)}) collective-permute-start(bf16[192,1024]{1,0:T(8,128)(2,1)S(1)} %collective-permute-done.6), channel_id=1, source_target_pairs={{0,112},{16,0},{32,16},{48,32},{64,48},{80,64},{96,80},{112,96},{1... | collective-permute-start | bytes 1179656 | tf_op jit(solution)/shard_map/ppermute | solution.py:25
  65.3 3.6 %collective-permute-start.3 = (bf16[256,1536]{1,0:T(8,128)(2,1)S(1)}, bf16[256,1536]{1,0:T(8,128)(2,1)S(1)}, u32[]{:S(2)}, u32[]{:S(2)}) collective-permute-start(bf16[256,1536]{1,0:T(8,128)(2,1)S(1)} %maximum_select_fusion), channel_id=1, source_target_pairs={{0,256},{16,272},{32,288},{48,304},{64,320},{80,336},{96,352},{112... | collective-permute-start | bytes 2359304 | tf_op jit(solution)/shard_map/ppermute | solution.py:20
  69.0 4.9 %collective-permute-start.15 = (bf16[192,1024]{1,0:T(8,128)(2,1)S(1)}, bf16[192,1024]{1,0:T(8,128)(2,1)S(1)}, u32[]{:S(2)}, u32[]{:S(2)}) collective-permute-start(bf16[192,1024]{1,0:T(8,128)(2,1)S(1)} %collective-permute-done.13), channel_id=1, source_target_pairs={{0,16},{16,32},{32,48},{48,64},{64,80},{80,96},{96,112},{112,0},{1... | collective-permute-start | bytes 1179656 | tf_op jit(solution)/shard_map/ppermute | solution.py:25
  73.8 1.9 %collective-permute-start.16 = (bf16[192,1024]{1,0:T(8,128)(2,1)S(1)}, bf16[192,1024]{1,0:T(8,128)(2,1)S(1)}, u32[]{:S(2)}, u32[]{:S(2)}) collective-permute-start(bf16[192,1024]{1,0:T(8,128)(2,1)S(1)} %collective-permute-done.14), channel_id=1, source_target_pairs={{0,112},{16,0},{32,16},{48,32},{64,48},{80,64},{96,80},{112,96},{1... | collective-permute-start | bytes 1179656 | tf_op jit(solution)/shard_map/ppermute | solution.py:25
  75.9 3.2 %collective-permute-start.21 = (bf16[128,1024]{1,0:T(8,128)(2,1)S(1)}, bf16[128,1024]{1,0:T(8,128)(2,1)S(1)}, u32[]{:S(2)}, u32[]{:S(2)}) collective-permute-start(bf16[128,1024]{1,0:T(8,128)(2,1)S(1)} %get-tuple-element.5), channel_id=1, source_target_pairs={{0,128},{16,144},{32,160},{48,176},{64,192},{80,208},{96,224},{112... | collective-permute-start | bytes 786440 | tf_op jit(solution)/shard_map/ppermute | solution.py:20
  79.1 0.2 collective-permute-done.8
  79.3 4.3 %collective-permute-start.9 = (bf16[96,1024]{1,0:T(8,128)(2,1)S(1)}, bf16[96,1024]{1,0:T(8,128)(2,1)S(1)}, u32[]{:S(2)}, u32[]{:S(2)}) collective-permute-start(bf16[96,1024]{1,0:T(8,128)(2,1)S(1)} %slice.79), channel_id=1, source_target_pairs={{0,16},{16,32},{32,48},{48,64},{64,80},{80,96},{96,112},{112,0},{1... | collective-permute-start | bytes 589832 | tf_op jit(solution)/shard_map/ppermute | solution.py:25
  83.8 1.9 %collective-permute-start.10 = (bf16[96,1024]{1,0:T(8,128)(2,1)S(1)}, bf16[96,1024]{1,0:T(8,128)(2,1)S(1)}, u32[]{:S(2)}, u32[]{:S(2)}) collective-permute-start(bf16[96,1024]{1,0:T(8,128)(2,1)S(1)} %slice.80), channel_id=1, source_target_pairs={{0,112},{16,0},{32,16},{48,32},{64,48},{80,64},{96,80},{112,96},{1... | collective-permute-start | bytes 589832 | tf_op jit(solution)/shard_map/ppermute | solution.py:25
  85.7 2.4 %collective-permute-done.16 = bf16[192,1024]{1,0:T(8,128)(2,1)S(1)} collective-permute-done((bf16[192,1024]{1,0:T(8,128)(2,1)S(1)}, bf16[192,1024]{1,0:T(8,128)(2,1)S(1)}, u32[]{:S(2)}, u32[]{:S(2)}) %collective-permute-start.16) | collective-permute-done | bytes 393248 | tf_op jit(solution)/shard_map/ppermute | solution.py:25
  88.1 2.2 %collective-permute-start.17 = (bf16[192,1024]{1,0:T(8,128)(2,1)S(1)}, bf16[192,1024]{1,0:T(8,128)(2,1)S(1)}, u32[]{:S(2)}, u32[]{:S(2)}) collective-permute-start(bf16[192,1024]{1,0:T(8,128)(2,1)S(1)} %collective-permute-done.15), channel_id=1, source_target_pairs={{0,16},{16,32},{32,48},{48,64},{64,80},{80,96},{96,112},{112,0},{1... | collective-permute-start | bytes 1179656 | tf_op jit(solution)/shard_map/ppermute | solution.py:25
  90.3 3.1 %collective-permute-start.18 = (bf16[192,1024]{1,0:T(8,128)(2,1)S(1)}, bf16[192,1024]{1,0:T(8,128)(2,1)S(1)}, u32[]{:S(2)}, u32[]{:S(2)}) collective-permute-start(bf16[192,1024]{1,0:T(8,128)(2,1)S(1)} %collective-permute-done.16), channel_id=1, source_target_pairs={{0,112},{16,0},{32,16},{48,32},{64,48},{80,64},{96,80},{112,96},{1... | collective-permute-start | bytes 1179656 | tf_op jit(solution)/shard_map/ppermute | solution.py:25
  93.7 5.9 %collective-permute-done.17 = bf16[192,1024]{1,0:T(8,128)(2,1)S(1)} collective-permute-done((bf16[192,1024]{1,0:T(8,128)(2,1)S(1)}, bf16[192,1024]{1,0:T(8,128)(2,1)S(1)}, u32[]{:S(2)}, u32[]{:S(2)}) %collective-permute-start.17) | collective-permute-done | bytes 393248 | tf_op jit(solution)/shard_map/ppermute | solution.py:25
  99.7 3.0 %collective-permute-start.19 = (bf16[96,1024]{1,0:T(8,128)(2,1)S(1)}, bf16[96,1024]{1,0:T(8,128)(2,1)S(1)}, u32[]{:S(2)}, u32[]{:S(2)}) collective-permute-start(bf16[96,1024]{1,0:T(8,128)(2,1)S(1)} %slice.81), channel_id=1, source_target_pairs={{0,16},{16,32},{32,48},{48,64},{64,80},{80,96},{96,112},{112,0},{1... | collective-permute-start | bytes 589832 | tf_op jit(solution)/shard_map/ppermute | solution.py:25
  102.7 2.3 %collective-permute-start.20 = (bf16[96,1024]{1,0:T(8,128)(2,1)S(1)}, bf16[96,1024]{1,0:T(8,128)(2,1)S(1)}, u32[]{:S(2)}, u32[]{:S(2)}) collective-permute-start(bf16[96,1024]{1,0:T(8,128)(2,1)S(1)} %slice.82), channel_id=1, source_target_pairs={{0,112},{16,0},{32,16},{48,32},{64,48},{80,64},{96,80},{112,96},{1... | collective-permute-start | bytes 589832 | tf_op jit(solution)/shard_map/ppermute | solution.py:25
  105.1 1.0 collective-permute-done.19
  106.1 4.2 %collective-permute-done.20 = bf16[96,1024]{1,0:T(8,128)(2,1)S(1)} collective-permute-done((bf16[96,1024]{1,0:T(8,128)(2,1)S(1)}, bf16[96,1024]{1,0:T(8,128)(2,1)S(1)}, u32[]{:S(2)}, u32[]{:S(2)}) %collective-permute-start.20) | collective-permute-done | bytes 196640 | tf_op jit(solution)/shard_map/ppermute | solution.py:25
  110.4 2.0 %fusion.32 = (f32[256]{0:T(256)S(1)}, f32[256,1024]{1,0:T(8,128)S(1)}) fusion(bf16[3072,1024]{1,0:T(8,128)(2,1)S(1)} %bitcast.104, bf16[256,1536]{1,0:T(8,128)(2,1)S(1)} %collective-permute-done.3, bf16[256,1536]{1,0:T(8,128)(2,1)S(1)} %maximum_select_fusion), kind=kOutput, calls=%fused_computation.84 | convolution fusion | flops 1614282496 | bytes 8913920 | tf_op jit(solution)/shard_map/dot_general | solution.py:111
  112.4 0.5 exponential_reduce_fusion
  113.0 5.7 %collective-permute-start.22 = (f32[8,128]{1,0:T(8,128)S(1)}, f32[8,128]{1,0:T(8,128)S(1)}, u32[]{:S(2)}, u32[]{:S(2)}) collective-permute-start(f32[8,128]{1,0:T(8,128)S(1)} %reshape.142), channel_id=1, source_target_pairs={{0,256},{16,272},{32,288},{48,304},{64,320},{80,336},{96,352},{112... | collective-permute-start | bytes 12296 | tf_op jit(solution)/shard_map/ppermute | solution.py:20
  118.7 0.8 collective-permute-done.22
  119.6 17.8 %all_to_all.10 = f32[32,8,128]{2,1,0:T(8,128)S(1)} all-to-all(f32[32,8,128]{2,1,0:T(8,128)S(1)} %bitcast.115), channel_id=1, replica_groups={{0,1,2,3,4,5,6,7,8,9,10,11,12,13,14,15,128,129,130,131,132,133,134,135,..., dimensions={0} | all-to-all | bytes 262144 | tf_op jit(solution)/shard_map/all_to_all | solution.py:35
  137.6 5.1 %fusion.15 = f32[3072,256]{1,0:T(8,128)S(1)} fusion(bf16[3072,1024]{1,0:T(8,128)(2,1)} %bitcast.105, f32[256,1024]{1,0:T(8,128)S(1)} %get-tuple-element.22, f32[256]{0:T(256)S(1)} %get-tuple-element.19, f32[256]{0:T(256)S(1)} %bitcast.134, f32[256]{0:T(256)S(1)} %maximum_multiply_fusion.1, bf16[128,1024]{1,0:T(8,128)(2,1)S(1)} %collective-permute-done.21, ...), kind=kOutput, calls=%fused_computation.21 | convolution fusion | flops 1614544896 | bytes 11013121 | tf_op jit(solution)/shard_map/dot_general | solution.py:155
  142.8 4.0 %collective-permute-start.23 = (bf16[16,96,256]{2,1,0:T(8,128)(2,1)S(1)}, bf16[16,96,256]{2,1,0:T(8,128)(2,1)S(1)}, u32[]{:S(2)}, u32[]{:S(2)}) collective-permute-start(bf16[16,96,256]{2,1,0:T(8,128)(2,1)S(1)} %bitcast.114), channel_id=1, source_target_pairs={{0,256},{16,272},{32,288},{48,304},{64,320},{80,336},{96,352},{112... | collective-permute-start | bytes 2359304 | tf_op jit(solution)/shard_map/ppermute | solution.py:20
  146.9 1.8 %collective-permute-done.23 = bf16[16,96,256]{2,1,0:T(8,128)(2,1)S(1)} collective-permute-done((bf16[16,96,256]{2,1,0:T(8,128)(2,1)S(1)}, bf16[16,96,256]{2,1,0:T(8,128)(2,1)S(1)}, u32[]{:S(2)}, u32[]{:S(2)}) %collective-permute-start.23) | collective-permute-done | bytes 786464 | tf_op jit(solution)/shard_map/ppermute | solution.py:20
  148.7 0.2 add_convert_fusion
  148.9 0.2 reshape.144
  149.1 1.0 copy.68
  150.1 3.9 %all-to-all-start.1 = ((bf16[32,96,128]{2,1,0:T(8,128)(2,1)}), bf16[32,96,128]{2,1,0:T(8,128)(2,1)S(1)}, u32[]{:S(2)}, u32[]{:S(2)}) async-start(bf16[32,96,128]{2,1,0:T(8,128)(2,1)} %bitcast.52), calls=%async_computation.1 | async-start | bytes 1572864 | tf_op jit(solution)/shard_map/all_to_all | solution.py:35
  154.1 0.5 fusion.29
  154.6 22.3 %all-to-all-done.1 = bf16[32,96,128]{2,1,0:T(8,128)(2,1)S(1)} async-done(((bf16[32,96,128]{2,1,0:T(8,128)(2,1)}), bf16[32,96,128]{2,1,0:T(8,128)(2,1)S(1)}, u32[]{:S(2)}, u32[]{:S(2)}) %all-to-all-start.1) | async-done | bytes 786464 | tf_op jit(solution)/shard_map/all_to_all | solution.py:35
  176.9 0.7 reduce_sum.92
  (71 shorter events, 1.7 us)
Async XLA Ops:
  0.6 29.7 %copy-start.1 = (bf16[128,1536]{1,0:T(8,128)(2,1)S(1)}, bf16[128,1536]{1,0:T(8,128)(2,1)}, u32[]{:S(2)}) copy-start(bf16[128,1536]{1,0:T(8,128)(2,1)} %param.5) | copy-start | bytes 1179652
  1.8 15.8 %collective-permute-start = (bf16[96,1024]{1,0:T(8,128)(2,1)S(1)}, bf16[96,1024]{1,0:T(8,128)(2,1)S(1)}, u32[]{:S(2)}, u32[]{:S(2)}) collective-permute-start(bf16[96,1024]{1,0:T(8,128)(2,1)S(1)} %get-tuple-element.14), channel_id=1, source_target_pairs={{0,256},{16,272},{32,288},{48,304},{64,320},{80,336},{96,352},{112... | collective-permute-start | bytes 589832 | tf_op jit(solution)/shard_map/ppermute | solution.py:20
  6.1 21.6 %collective-permute-start.11 = (bf16[96,2048]{1,0:T(8,128)(2,1)}, bf16[96,2048]{1,0:T(8,128)(2,1)S(1)}, u32[]{:S(2)}, u32[]{:S(2)}) collective-permute-start(bf16[96,2048]{1,0:T(8,128)(2,1)} %constant_dynamic-slice_fusion.7), channel_id=1, source_target_pairs={{0,128},{16,144},{32,160},{48,176},{64,192},{80,208},{96,224},{112... | collective-permute-start | bytes 1179656 | tf_op jit(solution)/shard_map/ppermute | solution.py:20
  17.6 12.7 %collective-permute-start.1 = (bf16[192,1024]{1,0:T(8,128)(2,1)S(1)}, bf16[192,1024]{1,0:T(8,128)(2,1)S(1)}, u32[]{:S(2)}, u32[]{:S(2)}) collective-permute-start(bf16[192,1024]{1,0:T(8,128)(2,1)S(1)} %pad_maximum_fusion), channel_id=1, source_target_pairs={{0,16},{16,32},{32,48},{48,64},{64,80},{80,96},{96,112},{112,0},{1... | collective-permute-start | bytes 1179656 | tf_op jit(solution)/shard_map/ppermute | solution.py:25
  22.1 27.1 %collective-permute-start.4 = (bf16[192,1024]{1,0:T(8,128)(2,1)S(1)}, bf16[192,1024]{1,0:T(8,128)(2,1)S(1)}, u32[]{:S(2)}, u32[]{:S(2)}) collective-permute-start(bf16[192,1024]{1,0:T(8,128)(2,1)S(1)} %pad_maximum_fusion), channel_id=1, source_target_pairs={{0,112},{16,0},{32,16},{48,32},{64,48},{80,64},{96,80},{112,96},{1... | collective-permute-start | bytes 1179656 | tf_op jit(solution)/shard_map/ppermute | solution.py:25
  27.8 24.2 %collective-permute-start.12 = (bf16[96,1024]{1,0:T(8,128)(2,1)S(1)}, bf16[96,1024]{1,0:T(8,128)(2,1)S(1)}, u32[]{:S(2)}, u32[]{:S(2)}) collective-permute-start(bf16[96,1024]{1,0:T(8,128)(2,1)S(1)} %get-tuple-element.16), channel_id=1, source_target_pairs={{0,256},{16,272},{32,288},{48,304},{64,320},{80,336},{96,352},{112... | collective-permute-start | bytes 589832 | tf_op jit(solution)/shard_map/ppermute | solution.py:20
  30.3 34.8 %collective-permute-start.2 = (bf16[128,1536]{1,0:T(8,128)(2,1)S(1)}, bf16[128,1536]{1,0:T(8,128)(2,1)S(1)}, u32[]{:S(2)}, u32[]{:S(2)}) collective-permute-start(bf16[128,1536]{1,0:T(8,128)(2,1)S(1)} %copy-done.1), channel_id=1, source_target_pairs={{0,128},{16,144},{32,160},{48,176},{64,192},{80,208},{96,224},{112... | collective-permute-start | bytes 1179656 | tf_op jit(solution)/shard_map/ppermute | solution.py:20
  44.8 13.9 %collective-permute-start.5 = (bf16[192,1024]{1,0:T(8,128)(2,1)S(1)}, bf16[192,1024]{1,0:T(8,128)(2,1)S(1)}, u32[]{:S(2)}, u32[]{:S(2)}) collective-permute-start(bf16[192,1024]{1,0:T(8,128)(2,1)S(1)} %collective-permute-done.1), channel_id=1, source_target_pairs={{0,16},{16,32},{32,48},{48,64},{64,80},{80,96},{96,112},{112,0},{1... | collective-permute-start | bytes 1179656 | tf_op jit(solution)/shard_map/ppermute | solution.py:25
  49.2 14.0 %collective-permute-start.6 = (bf16[192,1024]{1,0:T(8,128)(2,1)S(1)}, bf16[192,1024]{1,0:T(8,128)(2,1)S(1)}, u32[]{:S(2)}, u32[]{:S(2)}) collective-permute-start(bf16[192,1024]{1,0:T(8,128)(2,1)S(1)} %collective-permute-done.4), channel_id=1, source_target_pairs={{0,112},{16,0},{32,16},{48,32},{64,48},{80,64},{96,80},{112,96},{1... | collective-permute-start | bytes 1179656 | tf_op jit(solution)/shard_map/ppermute | solution.py:25
  52.0 16.9 %collective-permute-start.13 = (bf16[192,1024]{1,0:T(8,128)(2,1)S(1)}, bf16[192,1024]{1,0:T(8,128)(2,1)S(1)}, u32[]{:S(2)}, u32[]{:S(2)}) collective-permute-start(bf16[192,1024]{1,0:T(8,128)(2,1)S(1)} %pad_maximum_fusion.1), channel_id=1, source_target_pairs={{0,16},{16,32},{32,48},{48,64},{64,80},{80,96},{96,112},{112,0},{1... | collective-permute-start | bytes 1179656 | tf_op jit(solution)/shard_map/ppermute | solution.py:25
  56.6 17.2 %collective-permute-start.14 = (bf16[192,1024]{1,0:T(8,128)(2,1)S(1)}, bf16[192,1024]{1,0:T(8,128)(2,1)S(1)}, u32[]{:S(2)}, u32[]{:S(2)}) collective-permute-start(bf16[192,1024]{1,0:T(8,128)(2,1)S(1)} %pad_maximum_fusion.1), channel_id=1, source_target_pairs={{0,112},{16,0},{32,16},{48,32},{64,48},{80,64},{96,80},{112,96},{1... | collective-permute-start | bytes 1179656 | tf_op jit(solution)/shard_map/ppermute | solution.py:25
  58.6 17.2 %collective-permute-start.7 = (bf16[192,1024]{1,0:T(8,128)(2,1)S(1)}, bf16[192,1024]{1,0:T(8,128)(2,1)S(1)}, u32[]{:S(2)}, u32[]{:S(2)}) collective-permute-start(bf16[192,1024]{1,0:T(8,128)(2,1)S(1)} %collective-permute-done.5), channel_id=1, source_target_pairs={{0,16},{16,32},{32,48},{48,64},{64,80},{80,96},{96,112},{112,0},{1... | collective-permute-start | bytes 1179656 | tf_op jit(solution)/shard_map/ppermute | solution.py:25
  63.2 16.1 %collective-permute-start.8 = (bf16[192,1024]{1,0:T(8,128)(2,1)S(1)}, bf16[192,1024]{1,0:T(8,128)(2,1)S(1)}, u32[]{:S(2)}, u32[]{:S(2)}) collective-permute-start(bf16[192,1024]{1,0:T(8,128)(2,1)S(1)} %collective-permute-done.6), channel_id=1, source_target_pairs={{0,112},{16,0},{32,16},{48,32},{64,48},{80,64},{96,80},{112,96},{1... | collective-permute-start | bytes 1179656 | tf_op jit(solution)/shard_map/ppermute | solution.py:25
  65.3 45.0 %collective-permute-start.3 = (bf16[256,1536]{1,0:T(8,128)(2,1)S(1)}, bf16[256,1536]{1,0:T(8,128)(2,1)S(1)}, u32[]{:S(2)}, u32[]{:S(2)}) collective-permute-start(bf16[256,1536]{1,0:T(8,128)(2,1)S(1)} %maximum_select_fusion), channel_id=1, source_target_pairs={{0,256},{16,272},{32,288},{48,304},{64,320},{80,336},{96,352},{112... | collective-permute-start | bytes 2359304 | tf_op jit(solution)/shard_map/ppermute | solution.py:20
  69.0 14.8 %collective-permute-start.15 = (bf16[192,1024]{1,0:T(8,128)(2,1)S(1)}, bf16[192,1024]{1,0:T(8,128)(2,1)S(1)}, u32[]{:S(2)}, u32[]{:S(2)}) collective-permute-start(bf16[192,1024]{1,0:T(8,128)(2,1)S(1)} %collective-permute-done.13), channel_id=1, source_target_pairs={{0,16},{16,32},{32,48},{48,64},{64,80},{80,96},{96,112},{112,0},{1... | collective-permute-start | bytes 1179656 | tf_op jit(solution)/shard_map/ppermute | solution.py:25
  73.8 14.3 %collective-permute-start.16 = (bf16[192,1024]{1,0:T(8,128)(2,1)S(1)}, bf16[192,1024]{1,0:T(8,128)(2,1)S(1)}, u32[]{:S(2)}, u32[]{:S(2)}) collective-permute-start(bf16[192,1024]{1,0:T(8,128)(2,1)S(1)} %collective-permute-done.14), channel_id=1, source_target_pairs={{0,112},{16,0},{32,16},{48,32},{64,48},{80,64},{96,80},{112,96},{1... | collective-permute-start | bytes 1179656 | tf_op jit(solution)/shard_map/ppermute | solution.py:25
  75.9 36.5 %collective-permute-start.21 = (bf16[128,1024]{1,0:T(8,128)(2,1)S(1)}, bf16[128,1024]{1,0:T(8,128)(2,1)S(1)}, u32[]{:S(2)}, u32[]{:S(2)}) collective-permute-start(bf16[128,1024]{1,0:T(8,128)(2,1)S(1)} %get-tuple-element.5), channel_id=1, source_target_pairs={{0,128},{16,144},{32,160},{48,176},{64,192},{80,208},{96,224},{112... | collective-permute-start | bytes 786440 | tf_op jit(solution)/shard_map/ppermute | solution.py:20
  79.3 11.0 %collective-permute-start.9 = (bf16[96,1024]{1,0:T(8,128)(2,1)S(1)}, bf16[96,1024]{1,0:T(8,128)(2,1)S(1)}, u32[]{:S(2)}, u32[]{:S(2)}) collective-permute-start(bf16[96,1024]{1,0:T(8,128)(2,1)S(1)} %slice.79), channel_id=1, source_target_pairs={{0,16},{16,32},{32,48},{48,64},{64,80},{80,96},{96,112},{112,0},{1... | collective-permute-start | bytes 589832 | tf_op jit(solution)/shard_map/ppermute | solution.py:25
  83.8 9.6 %collective-permute-start.10 = (bf16[96,1024]{1,0:T(8,128)(2,1)S(1)}, bf16[96,1024]{1,0:T(8,128)(2,1)S(1)}, u32[]{:S(2)}, u32[]{:S(2)}) collective-permute-start(bf16[96,1024]{1,0:T(8,128)(2,1)S(1)} %slice.80), channel_id=1, source_target_pairs={{0,112},{16,0},{32,16},{48,32},{64,48},{80,64},{96,80},{112,96},{1... | collective-permute-start | bytes 589832 | tf_op jit(solution)/shard_map/ppermute | solution.py:25
  88.1 11.5 %collective-permute-start.17 = (bf16[192,1024]{1,0:T(8,128)(2,1)S(1)}, bf16[192,1024]{1,0:T(8,128)(2,1)S(1)}, u32[]{:S(2)}, u32[]{:S(2)}) collective-permute-start(bf16[192,1024]{1,0:T(8,128)(2,1)S(1)} %collective-permute-done.15), channel_id=1, source_target_pairs={{0,16},{16,32},{32,48},{48,64},{64,80},{80,96},{96,112},{112,0},{1... | collective-permute-start | bytes 1179656 | tf_op jit(solution)/shard_map/ppermute | solution.py:25
  90.3 12.3 %collective-permute-start.18 = (bf16[192,1024]{1,0:T(8,128)(2,1)S(1)}, bf16[192,1024]{1,0:T(8,128)(2,1)S(1)}, u32[]{:S(2)}, u32[]{:S(2)}) collective-permute-start(bf16[192,1024]{1,0:T(8,128)(2,1)S(1)} %collective-permute-done.16), channel_id=1, source_target_pairs={{0,112},{16,0},{32,16},{48,32},{64,48},{80,64},{96,80},{112,96},{1... | collective-permute-start | bytes 1179656 | tf_op jit(solution)/shard_map/ppermute | solution.py:25
  99.7 6.4 %collective-permute-start.19 = (bf16[96,1024]{1,0:T(8,128)(2,1)S(1)}, bf16[96,1024]{1,0:T(8,128)(2,1)S(1)}, u32[]{:S(2)}, u32[]{:S(2)}) collective-permute-start(bf16[96,1024]{1,0:T(8,128)(2,1)S(1)} %slice.81), channel_id=1, source_target_pairs={{0,16},{16,32},{32,48},{48,64},{64,80},{80,96},{96,112},{112,0},{1... | collective-permute-start | bytes 589832 | tf_op jit(solution)/shard_map/ppermute | solution.py:25
  102.7 7.6 %collective-permute-start.20 = (bf16[96,1024]{1,0:T(8,128)(2,1)S(1)}, bf16[96,1024]{1,0:T(8,128)(2,1)S(1)}, u32[]{:S(2)}, u32[]{:S(2)}) collective-permute-start(bf16[96,1024]{1,0:T(8,128)(2,1)S(1)} %slice.82), channel_id=1, source_target_pairs={{0,112},{16,0},{32,16},{48,32},{64,48},{80,64},{96,80},{112,96},{1... | collective-permute-start | bytes 589832 | tf_op jit(solution)/shard_map/ppermute | solution.py:25
  110.3 2.7 %copy-start = (bf16[2,2,8,96,1024]{4,3,2,1,0:T(8,128)(2,1)}, bf16[2,2,8,96,1024]{4,3,2,1,0:T(8,128)(2,1)S(1)}, u32[]{:S(2)}) copy-start(bf16[2,2,8,96,1024]{4,3,2,1,0:T(8,128)(2,1)S(1)} %bitcast_dynamic-update-slice_fusion) | copy-start | bytes 18874372
  110.3 9.2 %copy-start.2 = (f32[128]{0:T(128)S(1)}, f32[128]{0:T(128)}, u32[]{:S(2)}) copy-start(f32[128]{0:T(128)} %param.9) | copy-start | bytes 1540
  113.0 6.5 %collective-permute-start.22 = (f32[8,128]{1,0:T(8,128)S(1)}, f32[8,128]{1,0:T(8,128)S(1)}, u32[]{:S(2)}, u32[]{:S(2)}) collective-permute-start(f32[8,128]{1,0:T(8,128)S(1)} %reshape.142), channel_id=1, source_target_pairs={{0,256},{16,272},{32,288},{48,304},{64,320},{80,336},{96,352},{112... | collective-permute-start | bytes 12296 | tf_op jit(solution)/shard_map/ppermute | solution.py:20
  142.8 5.9 %collective-permute-start.23 = (bf16[16,96,256]{2,1,0:T(8,128)(2,1)S(1)}, bf16[16,96,256]{2,1,0:T(8,128)(2,1)S(1)}, u32[]{:S(2)}, u32[]{:S(2)}) collective-permute-start(bf16[16,96,256]{2,1,0:T(8,128)(2,1)S(1)} %bitcast.114), channel_id=1, source_target_pairs={{0,256},{16,272},{32,288},{48,304},{64,320},{80,336},{96,352},{112... | collective-permute-start | bytes 2359304 | tf_op jit(solution)/shard_map/ppermute | solution.py:20
  150.1 26.8 %all-to-all-start.1 = ((bf16[32,96,128]{2,1,0:T(8,128)(2,1)}), bf16[32,96,128]{2,1,0:T(8,128)(2,1)S(1)}, u32[]{:S(2)}, u32[]{:S(2)}) async-start(bf16[32,96,128]{2,1,0:T(8,128)(2,1)} %bitcast.52), calls=%async_computation.1 | async-start | bytes 1572864 | tf_op jit(solution)/shard_map/all_to_all | solution.py:35

commit v4 on v3

--- a/solution.py
+++ b/solution.py
@@ -53,17 +53,24 @@
     return lax.optimization_barrier((x,) + others)[0]
 
 
-def ring(block):
-    half = block.shape[0] // 2
-    fwd, bwd = block, block
-    parts = [(0, 0, block)]
-    for step in range(1, NY // 2):
-        fwd, bwd = along_y(fwd, 1), along_y(bwd, -1)
-        parts.append((-step, 0, fwd))
-        parts.append((step, 0, bwd))
-    parts.append((NY // 2, 0, along_y(fwd[:half], 1)))
-    parts.append((NY // 2, half, along_y(bwd[half:], -1)))
-    return parts
+def rings(blocks):
+    half = blocks[0].shape[0] // 2
+    all_parts, ends = [], {1: [], -1: []}
+    for block in blocks:
+        fwd, bwd = block, block
+        parts = [(0, 0, block)]
+        for step in range(1, NY // 2):
+            fwd, bwd = along_y(fwd, 1), along_y(bwd, -1)
+            parts.append((-step, 0, fwd))
+            parts.append((step, 0, bwd))
+        ends[1].append(fwd[:half])
+        ends[-1].append(bwd[half:])
+        all_parts.append(parts)
+    for way, at in ((1, 0), (-1, half)):
+        last = along_y(jnp.concatenate(ends[way]), way)
+        for parts, block in zip(all_parts, jnp.split(last, len(blocks))):
+            parts.append((NY // 2, at, block))
+    return all_parts
 
 
 def on_device(hidden, head, codes, exponents, loss_weight):
@@ -84,13 +91,14 @@
         )
 
     near = jnp.concatenate([columns(head, 0, 0), flip(columns(head, 1, 0), 1, 0)], axis=0)
-    near_parts = ring(near)
     away = lax.dynamic_slice_in_dim(head, (zh ^ 1) * 2 * width, 2 * width, axis=1)
     came = flip(away, 0, 1)
+    teacher = teacher_half(codes, exponents)
+    came = after(came, along_y(near, 1), along_y(near, -1), teacher)
     came_mine = lax.dynamic_slice_in_dim(came, s * width, width, axis=1)
     came_send = lax.dynamic_slice_in_dim(came, (s ^ 1) * width, width, axis=1)
     far = jnp.concatenate([came_mine, flip(came_send, 1, 0)], axis=0)
-    far_parts = ring(far)
+    near_parts, far_parts = rings([near, far])
 
     weights = jnp.zeros((2, NZH, NY, rows, width), head.dtype)
     for dz, parts in enumerate([near_parts, far_parts]):
@@ -104,7 +112,6 @@
     hidden = after(hidden, near_parts[1][2])
     h_sec = both(hidden, flip(hidden, 0, 1))
     h_all = jnp.concatenate([h_sec, flip(h_sec, 1, 0)], axis=1)
-    teacher = teacher_half(codes, exponents)
     t_send = after(columns(teacher, 0, 1), near_parts[3][2])
     scaled_t = both(columns(teacher, 0, 0), flip(t_send, 0, 1)).astype(jnp.float32)
 
@@ -152,10 +159,16 @@
         * (jnp.exp(scaled_s - student_lse[:, None]) - jnp.exp(scaled_t - teacher_lse[:, None]))
     ).astype(jnp.bfloat16)
 
-    g = lax.dot_general(
-        weights, logit_grad, (((1,), (1,)), ((), ())), preferred_element_type=jnp.float32
-    ).reshape(2, NQ, rows, 2 * tok)
-    g = g[0] + flip(g[1].astype(jnp.bfloat16), 1, 0).astype(jnp.float32)
+    logit_grad = after(logit_grad)
+
+    def grads(w):
+        return lax.dot_general(
+            w, logit_grad, (((1,), (1,)), ((), ())), preferred_element_type=jnp.float32
+        )
+
+    mine, theirs = jnp.split(weights, 2)
+    g = flip(grads(theirs).astype(jnp.bfloat16), 1, 0).astype(jnp.float32)
+    g = grads(mine) + g
     g = g.astype(jnp.bfloat16).reshape(NQ, rows, 2, tok)
     g = g.transpose(2, 0, 1, 3).reshape(NZH * NQ, rows, tok)
     g = exchange(g)

time: 180 us -> 187 us (1.039)
  blocking collectives: 17.8 us -> 0 us
  waiting for transfers between devices: 38.6 us -> 54.9 us
  local copies, waits for them, and re-layouts: 6.64 us -> 18 us
  starting transfers between devices: 99.8 us -> 95.9 us
    all_to_all x1 -> x0, blocking collectives: 17.8 us -> none  [exchange(): lax.all_to_all(x, ('section', 'dp', 'vocab'), split_axis=0, concat_axis=0...]
    ppermute x16 -> x14, waiting for transfers between devices: 13.7 us -> 25.7 us  [along_y(): return lax.ppermute(x, 'dp', perm)]
    all_to_all x1 -> x2, starting transfers between devices: 3.91 us -> 14.4 us  [exchange(): lax.all_to_all(x, ('section', 'dp', 'vocab'), split_axis=0, concat_axis=0...]
    ppermute x16 -> x14, starting transfers between devices: 49.2 us -> 40.6 us  [along_y(): return lax.ppermute(x, 'dp', perm)]
    split x0 -> x1, local copies, waits for them, and re-layouts: none -> 6.66 us  [on_device(): mine, theirs = jnp.split(weights, 2)]
    ppermute x8, starting transfers between devices: 46.6 us -> 40.9 us  [flip(): return lax.ppermute(x, ('section', 'dp'), perm)]
    dynamic_update_slice x18, local copies, waits for them, and re-layouts: 0.65 us -> 5.6 us  [on_device(): lax.dynamic_update_slice(weights, block, (at // rows, zh ^ dz, (y + dy) %...]
    all_to_all x1 -> x2, waiting for transfers between devices: 22.3 us -> 25.4 us  [exchange(): lax.all_to_all(x, ('section', 'dp', 'vocab'), split_axis=0, concat_axis=0...]
  transfers between devices with their start and end apart: 25 -> 24, of which waited for: 8 -> 11; matrix products, arithmetic and copies ran while one was open for 6% -> 12% of each run, Pallas kernels for 0% -> 0%
where the time goes in v4:
time: 187 us; the launch traced here: 184 us
  starting transfers between devices  95.9 us (51%)
  waiting for transfers between devices  54.9 us (29%)
  local copies, waits for them, and re-layouts  18 us (10%)
  other arithmetic  7.8 us (4%)
  matrix products  6.2 us (3%)
    ppermute x8, starting transfers between devices, flip(): return lax.ppermute(x, ('section', 'dp'), perm)  40.9 us
    ppermute x14, starting transfers between devices, along_y(): return lax.ppermute(x, 'dp', perm)  40.6 us
    ppermute x14, waiting for transfers between devices, along_y(): return lax.ppermute(x, 'dp', perm)  25.7 us
    all_to_all x2, waiting for transfers between devices, exchange(): lax.all_to_all(x, ('section', 'dp', 'vocab'), split_axis=0, concat_axis=0...  25.4 us
    all_to_all x2, starting transfers between devices, exchange(): lax.all_to_all(x, ('section', 'dp', 'vocab'), split_axis=0, concat_axis=0...  14.4 us
    split x1, local copies, waits for them, and re-layouts, on_device(): mine, theirs = jnp.split(weights, 2)  6.66 us
    dynamic_update_slice x18, local copies, waits for them, and re-layouts, on_device(): lax.dynamic_update_slice(weights, block, (at // rows, zh ^ dz, (y + dy) %...  5.6 us
    dot_general x2, matrix products, grads(): lax.dot_general(w, logit_grad, (((1,), (1,)), ((), ())), preferred_elemen...  4.26 us
  transfers between devices with their start and end apart: 24, of which 11 were waited for; matrix products, arithmetic and copies ran while one was open for 12% of the time, Pallas kernels for 0%

profile of v4, /device:TPU:25, one launch (start us, length us, event | category | flops | bytes accessed | tf_op | source)
XLA Modules:
  0.0 184.2 jit_solution(4584504219918979772)
XLA Ops:
  0.7 1.1 constant_dynamic-slice_fusion.9
  1.7 2.6 %collective-permute-start = (bf16[96,1024]{1,0:T(8,128)(2,1)S(1)}, bf16[96,1024]{1,0:T(8,128)(2,1)S(1)}, u32[]{:S(2)}, u32[]{:S(2)}) collective-permute-start(bf16[96,1024]{1,0:T(8,128)(2,1)S(1)} %get-tuple-element.18), channel_id=1, source_target_pairs={{0,256},{16,272},{32,288},{48,304},{64,320},{80,336},{96,352},{112... | collective-permute-start | bytes 589832 | tf_op jit(solution)/shard_map/ppermute | solution.py:20
  4.3 1.0 constant_dynamic-slice_fusion.7
  5.3 10.6 %collective-permute-start.9 = (bf16[96,2048]{1,0:T(8,128)(2,1)S(1)}, bf16[96,2048]{1,0:T(8,128)(2,1)S(1)}, u32[]{:S(2)}, u32[]{:S(2)}) collective-permute-start(bf16[96,2048]{1,0:T(8,128)(2,1)S(1)} %constant_dynamic-slice_fusion.7), channel_id=1, source_target_pairs={{0,128},{16,144},{32,160},{48,176},{64,192},{80,208},{96,224},{112... | collective-permute-start | bytes 1179656 | tf_op jit(solution)/shard_map/ppermute | solution.py:20
  16.9 4.4 %collective-permute-start.1 = (bf16[192,1024]{1,0:T(8,128)(2,1)S(1)}, bf16[192,1024]{1,0:T(8,128)(2,1)}, u32[]{:S(2)}, u32[]{:S(2)}) collective-permute-start(bf16[192,1024]{1,0:T(8,128)(2,1)S(1)} %pad_maximum_fusion), channel_id=1, source_target_pairs={{0,16},{16,32},{32,48},{48,64},{64,80},{80,96},{96,112},{112,0},{1... | collective-permute-start | bytes 1179656 | tf_op jit(solution)/shard_map/ppermute | solution.py:25
  21.3 1.9 %collective-permute-start.4 = (bf16[192,1024]{1,0:T(8,128)(2,1)S(1)}, bf16[192,1024]{1,0:T(8,128)(2,1)}, u32[]{:S(2)}, u32[]{:S(2)}) collective-permute-start(bf16[192,1024]{1,0:T(8,128)(2,1)S(1)} %pad_maximum_fusion), channel_id=1, source_target_pairs={{0,112},{16,0},{32,16},{48,32},{64,48},{80,64},{96,80},{112,96},{1... | collective-permute-start | bytes 1179656 | tf_op jit(solution)/shard_map/ppermute | solution.py:25
  23.8 2.9 %fusion = bf16[128,4096]{1,0:T(8,128)(2,1)S(1)} fusion(f32[16,8,32,128]{3,2,1,0:T(8,128)S(1)} %bitcast.116, s32[128,4096]{1,0:T(8,128)} %param.7), kind=kLoop, calls=%fused_computation.2 | loop fusion | flops 1572864 | bytes 5242880 | tf_op jit(solution)/shard_map/convert_element_type | solution.py:49
  26.8 2.7 %collective-permute-done.1 = bf16[192,1024]{1,0:T(8,128)(2,1)} collective-permute-done((bf16[192,1024]{1,0:T(8,128)(2,1)S(1)}, bf16[192,1024]{1,0:T(8,128)(2,1)}, u32[]{:S(2)}, u32[]{:S(2)}) %collective-permute-start.1) | collective-permute-done | bytes 393248 | tf_op jit(solution)/shard_map/ppermute | solution.py:25
  29.5 5.1 %collective-permute-done.4 = bf16[192,1024]{1,0:T(8,128)(2,1)} collective-permute-done((bf16[192,1024]{1,0:T(8,128)(2,1)S(1)}, bf16[192,1024]{1,0:T(8,128)(2,1)}, u32[]{:S(2)}, u32[]{:S(2)}) %collective-permute-start.4) | collective-permute-done | bytes 393248 | tf_op jit(solution)/shard_map/ppermute | solution.py:25
  34.6 3.3 %collective-permute-start.10 = (bf16[96,1024]{1,0:T(8,128)(2,1)S(1)}, bf16[96,1024]{1,0:T(8,128)(2,1)S(1)}, u32[]{:S(2)}, u32[]{:S(2)}) collective-permute-start(bf16[96,1024]{1,0:T(8,128)(2,1)S(1)} %get-tuple-element.20), channel_id=1, source_target_pairs={{0,256},{16,272},{32,288},{48,304},{64,320},{80,336},{96,352},{112... | collective-permute-start | bytes 589832 | tf_op jit(solution)/shard_map/ppermute | solution.py:20
  38.0 1.0 collective-permute-done.10
  39.1 1.9 %collective-permute-start.11 = (bf16[192,1024]{1,0:T(8,128)(2,1)S(1)}, bf16[192,1024]{1,0:T(8,128)(2,1)S(1)}, u32[]{:S(2)}, u32[]{:S(2)}) collective-permute-start(bf16[192,1024]{1,0:T(8,128)(2,1)S(1)} %pad_maximum_fusion.1), channel_id=1, source_target_pairs={{0,16},{16,32},{32,48},{48,64},{64,80},{80,96},{96,112},{112,0},{1... | collective-permute-start | bytes 1179656 | tf_op jit(solution)/shard_map/ppermute | solution.py:25
  41.0 3.4 %collective-permute-start.15 = (bf16[192,1024]{1,0:T(8,128)(2,1)S(1)}, bf16[192,1024]{1,0:T(8,128)(2,1)S(1)}, u32[]{:S(2)}, u32[]{:S(2)}) collective-permute-start(bf16[192,1024]{1,0:T(8,128)(2,1)S(1)} %pad_maximum_fusion.1), channel_id=1, source_target_pairs={{0,112},{16,0},{32,16},{48,32},{64,48},{80,64},{96,80},{112,96},{1... | collective-permute-start | bytes 1179656 | tf_op jit(solution)/shard_map/ppermute | solution.py:25
  44.4 3.1 %collective-permute-start.5 = (bf16[192,1024]{1,0:T(8,128)(2,1)}, bf16[192,1024]{1,0:T(8,128)(2,1)}, u32[]{:S(2)}, u32[]{:S(2)}) collective-permute-start(bf16[192,1024]{1,0:T(8,128)(2,1)} %collective-permute-done.1), channel_id=1, source_target_pairs={{0,16},{16,32},{32,48},{48,64},{64,80},{80,96},{96,112},{112,0},{1... | collective-permute-start | bytes 1179656 | tf_op jit(solution)/shard_map/ppermute | solution.py:25
  47.5 3.8 %collective-permute-done.11 = bf16[192,1024]{1,0:T(8,128)(2,1)S(1)} collective-permute-done((bf16[192,1024]{1,0:T(8,128)(2,1)S(1)}, bf16[192,1024]{1,0:T(8,128)(2,1)S(1)}, u32[]{:S(2)}, u32[]{:S(2)}) %collective-permute-start.11) | collective-permute-done | bytes 393248 | tf_op jit(solution)/shard_map/ppermute | solution.py:25
  51.3 3.4 %collective-permute-start.12 = (bf16[192,1024]{1,0:T(8,128)(2,1)S(1)}, bf16[192,1024]{1,0:T(8,128)(2,1)S(1)}, u32[]{:S(2)}, u32[]{:S(2)}) collective-permute-start(bf16[192,1024]{1,0:T(8,128)(2,1)S(1)} %collective-permute-done.11), channel_id=1, source_target_pairs={{0,16},{16,32},{32,48},{48,64},{64,80},{80,96},{96,112},{112,0},{1... | collective-permute-start | bytes 1179656 | tf_op jit(solution)/shard_map/ppermute | solution.py:25
  54.7 7.9 %collective-permute-start.2 = (bf16[128,1536]{1,0:T(8,128)(2,1)}, bf16[128,1536]{1,0:T(8,128)(2,1)}, u32[]{:S(2)}, u32[]{:S(2)}) collective-permute-start(bf16[128,1536]{1,0:T(8,128)(2,1)} %param.5), channel_id=1, source_target_pairs={{0,128},{16,144},{32,160},{48,176},{64,192},{80,208},{96,224},{112... | collective-permute-start | bytes 1179656 | tf_op jit(solution)/shard_map/ppermute | solution.py:20
  62.6 1.9 %collective-permute-start.6 = (bf16[192,1024]{1,0:T(8,128)(2,1)}, bf16[192,1024]{1,0:T(8,128)(2,1)}, u32[]{:S(2)}, u32[]{:S(2)}) collective-permute-start(bf16[192,1024]{1,0:T(8,128)(2,1)} %collective-permute-done.4), channel_id=1, source_target_pairs={{0,112},{16,0},{32,16},{48,32},{64,48},{80,64},{96,80},{112,96},{1... | collective-permute-start | bytes 1179656 | tf_op jit(solution)/shard_map/ppermute | solution.py:25
  64.6 1.9 %collective-permute-start.16 = (bf16[192,1024]{1,0:T(8,128)(2,1)S(1)}, bf16[192,1024]{1,0:T(8,128)(2,1)}, u32[]{:S(2)}, u32[]{:S(2)}) collective-permute-start(bf16[192,1024]{1,0:T(8,128)(2,1)S(1)} %collective-permute-done.15), channel_id=1, source_target_pairs={{0,112},{16,0},{32,16},{48,32},{64,48},{80,64},{96,80},{112,96},{1... | collective-permute-start | bytes 1179656 | tf_op jit(solution)/shard_map/ppermute | solution.py:25
  67.6 1.0 constant_dynamic-update-slice_fusion.12
  68.7 4.6 %collective-permute-start.7 = (bf16[192,1024]{1,0:T(8,128)(2,1)}, bf16[192,1024]{1,0:T(8,128)(2,1)S(1)}, u32[]{:S(2)}, u32[]{:S(2)}) collective-permute-start(bf16[192,1024]{1,0:T(8,128)(2,1)} %collective-permute-done.5), channel_id=1, source_target_pairs={{0,16},{16,32},{32,48},{48,64},{64,80},{80,96},{96,112},{112,0},{1... | collective-permute-start | bytes 1179656 | tf_op jit(solution)/shard_map/ppermute | solution.py:25
  73.2 3.4 %collective-permute-start.13 = (bf16[192,1024]{1,0:T(8,128)(2,1)S(1)}, bf16[192,1024]{1,0:T(8,128)(2,1)S(1)}, u32[]{:S(2)}, u32[]{:S(2)}) collective-permute-start(bf16[192,1024]{1,0:T(8,128)(2,1)S(1)} %collective-permute-done.12), channel_id=1, source_target_pairs={{0,16},{16,32},{32,48},{48,64},{64,80},{80,96},{96,112},{112,0},{1... | collective-permute-start | bytes 1179656 | tf_op jit(solution)/shard_map/ppermute | solution.py:25
  76.6 1.0 constant_dynamic-update-slice_fusion.11
  77.7 1.9 %collective-permute-start.8 = (bf16[192,1024]{1,0:T(8,128)(2,1)}, bf16[192,1024]{1,0:T(8,128)(2,1)S(1)}, u32[]{:S(2)}, u32[]{:S(2)}) collective-permute-start(bf16[192,1024]{1,0:T(8,128)(2,1)} %collective-permute-done.6), channel_id=1, source_target_pairs={{0,112},{16,0},{32,16},{48,32},{64,48},{80,64},{96,80},{112,96},{1... | collective-permute-start | bytes 1179656 | tf_op jit(solution)/shard_map/ppermute | solution.py:25
  79.6 2.9 %collective-permute-done.16 = bf16[192,1024]{1,0:T(8,128)(2,1)} collective-permute-done((bf16[192,1024]{1,0:T(8,128)(2,1)S(1)}, bf16[192,1024]{1,0:T(8,128)(2,1)}, u32[]{:S(2)}, u32[]{:S(2)}) %collective-permute-start.16) | collective-permute-done | bytes 393248 | tf_op jit(solution)/shard_map/ppermute | solution.py:25
  82.5 1.9 %collective-permute-start.17 = (bf16[192,1024]{1,0:T(8,128)(2,1)}, bf16[192,1024]{1,0:T(8,128)(2,1)S(1)}, u32[]{:S(2)}, u32[]{:S(2)}) collective-permute-start(bf16[192,1024]{1,0:T(8,128)(2,1)} %collective-permute-done.16), channel_id=1, source_target_pairs={{0,112},{16,0},{32,16},{48,32},{64,48},{80,64},{96,80},{112,96},{1... | collective-permute-start | bytes 1179656 | tf_op jit(solution)/shard_map/ppermute | solution.py:25
  84.5 1.5 maximum_select_fusion
  86.0 7.2 %collective-permute-start.3 = (bf16[256,1536]{1,0:T(8,128)(2,1)S(1)}, bf16[256,1536]{1,0:T(8,128)(2,1)S(1)}, u32[]{:S(2)}, u32[]{:S(2)}) collective-permute-start(bf16[256,1536]{1,0:T(8,128)(2,1)S(1)} %maximum_select_fusion), channel_id=1, source_target_pairs={{0,256},{16,272},{32,288},{48,304},{64,320},{80,336},{96,352},{112... | collective-permute-start | bytes 2359304 | tf_op jit(solution)/shard_map/ppermute | solution.py:20
  93.2 1.0 constant_dynamic-update-slice_fusion.10
  94.2 1.9 %collective-permute-start.19 = (bf16[128,1024]{1,0:T(8,128)(2,1)S(1)}, bf16[128,1024]{1,0:T(8,128)(2,1)S(1)}, u32[]{:S(2)}, u32[]{:S(2)}) collective-permute-start(bf16[128,1024]{1,0:T(8,128)(2,1)S(1)} %get-tuple-element.7), channel_id=1, source_target_pairs={{0,128},{16,144},{32,160},{48,176},{64,192},{80,208},{96,224},{112... | collective-permute-start | bytes 786440 | tf_op jit(solution)/shard_map/ppermute | solution.py:20
  96.2 4.9 %collective-permute-start.14 = (bf16[192,1024]{1,0:T(8,128)(2,1)S(1)}, bf16[192,1024]{1,0:T(8,128)(2,1)S(1)}, u32[]{:S(2)}, u32[]{:S(2)}) collective-permute-start(bf16[192,1024]{1,0:T(8,128)(2,1)S(1)} %pad_maximum_fusion.2), channel_id=1, source_target_pairs={{0,16},{16,32},{32,48},{48,64},{64,80},{80,96},{96,112},{112,0},{1... | collective-permute-start | bytes 1179656 | tf_op jit(solution)/shard_map/ppermute | solution.py:25
  101.1 1.0 constant_dynamic-update-slice_fusion.9
  102.2 1.9 %collective-permute-start.18 = (bf16[192,1024]{1,0:T(8,128)(2,1)S(1)}, bf16[192,1024]{1,0:T(8,128)(2,1)S(1)}, u32[]{:S(2)}, u32[]{:S(2)}) collective-permute-start(bf16[192,1024]{1,0:T(8,128)(2,1)S(1)} %pad_maximum_fusion.3), channel_id=1, source_target_pairs={{0,112},{16,0},{32,16},{48,32},{64,48},{80,64},{96,80},{112,96},{1... | collective-permute-start | bytes 1179656 | tf_op jit(solution)/shard_map/ppermute | solution.py:25
  104.3 5.3 %collective-permute-done.14 = bf16[192,1024]{1,0:T(8,128)(2,1)S(1)} collective-permute-done((bf16[192,1024]{1,0:T(8,128)(2,1)S(1)}, bf16[192,1024]{1,0:T(8,128)(2,1)S(1)}, u32[]{:S(2)}, u32[]{:S(2)}) %collective-permute-start.14) | collective-permute-done | bytes 393248 | tf_op jit(solution)/shard_map/ppermute | solution.py:25
  109.6 5.8 %collective-permute-done.18 = bf16[192,1024]{1,0:T(8,128)(2,1)S(1)} collective-permute-done((bf16[192,1024]{1,0:T(8,128)(2,1)S(1)}, bf16[192,1024]{1,0:T(8,128)(2,1)S(1)}, u32[]{:S(2)}, u32[]{:S(2)}) %collective-permute-start.18) | collective-permute-done | bytes 393248 | tf_op jit(solution)/shard_map/ppermute | solution.py:25
  115.7 1.0 constant_dynamic-update-slice_fusion.2
  116.9 1.9 %fusion.32 = (f32[256]{0:T(256)S(1)}, f32[256,1024]{1,0:T(8,128)S(1)}) fusion(bf16[3072,1024]{1,0:T(8,128)(2,1)S(1)} %bitcast.115, bf16[256,1536]{1,0:T(8,128)(2,1)S(1)} %collective-permute-done.3, bf16[256,1536]{1,0:T(8,128)(2,1)S(1)} %maximum_select_fusion), kind=kOutput, calls=%fused_computation.87 | convolution fusion | flops 1614282496 | bytes 8913920 | tf_op jit(solution)/shard_map/dot_general | solution.py:118
  119.5 3.3 %collective-permute-start.20 = (f32[8,128]{1,0:T(8,128)S(1)}, f32[8,128]{1,0:T(8,128)S(1)}, u32[]{:S(2)}, u32[]{:S(2)}) collective-permute-start(f32[8,128]{1,0:T(8,128)S(1)} %reshape.138), channel_id=1, source_target_pairs={{0,256},{16,272},{32,288},{48,304},{64,320},{80,336},{96,352},{112... | collective-permute-start | bytes 12296 | tf_op jit(solution)/shard_map/ppermute | solution.py:20
  124.5 9.5 %all-to-all-start = ((f32[32,8,128]{2,1,0:T(8,128)}), f32[32,8,128]{2,1,0:T(8,128)S(1)}, u32[]{:S(2)}, u32[]{:S(2)}) async-start(f32[32,8,128]{2,1,0:T(8,128)} %bitcast.41), calls=%async_computation | async-start | bytes 262144 | tf_op jit(solution)/shard_map/all_to_all | solution.py:35
  134.0 6.7 %fusion.31 = (bf16[1,2,8,96,1024]{4,3,2,1,0:T(8,128)(2,1)}, bf16[1,2,8,96,1024]{4,3,2,1,0:T(8,128)(2,1)}) fusion(bf16[2,2,8,96,1024]{4,3,2,1,0:T(8,128)(2,1)} %copy-done), kind=kLoop, calls=%fused_computation.86 | loop fusion | bytes 12582912 | tf_op jit(solution)/shard_map/split | solution.py:169
  140.6 3.1 %all-to-all-done = f32[32,8,128]{2,1,0:T(8,128)S(1)} async-done(((f32[32,8,128]{2,1,0:T(8,128)}), f32[32,8,128]{2,1,0:T(8,128)S(1)}, u32[]{:S(2)}, u32[]{:S(2)}) %all-to-all-start) | async-done | bytes 131104 | tf_op jit(solution)/shard_map/all_to_all | solution.py:35
  144.4 3.2 %convolution_convert_fusion = bf16[1536,256]{1,0:T(8,128)(2,1)S(1)} fusion(bf16[1536,1024]{1,0:T(8,128)(2,1)} %bitcast.118, bf16[256,1024]{1,0:T(8,128)(2,1)S(1)} %fusion.14), kind=kOutput, calls=%fused_computation | convolution fusion | flops 805699584 | bytes 4456448 | tf_op jit(solution)/shard_map/dot_general | solution.py:165
  147.6 4.0 %collective-permute-start.21 = (bf16[1536,256]{1,0:T(8,128)(2,1)S(1)}, bf16[1536,256]{1,0:T(8,128)(2,1)S(1)}, u32[]{:S(2)}, u32[]{:S(2)}) collective-permute-start(bf16[1536,256]{1,0:T(8,128)(2,1)S(1)} %convolution_convert_fusion), channel_id=1, source_target_pairs={{0,256},{16,272},{32,288},{48,304},{64,320},{80,336},{96,352},{112... | collective-permute-start | bytes 2359304 | tf_op jit(solution)/shard_map/ppermute | solution.py:20
  151.6 1.9 %collective-permute-done.21 = bf16[1536,256]{1,0:T(8,128)(2,1)S(1)} collective-permute-done((bf16[1536,256]{1,0:T(8,128)(2,1)S(1)}, bf16[1536,256]{1,0:T(8,128)(2,1)S(1)}, u32[]{:S(2)}, u32[]{:S(2)}) %collective-permute-start.21) | collective-permute-done | bytes 786464 | tf_op jit(solution)/shard_map/ppermute | solution.py:20
  153.5 1.0 add_convert_fusion
  154.8 1.0 copy.53
  155.8 4.9 %all-to-all-start.1 = ((bf16[32,96,128]{2,1,0:T(8,128)(2,1)}), bf16[32,96,128]{2,1,0:T(8,128)(2,1)S(1)}, u32[]{:S(2)}, u32[]{:S(2)}) async-start(bf16[32,96,128]{2,1,0:T(8,128)(2,1)} %bitcast.52), calls=%async_computation.1 | async-start | bytes 1572864 | tf_op jit(solution)/shard_map/all_to_all | solution.py:35
  161.3 22.2 %all-to-all-done.1 = bf16[32,96,128]{2,1,0:T(8,128)(2,1)S(1)} async-done(((bf16[32,96,128]{2,1,0:T(8,128)(2,1)}), bf16[32,96,128]{2,1,0:T(8,128)(2,1)S(1)}, u32[]{:S(2)}, u32[]{:S(2)}) %all-to-all-start.1) | async-done | bytes 786464 | tf_op jit(solution)/shard_map/all_to_all | solution.py:35
  (70 shorter events, 7.3 us)
Async XLA Ops:
  1.7 15.1 %collective-permute-start = (bf16[96,1024]{1,0:T(8,128)(2,1)S(1)}, bf16[96,1024]{1,0:T(8,128)(2,1)S(1)}, u32[]{:S(2)}, u32[]{:S(2)}) collective-permute-start(bf16[96,1024]{1,0:T(8,128)(2,1)S(1)} %get-tuple-element.18), channel_id=1, source_target_pairs={{0,256},{16,272},{32,288},{48,304},{64,320},{80,336},{96,352},{112... | collective-permute-start | bytes 589832 | tf_op jit(solution)/shard_map/ppermute | solution.py:20
  5.3 21.4 %collective-permute-start.9 = (bf16[96,2048]{1,0:T(8,128)(2,1)S(1)}, bf16[96,2048]{1,0:T(8,128)(2,1)S(1)}, u32[]{:S(2)}, u32[]{:S(2)}) collective-permute-start(bf16[96,2048]{1,0:T(8,128)(2,1)S(1)} %constant_dynamic-slice_fusion.7), channel_id=1, source_target_pairs={{0,128},{16,144},{32,160},{48,176},{64,192},{80,208},{96,224},{112... | collective-permute-start | bytes 1179656 | tf_op jit(solution)/shard_map/ppermute | solution.py:20
  16.9 12.6 %collective-permute-start.1 = (bf16[192,1024]{1,0:T(8,128)(2,1)S(1)}, bf16[192,1024]{1,0:T(8,128)(2,1)}, u32[]{:S(2)}, u32[]{:S(2)}) collective-permute-start(bf16[192,1024]{1,0:T(8,128)(2,1)S(1)} %pad_maximum_fusion), channel_id=1, source_target_pairs={{0,16},{16,32},{32,48},{48,64},{64,80},{80,96},{96,112},{112,0},{1... | collective-permute-start | bytes 1179656 | tf_op jit(solution)/shard_map/ppermute | solution.py:25
  21.3 13.3 %collective-permute-start.4 = (bf16[192,1024]{1,0:T(8,128)(2,1)S(1)}, bf16[192,1024]{1,0:T(8,128)(2,1)}, u32[]{:S(2)}, u32[]{:S(2)}) collective-permute-start(bf16[192,1024]{1,0:T(8,128)(2,1)S(1)} %pad_maximum_fusion), channel_id=1, source_target_pairs={{0,112},{16,0},{32,16},{48,32},{64,48},{80,64},{96,80},{112,96},{1... | collective-permute-start | bytes 1179656 | tf_op jit(solution)/shard_map/ppermute | solution.py:25
  34.6 4.4 %collective-permute-start.10 = (bf16[96,1024]{1,0:T(8,128)(2,1)S(1)}, bf16[96,1024]{1,0:T(8,128)(2,1)S(1)}, u32[]{:S(2)}, u32[]{:S(2)}) collective-permute-start(bf16[96,1024]{1,0:T(8,128)(2,1)S(1)} %get-tuple-element.20), channel_id=1, source_target_pairs={{0,256},{16,272},{32,288},{48,304},{64,320},{80,336},{96,352},{112... | collective-permute-start | bytes 589832 | tf_op jit(solution)/shard_map/ppermute | solution.py:20
  39.1 12.2 %collective-permute-start.11 = (bf16[192,1024]{1,0:T(8,128)(2,1)S(1)}, bf16[192,1024]{1,0:T(8,128)(2,1)S(1)}, u32[]{:S(2)}, u32[]{:S(2)}) collective-permute-start(bf16[192,1024]{1,0:T(8,128)(2,1)S(1)} %pad_maximum_fusion.1), channel_id=1, source_target_pairs={{0,16},{16,32},{32,48},{48,64},{64,80},{80,96},{96,112},{112,0},{1... | collective-permute-start | bytes 1179656 | tf_op jit(solution)/shard_map/ppermute | solution.py:25
  41.0 23.6 %collective-permute-start.15 = (bf16[192,1024]{1,0:T(8,128)(2,1)S(1)}, bf16[192,1024]{1,0:T(8,128)(2,1)S(1)}, u32[]{:S(2)}, u32[]{:S(2)}) collective-permute-start(bf16[192,1024]{1,0:T(8,128)(2,1)S(1)} %pad_maximum_fusion.1), channel_id=1, source_target_pairs={{0,112},{16,0},{32,16},{48,32},{64,48},{80,64},{96,80},{112,96},{1... | collective-permute-start | bytes 1179656 | tf_op jit(solution)/shard_map/ppermute | solution.py:25
  44.4 24.3 %collective-permute-start.5 = (bf16[192,1024]{1,0:T(8,128)(2,1)}, bf16[192,1024]{1,0:T(8,128)(2,1)}, u32[]{:S(2)}, u32[]{:S(2)}) collective-permute-start(bf16[192,1024]{1,0:T(8,128)(2,1)} %collective-permute-done.1), channel_id=1, source_target_pairs={{0,16},{16,32},{32,48},{48,64},{64,80},{80,96},{96,112},{112,0},{1... | collective-permute-start | bytes 1179656 | tf_op jit(solution)/shard_map/ppermute | solution.py:25
  51.3 22.0 %collective-permute-start.12 = (bf16[192,1024]{1,0:T(8,128)(2,1)S(1)}, bf16[192,1024]{1,0:T(8,128)(2,1)S(1)}, u32[]{:S(2)}, u32[]{:S(2)}) collective-permute-start(bf16[192,1024]{1,0:T(8,128)(2,1)S(1)} %collective-permute-done.11), channel_id=1, source_target_pairs={{0,16},{16,32},{32,48},{48,64},{64,80},{80,96},{96,112},{112,0},{1... | collective-permute-start | bytes 1179656 | tf_op jit(solution)/shard_map/ppermute | solution.py:25
  54.7 29.7 %collective-permute-start.2 = (bf16[128,1536]{1,0:T(8,128)(2,1)}, bf16[128,1536]{1,0:T(8,128)(2,1)}, u32[]{:S(2)}, u32[]{:S(2)}) collective-permute-start(bf16[128,1536]{1,0:T(8,128)(2,1)} %param.5), channel_id=1, source_target_pairs={{0,128},{16,144},{32,160},{48,176},{64,192},{80,208},{96,224},{112... | collective-permute-start | bytes 1179656 | tf_op jit(solution)/shard_map/ppermute | solution.py:20
  62.6 15.0 %collective-permute-start.6 = (bf16[192,1024]{1,0:T(8,128)(2,1)}, bf16[192,1024]{1,0:T(8,128)(2,1)}, u32[]{:S(2)}, u32[]{:S(2)}) collective-permute-start(bf16[192,1024]{1,0:T(8,128)(2,1)} %collective-permute-done.4), channel_id=1, source_target_pairs={{0,112},{16,0},{32,16},{48,32},{64,48},{80,64},{96,80},{112,96},{1... | collective-permute-start | bytes 1179656 | tf_op jit(solution)/shard_map/ppermute | solution.py:25
  64.6 18.0 %collective-permute-start.16 = (bf16[192,1024]{1,0:T(8,128)(2,1)S(1)}, bf16[192,1024]{1,0:T(8,128)(2,1)}, u32[]{:S(2)}, u32[]{:S(2)}) collective-permute-start(bf16[192,1024]{1,0:T(8,128)(2,1)S(1)} %collective-permute-done.15), channel_id=1, source_target_pairs={{0,112},{16,0},{32,16},{48,32},{64,48},{80,64},{96,80},{112,96},{1... | collective-permute-start | bytes 1179656 | tf_op jit(solution)/shard_map/ppermute | solution.py:25
  68.7 25.6 %collective-permute-start.7 = (bf16[192,1024]{1,0:T(8,128)(2,1)}, bf16[192,1024]{1,0:T(8,128)(2,1)S(1)}, u32[]{:S(2)}, u32[]{:S(2)}) collective-permute-start(bf16[192,1024]{1,0:T(8,128)(2,1)} %collective-permute-done.5), channel_id=1, source_target_pairs={{0,16},{16,32},{32,48},{48,64},{64,80},{80,96},{96,112},{112,0},{1... | collective-permute-start | bytes 1179656 | tf_op jit(solution)/shard_map/ppermute | solution.py:25
  73.2 22.9 %collective-permute-start.13 = (bf16[192,1024]{1,0:T(8,128)(2,1)S(1)}, bf16[192,1024]{1,0:T(8,128)(2,1)S(1)}, u32[]{:S(2)}, u32[]{:S(2)}) collective-permute-start(bf16[192,1024]{1,0:T(8,128)(2,1)S(1)} %collective-permute-done.12), channel_id=1, source_target_pairs={{0,16},{16,32},{32,48},{48,64},{64,80},{80,96},{96,112},{112,0},{1... | collective-permute-start | bytes 1179656 | tf_op jit(solution)/shard_map/ppermute | solution.py:25
  77.7 24.5 %collective-permute-start.8 = (bf16[192,1024]{1,0:T(8,128)(2,1)}, bf16[192,1024]{1,0:T(8,128)(2,1)S(1)}, u32[]{:S(2)}, u32[]{:S(2)}) collective-permute-start(bf16[192,1024]{1,0:T(8,128)(2,1)} %collective-permute-done.6), channel_id=1, source_target_pairs={{0,112},{16,0},{32,16},{48,32},{64,48},{80,64},{96,80},{112,96},{1... | collective-permute-start | bytes 1179656 | tf_op jit(solution)/shard_map/ppermute | solution.py:25
  82.5 19.6 %collective-permute-start.17 = (bf16[192,1024]{1,0:T(8,128)(2,1)}, bf16[192,1024]{1,0:T(8,128)(2,1)S(1)}, u32[]{:S(2)}, u32[]{:S(2)}) collective-permute-start(bf16[192,1024]{1,0:T(8,128)(2,1)} %collective-permute-done.16), channel_id=1, source_target_pairs={{0,112},{16,0},{32,16},{48,32},{64,48},{80,64},{96,80},{112,96},{1... | collective-permute-start | bytes 1179656 | tf_op jit(solution)/shard_map/ppermute | solution.py:25
  86.0 30.9 %collective-permute-start.3 = (bf16[256,1536]{1,0:T(8,128)(2,1)S(1)}, bf16[256,1536]{1,0:T(8,128)(2,1)S(1)}, u32[]{:S(2)}, u32[]{:S(2)}) collective-permute-start(bf16[256,1536]{1,0:T(8,128)(2,1)S(1)} %maximum_select_fusion), channel_id=1, source_target_pairs={{0,256},{16,272},{32,288},{48,304},{64,320},{80,336},{96,352},{112... | collective-permute-start | bytes 2359304 | tf_op jit(solution)/shard_map/ppermute | solution.py:20
  94.2 24.6 %collective-permute-start.19 = (bf16[128,1024]{1,0:T(8,128)(2,1)S(1)}, bf16[128,1024]{1,0:T(8,128)(2,1)S(1)}, u32[]{:S(2)}, u32[]{:S(2)}) collective-permute-start(bf16[128,1024]{1,0:T(8,128)(2,1)S(1)} %get-tuple-element.7), channel_id=1, source_target_pairs={{0,128},{16,144},{32,160},{48,176},{64,192},{80,208},{96,224},{112... | collective-permute-start | bytes 786440 | tf_op jit(solution)/shard_map/ppermute | solution.py:20
  96.2 13.4 %collective-permute-start.14 = (bf16[192,1024]{1,0:T(8,128)(2,1)S(1)}, bf16[192,1024]{1,0:T(8,128)(2,1)S(1)}, u32[]{:S(2)}, u32[]{:S(2)}) collective-permute-start(bf16[192,1024]{1,0:T(8,128)(2,1)S(1)} %pad_maximum_fusion.2), channel_id=1, source_target_pairs={{0,16},{16,32},{32,48},{48,64},{64,80},{80,96},{96,112},{112,0},{1... | collective-permute-start | bytes 1179656 | tf_op jit(solution)/shard_map/ppermute | solution.py:25
  102.2 13.2 %collective-permute-start.18 = (bf16[192,1024]{1,0:T(8,128)(2,1)S(1)}, bf16[192,1024]{1,0:T(8,128)(2,1)S(1)}, u32[]{:S(2)}, u32[]{:S(2)}) collective-permute-start(bf16[192,1024]{1,0:T(8,128)(2,1)S(1)} %pad_maximum_fusion.3), channel_id=1, source_target_pairs={{0,112},{16,0},{32,16},{48,32},{64,48},{80,64},{96,80},{112,96},{1... | collective-permute-start | bytes 1179656 | tf_op jit(solution)/shard_map/ppermute | solution.py:25
  116.9 2.6 %copy-start = (bf16[2,2,8,96,1024]{4,3,2,1,0:T(8,128)(2,1)}, bf16[2,2,8,96,1024]{4,3,2,1,0:T(8,128)(2,1)S(1)}, u32[]{:S(2)}) copy-start(bf16[2,2,8,96,1024]{4,3,2,1,0:T(8,128)(2,1)S(1)} %fusion.15) | copy-start | bytes 18874372
  116.9 6.9 %copy-start.2 = (f32[128]{0:T(128)S(1)}, f32[128]{0:T(128)}, u32[]{:S(2)}) copy-start(f32[128]{0:T(128)} %param.9) | copy-start | bytes 1540
  119.5 4.1 %collective-permute-start.20 = (f32[8,128]{1,0:T(8,128)S(1)}, f32[8,128]{1,0:T(8,128)S(1)}, u32[]{:S(2)}, u32[]{:S(2)}) collective-permute-start(f32[8,128]{1,0:T(8,128)S(1)} %reshape.138), channel_id=1, source_target_pairs={{0,256},{16,272},{32,288},{48,304},{64,320},{80,336},{96,352},{112... | collective-permute-start | bytes 12296 | tf_op jit(solution)/shard_map/ppermute | solution.py:20
  124.5 19.3 %all-to-all-start = ((f32[32,8,128]{2,1,0:T(8,128)}), f32[32,8,128]{2,1,0:T(8,128)S(1)}, u32[]{:S(2)}, u32[]{:S(2)}) async-start(f32[32,8,128]{2,1,0:T(8,128)} %bitcast.41), calls=%async_computation | async-start | bytes 262144 | tf_op jit(solution)/shard_map/all_to_all | solution.py:35
  143.8 9.8 %copy-start.1 = (bf16[1,2,8,96,1024]{4,3,2,1,0:T(8,128)(2,1)S(1)}, bf16[1,2,8,96,1024]{4,3,2,1,0:T(8,128)(2,1)}, u32[]{:S(2)}) copy-start(bf16[1,2,8,96,1024]{4,3,2,1,0:T(8,128)(2,1)} %get-tuple-element.14) | copy-start | bytes 9437188
  147.6 5.9 %collective-permute-start.21 = (bf16[1536,256]{1,0:T(8,128)(2,1)S(1)}, bf16[1536,256]{1,0:T(8,128)(2,1)S(1)}, u32[]{:S(2)}, u32[]{:S(2)}) collective-permute-start(bf16[1536,256]{1,0:T(8,128)(2,1)S(1)} %convolution_convert_fusion), channel_id=1, source_target_pairs={{0,256},{16,272},{32,288},{48,304},{64,320},{80,336},{96,352},{112... | collective-permute-start | bytes 2359304 | tf_op jit(solution)/shard_map/ppermute | solution.py:20
  155.8 27.7 %all-to-all-start.1 = ((bf16[32,96,128]{2,1,0:T(8,128)(2,1)}), bf16[32,96,128]{2,1,0:T(8,128)(2,1)S(1)}, u32[]{:S(2)}, u32[]{:S(2)}) async-start(bf16[32,96,128]{2,1,0:T(8,128)(2,1)} %bitcast.52), calls=%async_computation.1 | async-start | bytes 1572864 | tf_op jit(solution)/shard_map/all_to_all | solution.py:35

commit v5 on v3

--- a/solution.py
+++ b/solution.py
@@ -1,6 +1,8 @@
 import jax
 import jax.numpy as jnp
 from jax import lax
+from jax.experimental import pallas as pl
+from jax.experimental.pallas import tpu as pltpu
 from jax.sharding import PartitionSpec as P
 
 GROUP = 128
@@ -8,6 +10,8 @@
 NY = 8
 NZH = 2
 NQ = 16
+NX = 4
+NZL = 4
 
 
 def flip(x, ds, dz):
@@ -25,13 +29,31 @@
     return lax.ppermute(x, "dp", perm)
 
 
-def exchange(x):
+def exchange(x, axis):
     n = NZH * NY * NQ
-    groups = [
-        [s * n + (zh * NY + y) * NQ + q for zh in range(NZH) for q in range(NQ)]
-        for s in range(2)
-        for y in range(NY)
-    ]
+
+    def device(s, y, zh, x, zl):
+        return s * n + (zh * NY + y) * NQ + x * NZL + zl
+
+    rest = [(s, y) for s in range(2) for y in range(NY)]
+    if axis == "x":
+        groups = [
+            [device(s, y, zh, x, zl) for x in range(NX)]
+            for s, y in rest
+            for zh in range(NZH)
+            for zl in range(NZL)
+        ]
+    elif axis == "z":
+        groups = [
+            [device(s, y, zh, x, zl) for zh in range(NZH) for zl in range(NZL)]
+            for s, y in rest
+            for x in range(NX)
+        ]
+    else:
+        groups = [
+            [device(s, y, zh, x, zl) for zh in range(NZH) for x in range(NX) for zl in range(NZL)]
+            for s, y in rest
+        ]
     return lax.all_to_all(
         x,
         ("section", "dp", "vocab"),
@@ -53,17 +75,41 @@
     return lax.optimization_barrier((x,) + others)[0]
 
 
-def ring(block):
+def ring_step(parts, *others):
+    block = parts[0][2]
     half = block.shape[0] // 2
-    fwd, bwd = block, block
-    parts = [(0, 0, block)]
-    for step in range(1, NY // 2):
-        fwd, bwd = along_y(fwd, 1), along_y(bwd, -1)
-        parts.append((-step, 0, fwd))
-        parts.append((step, 0, bwd))
-    parts.append((NY // 2, 0, along_y(fwd[:half], 1)))
-    parts.append((NY // 2, half, along_y(bwd[half:], -1)))
-    return parts
+    k = len(parts) // 2 + 1
+    fwd, bwd = (block, block) if k == 1 else (parts[-2][2], parts[-1][2])
+    if k == NY // 2:
+        fwd, bwd = fwd[:half], bwd[half:]
+    fwd = along_y(after(fwd, *others) if others else fwd, 1)
+    bwd = along_y(after(bwd, *others) if others else bwd, -1)
+    return parts + [(-k, 0, fwd), (k, half if k == NY // 2 else 0, bwd)]
+
+
+def came_in(parts):
+    return parts[-2][2], parts[-1][2]
+
+
+def split_columns(x, s):
+    rows, cols = x.shape
+    half = cols // 2
+
+    def kernel(s_ref, x_ref, mine_ref, send_ref):
+        at = s_ref[0] * half
+        mine_ref[...] = x_ref[:, pl.ds(pl.multiple_of(at, half), half)]
+        send_ref[...] = x_ref[:, pl.ds(pl.multiple_of(half - at, half), half)]
+
+    return pl.pallas_call(
+        kernel,
+        in_specs=[
+            pl.BlockSpec(memory_space=pltpu.SMEM),
+            pl.BlockSpec(memory_space=pltpu.VMEM),
+        ],
+        out_specs=[pl.BlockSpec(memory_space=pltpu.VMEM)] * 2,
+        out_shape=[jax.ShapeDtypeStruct((rows, half), x.dtype)] * 2,
+        cost_estimate=pl.CostEstimate(flops=10000000000, bytes_accessed=1000000, transcendentals=0),
+    )(s[None], x)
 
 
 def on_device(hidden, head, codes, exponents, loss_weight):
@@ -84,13 +130,21 @@
         )
 
     near = jnp.concatenate([columns(head, 0, 0), flip(columns(head, 1, 0), 1, 0)], axis=0)
-    near_parts = ring(near)
     away = lax.dynamic_slice_in_dim(head, (zh ^ 1) * 2 * width, 2 * width, axis=1)
     came = flip(away, 0, 1)
-    came_mine = lax.dynamic_slice_in_dim(came, s * width, width, axis=1)
-    came_send = lax.dynamic_slice_in_dim(came, (s ^ 1) * width, width, axis=1)
-    far = jnp.concatenate([came_mine, flip(came_send, 1, 0)], axis=0)
-    far_parts = ring(far)
+    teacher = teacher_half(codes, exponents)
+    near_one = ring_step([(0, 0, near)])
+    near_two = ring_step(near_one)
+    came_mine, came_send = split_columns(came, s)
+    came_mine = after(came_mine, *came_in(near_two))
+    came_flip = flip(came_send, 1, 0)
+    far = jnp.concatenate([came_mine, came_flip], axis=0)
+    far_one = ring_step([(0, 0, far)])
+    near_three = ring_step(near_two)
+    far_two = ring_step(far_one, *came_in(near_three))
+    far_three = ring_step(far_two)
+    near_parts = ring_step(near_three)
+    far_parts = ring_step(far_three)
 
     weights = jnp.zeros((2, NZH, NY, rows, width), head.dtype)
     for dz, parts in enumerate([near_parts, far_parts]):
@@ -101,11 +155,10 @@
             )
     weights = weights.reshape(2 * NZH * NY * rows, width)
 
-    hidden = after(hidden, near_parts[1][2])
-    h_sec = both(hidden, flip(hidden, 0, 1))
+    h_other = flip(after(hidden, came_flip), 0, 1)
+    h_sec = both(hidden, after(h_other, *came_in(far_two)))
     h_all = jnp.concatenate([h_sec, flip(h_sec, 1, 0)], axis=1)
-    teacher = teacher_half(codes, exponents)
-    t_send = after(columns(teacher, 0, 1), near_parts[3][2])
+    t_send = after(columns(teacher, 0, 1), *came_in(far_one))
     scaled_t = both(columns(teacher, 0, 0), flip(t_send, 0, 1)).astype(jnp.float32)
 
     logits = jnp.dot(h_all, weights, preferred_element_type=jnp.float32)
@@ -121,21 +174,24 @@
         ]
     ).reshape(8, tok)
 
-    stats = jnp.stack([stats, flip(stats, 1, 0)])
-    top = jnp.max(stats[:, 0:2], axis=0)
-    s_sum = jnp.sum(stats[:, 2:4] * jnp.exp(stats[:, 0:2] - top), axis=0)
-    rest = jnp.sum(stats[:, 4:8], axis=0)
+    def merged(parts):
+        top = jnp.max(parts[:, 0:2], axis=0)
+        s_sum = jnp.sum(parts[:, 2:4] * jnp.exp(parts[:, 0:2] - top), axis=0)
+        return top, s_sum, jnp.sum(parts[:, 4:8], axis=0)
+
+    stats = jnp.concatenate(merged(jnp.stack([stats, flip(stats, 1, 0)])))
+    top, s_sum, rest = merged(exchange(jnp.broadcast_to(stats, (NX, 8, tok)), "x"))
     tiles = [
         jnp.concatenate([top, s_sum, rest[0:2], rest[2 + z : 3 + z], loss_weight[None]])
         for z in range(NZH)
     ]
-    parts = jnp.broadcast_to(jnp.stack(tiles)[:, None], (NZH, NQ, 8, tok))
-    parts = exchange(parts.reshape(NZH * NQ, 8, tok))
+    parts = jnp.broadcast_to(jnp.stack(tiles)[:, None], (NZH, NZL, 8, tok))
+    parts = exchange(parts.reshape(NZH * NZL, 8, tok), "z")
     top = jnp.max(parts[:, 0:2], axis=0)
     s_sum = jnp.sum(parts[:, 2:4] * jnp.exp(parts[:, 0:2] - top), axis=0)
     t_sum = jnp.sum(parts[:, 4:6], axis=0)
     cross = jnp.sum(parts[:, 6], axis=0)
-    weight = jnp.concatenate([parts[0, 7], parts[NQ, 7]])
+    weight = jnp.concatenate([parts[0, 7], parts[NZL, 7]])
     student_lse = top + jnp.log(s_sum)
     teacher_lse = jnp.log(t_sum)
 
@@ -156,9 +212,10 @@
         weights, logit_grad, (((1,), (1,)), ((), ())), preferred_element_type=jnp.float32
     ).reshape(2, NQ, rows, 2 * tok)
     g = g[0] + flip(g[1].astype(jnp.bfloat16), 1, 0).astype(jnp.float32)
-    g = g.astype(jnp.bfloat16).reshape(NQ, rows, 2, tok)
-    g = g.transpose(2, 0, 1, 3).reshape(NZH * NQ, rows, tok)
-    g = exchange(g)
+    g = g.astype(jnp.bfloat16).reshape(NX, NZL * rows, 2 * tok)
+    g = jnp.sum(exchange(g, "x").reshape(g.shape).astype(jnp.float32), axis=0)
+    g = g.astype(jnp.bfloat16).reshape(NZL, rows, NZH, tok)
+    g = exchange(g.transpose(2, 0, 1, 3).reshape(NZH * NZL, rows, tok), "z")
     g = jnp.sum(g.astype(jnp.float32), axis=0)
     return (kl_loss, g.T.astype(jnp.bfloat16))
 

time: 180 us -> 187 us (1.039)
  blocking collectives: 17.8 us -> 34.3 us
  waiting for transfers between devices: 38.6 us -> 29.4 us
  starting transfers between devices: 99.8 us -> 96.9 us
    all_to_all x1 -> x3, blocking collectives: 17.8 us -> 34.3 us  [exchange(): lax.all_to_all(x, ('section', 'dp', 'vocab'), split_axis=0, concat_axis=0...]
    all_to_all x1, waiting for transfers between devices: 22.3 us -> 7.95 us  [exchange(): lax.all_to_all(x, ('section', 'dp', 'vocab'), split_axis=0, concat_axis=0...]
    ppermute x16, waiting for transfers between devices: 13.7 us -> 18.6 us  [along_y(): return lax.ppermute(x, 'dp', perm)]
    ppermute x8, starting transfers between devices: 46.6 us -> 42.8 us  [flip(): return lax.ppermute(x, ('section', 'dp'), perm)]
  transfers between devices with their start and end apart: 25 -> 25, of which waited for: 8 -> 9; matrix products, arithmetic and copies ran while one was open for 6% -> 6% of each run, Pallas kernels for 0% -> 1%
where the time goes in v5:
time: 187 us; the launch traced here: 183 us
  starting transfers between devices  96.9 us (52%)
  blocking collectives  34.3 us (18%)
  waiting for transfers between devices  29.4 us (16%)
  matrix products  7.08 us (4%)
  local copies, waits for them, and re-layouts  6.2 us (3%)
  other arithmetic  6.16 us (3%)
    ppermute x16, starting transfers between devices, along_y(): return lax.ppermute(x, 'dp', perm)  50.7 us
    ppermute x8, starting transfers between devices, flip(): return lax.ppermute(x, ('section', 'dp'), perm)  42.8 us
    all_to_all x3, blocking collectives, exchange(): lax.all_to_all(x, ('section', 'dp', 'vocab'), split_axis=0, concat_axis=0...  34.3 us
    ppermute x16, waiting for transfers between devices, along_y(): return lax.ppermute(x, 'dp', perm)  18.6 us
    all_to_all x1, waiting for transfers between devices, exchange(): lax.all_to_all(x, ('section', 'dp', 'vocab'), split_axis=0, concat_axis=0...  7.95 us
    dot_general x1, matrix products, on_device(): lax.dot_general(weights, logit_grad, (((1,), (1,)), ((), ())), preferred_...  5.08 us
  transfers between devices with their start and end apart: 25, of which 9 were waited for; matrix products, arithmetic and copies ran while one was open for 6% of the time, Pallas kernels for 1%

profile of v5, /device:TPU:25, one launch (start us, length us, event | category | flops | bytes accessed | tf_op | source)
XLA Modules:
  0.0 183.3 jit_solution(10175681044714614230)
XLA Ops:
  0.7 1.1 constant_dynamic-slice_fusion.6
  1.7 2.6 %collective-permute-start.3 = (bf16[96,1024]{1,0:T(8,128)(2,1)S(1)}, bf16[96,1024]{1,0:T(8,128)(2,1)S(1)}, u32[]{:S(2)}, u32[]{:S(2)}) collective-permute-start(bf16[96,1024]{1,0:T(8,128)(2,1)S(1)} %get-tuple-element.26), channel_id=1, source_target_pairs={{0,256},{16,272},{32,288},{48,304},{64,320},{80,336},{96,352},{112... | collective-permute-start | bytes 589832 | tf_op jit(solution)/shard_map/ppermute | solution.py:24
  4.3 1.8 constant_dynamic-slice_fusion.7
  6.1 10.6 %collective-permute-start = (bf16[96,2048]{1,0:T(8,128)(2,1)}, bf16[96,2048]{1,0:T(8,128)(2,1)}, u32[]{:S(2)}, u32[]{:S(2)}) collective-permute-start(bf16[96,2048]{1,0:T(8,128)(2,1)} %constant_dynamic-slice_fusion.7), channel_id=1, source_target_pairs={{0,128},{16,144},{32,160},{48,176},{64,192},{80,208},{96,224},{112... | collective-permute-start | bytes 1179656 | tf_op jit(solution)/shard_map/ppermute | solution.py:24
  16.7 0.7 exponential_multiply_fusion
  17.6 4.4 %collective-permute-start.4 = (bf16[192,1024]{1,0:T(8,128)(2,1)S(1)}, bf16[192,1024]{1,0:T(8,128)(2,1)S(1)}, u32[]{:S(2)}, u32[]{:S(2)}) collective-permute-start(bf16[192,1024]{1,0:T(8,128)(2,1)S(1)} %pad_maximum_fusion), channel_id=1, source_target_pairs={{0,16},{16,32},{32,48},{48,64},{64,80},{80,96},{96,112},{112,0},{1... | collective-permute-start | bytes 1179656 | tf_op jit(solution)/shard_map/ppermute | solution.py:29
  22.0 1.9 %collective-permute-start.6 = (bf16[192,1024]{1,0:T(8,128)(2,1)S(1)}, bf16[192,1024]{1,0:T(8,128)(2,1)S(1)}, u32[]{:S(2)}, u32[]{:S(2)}) collective-permute-start(bf16[192,1024]{1,0:T(8,128)(2,1)S(1)} %pad_maximum_fusion), channel_id=1, source_target_pairs={{0,112},{16,0},{32,16},{48,32},{64,48},{80,64},{96,80},{112,96},{1... | collective-permute-start | bytes 1179656 | tf_op jit(solution)/shard_map/ppermute | solution.py:29
  24.0 0.6 mul.74
  24.6 2.9 %fusion = bf16[128,4096]{1,0:T(8,128)(2,1)S(1)} fusion(f32[16,8,32,128]{3,2,1,0:T(8,128)S(1)} %bitcast.105, s32[128,4096]{1,0:T(8,128)} %param.7), kind=kLoop, calls=%fused_computation.1 | loop fusion | flops 1572864 | bytes 5242880 | tf_op jit(solution)/shard_map/convert_element_type | solution.py:71
  27.7 2.5 %collective-permute-done.4 = bf16[192,1024]{1,0:T(8,128)(2,1)S(1)} collective-permute-done((bf16[192,1024]{1,0:T(8,128)(2,1)S(1)}, bf16[192,1024]{1,0:T(8,128)(2,1)S(1)}, u32[]{:S(2)}, u32[]{:S(2)}) %collective-permute-start.4) | collective-permute-done | bytes 393248 | tf_op jit(solution)/shard_map/ppermute | solution.py:29
  30.2 5.3 %collective-permute-start.5 = (bf16[192,1024]{1,0:T(8,128)(2,1)S(1)}, bf16[192,1024]{1,0:T(8,128)(2,1)S(1)}, u32[]{:S(2)}, u32[]{:S(2)}) collective-permute-start(bf16[192,1024]{1,0:T(8,128)(2,1)S(1)} %collective-permute-done.4), channel_id=1, source_target_pairs={{0,16},{16,32},{32,48},{48,64},{64,80},{80,96},{96,112},{112,0},{1... | collective-permute-start | bytes 1179656 | tf_op jit(solution)/shard_map/ppermute | solution.py:29
  35.5 1.9 %collective-permute-start.7 = (bf16[192,1024]{1,0:T(8,128)(2,1)S(1)}, bf16[192,1024]{1,0:T(8,128)(2,1)S(1)}, u32[]{:S(2)}, u32[]{:S(2)}) collective-permute-start(bf16[192,1024]{1,0:T(8,128)(2,1)S(1)} %collective-permute-done.6), channel_id=1, source_target_pairs={{0,112},{16,0},{32,16},{48,32},{64,48},{80,64},{96,80},{112,96},{1... | collective-permute-start | bytes 1179656 | tf_op jit(solution)/shard_map/ppermute | solution.py:29
  37.5 1.8 shard_map.68
  39.3 3.4 %collective-permute-start.1 = (bf16[96,1024]{1,0:T(8,128)(2,1)}, bf16[96,1024]{1,0:T(8,128)(2,1)S(1)}, u32[]{:S(2)}, u32[]{:S(2)}) collective-permute-start(bf16[96,1024]{1,0:T(8,128)(2,1)} %get-tuple-element.10), channel_id=1, source_target_pairs={{0,256},{16,272},{32,288},{48,304},{64,320},{80,336},{96,352},{112... | collective-permute-start | bytes 589832 | tf_op jit(solution)/shard_map/ppermute | solution.py:24
  42.7 0.8 broadcast_in_dim.11
  44.0 3.9 %collective-permute-start.2 = (bf16[128,1536]{1,0:T(8,128)(2,1)S(1)}, bf16[128,1536]{1,0:T(8,128)(2,1)S(1)}, u32[]{:S(2)}, u32[]{:S(2)}) collective-permute-start(bf16[128,1536]{1,0:T(8,128)(2,1)S(1)} %copy-done.1), channel_id=1, source_target_pairs={{0,128},{16,144},{32,160},{48,176},{64,192},{80,208},{96,224},{112... | collective-permute-start | bytes 1179656 | tf_op jit(solution)/shard_map/ppermute | solution.py:24
  47.9 4.4 %collective-permute-start.8 = (bf16[192,1024]{1,0:T(8,128)(2,1)S(1)}, bf16[192,1024]{1,0:T(8,128)(2,1)S(1)}, u32[]{:S(2)}, u32[]{:S(2)}) collective-permute-start(bf16[192,1024]{1,0:T(8,128)(2,1)S(1)} %constant_dynamic-update-slice_fusion.14), channel_id=1, source_target_pairs={{0,16},{16,32},{32,48},{48,64},{64,80},{80,96},{96,112},{112,0},{1... | collective-permute-start | bytes 1179656 | tf_op jit(solution)/shard_map/ppermute | solution.py:29
  52.4 1.9 %collective-permute-start.12 = (bf16[192,1024]{1,0:T(8,128)(2,1)S(1)}, bf16[192,1024]{1,0:T(8,128)(2,1)S(1)}, u32[]{:S(2)}, u32[]{:S(2)}) collective-permute-start(bf16[192,1024]{1,0:T(8,128)(2,1)S(1)} %constant_dynamic-update-slice_fusion.14), channel_id=1, source_target_pairs={{0,112},{16,0},{32,16},{48,32},{64,48},{80,64},{96,80},{112,96},{1... | collective-permute-start | bytes 1179656 | tf_op jit(solution)/shard_map/ppermute | solution.py:29
  54.3 4.6 %collective-permute-start.9 = (bf16[192,1024]{1,0:T(8,128)(2,1)S(1)}, bf16[192,1024]{1,0:T(8,128)(2,1)S(1)}, u32[]{:S(2)}, u32[]{:S(2)}) collective-permute-start(bf16[192,1024]{1,0:T(8,128)(2,1)S(1)} %collective-permute-done.5), channel_id=1, source_target_pairs={{0,16},{16,32},{32,48},{48,64},{64,80},{80,96},{96,112},{112,0},{1... | collective-permute-start | bytes 1179656 | tf_op jit(solution)/shard_map/ppermute | solution.py:29
  58.9 1.9 %collective-permute-start.10 = (bf16[192,1024]{1,0:T(8,128)(2,1)S(1)}, bf16[192,1024]{1,0:T(8,128)(2,1)S(1)}, u32[]{:S(2)}, u32[]{:S(2)}) collective-permute-start(bf16[192,1024]{1,0:T(8,128)(2,1)S(1)} %collective-permute-done.7), channel_id=1, source_target_pairs={{0,112},{16,0},{32,16},{48,32},{64,48},{80,64},{96,80},{112,96},{1... | collective-permute-start | bytes 1179656 | tf_op jit(solution)/shard_map/ppermute | solution.py:29
  61.0 7.6 %collective-permute-done.9 = bf16[192,1024]{1,0:T(8,128)(2,1)S(1)} collective-permute-done((bf16[192,1024]{1,0:T(8,128)(2,1)S(1)}, bf16[192,1024]{1,0:T(8,128)(2,1)S(1)}, u32[]{:S(2)}, u32[]{:S(2)}) %collective-permute-start.9) | collective-permute-done | bytes 393248 | tf_op jit(solution)/shard_map/ppermute | solution.py:29
  68.6 5.3 %collective-permute-start.15 = (bf16[96,1024]{1,0:T(8,128)(2,1)S(1)}, bf16[96,1024]{1,0:T(8,128)(2,1)S(1)}, u32[]{:S(2)}, u32[]{:S(2)}) collective-permute-start(bf16[96,1024]{1,0:T(8,128)(2,1)S(1)} %slice.92), channel_id=1, source_target_pairs={{0,16},{16,32},{32,48},{48,64},{64,80},{80,96},{96,112},{112,0},{1... | collective-permute-start | bytes 589832 | tf_op jit(solution)/shard_map/ppermute | solution.py:29
  74.0 1.9 %collective-permute-start.16 = (bf16[96,1024]{1,0:T(8,128)(2,1)S(1)}, bf16[96,1024]{1,0:T(8,128)(2,1)S(1)}, u32[]{:S(2)}, u32[]{:S(2)}) collective-permute-start(bf16[96,1024]{1,0:T(8,128)(2,1)S(1)} %slice.93), channel_id=1, source_target_pairs={{0,112},{16,0},{32,16},{48,32},{64,48},{80,64},{96,80},{112,96},{1... | collective-permute-start | bytes 589832 | tf_op jit(solution)/shard_map/ppermute | solution.py:29
  75.9 4.6 %collective-permute-start.11 = (bf16[192,1024]{1,0:T(8,128)(2,1)S(1)}, bf16[192,1024]{1,0:T(8,128)(2,1)S(1)}, u32[]{:S(2)}, u32[]{:S(2)}) collective-permute-start(bf16[192,1024]{1,0:T(8,128)(2,1)S(1)} %collective-permute-done.8), channel_id=1, source_target_pairs={{0,16},{16,32},{32,48},{48,64},{64,80},{80,96},{96,112},{112,0},{1... | collective-permute-start | bytes 1179656 | tf_op jit(solution)/shard_map/ppermute | solution.py:29
  80.5 1.9 %collective-permute-start.13 = (bf16[192,1024]{1,0:T(8,128)(2,1)S(1)}, bf16[192,1024]{1,0:T(8,128)(2,1)S(1)}, u32[]{:S(2)}, u32[]{:S(2)}) collective-permute-start(bf16[192,1024]{1,0:T(8,128)(2,1)S(1)} %collective-permute-done.12), channel_id=1, source_target_pairs={{0,112},{16,0},{32,16},{48,32},{64,48},{80,64},{96,80},{112,96},{1... | collective-permute-start | bytes 1179656 | tf_op jit(solution)/shard_map/ppermute | solution.py:29
  82.5 5.7 %collective-permute-start.21 = (bf16[128,1024]{1,0:T(8,128)(2,1)S(1)}, bf16[128,1024]{1,0:T(8,128)(2,1)S(1)}, u32[]{:S(2)}, u32[]{:S(2)}) collective-permute-start(bf16[128,1024]{1,0:T(8,128)(2,1)S(1)} %get-tuple-element.17), channel_id=1, source_target_pairs={{0,128},{16,144},{32,160},{48,176},{64,192},{80,208},{96,224},{112... | collective-permute-start | bytes 786440 | tf_op jit(solution)/shard_map/ppermute | solution.py:24
  88.5 3.3 %collective-permute-done.13 = bf16[192,1024]{1,0:T(8,128)(2,1)S(1)} collective-permute-done((bf16[192,1024]{1,0:T(8,128)(2,1)S(1)}, bf16[192,1024]{1,0:T(8,128)(2,1)S(1)}, u32[]{:S(2)}, u32[]{:S(2)}) %collective-permute-start.13) | collective-permute-done | bytes 393248 | tf_op jit(solution)/shard_map/ppermute | solution.py:29
  91.8 1.9 %collective-permute-start.17 = (bf16[192,1024]{1,0:T(8,128)(2,1)S(1)}, bf16[192,1024]{1,0:T(8,128)(2,1)S(1)}, u32[]{:S(2)}, u32[]{:S(2)}) collective-permute-start(bf16[192,1024]{1,0:T(8,128)(2,1)S(1)} %collective-permute-done.11), channel_id=1, source_target_pairs={{0,16},{16,32},{32,48},{48,64},{64,80},{80,96},{96,112},{112,0},{1... | collective-permute-start | bytes 1179656 | tf_op jit(solution)/shard_map/ppermute | solution.py:29
  93.8 3.4 %collective-permute-start.18 = (bf16[192,1024]{1,0:T(8,128)(2,1)S(1)}, bf16[192,1024]{1,0:T(8,128)(2,1)S(1)}, u32[]{:S(2)}, u32[]{:S(2)}) collective-permute-start(bf16[192,1024]{1,0:T(8,128)(2,1)S(1)} %collective-permute-done.13), channel_id=1, source_target_pairs={{0,112},{16,0},{32,16},{48,32},{64,48},{80,64},{96,80},{112,96},{1... | collective-permute-start | bytes 1179656 | tf_op jit(solution)/shard_map/ppermute | solution.py:29
  97.3 5.7 %collective-permute-start.14 = (bf16[256,1536]{1,0:T(8,128)(2,1)S(1)}, bf16[256,1536]{1,0:T(8,128)(2,1)S(1)}, u32[]{:S(2)}, u32[]{:S(2)}) collective-permute-start(bf16[256,1536]{1,0:T(8,128)(2,1)S(1)} %maximum_select_fusion), channel_id=1, source_target_pairs={{0,256},{16,272},{32,288},{48,304},{64,320},{80,336},{96,352},{112... | collective-permute-start | bytes 2359304 | tf_op jit(solution)/shard_map/ppermute | solution.py:24
  103.2 2.9 %collective-permute-start.19 = (bf16[96,1024]{1,0:T(8,128)(2,1)S(1)}, bf16[96,1024]{1,0:T(8,128)(2,1)S(1)}, u32[]{:S(2)}, u32[]{:S(2)}) collective-permute-start(bf16[96,1024]{1,0:T(8,128)(2,1)S(1)} %slice.94), channel_id=1, source_target_pairs={{0,16},{16,32},{32,48},{48,64},{64,80},{80,96},{96,112},{112,0},{1... | collective-permute-start | bytes 589832 | tf_op jit(solution)/shard_map/ppermute | solution.py:29
  106.1 2.4 %collective-permute-start.20 = (bf16[96,1024]{1,0:T(8,128)(2,1)S(1)}, bf16[96,1024]{1,0:T(8,128)(2,1)S(1)}, u32[]{:S(2)}, u32[]{:S(2)}) collective-permute-start(bf16[96,1024]{1,0:T(8,128)(2,1)S(1)} %slice.95), channel_id=1, source_target_pairs={{0,112},{16,0},{32,16},{48,32},{64,48},{80,64},{96,80},{112,96},{1... | collective-permute-start | bytes 589832 | tf_op jit(solution)/shard_map/ppermute | solution.py:29
  108.6 1.0 collective-permute-done.19
  109.6 4.1 %collective-permute-done.20 = bf16[96,1024]{1,0:T(8,128)(2,1)S(1)} collective-permute-done((bf16[96,1024]{1,0:T(8,128)(2,1)S(1)}, bf16[96,1024]{1,0:T(8,128)(2,1)S(1)}, u32[]{:S(2)}, u32[]{:S(2)}) %collective-permute-start.20) | collective-permute-done | bytes 196640 | tf_op jit(solution)/shard_map/ppermute | solution.py:29
  113.8 2.0 %fusion.33 = (f32[256]{0:T(256)S(1)}, f32[256,1024]{1,0:T(8,128)S(1)}) fusion(bf16[3072,1024]{1,0:T(8,128)(2,1)S(1)} %bitcast.106, bf16[256,1536]{1,0:T(8,128)(2,1)S(1)} %collective-permute-done.14, bf16[256,1536]{1,0:T(8,128)(2,1)S(1)} %maximum_select_fusion), kind=kOutput, calls=%fused_computation.88 | convolution fusion | flops 1614282496 | bytes 8913920 | tf_op jit(solution)/shard_map/dot_general | solution.py:164
  115.8 0.5 exponential_reduce_fusion
  116.4 5.7 %collective-permute-start.22 = (f32[8,128]{1,0:T(8,128)S(1)}, f32[8,128]{1,0:T(8,128)S(1)}, u32[]{:S(2)}, u32[]{:S(2)}) collective-permute-start(f32[8,128]{1,0:T(8,128)S(1)} %reshape.146), channel_id=1, source_target_pairs={{0,256},{16,272},{32,288},{48,304},{64,320},{80,336},{96,352},{112... | collective-permute-start | bytes 12296 | tf_op jit(solution)/shard_map/ppermute | solution.py:24
  122.1 0.8 collective-permute-done.22
  123.0 8.0 %all_to_all.20 = f32[4,8,128]{2,1,0:T(8,128)S(1)} all-to-all(f32[4,8,128]{2,1,0:T(8,128)S(1)} %broadcast_in_dim.12), channel_id=1, replica_groups={{0,4,8,12},{1,5,9,13},{2,6,10,14},{3,7,11,15},{128,132,136,140},{129,13..., dimensions={0} | all-to-all | bytes 32768 | tf_op jit(solution)/shard_map/all_to_all | solution.py:57
  131.1 11.8 %all_to_all.21 = f32[8,8,128]{2,1,0:T(8,128)S(1)} all-to-all(f32[8,8,128]{2,1,0:T(8,128)S(1)} %bitcast.126), channel_id=1, replica_groups={{0,1,2,3,128,129,130,131},{4,5,6,7,132,133,134,135},{8,9,10,11,136,137,..., dimensions={0} | all-to-all | bytes 65536 | tf_op jit(solution)/shard_map/all_to_all | solution.py:57
  143.0 5.1 %fusion.15 = f32[3072,256]{1,0:T(8,128)S(1)} fusion(bf16[3072,1024]{1,0:T(8,128)(2,1)} %bitcast.107, f32[256,1024]{1,0:T(8,128)S(1)} %get-tuple-element.32, f32[256]{0:T(256)S(1)} %get-tuple-element.29, f32[256]{0:T(256)S(1)} %bitcast.137, f32[256]{0:T(256)S(1)} %maximum_multiply_fusion.1, bf16[128,1024]{1,0:T(8,128)(2,1)S(1)} %collective-permute-done.21, ...), kind=kOutput, calls=%fused_computation.21 | convolution fusion | flops 1614544896 | bytes 11013121 | tf_op jit(solution)/shard_map/dot_general | solution.py:211
  148.2 5.1 %collective-permute-start.23 = (bf16[16,96,256]{2,1,0:T(8,128)(2,1)S(1)}, bf16[16,96,256]{2,1,0:T(8,128)(2,1)S(1)}, u32[]{:S(2)}, u32[]{:S(2)}) collective-permute-start(bf16[16,96,256]{2,1,0:T(8,128)(2,1)S(1)} %bitcast.116), channel_id=1, source_target_pairs={{0,256},{16,272},{32,288},{48,304},{64,320},{80,336},{96,352},{112... | collective-permute-start | bytes 2359304 | tf_op jit(solution)/shard_map/ppermute | solution.py:24
  153.4 1.8 collective-permute-done.23
  155.4 14.4 %all_to_all.22 = bf16[4,384,256]{2,1,0:T(8,128)(2,1)S(1)} all-to-all(bf16[4,384,256]{2,1,0:T(8,128)(2,1)S(1)} %bitcast.109), channel_id=1, replica_groups={{0,4,8,12},{1,5,9,13},{2,6,10,14},{3,7,11,15},{128,132,136,140},{129,13..., dimensions={0} | all-to-all | bytes 1572864 | tf_op jit(solution)/shard_map/all_to_all | solution.py:57
  170.1 0.7 copy.70
  170.8 3.4 %all-to-all-start.3 = ((bf16[8,96,128]{2,1,0:T(8,128)(2,1)}), bf16[8,96,128]{2,1,0:T(8,128)(2,1)S(1)}, u32[]{:S(2)}, u32[]{:S(2)}) async-start(bf16[8,96,128]{2,1,0:T(8,128)(2,1)} %bitcast.54), calls=%async_computation.3 | async-start | bytes 393216 | tf_op jit(solution)/shard_map/all_to_all | solution.py:57
  174.8 7.9 %all-to-all-done.3 = bf16[8,96,128]{2,1,0:T(8,128)(2,1)S(1)} async-done(((bf16[8,96,128]{2,1,0:T(8,128)(2,1)}), bf16[8,96,128]{2,1,0:T(8,128)(2,1)S(1)}, u32[]{:S(2)}, u32[]{:S(2)}) %all-to-all-start.3) | async-done | bytes 196640 | tf_op jit(solution)/shard_map/all_to_all | solution.py:57
  182.7 0.6 reduce_sum.125
  (82 shorter events, 3.0 us)
Async XLA Ops:
  1.7 15.8 %collective-permute-start.3 = (bf16[96,1024]{1,0:T(8,128)(2,1)S(1)}, bf16[96,1024]{1,0:T(8,128)(2,1)S(1)}, u32[]{:S(2)}, u32[]{:S(2)}) collective-permute-start(bf16[96,1024]{1,0:T(8,128)(2,1)S(1)} %get-tuple-element.26), channel_id=1, source_target_pairs={{0,256},{16,272},{32,288},{48,304},{64,320},{80,336},{96,352},{112... | collective-permute-start | bytes 589832 | tf_op jit(solution)/shard_map/ppermute | solution.py:24
  6.1 31.4 %collective-permute-start = (bf16[96,2048]{1,0:T(8,128)(2,1)}, bf16[96,2048]{1,0:T(8,128)(2,1)}, u32[]{:S(2)}, u32[]{:S(2)}) collective-permute-start(bf16[96,2048]{1,0:T(8,128)(2,1)} %constant_dynamic-slice_fusion.7), channel_id=1, source_target_pairs={{0,128},{16,144},{32,160},{48,176},{64,192},{80,208},{96,224},{112... | collective-permute-start | bytes 1179656 | tf_op jit(solution)/shard_map/ppermute | solution.py:24
  17.6 12.6 %collective-permute-start.4 = (bf16[192,1024]{1,0:T(8,128)(2,1)S(1)}, bf16[192,1024]{1,0:T(8,128)(2,1)S(1)}, u32[]{:S(2)}, u32[]{:S(2)}) collective-permute-start(bf16[192,1024]{1,0:T(8,128)(2,1)S(1)} %pad_maximum_fusion), channel_id=1, source_target_pairs={{0,16},{16,32},{32,48},{48,64},{64,80},{80,96},{96,112},{112,0},{1... | collective-permute-start | bytes 1179656 | tf_op jit(solution)/shard_map/ppermute | solution.py:29
  22.0 13.5 %collective-permute-start.6 = (bf16[192,1024]{1,0:T(8,128)(2,1)S(1)}, bf16[192,1024]{1,0:T(8,128)(2,1)S(1)}, u32[]{:S(2)}, u32[]{:S(2)}) collective-permute-start(bf16[192,1024]{1,0:T(8,128)(2,1)S(1)} %pad_maximum_fusion), channel_id=1, source_target_pairs={{0,112},{16,0},{32,16},{48,32},{64,48},{80,64},{96,80},{112,96},{1... | collective-permute-start | bytes 1179656 | tf_op jit(solution)/shard_map/ppermute | solution.py:29
  30.2 17.6 %collective-permute-start.5 = (bf16[192,1024]{1,0:T(8,128)(2,1)S(1)}, bf16[192,1024]{1,0:T(8,128)(2,1)S(1)}, u32[]{:S(2)}, u32[]{:S(2)}) collective-permute-start(bf16[192,1024]{1,0:T(8,128)(2,1)S(1)} %collective-permute-done.4), channel_id=1, source_target_pairs={{0,16},{16,32},{32,48},{48,64},{64,80},{80,96},{96,112},{112,0},{1... | collective-permute-start | bytes 1179656 | tf_op jit(solution)/shard_map/ppermute | solution.py:29
  35.5 12.3 %collective-permute-start.7 = (bf16[192,1024]{1,0:T(8,128)(2,1)S(1)}, bf16[192,1024]{1,0:T(8,128)(2,1)S(1)}, u32[]{:S(2)}, u32[]{:S(2)}) collective-permute-start(bf16[192,1024]{1,0:T(8,128)(2,1)S(1)} %collective-permute-done.6), channel_id=1, source_target_pairs={{0,112},{16,0},{32,16},{48,32},{64,48},{80,64},{96,80},{112,96},{1... | collective-permute-start | bytes 1179656 | tf_op jit(solution)/shard_map/ppermute | solution.py:29
  39.3 4.7 %copy-start.1 = (bf16[128,1536]{1,0:T(8,128)(2,1)S(1)}, bf16[128,1536]{1,0:T(8,128)(2,1)}, u32[]{:S(2)}) copy-start(bf16[128,1536]{1,0:T(8,128)(2,1)} %param.5) | copy-start | bytes 1179652
  39.3 8.6 %copy-start.2 = (bf16[96,1024]{1,0:T(8,128)(2,1)S(1)}, bf16[96,1024]{1,0:T(8,128)(2,1)}, u32[]{:S(2)}) copy-start(bf16[96,1024]{1,0:T(8,128)(2,1)} %get-tuple-element.13) | copy-start | bytes 589828
  39.3 4.7 %collective-permute-start.1 = (bf16[96,1024]{1,0:T(8,128)(2,1)}, bf16[96,1024]{1,0:T(8,128)(2,1)S(1)}, u32[]{:S(2)}, u32[]{:S(2)}) collective-permute-start(bf16[96,1024]{1,0:T(8,128)(2,1)} %get-tuple-element.10), channel_id=1, source_target_pairs={{0,256},{16,272},{32,288},{48,304},{64,320},{80,336},{96,352},{112... | collective-permute-start | bytes 589832 | tf_op jit(solution)/shard_map/ppermute | solution.py:24
  44.0 44.5 %collective-permute-start.2 = (bf16[128,1536]{1,0:T(8,128)(2,1)S(1)}, bf16[128,1536]{1,0:T(8,128)(2,1)S(1)}, u32[]{:S(2)}, u32[]{:S(2)}) collective-permute-start(bf16[128,1536]{1,0:T(8,128)(2,1)S(1)} %copy-done.1), channel_id=1, source_target_pairs={{0,128},{16,144},{32,160},{48,176},{64,192},{80,208},{96,224},{112... | collective-permute-start | bytes 1179656 | tf_op jit(solution)/shard_map/ppermute | solution.py:24
  47.9 27.9 %collective-permute-start.8 = (bf16[192,1024]{1,0:T(8,128)(2,1)S(1)}, bf16[192,1024]{1,0:T(8,128)(2,1)S(1)}, u32[]{:S(2)}, u32[]{:S(2)}) collective-permute-start(bf16[192,1024]{1,0:T(8,128)(2,1)S(1)} %constant_dynamic-update-slice_fusion.14), channel_id=1, source_target_pairs={{0,16},{16,32},{32,48},{48,64},{64,80},{80,96},{96,112},{112,0},{1... | collective-permute-start | bytes 1179656 | tf_op jit(solution)/shard_map/ppermute | solution.py:29
  52.4 28.1 %collective-permute-start.12 = (bf16[192,1024]{1,0:T(8,128)(2,1)S(1)}, bf16[192,1024]{1,0:T(8,128)(2,1)S(1)}, u32[]{:S(2)}, u32[]{:S(2)}) collective-permute-start(bf16[192,1024]{1,0:T(8,128)(2,1)S(1)} %constant_dynamic-update-slice_fusion.14), channel_id=1, source_target_pairs={{0,112},{16,0},{32,16},{48,32},{64,48},{80,64},{96,80},{112,96},{1... | collective-permute-start | bytes 1179656 | tf_op jit(solution)/shard_map/ppermute | solution.py:29
  54.3 14.3 %collective-permute-start.9 = (bf16[192,1024]{1,0:T(8,128)(2,1)S(1)}, bf16[192,1024]{1,0:T(8,128)(2,1)S(1)}, u32[]{:S(2)}, u32[]{:S(2)}) collective-permute-start(bf16[192,1024]{1,0:T(8,128)(2,1)S(1)} %collective-permute-done.5), channel_id=1, source_target_pairs={{0,16},{16,32},{32,48},{48,64},{64,80},{80,96},{96,112},{112,0},{1... | collective-permute-start | bytes 1179656 | tf_op jit(solution)/shard_map/ppermute | solution.py:29
  58.9 15.1 %collective-permute-start.10 = (bf16[192,1024]{1,0:T(8,128)(2,1)S(1)}, bf16[192,1024]{1,0:T(8,128)(2,1)S(1)}, u32[]{:S(2)}, u32[]{:S(2)}) collective-permute-start(bf16[192,1024]{1,0:T(8,128)(2,1)S(1)} %collective-permute-done.7), channel_id=1, source_target_pairs={{0,112},{16,0},{32,16},{48,32},{64,48},{80,64},{96,80},{112,96},{1... | collective-permute-start | bytes 1179656 | tf_op jit(solution)/shard_map/ppermute | solution.py:29
  68.6 13.9 %collective-permute-start.15 = (bf16[96,1024]{1,0:T(8,128)(2,1)S(1)}, bf16[96,1024]{1,0:T(8,128)(2,1)S(1)}, u32[]{:S(2)}, u32[]{:S(2)}) collective-permute-start(bf16[96,1024]{1,0:T(8,128)(2,1)S(1)} %slice.92), channel_id=1, source_target_pairs={{0,16},{16,32},{32,48},{48,64},{64,80},{80,96},{96,112},{112,0},{1... | collective-permute-start | bytes 589832 | tf_op jit(solution)/shard_map/ppermute | solution.py:29
  74.0 14.3 %collective-permute-start.16 = (bf16[96,1024]{1,0:T(8,128)(2,1)S(1)}, bf16[96,1024]{1,0:T(8,128)(2,1)S(1)}, u32[]{:S(2)}, u32[]{:S(2)}) collective-permute-start(bf16[96,1024]{1,0:T(8,128)(2,1)S(1)} %slice.93), channel_id=1, source_target_pairs={{0,112},{16,0},{32,16},{48,32},{64,48},{80,64},{96,80},{112,96},{1... | collective-permute-start | bytes 589832 | tf_op jit(solution)/shard_map/ppermute | solution.py:29
  75.9 12.6 %collective-permute-start.11 = (bf16[192,1024]{1,0:T(8,128)(2,1)S(1)}, bf16[192,1024]{1,0:T(8,128)(2,1)S(1)}, u32[]{:S(2)}, u32[]{:S(2)}) collective-permute-start(bf16[192,1024]{1,0:T(8,128)(2,1)S(1)} %collective-permute-done.8), channel_id=1, source_target_pairs={{0,16},{16,32},{32,48},{48,64},{64,80},{80,96},{96,112},{112,0},{1... | collective-permute-start | bytes 1179656 | tf_op jit(solution)/shard_map/ppermute | solution.py:29
  80.5 11.4 %collective-permute-start.13 = (bf16[192,1024]{1,0:T(8,128)(2,1)S(1)}, bf16[192,1024]{1,0:T(8,128)(2,1)S(1)}, u32[]{:S(2)}, u32[]{:S(2)}) collective-permute-start(bf16[192,1024]{1,0:T(8,128)(2,1)S(1)} %collective-permute-done.12), channel_id=1, source_target_pairs={{0,112},{16,0},{32,16},{48,32},{64,48},{80,64},{96,80},{112,96},{1... | collective-permute-start | bytes 1179656 | tf_op jit(solution)/shard_map/ppermute | solution.py:29
  82.5 33.2 %collective-permute-start.21 = (bf16[128,1024]{1,0:T(8,128)(2,1)S(1)}, bf16[128,1024]{1,0:T(8,128)(2,1)S(1)}, u32[]{:S(2)}, u32[]{:S(2)}) collective-permute-start(bf16[128,1024]{1,0:T(8,128)(2,1)S(1)} %get-tuple-element.17), channel_id=1, source_target_pairs={{0,128},{16,144},{32,160},{48,176},{64,192},{80,208},{96,224},{112... | collective-permute-start | bytes 786440 | tf_op jit(solution)/shard_map/ppermute | solution.py:24
  91.8 11.3 %collective-permute-start.17 = (bf16[192,1024]{1,0:T(8,128)(2,1)S(1)}, bf16[192,1024]{1,0:T(8,128)(2,1)S(1)}, u32[]{:S(2)}, u32[]{:S(2)}) collective-permute-start(bf16[192,1024]{1,0:T(8,128)(2,1)S(1)} %collective-permute-done.11), channel_id=1, source_target_pairs={{0,16},{16,32},{32,48},{48,64},{64,80},{80,96},{96,112},{112,0},{1... | collective-permute-start | bytes 1179656 | tf_op jit(solution)/shard_map/ppermute | solution.py:29
  93.8 12.3 %collective-permute-start.18 = (bf16[192,1024]{1,0:T(8,128)(2,1)S(1)}, bf16[192,1024]{1,0:T(8,128)(2,1)S(1)}, u32[]{:S(2)}, u32[]{:S(2)}) collective-permute-start(bf16[192,1024]{1,0:T(8,128)(2,1)S(1)} %collective-permute-done.13), channel_id=1, source_target_pairs={{0,112},{16,0},{32,16},{48,32},{64,48},{80,64},{96,80},{112,96},{1... | collective-permute-start | bytes 1179656 | tf_op jit(solution)/shard_map/ppermute | solution.py:29
  97.3 16.4 %collective-permute-start.14 = (bf16[256,1536]{1,0:T(8,128)(2,1)S(1)}, bf16[256,1536]{1,0:T(8,128)(2,1)S(1)}, u32[]{:S(2)}, u32[]{:S(2)}) collective-permute-start(bf16[256,1536]{1,0:T(8,128)(2,1)S(1)} %maximum_select_fusion), channel_id=1, source_target_pairs={{0,256},{16,272},{32,288},{48,304},{64,320},{80,336},{96,352},{112... | collective-permute-start | bytes 2359304 | tf_op jit(solution)/shard_map/ppermute | solution.py:24
  103.2 6.4 %collective-permute-start.19 = (bf16[96,1024]{1,0:T(8,128)(2,1)S(1)}, bf16[96,1024]{1,0:T(8,128)(2,1)S(1)}, u32[]{:S(2)}, u32[]{:S(2)}) collective-permute-start(bf16[96,1024]{1,0:T(8,128)(2,1)S(1)} %slice.94), channel_id=1, source_target_pairs={{0,16},{16,32},{32,48},{48,64},{64,80},{80,96},{96,112},{112,0},{1... | collective-permute-start | bytes 589832 | tf_op jit(solution)/shard_map/ppermute | solution.py:29
  106.1 7.6 %collective-permute-start.20 = (bf16[96,1024]{1,0:T(8,128)(2,1)S(1)}, bf16[96,1024]{1,0:T(8,128)(2,1)S(1)}, u32[]{:S(2)}, u32[]{:S(2)}) collective-permute-start(bf16[96,1024]{1,0:T(8,128)(2,1)S(1)} %slice.95), channel_id=1, source_target_pairs={{0,112},{16,0},{32,16},{48,32},{64,48},{80,64},{96,80},{112,96},{1... | collective-permute-start | bytes 589832 | tf_op jit(solution)/shard_map/ppermute | solution.py:29
  113.7 2.7 %copy-start = (bf16[2,2,8,96,1024]{4,3,2,1,0:T(8,128)(2,1)}, bf16[2,2,8,96,1024]{4,3,2,1,0:T(8,128)(2,1)S(1)}, u32[]{:S(2)}) copy-start(bf16[2,2,8,96,1024]{4,3,2,1,0:T(8,128)(2,1)S(1)} %bitcast_dynamic-update-slice_fusion) | copy-start | bytes 18874372
  113.7 17.3 %copy-start.3 = (f32[128]{0:T(128)S(1)}, f32[128]{0:T(128)}, u32[]{:S(2)}) copy-start(f32[128]{0:T(128)} %param.9) | copy-start | bytes 1540
  116.4 6.5 %collective-permute-start.22 = (f32[8,128]{1,0:T(8,128)S(1)}, f32[8,128]{1,0:T(8,128)S(1)}, u32[]{:S(2)}, u32[]{:S(2)}) collective-permute-start(f32[8,128]{1,0:T(8,128)S(1)} %reshape.146), channel_id=1, source_target_pairs={{0,256},{16,272},{32,288},{48,304},{64,320},{80,336},{96,352},{112... | collective-permute-start | bytes 12296 | tf_op jit(solution)/shard_map/ppermute | solution.py:24
  148.2 7.0 %collective-permute-start.23 = (bf16[16,96,256]{2,1,0:T(8,128)(2,1)S(1)}, bf16[16,96,256]{2,1,0:T(8,128)(2,1)S(1)}, u32[]{:S(2)}, u32[]{:S(2)}) collective-permute-start(bf16[16,96,256]{2,1,0:T(8,128)(2,1)S(1)} %bitcast.116), channel_id=1, source_target_pairs={{0,256},{16,272},{32,288},{48,304},{64,320},{80,336},{96,352},{112... | collective-permute-start | bytes 2359304 | tf_op jit(solution)/shard_map/ppermute | solution.py:24
  170.8 11.9 %all-to-all-start.3 = ((bf16[8,96,128]{2,1,0:T(8,128)(2,1)}), bf16[8,96,128]{2,1,0:T(8,128)(2,1)S(1)}, u32[]{:S(2)}, u32[]{:S(2)}) async-start(bf16[8,96,128]{2,1,0:T(8,128)(2,1)} %bitcast.54), calls=%async_computation.3 | async-start | bytes 393216 | tf_op jit(solution)/shard_map/all_to_all | solution.py:57

commit v6 on v3

--- a/solution.py
+++ b/solution.py
@@ -1,6 +1,8 @@
 import jax
 import jax.numpy as jnp
 from jax import lax
+from jax.experimental import pallas as pl
+from jax.experimental.pallas import tpu as pltpu
 from jax.sharding import PartitionSpec as P
 
 GROUP = 128
@@ -66,6 +68,60 @@
     return parts
 
 
+TILE = 256
+
+
+def grad_rows(w_ref, section, at, logit_grad):
+    rows = w_ref[section, pl.ds(pl.multiple_of(at, TILE), TILE), :]
+    return lax.dot_general(
+        rows, logit_grad, (((1,), (1,)), ((), ())), preferred_element_type=jnp.float32
+    )
+
+
+def first_grads_kernel(s_ref, t_ref, row_ref, w_ref, lg_ref, g_ref):
+    student_lse, teacher_lse, weight = row_ref[:, 0:1], row_ref[:, 1:2], row_ref[:, 2:3]
+    student = jnp.exp(s_ref[...] - student_lse)
+    teacher = jnp.exp(t_ref[...].astype(jnp.float32) - teacher_lse)
+    lg_ref[...] = (weight * TEMP * (student - teacher)).astype(jnp.bfloat16)
+    logit_grad = lg_ref[...]
+    tok = g_ref.shape[2]
+
+    def step(k, carry):
+        g = grad_rows(w_ref, 1, k * TILE, logit_grad).astype(jnp.bfloat16)
+        for z in range(NZH):
+            g_ref[z, pl.ds(pl.multiple_of(k * TILE, TILE), TILE), :] = g[:, z * tok : (z + 1) * tok]
+        return carry
+
+    lax.fori_loop(0, g_ref.shape[1] // TILE, step, 0)
+
+
+def second_grads_kernel(lg_ref, w_ref, g_ref):
+    logit_grad = lg_ref[...]
+    tok = g_ref.shape[2]
+
+    def step(k, carry):
+        g = grad_rows(w_ref, 0, k * TILE, logit_grad)
+        for z in range(NZH):
+            g_ref[z, pl.ds(pl.multiple_of(k * TILE, TILE), TILE), :] = g[:, z * tok : (z + 1) * tok]
+        return carry
+
+    lax.fori_loop(0, g_ref.shape[1] // TILE, step, 0)
+
+
+def in_vmem(kernel, ins, outs):
+    whole = pl.BlockSpec(memory_space=pltpu.VMEM)
+    return pl.pallas_call(
+        kernel,
+        in_specs=[whole] * len(ins),
+        out_specs=[whole] * len(outs),
+        out_shape=outs,
+        compiler_params=pltpu.CompilerParams(vmem_limit_bytes=40 * 2**20),
+        cost_estimate=pl.CostEstimate(
+            flops=10**9, bytes_accessed=5 * 10**6, transcendentals=5 * 10**5
+        ),
+    )(*ins)
+
+
 def on_device(hidden, head, codes, exponents, loss_weight):
     s = lax.axis_index("section")
     dp = lax.axis_index("dp")
@@ -106,18 +162,19 @@
     h_all = jnp.concatenate([h_sec, flip(h_sec, 1, 0)], axis=1)
     teacher = teacher_half(codes, exponents)
     t_send = after(columns(teacher, 0, 1), near_parts[3][2])
-    scaled_t = both(columns(teacher, 0, 0), flip(t_send, 0, 1)).astype(jnp.float32)
+    scaled_t = both(columns(teacher, 0, 0), flip(t_send, 0, 1))
 
     logits = jnp.dot(h_all, weights, preferred_element_type=jnp.float32)
     scaled_s = logits / TEMP
     m = jnp.max(scaled_s, axis=1)
-    t_exp = jnp.exp(scaled_t)
+    t_wide = scaled_t.astype(jnp.float32)
+    t_exp = jnp.exp(t_wide)
     stats = jnp.stack(
         [
             m,
             jnp.sum(jnp.exp(scaled_s - m[:, None]), axis=1),
             jnp.sum(t_exp, axis=1),
-            jnp.sum(t_exp * (scaled_t - scaled_s), axis=1),
+            jnp.sum(t_exp * (t_wide - scaled_s), axis=1),
         ]
     ).reshape(8, tok)
 
@@ -146,18 +203,25 @@
     kl_loss = TEMP * TEMP * kl_loss
 
     student_lse, teacher_lse = student_lse.reshape(2 * tok), teacher_lse.reshape(2 * tok)
-    logit_grad = (
-        weight[:, None]
-        * TEMP
-        * (jnp.exp(scaled_s - student_lse[:, None]) - jnp.exp(scaled_t - teacher_lse[:, None]))
-    ).astype(jnp.bfloat16)
-
-    g = lax.dot_general(
-        weights, logit_grad, (((1,), (1,)), ((), ())), preferred_element_type=jnp.float32
-    ).reshape(2, NQ, rows, 2 * tok)
-    g = g[0] + flip(g[1].astype(jnp.bfloat16), 1, 0).astype(jnp.float32)
-    g = g.astype(jnp.bfloat16).reshape(NQ, rows, 2, tok)
-    g = g.transpose(2, 0, 1, 3).reshape(NZH * NQ, rows, tok)
+    per_row = jnp.stack([student_lse, teacher_lse, weight], axis=1)
+    w = weights.reshape(2, -1, width)
+    feats = w.shape[1]
+    logit_grad, g = in_vmem(
+        first_grads_kernel,
+        (scaled_s, scaled_t, per_row, w),
+        (
+            jax.ShapeDtypeStruct(scaled_s.shape, jnp.bfloat16),
+            jax.ShapeDtypeStruct((NZH, feats, tok), jnp.bfloat16),
+        ),
+    )
+    theirs = flip(g, 1, 0)
+    (mine,) = in_vmem(
+        second_grads_kernel,
+        (logit_grad, w),
+        (jax.ShapeDtypeStruct((NZH, feats, tok), jnp.float32),),
+    )
+    g = (mine + theirs.astype(jnp.float32)).astype(jnp.bfloat16)
+    g = g.reshape(NZH * NQ, rows, tok)
     g = exchange(g)
     g = jnp.sum(g.astype(jnp.float32), axis=0)
     return (kl_loss, g.T.astype(jnp.bfloat16))

time: 180 us -> 179 us (level)
  matrix products: 7.09 us -> 2 us
  Pallas kernels: 0 us -> 4.57 us
    dot_general x1 -> x0, matrix products: 5.08 us -> none  [on_device(): lax.dot_general(weights, logit_grad, (((1,), (1,)), ((), ())), preferred_...]
    pallas_call x0 -> x2, Pallas kernels: none -> 4.57 us  [in_vmem(): pl.pallas_call(kernel, in_specs=[whole] * len(ins), out_specs=[whole] * l...]
    unnamed x6 -> x10, local copies, waits for them, and re-layouts: 0.07 us -> 2.82 us
  transfers between devices with their start and end apart: 25 -> 25, of which waited for: 8 -> 7; matrix products, arithmetic and copies ran while one was open for 6% -> 5% of each run, Pallas kernels for 0% -> 1%
where the time goes in v6:
time: 179 us; the launch traced here: 177 us
  starting transfers between devices  99.6 us (56%)
  waiting for transfers between devices  37.5 us (21%)
  blocking collectives  17.8 us (10%)
  local copies, waits for them, and re-layouts  7.43 us (4%)
  other arithmetic  6.99 us (4%)
  Pallas kernels  4.57 us (3%)
  matrix products  2 us (1%)
    ppermute x16, starting transfers between devices, along_y(): return lax.ppermute(x, 'dp', perm)  49.2 us
    ppermute x8, starting transfers between devices, flip(): return lax.ppermute(x, ('section', 'dp'), perm)  46.4 us
    all_to_all x1, waiting for transfers between devices, exchange(): lax.all_to_all(x, ('section', 'dp', 'vocab'), split_axis=0, concat_axis=0...  23 us
    all_to_all x1, blocking collectives, exchange(): lax.all_to_all(x, ('section', 'dp', 'vocab'), split_axis=0, concat_axis=0...  17.8 us
    ppermute x16, waiting for transfers between devices, along_y(): return lax.ppermute(x, 'dp', perm)  13.7 us
    pallas_call x2, Pallas kernels, in_vmem(): pl.pallas_call(kernel, in_specs=[whole] * len(ins), out_specs=[whole] * l...  4.57 us
    all_to_all x1, starting transfers between devices, exchange(): lax.all_to_all(x, ('section', 'dp', 'vocab'), split_axis=0, concat_axis=0...  3.91 us
  transfers between devices with their start and end apart: 25, of which 7 were waited for; matrix products, arithmetic and copies ran while one was open for 5% of the time, Pallas kernels for 1%

profile of v6, /device:TPU:25, one launch (start us, length us, event | category | flops | bytes accessed | tf_op | source)
XLA Modules:
  0.0 177.5 jit_solution(15495838854342532810)
XLA Ops:
  0.7 1.1 constant_dynamic-slice_fusion.9
  1.8 2.6 %collective-permute-start = (bf16[96,1024]{1,0:T(8,128)(2,1)S(1)}, bf16[96,1024]{1,0:T(8,128)(2,1)S(1)}, u32[]{:S(2)}, u32[]{:S(2)}) collective-permute-start(bf16[96,1024]{1,0:T(8,128)(2,1)S(1)} %get-tuple-element.19), channel_id=1, source_target_pairs={{0,256},{16,272},{32,288},{48,304},{64,320},{80,336},{96,352},{112... | collective-permute-start | bytes 589832 | tf_op jit(solution)/shard_map/ppermute | solution.py:22
  4.4 1.0 constant_dynamic-slice_fusion.7
  5.4 10.6 %collective-permute-start.11 = (bf16[96,2048]{1,0:T(8,128)(2,1)S(1)}, bf16[96,2048]{1,0:T(8,128)(2,1)S(1)}, u32[]{:S(2)}, u32[]{:S(2)}) collective-permute-start(bf16[96,2048]{1,0:T(8,128)(2,1)S(1)} %constant_dynamic-slice_fusion.7), channel_id=1, source_target_pairs={{0,128},{16,144},{32,160},{48,176},{64,192},{80,208},{96,224},{112... | collective-permute-start | bytes 1179656 | tf_op jit(solution)/shard_map/ppermute | solution.py:22
  16.0 0.7 exponential_multiply_fusion
  16.9 4.4 %collective-permute-start.1 = (bf16[192,1024]{1,0:T(8,128)(2,1)S(1)}, bf16[192,1024]{1,0:T(8,128)(2,1)S(1)}, u32[]{:S(2)}, u32[]{:S(2)}) collective-permute-start(bf16[192,1024]{1,0:T(8,128)(2,1)S(1)} %pad_maximum_fusion), channel_id=1, source_target_pairs={{0,16},{16,32},{32,48},{48,64},{64,80},{80,96},{96,112},{112,0},{1... | collective-permute-start | bytes 1179656 | tf_op jit(solution)/shard_map/ppermute | solution.py:27
  21.3 1.9 %collective-permute-start.4 = (bf16[192,1024]{1,0:T(8,128)(2,1)S(1)}, bf16[192,1024]{1,0:T(8,128)(2,1)S(1)}, u32[]{:S(2)}, u32[]{:S(2)}) collective-permute-start(bf16[192,1024]{1,0:T(8,128)(2,1)S(1)} %pad_maximum_fusion), channel_id=1, source_target_pairs={{0,112},{16,0},{32,16},{48,32},{64,48},{80,64},{96,80},{112,96},{1... | collective-permute-start | bytes 1179656 | tf_op jit(solution)/shard_map/ppermute | solution.py:27
  23.3 0.6 mul.60
  23.9 2.9 %fusion = bf16[128,4096]{1,0:T(8,128)(2,1)S(1)} fusion(f32[16,8,32,128]{3,2,1,0:T(8,128)S(1)} %bitcast.103, s32[128,4096]{1,0:T(8,128)} %param.7), kind=kLoop, calls=%fused_computation.1 | loop fusion | flops 1572864 | bytes 5242880 | tf_op jit(solution)/shard_map/convert_element_type | solution.py:51
  27.0 2.5 %collective-permute-start.12 = (bf16[96,1024]{1,0:T(8,128)(2,1)S(1)}, bf16[96,1024]{1,0:T(8,128)(2,1)S(1)}, u32[]{:S(2)}, u32[]{:S(2)}) collective-permute-start(bf16[96,1024]{1,0:T(8,128)(2,1)S(1)} %get-tuple-element.21), channel_id=1, source_target_pairs={{0,256},{16,272},{32,288},{48,304},{64,320},{80,336},{96,352},{112... | collective-permute-start | bytes 589832 | tf_op jit(solution)/shard_map/ppermute | solution.py:22
  29.6 14.2 %collective-permute-start.2 = (bf16[128,1536]{1,0:T(8,128)(2,1)S(1)}, bf16[128,1536]{1,0:T(8,128)(2,1)S(1)}, u32[]{:S(2)}, u32[]{:S(2)}) collective-permute-start(bf16[128,1536]{1,0:T(8,128)(2,1)S(1)} %copy-done.3), channel_id=1, source_target_pairs={{0,128},{16,144},{32,160},{48,176},{64,192},{80,208},{96,224},{112... | collective-permute-start | bytes 1179656 | tf_op jit(solution)/shard_map/ppermute | solution.py:22
  43.8 4.4 %collective-permute-start.5 = (bf16[192,1024]{1,0:T(8,128)(2,1)S(1)}, bf16[192,1024]{1,0:T(8,128)(2,1)S(1)}, u32[]{:S(2)}, u32[]{:S(2)}) collective-permute-start(bf16[192,1024]{1,0:T(8,128)(2,1)S(1)} %collective-permute-done.1), channel_id=1, source_target_pairs={{0,16},{16,32},{32,48},{48,64},{64,80},{80,96},{96,112},{112,0},{1... | collective-permute-start | bytes 1179656 | tf_op jit(solution)/shard_map/ppermute | solution.py:27
  48.3 1.9 %collective-permute-start.6 = (bf16[192,1024]{1,0:T(8,128)(2,1)S(1)}, bf16[192,1024]{1,0:T(8,128)(2,1)S(1)}, u32[]{:S(2)}, u32[]{:S(2)}) collective-permute-start(bf16[192,1024]{1,0:T(8,128)(2,1)S(1)} %collective-permute-done.4), channel_id=1, source_target_pairs={{0,112},{16,0},{32,16},{48,32},{64,48},{80,64},{96,80},{112,96},{1... | collective-permute-start | bytes 1179656 | tf_op jit(solution)/shard_map/ppermute | solution.py:27
  50.2 0.8 broadcast_in_dim.6
  51.1 4.6 %collective-permute-start.13 = (bf16[192,1024]{1,0:T(8,128)(2,1)S(1)}, bf16[192,1024]{1,0:T(8,128)(2,1)S(1)}, u32[]{:S(2)}, u32[]{:S(2)}) collective-permute-start(bf16[192,1024]{1,0:T(8,128)(2,1)S(1)} %pad_maximum_fusion.1), channel_id=1, source_target_pairs={{0,16},{16,32},{32,48},{48,64},{64,80},{80,96},{96,112},{112,0},{1... | collective-permute-start | bytes 1179656 | tf_op jit(solution)/shard_map/ppermute | solution.py:27
  55.7 1.9 %collective-permute-start.14 = (bf16[192,1024]{1,0:T(8,128)(2,1)S(1)}, bf16[192,1024]{1,0:T(8,128)(2,1)S(1)}, u32[]{:S(2)}, u32[]{:S(2)}) collective-permute-start(bf16[192,1024]{1,0:T(8,128)(2,1)S(1)} %pad_maximum_fusion.1), channel_id=1, source_target_pairs={{0,112},{16,0},{32,16},{48,32},{64,48},{80,64},{96,80},{112,96},{1... | collective-permute-start | bytes 1179656 | tf_op jit(solution)/shard_map/ppermute | solution.py:27
  57.7 4.6 %collective-permute-start.7 = (bf16[192,1024]{1,0:T(8,128)(2,1)S(1)}, bf16[192,1024]{1,0:T(8,128)(2,1)S(1)}, u32[]{:S(2)}, u32[]{:S(2)}) collective-permute-start(bf16[192,1024]{1,0:T(8,128)(2,1)S(1)} %collective-permute-done.5), channel_id=1, source_target_pairs={{0,16},{16,32},{32,48},{48,64},{64,80},{80,96},{96,112},{112,0},{1... | collective-permute-start | bytes 1179656 | tf_op jit(solution)/shard_map/ppermute | solution.py:27
  62.3 1.9 %collective-permute-start.8 = (bf16[192,1024]{1,0:T(8,128)(2,1)S(1)}, bf16[192,1024]{1,0:T(8,128)(2,1)S(1)}, u32[]{:S(2)}, u32[]{:S(2)}) collective-permute-start(bf16[192,1024]{1,0:T(8,128)(2,1)S(1)} %collective-permute-done.6), channel_id=1, source_target_pairs={{0,112},{16,0},{32,16},{48,32},{64,48},{80,64},{96,80},{112,96},{1... | collective-permute-start | bytes 1179656 | tf_op jit(solution)/shard_map/ppermute | solution.py:27
  64.2 0.2 maximum_select_fusion
  64.4 3.6 %collective-permute-start.3 = (bf16[256,1536]{1,0:T(8,128)(2,1)S(1)}, bf16[256,1536]{1,0:T(8,128)(2,1)S(1)}, u32[]{:S(2)}, u32[]{:S(2)}) collective-permute-start(bf16[256,1536]{1,0:T(8,128)(2,1)S(1)} %maximum_select_fusion), channel_id=1, source_target_pairs={{0,256},{16,272},{32,288},{48,304},{64,320},{80,336},{96,352},{112... | collective-permute-start | bytes 2359304 | tf_op jit(solution)/shard_map/ppermute | solution.py:22
  68.0 4.9 %collective-permute-start.15 = (bf16[192,1024]{1,0:T(8,128)(2,1)S(1)}, bf16[192,1024]{1,0:T(8,128)(2,1)S(1)}, u32[]{:S(2)}, u32[]{:S(2)}) collective-permute-start(bf16[192,1024]{1,0:T(8,128)(2,1)S(1)} %collective-permute-done.13), channel_id=1, source_target_pairs={{0,16},{16,32},{32,48},{48,64},{64,80},{80,96},{96,112},{112,0},{1... | collective-permute-start | bytes 1179656 | tf_op jit(solution)/shard_map/ppermute | solution.py:27
  72.9 1.9 %collective-permute-start.16 = (bf16[192,1024]{1,0:T(8,128)(2,1)S(1)}, bf16[192,1024]{1,0:T(8,128)(2,1)S(1)}, u32[]{:S(2)}, u32[]{:S(2)}) collective-permute-start(bf16[192,1024]{1,0:T(8,128)(2,1)S(1)} %collective-permute-done.14), channel_id=1, source_target_pairs={{0,112},{16,0},{32,16},{48,32},{64,48},{80,64},{96,80},{112,96},{1... | collective-permute-start | bytes 1179656 | tf_op jit(solution)/shard_map/ppermute | solution.py:27
  74.9 3.2 %collective-permute-start.21 = (bf16[128,1024]{1,0:T(8,128)(2,1)S(1)}, bf16[128,1024]{1,0:T(8,128)(2,1)S(1)}, u32[]{:S(2)}, u32[]{:S(2)}) collective-permute-start(bf16[128,1024]{1,0:T(8,128)(2,1)S(1)} %get-tuple-element.7), channel_id=1, source_target_pairs={{0,128},{16,144},{32,160},{48,176},{64,192},{80,208},{96,224},{112... | collective-permute-start | bytes 786440 | tf_op jit(solution)/shard_map/ppermute | solution.py:22
  78.2 0.2 collective-permute-done.8
  78.4 4.3 %collective-permute-start.9 = (bf16[96,1024]{1,0:T(8,128)(2,1)S(1)}, bf16[96,1024]{1,0:T(8,128)(2,1)S(1)}, u32[]{:S(2)}, u32[]{:S(2)}) collective-permute-start(bf16[96,1024]{1,0:T(8,128)(2,1)S(1)} %slice.68), channel_id=1, source_target_pairs={{0,16},{16,32},{32,48},{48,64},{64,80},{80,96},{96,112},{112,0},{1... | collective-permute-start | bytes 589832 | tf_op jit(solution)/shard_map/ppermute | solution.py:27
  82.9 1.9 %collective-permute-start.10 = (bf16[96,1024]{1,0:T(8,128)(2,1)S(1)}, bf16[96,1024]{1,0:T(8,128)(2,1)S(1)}, u32[]{:S(2)}, u32[]{:S(2)}) collective-permute-start(bf16[96,1024]{1,0:T(8,128)(2,1)S(1)} %slice.69), channel_id=1, source_target_pairs={{0,112},{16,0},{32,16},{48,32},{64,48},{80,64},{96,80},{112,96},{1... | collective-permute-start | bytes 589832 | tf_op jit(solution)/shard_map/ppermute | solution.py:27
  84.8 2.4 %collective-permute-done.16 = bf16[192,1024]{1,0:T(8,128)(2,1)S(1)} collective-permute-done((bf16[192,1024]{1,0:T(8,128)(2,1)S(1)}, bf16[192,1024]{1,0:T(8,128)(2,1)S(1)}, u32[]{:S(2)}, u32[]{:S(2)}) %collective-permute-start.16) | collective-permute-done | bytes 393248 | tf_op jit(solution)/shard_map/ppermute | solution.py:27
  87.2 2.2 %collective-permute-start.17 = (bf16[192,1024]{1,0:T(8,128)(2,1)S(1)}, bf16[192,1024]{1,0:T(8,128)(2,1)S(1)}, u32[]{:S(2)}, u32[]{:S(2)}) collective-permute-start(bf16[192,1024]{1,0:T(8,128)(2,1)S(1)} %collective-permute-done.15), channel_id=1, source_target_pairs={{0,16},{16,32},{32,48},{48,64},{64,80},{80,96},{96,112},{112,0},{1... | collective-permute-start | bytes 1179656 | tf_op jit(solution)/shard_map/ppermute | solution.py:27
  89.4 3.1 %collective-permute-start.18 = (bf16[192,1024]{1,0:T(8,128)(2,1)S(1)}, bf16[192,1024]{1,0:T(8,128)(2,1)S(1)}, u32[]{:S(2)}, u32[]{:S(2)}) collective-permute-start(bf16[192,1024]{1,0:T(8,128)(2,1)S(1)} %collective-permute-done.16), channel_id=1, source_target_pairs={{0,112},{16,0},{32,16},{48,32},{64,48},{80,64},{96,80},{112,96},{1... | collective-permute-start | bytes 1179656 | tf_op jit(solution)/shard_map/ppermute | solution.py:27
  92.8 5.9 %collective-permute-done.17 = bf16[192,1024]{1,0:T(8,128)(2,1)S(1)} collective-permute-done((bf16[192,1024]{1,0:T(8,128)(2,1)S(1)}, bf16[192,1024]{1,0:T(8,128)(2,1)S(1)}, u32[]{:S(2)}, u32[]{:S(2)}) %collective-permute-start.17) | collective-permute-done | bytes 393248 | tf_op jit(solution)/shard_map/ppermute | solution.py:27
  98.7 3.0 %collective-permute-start.19 = (bf16[96,1024]{1,0:T(8,128)(2,1)S(1)}, bf16[96,1024]{1,0:T(8,128)(2,1)S(1)}, u32[]{:S(2)}, u32[]{:S(2)}) collective-permute-start(bf16[96,1024]{1,0:T(8,128)(2,1)S(1)} %slice.70), channel_id=1, source_target_pairs={{0,16},{16,32},{32,48},{48,64},{64,80},{80,96},{96,112},{112,0},{1... | collective-permute-start | bytes 589832 | tf_op jit(solution)/shard_map/ppermute | solution.py:27
  101.7 2.3 %collective-permute-start.20 = (bf16[96,1024]{1,0:T(8,128)(2,1)S(1)}, bf16[96,1024]{1,0:T(8,128)(2,1)S(1)}, u32[]{:S(2)}, u32[]{:S(2)}) collective-permute-start(bf16[96,1024]{1,0:T(8,128)(2,1)S(1)} %slice.71), channel_id=1, source_target_pairs={{0,112},{16,0},{32,16},{48,32},{64,48},{80,64},{96,80},{112,96},{1... | collective-permute-start | bytes 589832 | tf_op jit(solution)/shard_map/ppermute | solution.py:27
  104.2 1.0 collective-permute-done.19
  105.2 4.2 %collective-permute-done.20 = bf16[96,1024]{1,0:T(8,128)(2,1)S(1)} collective-permute-done((bf16[96,1024]{1,0:T(8,128)(2,1)S(1)}, bf16[96,1024]{1,0:T(8,128)(2,1)S(1)}, u32[]{:S(2)}, u32[]{:S(2)}) %collective-permute-start.20) | collective-permute-done | bytes 196640 | tf_op jit(solution)/shard_map/ppermute | solution.py:27
  109.4 2.0 %fusion.23 = (f32[256]{0:T(256)S(1)}, f32[256,1024]{1,0:T(8,128)S(1)}) fusion(bf16[3072,1024]{1,0:T(8,128)(2,1)S(1)} %bitcast.100, bf16[256,1536]{1,0:T(8,128)(2,1)S(1)} %collective-permute-done.3, bf16[256,1536]{1,0:T(8,128)(2,1)S(1)} %maximum_select_fusion), kind=kOutput, calls=%fused_computation.74 | convolution fusion | flops 1614282496 | bytes 8913920 | tf_op jit(solution)/shard_map/dot_general | solution.py:167
  111.4 0.6 exponential_reduce_fusion
  112.1 5.7 %collective-permute-start.22 = (f32[8,128]{1,0:T(8,128)S(1)}, f32[8,128]{1,0:T(8,128)S(1)}, u32[]{:S(2)}, u32[]{:S(2)}) collective-permute-start(f32[8,128]{1,0:T(8,128)S(1)} %reshape.130), channel_id=1, source_target_pairs={{0,256},{16,272},{32,288},{48,304},{64,320},{80,336},{96,352},{112... | collective-permute-start | bytes 12296 | tf_op jit(solution)/shard_map/ppermute | solution.py:22
  117.7 0.8 collective-permute-done.22
  118.7 17.8 %all_to_all.10 = f32[32,8,128]{2,1,0:T(8,128)S(1)} all-to-all(f32[32,8,128]{2,1,0:T(8,128)S(1)} %bitcast.110), channel_id=1, replica_groups={{0,1,2,3,4,5,6,7,8,9,10,11,12,13,14,15,128,129,130,131,132,133,134,135,..., dimensions={0} | all-to-all | bytes 262144 | tf_op jit(solution)/shard_map/all_to_all | solution.py:37
  136.8 2.8 %copy-done.1 = bf16[2,2,8,96,1024]{4,3,2,1,0:T(8,128)(2,1)S(1)} copy-done((bf16[2,2,8,96,1024]{4,3,2,1,0:T(8,128)(2,1)S(1)}, bf16[2,2,8,96,1024]{4,3,2,1,0:T(8,128)(2,1)}, u32[]{:S(2)}) %copy-start.1) | copy-done | bytes 6291480
  139.6 2.5 %shard_map.68 = (bf16[256,1024]{1,0:T(8,128)(2,1)S(1)}, bf16[2,1536,128]{2,1,0:T(8,128)(2,1)S(1)}) custom-call(f32[256,1024]{1,0:T(8,128)S(1)} %get-tuple-element.25.s_ref, bf16[256,1024]{1,0:T(8,128)(2,1)S(1)} %get-tuple-element.15.t_ref, f32[256,3]{1,0:T(8,128)S(1)} %copy.71.row_ref, bf16[2,1536,1024]{2,1,0:T(8,128)(2,1)S(1)} %bitcast.101), custom_call_target="tpu_custom_call" | custom-call | flops 1000000000 | bytes 5000000 | tf_op jit(solution)/shard_map/pallas_call | solution.py:113
  142.1 4.0 %collective-permute-start.23 = (bf16[2,1536,128]{2,1,0:T(8,128)(2,1)S(1)}, bf16[2,1536,128]{2,1,0:T(8,128)(2,1)S(1)}, u32[]{:S(2)}, u32[]{:S(2)}) collective-permute-start(bf16[2,1536,128]{2,1,0:T(8,128)(2,1)S(1)} %get-tuple-element.9), channel_id=1, source_target_pairs={{0,256},{16,272},{32,288},{48,304},{64,320},{80,336},{96,352},{112... | collective-permute-start | bytes 2359304 | tf_op jit(solution)/shard_map/ppermute | solution.py:22
  146.2 2.1 %shard_map.69 = f32[2,1536,128]{2,1,0:T(8,128)S(1)} custom-call(bf16[256,1024]{1,0:T(8,128)(2,1)S(1)} %get-tuple-element.8.lg_ref, bf16[2,1536,1024]{2,1,0:T(8,128)(2,1)S(1)} %bitcast.102), custom_call_target="tpu_custom_call" | custom-call | flops 1000000000 | bytes 5000000 | tf_op jit(solution)/shard_map/pallas_call | solution.py:113
  148.2 1.0 add_convert_fusion
  149.3 3.9 %all-to-all-start.1 = ((bf16[32,96,128]{2,1,0:T(8,128)(2,1)}), bf16[32,96,128]{2,1,0:T(8,128)(2,1)S(1)}, u32[]{:S(2)}, u32[]{:S(2)}) async-start(bf16[32,96,128]{2,1,0:T(8,128)(2,1)} %bitcast.51), calls=%async_computation.1 | async-start | bytes 1572864 | tf_op jit(solution)/shard_map/all_to_all | solution.py:37
  153.3 0.5 fusion.20
  153.8 23.0 %all-to-all-done.1 = bf16[32,96,128]{2,1,0:T(8,128)(2,1)S(1)} async-done(((bf16[32,96,128]{2,1,0:T(8,128)(2,1)}), bf16[32,96,128]{2,1,0:T(8,128)(2,1)S(1)}, u32[]{:S(2)}, u32[]{:S(2)}) %all-to-all-start.1) | async-done | bytes 786464 | tf_op jit(solution)/shard_map/all_to_all | solution.py:37
  176.7 0.7 reduce_sum.92
  (75 shorter events, 1.5 us)
Async XLA Ops:
  0.6 29.0 %copy-start.3 = (bf16[128,1536]{1,0:T(8,128)(2,1)S(1)}, bf16[128,1536]{1,0:T(8,128)(2,1)}, u32[]{:S(2)}) copy-start(bf16[128,1536]{1,0:T(8,128)(2,1)} %param.5) | copy-start | bytes 1179652
  1.8 15.1 %collective-permute-start = (bf16[96,1024]{1,0:T(8,128)(2,1)S(1)}, bf16[96,1024]{1,0:T(8,128)(2,1)S(1)}, u32[]{:S(2)}, u32[]{:S(2)}) collective-permute-start(bf16[96,1024]{1,0:T(8,128)(2,1)S(1)} %get-tuple-element.19), channel_id=1, source_target_pairs={{0,256},{16,272},{32,288},{48,304},{64,320},{80,336},{96,352},{112... | collective-permute-start | bytes 589832 | tf_op jit(solution)/shard_map/ppermute | solution.py:22
  5.4 21.6 %collective-permute-start.11 = (bf16[96,2048]{1,0:T(8,128)(2,1)S(1)}, bf16[96,2048]{1,0:T(8,128)(2,1)S(1)}, u32[]{:S(2)}, u32[]{:S(2)}) collective-permute-start(bf16[96,2048]{1,0:T(8,128)(2,1)S(1)} %constant_dynamic-slice_fusion.7), channel_id=1, source_target_pairs={{0,128},{16,144},{32,160},{48,176},{64,192},{80,208},{96,224},{112... | collective-permute-start | bytes 1179656 | tf_op jit(solution)/shard_map/ppermute | solution.py:22
  16.9 12.7 %collective-permute-start.1 = (bf16[192,1024]{1,0:T(8,128)(2,1)S(1)}, bf16[192,1024]{1,0:T(8,128)(2,1)S(1)}, u32[]{:S(2)}, u32[]{:S(2)}) collective-permute-start(bf16[192,1024]{1,0:T(8,128)(2,1)S(1)} %pad_maximum_fusion), channel_id=1, source_target_pairs={{0,16},{16,32},{32,48},{48,64},{64,80},{80,96},{96,112},{112,0},{1... | collective-permute-start | bytes 1179656 | tf_op jit(solution)/shard_map/ppermute | solution.py:27
  21.3 26.9 %collective-permute-start.4 = (bf16[192,1024]{1,0:T(8,128)(2,1)S(1)}, bf16[192,1024]{1,0:T(8,128)(2,1)S(1)}, u32[]{:S(2)}, u32[]{:S(2)}) collective-permute-start(bf16[192,1024]{1,0:T(8,128)(2,1)S(1)} %pad_maximum_fusion), channel_id=1, source_target_pairs={{0,112},{16,0},{32,16},{48,32},{64,48},{80,64},{96,80},{112,96},{1... | collective-permute-start | bytes 1179656 | tf_op jit(solution)/shard_map/ppermute | solution.py:27
  27.0 24.0 %collective-permute-start.12 = (bf16[96,1024]{1,0:T(8,128)(2,1)S(1)}, bf16[96,1024]{1,0:T(8,128)(2,1)S(1)}, u32[]{:S(2)}, u32[]{:S(2)}) collective-permute-start(bf16[96,1024]{1,0:T(8,128)(2,1)S(1)} %get-tuple-element.21), channel_id=1, source_target_pairs={{0,256},{16,272},{32,288},{48,304},{64,320},{80,336},{96,352},{112... | collective-permute-start | bytes 589832 | tf_op jit(solution)/shard_map/ppermute | solution.py:22
  29.6 34.6 %collective-permute-start.2 = (bf16[128,1536]{1,0:T(8,128)(2,1)S(1)}, bf16[128,1536]{1,0:T(8,128)(2,1)S(1)}, u32[]{:S(2)}, u32[]{:S(2)}) collective-permute-start(bf16[128,1536]{1,0:T(8,128)(2,1)S(1)} %copy-done.3), channel_id=1, source_target_pairs={{0,128},{16,144},{32,160},{48,176},{64,192},{80,208},{96,224},{112... | collective-permute-start | bytes 1179656 | tf_op jit(solution)/shard_map/ppermute | solution.py:22
  43.8 13.9 %collective-permute-start.5 = (bf16[192,1024]{1,0:T(8,128)(2,1)S(1)}, bf16[192,1024]{1,0:T(8,128)(2,1)S(1)}, u32[]{:S(2)}, u32[]{:S(2)}) collective-permute-start(bf16[192,1024]{1,0:T(8,128)(2,1)S(1)} %collective-permute-done.1), channel_id=1, source_target_pairs={{0,16},{16,32},{32,48},{48,64},{64,80},{80,96},{96,112},{112,0},{1... | collective-permute-start | bytes 1179656 | tf_op jit(solution)/shard_map/ppermute | solution.py:27
  48.3 14.0 %collective-permute-start.6 = (bf16[192,1024]{1,0:T(8,128)(2,1)S(1)}, bf16[192,1024]{1,0:T(8,128)(2,1)S(1)}, u32[]{:S(2)}, u32[]{:S(2)}) collective-permute-start(bf16[192,1024]{1,0:T(8,128)(2,1)S(1)} %collective-permute-done.4), channel_id=1, source_target_pairs={{0,112},{16,0},{32,16},{48,32},{64,48},{80,64},{96,80},{112,96},{1... | collective-permute-start | bytes 1179656 | tf_op jit(solution)/shard_map/ppermute | solution.py:27
  51.1 16.9 %collective-permute-start.13 = (bf16[192,1024]{1,0:T(8,128)(2,1)S(1)}, bf16[192,1024]{1,0:T(8,128)(2,1)S(1)}, u32[]{:S(2)}, u32[]{:S(2)}) collective-permute-start(bf16[192,1024]{1,0:T(8,128)(2,1)S(1)} %pad_maximum_fusion.1), channel_id=1, source_target_pairs={{0,16},{16,32},{32,48},{48,64},{64,80},{80,96},{96,112},{112,0},{1... | collective-permute-start | bytes 1179656 | tf_op jit(solution)/shard_map/ppermute | solution.py:27
  55.7 17.2 %collective-permute-start.14 = (bf16[192,1024]{1,0:T(8,128)(2,1)S(1)}, bf16[192,1024]{1,0:T(8,128)(2,1)S(1)}, u32[]{:S(2)}, u32[]{:S(2)}) collective-permute-start(bf16[192,1024]{1,0:T(8,128)(2,1)S(1)} %pad_maximum_fusion.1), channel_id=1, source_target_pairs={{0,112},{16,0},{32,16},{48,32},{64,48},{80,64},{96,80},{112,96},{1... | collective-permute-start | bytes 1179656 | tf_op jit(solution)/shard_map/ppermute | solution.py:27
  57.7 17.2 %collective-permute-start.7 = (bf16[192,1024]{1,0:T(8,128)(2,1)S(1)}, bf16[192,1024]{1,0:T(8,128)(2,1)S(1)}, u32[]{:S(2)}, u32[]{:S(2)}) collective-permute-start(bf16[192,1024]{1,0:T(8,128)(2,1)S(1)} %collective-permute-done.5), channel_id=1, source_target_pairs={{0,16},{16,32},{32,48},{48,64},{64,80},{80,96},{96,112},{112,0},{1... | collective-permute-start | bytes 1179656 | tf_op jit(solution)/shard_map/ppermute | solution.py:27
  62.3 16.1 %collective-permute-start.8 = (bf16[192,1024]{1,0:T(8,128)(2,1)S(1)}, bf16[192,1024]{1,0:T(8,128)(2,1)S(1)}, u32[]{:S(2)}, u32[]{:S(2)}) collective-permute-start(bf16[192,1024]{1,0:T(8,128)(2,1)S(1)} %collective-permute-done.6), channel_id=1, source_target_pairs={{0,112},{16,0},{32,16},{48,32},{64,48},{80,64},{96,80},{112,96},{1... | collective-permute-start | bytes 1179656 | tf_op jit(solution)/shard_map/ppermute | solution.py:27
  64.4 45.0 %collective-permute-start.3 = (bf16[256,1536]{1,0:T(8,128)(2,1)S(1)}, bf16[256,1536]{1,0:T(8,128)(2,1)S(1)}, u32[]{:S(2)}, u32[]{:S(2)}) collective-permute-start(bf16[256,1536]{1,0:T(8,128)(2,1)S(1)} %maximum_select_fusion), channel_id=1, source_target_pairs={{0,256},{16,272},{32,288},{48,304},{64,320},{80,336},{96,352},{112... | collective-permute-start | bytes 2359304 | tf_op jit(solution)/shard_map/ppermute | solution.py:22
  68.0 14.8 %collective-permute-start.15 = (bf16[192,1024]{1,0:T(8,128)(2,1)S(1)}, bf16[192,1024]{1,0:T(8,128)(2,1)S(1)}, u32[]{:S(2)}, u32[]{:S(2)}) collective-permute-start(bf16[192,1024]{1,0:T(8,128)(2,1)S(1)} %collective-permute-done.13), channel_id=1, source_target_pairs={{0,16},{16,32},{32,48},{48,64},{64,80},{80,96},{96,112},{112,0},{1... | collective-permute-start | bytes 1179656 | tf_op jit(solution)/shard_map/ppermute | solution.py:27
  72.9 14.3 %collective-permute-start.16 = (bf16[192,1024]{1,0:T(8,128)(2,1)S(1)}, bf16[192,1024]{1,0:T(8,128)(2,1)S(1)}, u32[]{:S(2)}, u32[]{:S(2)}) collective-permute-start(bf16[192,1024]{1,0:T(8,128)(2,1)S(1)} %collective-permute-done.14), channel_id=1, source_target_pairs={{0,112},{16,0},{32,16},{48,32},{64,48},{80,64},{96,80},{112,96},{1... | collective-permute-start | bytes 1179656 | tf_op jit(solution)/shard_map/ppermute | solution.py:27
  74.9 36.5 %collective-permute-start.21 = (bf16[128,1024]{1,0:T(8,128)(2,1)S(1)}, bf16[128,1024]{1,0:T(8,128)(2,1)S(1)}, u32[]{:S(2)}, u32[]{:S(2)}) collective-permute-start(bf16[128,1024]{1,0:T(8,128)(2,1)S(1)} %get-tuple-element.7), channel_id=1, source_target_pairs={{0,128},{16,144},{32,160},{48,176},{64,192},{80,208},{96,224},{112... | collective-permute-start | bytes 786440 | tf_op jit(solution)/shard_map/ppermute | solution.py:22
  78.4 11.0 %collective-permute-start.9 = (bf16[96,1024]{1,0:T(8,128)(2,1)S(1)}, bf16[96,1024]{1,0:T(8,128)(2,1)S(1)}, u32[]{:S(2)}, u32[]{:S(2)}) collective-permute-start(bf16[96,1024]{1,0:T(8,128)(2,1)S(1)} %slice.68), channel_id=1, source_target_pairs={{0,16},{16,32},{32,48},{48,64},{64,80},{80,96},{96,112},{112,0},{1... | collective-permute-start | bytes 589832 | tf_op jit(solution)/shard_map/ppermute | solution.py:27
  82.9 9.6 %collective-permute-start.10 = (bf16[96,1024]{1,0:T(8,128)(2,1)S(1)}, bf16[96,1024]{1,0:T(8,128)(2,1)S(1)}, u32[]{:S(2)}, u32[]{:S(2)}) collective-permute-start(bf16[96,1024]{1,0:T(8,128)(2,1)S(1)} %slice.69), channel_id=1, source_target_pairs={{0,112},{16,0},{32,16},{48,32},{64,48},{80,64},{96,80},{112,96},{1... | collective-permute-start | bytes 589832 | tf_op jit(solution)/shard_map/ppermute | solution.py:27
  87.2 11.5 %collective-permute-start.17 = (bf16[192,1024]{1,0:T(8,128)(2,1)S(1)}, bf16[192,1024]{1,0:T(8,128)(2,1)S(1)}, u32[]{:S(2)}, u32[]{:S(2)}) collective-permute-start(bf16[192,1024]{1,0:T(8,128)(2,1)S(1)} %collective-permute-done.15), channel_id=1, source_target_pairs={{0,16},{16,32},{32,48},{48,64},{64,80},{80,96},{96,112},{112,0},{1... | collective-permute-start | bytes 1179656 | tf_op jit(solution)/shard_map/ppermute | solution.py:27
  89.4 12.3 %collective-permute-start.18 = (bf16[192,1024]{1,0:T(8,128)(2,1)S(1)}, bf16[192,1024]{1,0:T(8,128)(2,1)S(1)}, u32[]{:S(2)}, u32[]{:S(2)}) collective-permute-start(bf16[192,1024]{1,0:T(8,128)(2,1)S(1)} %collective-permute-done.16), channel_id=1, source_target_pairs={{0,112},{16,0},{32,16},{48,32},{64,48},{80,64},{96,80},{112,96},{1... | collective-permute-start | bytes 1179656 | tf_op jit(solution)/shard_map/ppermute | solution.py:27
  98.7 6.4 %collective-permute-start.19 = (bf16[96,1024]{1,0:T(8,128)(2,1)S(1)}, bf16[96,1024]{1,0:T(8,128)(2,1)S(1)}, u32[]{:S(2)}, u32[]{:S(2)}) collective-permute-start(bf16[96,1024]{1,0:T(8,128)(2,1)S(1)} %slice.70), channel_id=1, source_target_pairs={{0,16},{16,32},{32,48},{48,64},{64,80},{80,96},{96,112},{112,0},{1... | collective-permute-start | bytes 589832 | tf_op jit(solution)/shard_map/ppermute | solution.py:27
  101.7 7.6 %collective-permute-start.20 = (bf16[96,1024]{1,0:T(8,128)(2,1)S(1)}, bf16[96,1024]{1,0:T(8,128)(2,1)S(1)}, u32[]{:S(2)}, u32[]{:S(2)}) collective-permute-start(bf16[96,1024]{1,0:T(8,128)(2,1)S(1)} %slice.71), channel_id=1, source_target_pairs={{0,112},{16,0},{32,16},{48,32},{64,48},{80,64},{96,80},{112,96},{1... | collective-permute-start | bytes 589832 | tf_op jit(solution)/shard_map/ppermute | solution.py:27
  109.4 2.6 %copy-start = (bf16[2,2,8,96,1024]{4,3,2,1,0:T(8,128)(2,1)}, bf16[2,2,8,96,1024]{4,3,2,1,0:T(8,128)(2,1)S(1)}, u32[]{:S(2)}) copy-start(bf16[2,2,8,96,1024]{4,3,2,1,0:T(8,128)(2,1)S(1)} %bitcast_dynamic-update-slice_fusion) | copy-start | bytes 18874372
  109.4 9.2 %copy-start.4 = (f32[128]{0:T(128)S(1)}, f32[128]{0:T(128)}, u32[]{:S(2)}) copy-start(f32[128]{0:T(128)} %param.9) | copy-start | bytes 1540
  112.1 6.5 %collective-permute-start.22 = (f32[8,128]{1,0:T(8,128)S(1)}, f32[8,128]{1,0:T(8,128)S(1)}, u32[]{:S(2)}, u32[]{:S(2)}) collective-permute-start(f32[8,128]{1,0:T(8,128)S(1)} %reshape.130), channel_id=1, source_target_pairs={{0,256},{16,272},{32,288},{48,304},{64,320},{80,336},{96,352},{112... | collective-permute-start | bytes 12296 | tf_op jit(solution)/shard_map/ppermute | solution.py:22
  136.8 2.8 %copy-start.1 = (bf16[2,2,8,96,1024]{4,3,2,1,0:T(8,128)(2,1)S(1)}, bf16[2,2,8,96,1024]{4,3,2,1,0:T(8,128)(2,1)}, u32[]{:S(2)}) copy-start(bf16[2,2,8,96,1024]{4,3,2,1,0:T(8,128)(2,1)} %copy-done) | copy-start | bytes 18874372
  139.6 6.6 %copy-start.2 = (bf16[2,2,8,96,1024]{4,3,2,1,0:T(8,128)(2,1)S(1)}, bf16[2,2,8,96,1024]{4,3,2,1,0:T(8,128)(2,1)}, u32[]{:S(2)}) copy-start(bf16[2,2,8,96,1024]{4,3,2,1,0:T(8,128)(2,1)} %copy-done) | copy-start | bytes 18874372
  142.1 6.1 %collective-permute-start.23 = (bf16[2,1536,128]{2,1,0:T(8,128)(2,1)S(1)}, bf16[2,1536,128]{2,1,0:T(8,128)(2,1)S(1)}, u32[]{:S(2)}, u32[]{:S(2)}) collective-permute-start(bf16[2,1536,128]{2,1,0:T(8,128)(2,1)S(1)} %get-tuple-element.9), channel_id=1, source_target_pairs={{0,256},{16,272},{32,288},{48,304},{64,320},{80,336},{96,352},{112... | collective-permute-start | bytes 2359304 | tf_op jit(solution)/shard_map/ppermute | solution.py:22
  149.3 27.5 %all-to-all-start.1 = ((bf16[32,96,128]{2,1,0:T(8,128)(2,1)}), bf16[32,96,128]{2,1,0:T(8,128)(2,1)S(1)}, u32[]{:S(2)}, u32[]{:S(2)}) async-start(bf16[32,96,128]{2,1,0:T(8,128)(2,1)} %bitcast.51), calls=%async_computation.1 | async-start | bytes 1572864 | tf_op jit(solution)/shard_map/all_to_all | solution.py:37

commit v7 on v6

--- a/solution.py
+++ b/solution.py
@@ -115,7 +115,7 @@
         in_specs=[whole] * len(ins),
         out_specs=[whole] * len(outs),
         out_shape=outs,
-        compiler_params=pltpu.CompilerParams(vmem_limit_bytes=40 * 2**20),
+        compiler_params=pltpu.CompilerParams(vmem_limit_bytes=4 * 2**20),
         cost_estimate=pl.CostEstimate(
             flops=10**9, bytes_accessed=5 * 10**6, transcendentals=5 * 10**5
         ),

time: 179 us -> 179 us (level)
  no operation moved by 1% of the time
where the time goes in v7:
time: 179 us; the launch traced here: 177 us
  starting transfers between devices  99.6 us (56%)
  waiting for transfers between devices  37.5 us (21%)
  blocking collectives  17.8 us (10%)
  local copies, waits for them, and re-layouts  7.43 us (4%)
  other arithmetic  6.99 us (4%)
  Pallas kernels  4.57 us (3%)
  matrix products  2 us (1%)
    ppermute x16, starting transfers between devices, along_y(): return lax.ppermute(x, 'dp', perm)  49.2 us
    ppermute x8, starting transfers between devices, flip(): return lax.ppermute(x, ('section', 'dp'), perm)  46.4 us
    all_to_all x1, waiting for transfers between devices, exchange(): lax.all_to_all(x, ('section', 'dp', 'vocab'), split_axis=0, concat_axis=0...  23 us
    all_to_all x1, blocking collectives, exchange(): lax.all_to_all(x, ('section', 'dp', 'vocab'), split_axis=0, concat_axis=0...  17.8 us
    ppermute x16, waiting for transfers between devices, along_y(): return lax.ppermute(x, 'dp', perm)  13.7 us
    pallas_call x2, Pallas kernels, in_vmem(): pl.pallas_call(kernel, in_specs=[whole] * len(ins), out_specs=[whole] * l...  4.57 us
    all_to_all x1, starting transfers between devices, exchange(): lax.all_to_all(x, ('section', 'dp', 'vocab'), split_axis=0, concat_axis=0...  3.91 us
  transfers between devices with their start and end apart: 25, of which 7 were waited for; matrix products, arithmetic and copies ran while one was open for 5% of the time, Pallas kernels for 1%

profile of v7, /device:TPU:25, one launch (start us, length us, event | category | flops | bytes accessed | tf_op | source)
XLA Modules:
  0.0 177.5 jit_solution(1695579358897790569)
XLA Ops:
  0.7 1.1 constant_dynamic-slice_fusion.9
  1.8 2.6 %collective-permute-start = (bf16[96,1024]{1,0:T(8,128)(2,1)S(1)}, bf16[96,1024]{1,0:T(8,128)(2,1)S(1)}, u32[]{:S(2)}, u32[]{:S(2)}) collective-permute-start(bf16[96,1024]{1,0:T(8,128)(2,1)S(1)} %get-tuple-element.19), channel_id=1, source_target_pairs={{0,256},{16,272},{32,288},{48,304},{64,320},{80,336},{96,352},{112... | collective-permute-start | bytes 589832 | tf_op jit(solution)/shard_map/ppermute | solution.py:22
  4.4 1.0 constant_dynamic-slice_fusion.7
  5.4 10.6 %collective-permute-start.11 = (bf16[96,2048]{1,0:T(8,128)(2,1)S(1)}, bf16[96,2048]{1,0:T(8,128)(2,1)S(1)}, u32[]{:S(2)}, u32[]{:S(2)}) collective-permute-start(bf16[96,2048]{1,0:T(8,128)(2,1)S(1)} %constant_dynamic-slice_fusion.7), channel_id=1, source_target_pairs={{0,128},{16,144},{32,160},{48,176},{64,192},{80,208},{96,224},{112... | collective-permute-start | bytes 1179656 | tf_op jit(solution)/shard_map/ppermute | solution.py:22
  16.0 0.7 exponential_multiply_fusion
  16.9 4.4 %collective-permute-start.1 = (bf16[192,1024]{1,0:T(8,128)(2,1)S(1)}, bf16[192,1024]{1,0:T(8,128)(2,1)S(1)}, u32[]{:S(2)}, u32[]{:S(2)}) collective-permute-start(bf16[192,1024]{1,0:T(8,128)(2,1)S(1)} %pad_maximum_fusion), channel_id=1, source_target_pairs={{0,16},{16,32},{32,48},{48,64},{64,80},{80,96},{96,112},{112,0},{1... | collective-permute-start | bytes 1179656 | tf_op jit(solution)/shard_map/ppermute | solution.py:27
  21.3 1.9 %collective-permute-start.4 = (bf16[192,1024]{1,0:T(8,128)(2,1)S(1)}, bf16[192,1024]{1,0:T(8,128)(2,1)S(1)}, u32[]{:S(2)}, u32[]{:S(2)}) collective-permute-start(bf16[192,1024]{1,0:T(8,128)(2,1)S(1)} %pad_maximum_fusion), channel_id=1, source_target_pairs={{0,112},{16,0},{32,16},{48,32},{64,48},{80,64},{96,80},{112,96},{1... | collective-permute-start | bytes 1179656 | tf_op jit(solution)/shard_map/ppermute | solution.py:27
  23.3 0.6 mul.60
  23.9 2.9 %fusion = bf16[128,4096]{1,0:T(8,128)(2,1)S(1)} fusion(f32[16,8,32,128]{3,2,1,0:T(8,128)S(1)} %bitcast.103, s32[128,4096]{1,0:T(8,128)} %param.7), kind=kLoop, calls=%fused_computation.1 | loop fusion | flops 1572864 | bytes 5242880 | tf_op jit(solution)/shard_map/convert_element_type | solution.py:51
  27.0 2.5 %collective-permute-start.12 = (bf16[96,1024]{1,0:T(8,128)(2,1)S(1)}, bf16[96,1024]{1,0:T(8,128)(2,1)S(1)}, u32[]{:S(2)}, u32[]{:S(2)}) collective-permute-start(bf16[96,1024]{1,0:T(8,128)(2,1)S(1)} %get-tuple-element.21), channel_id=1, source_target_pairs={{0,256},{16,272},{32,288},{48,304},{64,320},{80,336},{96,352},{112... | collective-permute-start | bytes 589832 | tf_op jit(solution)/shard_map/ppermute | solution.py:22
  29.6 14.2 %collective-permute-start.2 = (bf16[128,1536]{1,0:T(8,128)(2,1)S(1)}, bf16[128,1536]{1,0:T(8,128)(2,1)S(1)}, u32[]{:S(2)}, u32[]{:S(2)}) collective-permute-start(bf16[128,1536]{1,0:T(8,128)(2,1)S(1)} %copy-done.3), channel_id=1, source_target_pairs={{0,128},{16,144},{32,160},{48,176},{64,192},{80,208},{96,224},{112... | collective-permute-start | bytes 1179656 | tf_op jit(solution)/shard_map/ppermute | solution.py:22
  43.8 4.4 %collective-permute-start.5 = (bf16[192,1024]{1,0:T(8,128)(2,1)S(1)}, bf16[192,1024]{1,0:T(8,128)(2,1)S(1)}, u32[]{:S(2)}, u32[]{:S(2)}) collective-permute-start(bf16[192,1024]{1,0:T(8,128)(2,1)S(1)} %collective-permute-done.1), channel_id=1, source_target_pairs={{0,16},{16,32},{32,48},{48,64},{64,80},{80,96},{96,112},{112,0},{1... | collective-permute-start | bytes 1179656 | tf_op jit(solution)/shard_map/ppermute | solution.py:27
  48.3 1.9 %collective-permute-start.6 = (bf16[192,1024]{1,0:T(8,128)(2,1)S(1)}, bf16[192,1024]{1,0:T(8,128)(2,1)S(1)}, u32[]{:S(2)}, u32[]{:S(2)}) collective-permute-start(bf16[192,1024]{1,0:T(8,128)(2,1)S(1)} %collective-permute-done.4), channel_id=1, source_target_pairs={{0,112},{16,0},{32,16},{48,32},{64,48},{80,64},{96,80},{112,96},{1... | collective-permute-start | bytes 1179656 | tf_op jit(solution)/shard_map/ppermute | solution.py:27
  50.2 0.8 broadcast_in_dim.6
  51.1 4.6 %collective-permute-start.13 = (bf16[192,1024]{1,0:T(8,128)(2,1)S(1)}, bf16[192,1024]{1,0:T(8,128)(2,1)S(1)}, u32[]{:S(2)}, u32[]{:S(2)}) collective-permute-start(bf16[192,1024]{1,0:T(8,128)(2,1)S(1)} %pad_maximum_fusion.1), channel_id=1, source_target_pairs={{0,16},{16,32},{32,48},{48,64},{64,80},{80,96},{96,112},{112,0},{1... | collective-permute-start | bytes 1179656 | tf_op jit(solution)/shard_map/ppermute | solution.py:27
  55.7 1.9 %collective-permute-start.14 = (bf16[192,1024]{1,0:T(8,128)(2,1)S(1)}, bf16[192,1024]{1,0:T(8,128)(2,1)S(1)}, u32[]{:S(2)}, u32[]{:S(2)}) collective-permute-start(bf16[192,1024]{1,0:T(8,128)(2,1)S(1)} %pad_maximum_fusion.1), channel_id=1, source_target_pairs={{0,112},{16,0},{32,16},{48,32},{64,48},{80,64},{96,80},{112,96},{1... | collective-permute-start | bytes 1179656 | tf_op jit(solution)/shard_map/ppermute | solution.py:27
  57.7 4.6 %collective-permute-start.7 = (bf16[192,1024]{1,0:T(8,128)(2,1)S(1)}, bf16[192,1024]{1,0:T(8,128)(2,1)S(1)}, u32[]{:S(2)}, u32[]{:S(2)}) collective-permute-start(bf16[192,1024]{1,0:T(8,128)(2,1)S(1)} %collective-permute-done.5), channel_id=1, source_target_pairs={{0,16},{16,32},{32,48},{48,64},{64,80},{80,96},{96,112},{112,0},{1... | collective-permute-start | bytes 1179656 | tf_op jit(solution)/shard_map/ppermute | solution.py:27
  62.3 1.9 %collective-permute-start.8 = (bf16[192,1024]{1,0:T(8,128)(2,1)S(1)}, bf16[192,1024]{1,0:T(8,128)(2,1)S(1)}, u32[]{:S(2)}, u32[]{:S(2)}) collective-permute-start(bf16[192,1024]{1,0:T(8,128)(2,1)S(1)} %collective-permute-done.6), channel_id=1, source_target_pairs={{0,112},{16,0},{32,16},{48,32},{64,48},{80,64},{96,80},{112,96},{1... | collective-permute-start | bytes 1179656 | tf_op jit(solution)/shard_map/ppermute | solution.py:27
  64.2 0.2 maximum_select_fusion
  64.4 3.6 %collective-permute-start.3 = (bf16[256,1536]{1,0:T(8,128)(2,1)S(1)}, bf16[256,1536]{1,0:T(8,128)(2,1)S(1)}, u32[]{:S(2)}, u32[]{:S(2)}) collective-permute-start(bf16[256,1536]{1,0:T(8,128)(2,1)S(1)} %maximum_select_fusion), channel_id=1, source_target_pairs={{0,256},{16,272},{32,288},{48,304},{64,320},{80,336},{96,352},{112... | collective-permute-start | bytes 2359304 | tf_op jit(solution)/shard_map/ppermute | solution.py:22
  68.0 4.9 %collective-permute-start.15 = (bf16[192,1024]{1,0:T(8,128)(2,1)S(1)}, bf16[192,1024]{1,0:T(8,128)(2,1)S(1)}, u32[]{:S(2)}, u32[]{:S(2)}) collective-permute-start(bf16[192,1024]{1,0:T(8,128)(2,1)S(1)} %collective-permute-done.13), channel_id=1, source_target_pairs={{0,16},{16,32},{32,48},{48,64},{64,80},{80,96},{96,112},{112,0},{1... | collective-permute-start | bytes 1179656 | tf_op jit(solution)/shard_map/ppermute | solution.py:27
  72.9 1.9 %collective-permute-start.16 = (bf16[192,1024]{1,0:T(8,128)(2,1)S(1)}, bf16[192,1024]{1,0:T(8,128)(2,1)S(1)}, u32[]{:S(2)}, u32[]{:S(2)}) collective-permute-start(bf16[192,1024]{1,0:T(8,128)(2,1)S(1)} %collective-permute-done.14), channel_id=1, source_target_pairs={{0,112},{16,0},{32,16},{48,32},{64,48},{80,64},{96,80},{112,96},{1... | collective-permute-start | bytes 1179656 | tf_op jit(solution)/shard_map/ppermute | solution.py:27
  74.9 3.2 %collective-permute-start.21 = (bf16[128,1024]{1,0:T(8,128)(2,1)S(1)}, bf16[128,1024]{1,0:T(8,128)(2,1)S(1)}, u32[]{:S(2)}, u32[]{:S(2)}) collective-permute-start(bf16[128,1024]{1,0:T(8,128)(2,1)S(1)} %get-tuple-element.7), channel_id=1, source_target_pairs={{0,128},{16,144},{32,160},{48,176},{64,192},{80,208},{96,224},{112... | collective-permute-start | bytes 786440 | tf_op jit(solution)/shard_map/ppermute | solution.py:22
  78.2 0.2 collective-permute-done.8
  78.4 4.3 %collective-permute-start.9 = (bf16[96,1024]{1,0:T(8,128)(2,1)S(1)}, bf16[96,1024]{1,0:T(8,128)(2,1)S(1)}, u32[]{:S(2)}, u32[]{:S(2)}) collective-permute-start(bf16[96,1024]{1,0:T(8,128)(2,1)S(1)} %slice.68), channel_id=1, source_target_pairs={{0,16},{16,32},{32,48},{48,64},{64,80},{80,96},{96,112},{112,0},{1... | collective-permute-start | bytes 589832 | tf_op jit(solution)/shard_map/ppermute | solution.py:27
  82.9 1.9 %collective-permute-start.10 = (bf16[96,1024]{1,0:T(8,128)(2,1)S(1)}, bf16[96,1024]{1,0:T(8,128)(2,1)S(1)}, u32[]{:S(2)}, u32[]{:S(2)}) collective-permute-start(bf16[96,1024]{1,0:T(8,128)(2,1)S(1)} %slice.69), channel_id=1, source_target_pairs={{0,112},{16,0},{32,16},{48,32},{64,48},{80,64},{96,80},{112,96},{1... | collective-permute-start | bytes 589832 | tf_op jit(solution)/shard_map/ppermute | solution.py:27
  84.8 2.4 %collective-permute-done.16 = bf16[192,1024]{1,0:T(8,128)(2,1)S(1)} collective-permute-done((bf16[192,1024]{1,0:T(8,128)(2,1)S(1)}, bf16[192,1024]{1,0:T(8,128)(2,1)S(1)}, u32[]{:S(2)}, u32[]{:S(2)}) %collective-permute-start.16) | collective-permute-done | bytes 393248 | tf_op jit(solution)/shard_map/ppermute | solution.py:27
  87.2 2.2 %collective-permute-start.17 = (bf16[192,1024]{1,0:T(8,128)(2,1)S(1)}, bf16[192,1024]{1,0:T(8,128)(2,1)S(1)}, u32[]{:S(2)}, u32[]{:S(2)}) collective-permute-start(bf16[192,1024]{1,0:T(8,128)(2,1)S(1)} %collective-permute-done.15), channel_id=1, source_target_pairs={{0,16},{16,32},{32,48},{48,64},{64,80},{80,96},{96,112},{112,0},{1... | collective-permute-start | bytes 1179656 | tf_op jit(solution)/shard_map/ppermute | solution.py:27
  89.4 3.1 %collective-permute-start.18 = (bf16[192,1024]{1,0:T(8,128)(2,1)S(1)}, bf16[192,1024]{1,0:T(8,128)(2,1)S(1)}, u32[]{:S(2)}, u32[]{:S(2)}) collective-permute-start(bf16[192,1024]{1,0:T(8,128)(2,1)S(1)} %collective-permute-done.16), channel_id=1, source_target_pairs={{0,112},{16,0},{32,16},{48,32},{64,48},{80,64},{96,80},{112,96},{1... | collective-permute-start | bytes 1179656 | tf_op jit(solution)/shard_map/ppermute | solution.py:27
  92.8 5.9 %collective-permute-done.17 = bf16[192,1024]{1,0:T(8,128)(2,1)S(1)} collective-permute-done((bf16[192,1024]{1,0:T(8,128)(2,1)S(1)}, bf16[192,1024]{1,0:T(8,128)(2,1)S(1)}, u32[]{:S(2)}, u32[]{:S(2)}) %collective-permute-start.17) | collective-permute-done | bytes 393248 | tf_op jit(solution)/shard_map/ppermute | solution.py:27
  98.7 3.0 %collective-permute-start.19 = (bf16[96,1024]{1,0:T(8,128)(2,1)S(1)}, bf16[96,1024]{1,0:T(8,128)(2,1)S(1)}, u32[]{:S(2)}, u32[]{:S(2)}) collective-permute-start(bf16[96,1024]{1,0:T(8,128)(2,1)S(1)} %slice.70), channel_id=1, source_target_pairs={{0,16},{16,32},{32,48},{48,64},{64,80},{80,96},{96,112},{112,0},{1... | collective-permute-start | bytes 589832 | tf_op jit(solution)/shard_map/ppermute | solution.py:27
  101.7 2.3 %collective-permute-start.20 = (bf16[96,1024]{1,0:T(8,128)(2,1)S(1)}, bf16[96,1024]{1,0:T(8,128)(2,1)S(1)}, u32[]{:S(2)}, u32[]{:S(2)}) collective-permute-start(bf16[96,1024]{1,0:T(8,128)(2,1)S(1)} %slice.71), channel_id=1, source_target_pairs={{0,112},{16,0},{32,16},{48,32},{64,48},{80,64},{96,80},{112,96},{1... | collective-permute-start | bytes 589832 | tf_op jit(solution)/shard_map/ppermute | solution.py:27
  104.2 1.0 collective-permute-done.19
  105.2 4.2 %collective-permute-done.20 = bf16[96,1024]{1,0:T(8,128)(2,1)S(1)} collective-permute-done((bf16[96,1024]{1,0:T(8,128)(2,1)S(1)}, bf16[96,1024]{1,0:T(8,128)(2,1)S(1)}, u32[]{:S(2)}, u32[]{:S(2)}) %collective-permute-start.20) | collective-permute-done | bytes 196640 | tf_op jit(solution)/shard_map/ppermute | solution.py:27
  109.4 2.0 %fusion.23 = (f32[256]{0:T(256)S(1)}, f32[256,1024]{1,0:T(8,128)S(1)}) fusion(bf16[3072,1024]{1,0:T(8,128)(2,1)S(1)} %bitcast.100, bf16[256,1536]{1,0:T(8,128)(2,1)S(1)} %collective-permute-done.3, bf16[256,1536]{1,0:T(8,128)(2,1)S(1)} %maximum_select_fusion), kind=kOutput, calls=%fused_computation.74 | convolution fusion | flops 1614282496 | bytes 8913920 | tf_op jit(solution)/shard_map/dot_general | solution.py:167
  111.4 0.6 exponential_reduce_fusion
  112.1 5.7 %collective-permute-start.22 = (f32[8,128]{1,0:T(8,128)S(1)}, f32[8,128]{1,0:T(8,128)S(1)}, u32[]{:S(2)}, u32[]{:S(2)}) collective-permute-start(f32[8,128]{1,0:T(8,128)S(1)} %reshape.130), channel_id=1, source_target_pairs={{0,256},{16,272},{32,288},{48,304},{64,320},{80,336},{96,352},{112... | collective-permute-start | bytes 12296 | tf_op jit(solution)/shard_map/ppermute | solution.py:22
  117.7 0.8 collective-permute-done.22
  118.7 17.8 %all_to_all.10 = f32[32,8,128]{2,1,0:T(8,128)S(1)} all-to-all(f32[32,8,128]{2,1,0:T(8,128)S(1)} %bitcast.110), channel_id=1, replica_groups={{0,1,2,3,4,5,6,7,8,9,10,11,12,13,14,15,128,129,130,131,132,133,134,135,..., dimensions={0} | all-to-all | bytes 262144 | tf_op jit(solution)/shard_map/all_to_all | solution.py:37
  136.8 2.8 %copy-done.1 = bf16[2,2,8,96,1024]{4,3,2,1,0:T(8,128)(2,1)S(1)} copy-done((bf16[2,2,8,96,1024]{4,3,2,1,0:T(8,128)(2,1)S(1)}, bf16[2,2,8,96,1024]{4,3,2,1,0:T(8,128)(2,1)}, u32[]{:S(2)}) %copy-start.1) | copy-done | bytes 6291480
  139.6 2.5 %shard_map.68 = (bf16[256,1024]{1,0:T(8,128)(2,1)S(1)}, bf16[2,1536,128]{2,1,0:T(8,128)(2,1)S(1)}) custom-call(f32[256,1024]{1,0:T(8,128)S(1)} %get-tuple-element.25.s_ref, bf16[256,1024]{1,0:T(8,128)(2,1)S(1)} %get-tuple-element.15.t_ref, f32[256,3]{1,0:T(8,128)S(1)} %copy.71.row_ref, bf16[2,1536,1024]{2,1,0:T(8,128)(2,1)S(1)} %bitcast.101), custom_call_target="tpu_custom_call" | custom-call | flops 1000000000 | bytes 5000000 | tf_op jit(solution)/shard_map/pallas_call | solution.py:113
  142.1 4.0 %collective-permute-start.23 = (bf16[2,1536,128]{2,1,0:T(8,128)(2,1)S(1)}, bf16[2,1536,128]{2,1,0:T(8,128)(2,1)S(1)}, u32[]{:S(2)}, u32[]{:S(2)}) collective-permute-start(bf16[2,1536,128]{2,1,0:T(8,128)(2,1)S(1)} %get-tuple-element.9), channel_id=1, source_target_pairs={{0,256},{16,272},{32,288},{48,304},{64,320},{80,336},{96,352},{112... | collective-permute-start | bytes 2359304 | tf_op jit(solution)/shard_map/ppermute | solution.py:22
  146.2 2.1 %shard_map.69 = f32[2,1536,128]{2,1,0:T(8,128)S(1)} custom-call(bf16[256,1024]{1,0:T(8,128)(2,1)S(1)} %get-tuple-element.8.lg_ref, bf16[2,1536,1024]{2,1,0:T(8,128)(2,1)S(1)} %bitcast.102), custom_call_target="tpu_custom_call" | custom-call | flops 1000000000 | bytes 5000000 | tf_op jit(solution)/shard_map/pallas_call | solution.py:113
  148.2 1.0 add_convert_fusion
  149.3 3.9 %all-to-all-start.1 = ((bf16[32,96,128]{2,1,0:T(8,128)(2,1)}), bf16[32,96,128]{2,1,0:T(8,128)(2,1)S(1)}, u32[]{:S(2)}, u32[]{:S(2)}) async-start(bf16[32,96,128]{2,1,0:T(8,128)(2,1)} %bitcast.51), calls=%async_computation.1 | async-start | bytes 1572864 | tf_op jit(solution)/shard_map/all_to_all | solution.py:37
  153.3 0.5 fusion.20
  153.8 23.0 %all-to-all-done.1 = bf16[32,96,128]{2,1,0:T(8,128)(2,1)S(1)} async-done(((bf16[32,96,128]{2,1,0:T(8,128)(2,1)}), bf16[32,96,128]{2,1,0:T(8,128)(2,1)S(1)}, u32[]{:S(2)}, u32[]{:S(2)}) %all-to-all-start.1) | async-done | bytes 786464 | tf_op jit(solution)/shard_map/all_to_all | solution.py:37
  176.7 0.7 reduce_sum.92
  (75 shorter events, 1.5 us)
Async XLA Ops:
  0.6 29.0 %copy-start.3 = (bf16[128,1536]{1,0:T(8,128)(2,1)S(1)}, bf16[128,1536]{1,0:T(8,128)(2,1)}, u32[]{:S(2)}) copy-start(bf16[128,1536]{1,0:T(8,128)(2,1)} %param.5) | copy-start | bytes 1179652
  1.8 15.1 %collective-permute-start = (bf16[96,1024]{1,0:T(8,128)(2,1)S(1)}, bf16[96,1024]{1,0:T(8,128)(2,1)S(1)}, u32[]{:S(2)}, u32[]{:S(2)}) collective-permute-start(bf16[96,1024]{1,0:T(8,128)(2,1)S(1)} %get-tuple-element.19), channel_id=1, source_target_pairs={{0,256},{16,272},{32,288},{48,304},{64,320},{80,336},{96,352},{112... | collective-permute-start | bytes 589832 | tf_op jit(solution)/shard_map/ppermute | solution.py:22
  5.4 21.6 %collective-permute-start.11 = (bf16[96,2048]{1,0:T(8,128)(2,1)S(1)}, bf16[96,2048]{1,0:T(8,128)(2,1)S(1)}, u32[]{:S(2)}, u32[]{:S(2)}) collective-permute-start(bf16[96,2048]{1,0:T(8,128)(2,1)S(1)} %constant_dynamic-slice_fusion.7), channel_id=1, source_target_pairs={{0,128},{16,144},{32,160},{48,176},{64,192},{80,208},{96,224},{112... | collective-permute-start | bytes 1179656 | tf_op jit(solution)/shard_map/ppermute | solution.py:22
  16.9 12.7 %collective-permute-start.1 = (bf16[192,1024]{1,0:T(8,128)(2,1)S(1)}, bf16[192,1024]{1,0:T(8,128)(2,1)S(1)}, u32[]{:S(2)}, u32[]{:S(2)}) collective-permute-start(bf16[192,1024]{1,0:T(8,128)(2,1)S(1)} %pad_maximum_fusion), channel_id=1, source_target_pairs={{0,16},{16,32},{32,48},{48,64},{64,80},{80,96},{96,112},{112,0},{1... | collective-permute-start | bytes 1179656 | tf_op jit(solution)/shard_map/ppermute | solution.py:27
  21.3 26.9 %collective-permute-start.4 = (bf16[192,1024]{1,0:T(8,128)(2,1)S(1)}, bf16[192,1024]{1,0:T(8,128)(2,1)S(1)}, u32[]{:S(2)}, u32[]{:S(2)}) collective-permute-start(bf16[192,1024]{1,0:T(8,128)(2,1)S(1)} %pad_maximum_fusion), channel_id=1, source_target_pairs={{0,112},{16,0},{32,16},{48,32},{64,48},{80,64},{96,80},{112,96},{1... | collective-permute-start | bytes 1179656 | tf_op jit(solution)/shard_map/ppermute | solution.py:27
  27.0 24.0 %collective-permute-start.12 = (bf16[96,1024]{1,0:T(8,128)(2,1)S(1)}, bf16[96,1024]{1,0:T(8,128)(2,1)S(1)}, u32[]{:S(2)}, u32[]{:S(2)}) collective-permute-start(bf16[96,1024]{1,0:T(8,128)(2,1)S(1)} %get-tuple-element.21), channel_id=1, source_target_pairs={{0,256},{16,272},{32,288},{48,304},{64,320},{80,336},{96,352},{112... | collective-permute-start | bytes 589832 | tf_op jit(solution)/shard_map/ppermute | solution.py:22
  29.6 34.6 %collective-permute-start.2 = (bf16[128,1536]{1,0:T(8,128)(2,1)S(1)}, bf16[128,1536]{1,0:T(8,128)(2,1)S(1)}, u32[]{:S(2)}, u32[]{:S(2)}) collective-permute-start(bf16[128,1536]{1,0:T(8,128)(2,1)S(1)} %copy-done.3), channel_id=1, source_target_pairs={{0,128},{16,144},{32,160},{48,176},{64,192},{80,208},{96,224},{112... | collective-permute-start | bytes 1179656 | tf_op jit(solution)/shard_map/ppermute | solution.py:22
  43.8 13.9 %collective-permute-start.5 = (bf16[192,1024]{1,0:T(8,128)(2,1)S(1)}, bf16[192,1024]{1,0:T(8,128)(2,1)S(1)}, u32[]{:S(2)}, u32[]{:S(2)}) collective-permute-start(bf16[192,1024]{1,0:T(8,128)(2,1)S(1)} %collective-permute-done.1), channel_id=1, source_target_pairs={{0,16},{16,32},{32,48},{48,64},{64,80},{80,96},{96,112},{112,0},{1... | collective-permute-start | bytes 1179656 | tf_op jit(solution)/shard_map/ppermute | solution.py:27
  48.3 14.0 %collective-permute-start.6 = (bf16[192,1024]{1,0:T(8,128)(2,1)S(1)}, bf16[192,1024]{1,0:T(8,128)(2,1)S(1)}, u32[]{:S(2)}, u32[]{:S(2)}) collective-permute-start(bf16[192,1024]{1,0:T(8,128)(2,1)S(1)} %collective-permute-done.4), channel_id=1, source_target_pairs={{0,112},{16,0},{32,16},{48,32},{64,48},{80,64},{96,80},{112,96},{1... | collective-permute-start | bytes 1179656 | tf_op jit(solution)/shard_map/ppermute | solution.py:27
  51.1 16.9 %collective-permute-start.13 = (bf16[192,1024]{1,0:T(8,128)(2,1)S(1)}, bf16[192,1024]{1,0:T(8,128)(2,1)S(1)}, u32[]{:S(2)}, u32[]{:S(2)}) collective-permute-start(bf16[192,1024]{1,0:T(8,128)(2,1)S(1)} %pad_maximum_fusion.1), channel_id=1, source_target_pairs={{0,16},{16,32},{32,48},{48,64},{64,80},{80,96},{96,112},{112,0},{1... | collective-permute-start | bytes 1179656 | tf_op jit(solution)/shard_map/ppermute | solution.py:27
  55.7 17.2 %collective-permute-start.14 = (bf16[192,1024]{1,0:T(8,128)(2,1)S(1)}, bf16[192,1024]{1,0:T(8,128)(2,1)S(1)}, u32[]{:S(2)}, u32[]{:S(2)}) collective-permute-start(bf16[192,1024]{1,0:T(8,128)(2,1)S(1)} %pad_maximum_fusion.1), channel_id=1, source_target_pairs={{0,112},{16,0},{32,16},{48,32},{64,48},{80,64},{96,80},{112,96},{1... | collective-permute-start | bytes 1179656 | tf_op jit(solution)/shard_map/ppermute | solution.py:27
  57.7 17.2 %collective-permute-start.7 = (bf16[192,1024]{1,0:T(8,128)(2,1)S(1)}, bf16[192,1024]{1,0:T(8,128)(2,1)S(1)}, u32[]{:S(2)}, u32[]{:S(2)}) collective-permute-start(bf16[192,1024]{1,0:T(8,128)(2,1)S(1)} %collective-permute-done.5), channel_id=1, source_target_pairs={{0,16},{16,32},{32,48},{48,64},{64,80},{80,96},{96,112},{112,0},{1... | collective-permute-start | bytes 1179656 | tf_op jit(solution)/shard_map/ppermute | solution.py:27
  62.3 16.1 %collective-permute-start.8 = (bf16[192,1024]{1,0:T(8,128)(2,1)S(1)}, bf16[192,1024]{1,0:T(8,128)(2,1)S(1)}, u32[]{:S(2)}, u32[]{:S(2)}) collective-permute-start(bf16[192,1024]{1,0:T(8,128)(2,1)S(1)} %collective-permute-done.6), channel_id=1, source_target_pairs={{0,112},{16,0},{32,16},{48,32},{64,48},{80,64},{96,80},{112,96},{1... | collective-permute-start | bytes 1179656 | tf_op jit(solution)/shard_map/ppermute | solution.py:27
  64.4 45.0 %collective-permute-start.3 = (bf16[256,1536]{1,0:T(8,128)(2,1)S(1)}, bf16[256,1536]{1,0:T(8,128)(2,1)S(1)}, u32[]{:S(2)}, u32[]{:S(2)}) collective-permute-start(bf16[256,1536]{1,0:T(8,128)(2,1)S(1)} %maximum_select_fusion), channel_id=1, source_target_pairs={{0,256},{16,272},{32,288},{48,304},{64,320},{80,336},{96,352},{112... | collective-permute-start | bytes 2359304 | tf_op jit(solution)/shard_map/ppermute | solution.py:22
  68.0 14.8 %collective-permute-start.15 = (bf16[192,1024]{1,0:T(8,128)(2,1)S(1)}, bf16[192,1024]{1,0:T(8,128)(2,1)S(1)}, u32[]{:S(2)}, u32[]{:S(2)}) collective-permute-start(bf16[192,1024]{1,0:T(8,128)(2,1)S(1)} %collective-permute-done.13), channel_id=1, source_target_pairs={{0,16},{16,32},{32,48},{48,64},{64,80},{80,96},{96,112},{112,0},{1... | collective-permute-start | bytes 1179656 | tf_op jit(solution)/shard_map/ppermute | solution.py:27
  72.9 14.3 %collective-permute-start.16 = (bf16[192,1024]{1,0:T(8,128)(2,1)S(1)}, bf16[192,1024]{1,0:T(8,128)(2,1)S(1)}, u32[]{:S(2)}, u32[]{:S(2)}) collective-permute-start(bf16[192,1024]{1,0:T(8,128)(2,1)S(1)} %collective-permute-done.14), channel_id=1, source_target_pairs={{0,112},{16,0},{32,16},{48,32},{64,48},{80,64},{96,80},{112,96},{1... | collective-permute-start | bytes 1179656 | tf_op jit(solution)/shard_map/ppermute | solution.py:27
  74.9 36.5 %collective-permute-start.21 = (bf16[128,1024]{1,0:T(8,128)(2,1)S(1)}, bf16[128,1024]{1,0:T(8,128)(2,1)S(1)}, u32[]{:S(2)}, u32[]{:S(2)}) collective-permute-start(bf16[128,1024]{1,0:T(8,128)(2,1)S(1)} %get-tuple-element.7), channel_id=1, source_target_pairs={{0,128},{16,144},{32,160},{48,176},{64,192},{80,208},{96,224},{112... | collective-permute-start | bytes 786440 | tf_op jit(solution)/shard_map/ppermute | solution.py:22
  78.4 11.0 %collective-permute-start.9 = (bf16[96,1024]{1,0:T(8,128)(2,1)S(1)}, bf16[96,1024]{1,0:T(8,128)(2,1)S(1)}, u32[]{:S(2)}, u32[]{:S(2)}) collective-permute-start(bf16[96,1024]{1,0:T(8,128)(2,1)S(1)} %slice.68), channel_id=1, source_target_pairs={{0,16},{16,32},{32,48},{48,64},{64,80},{80,96},{96,112},{112,0},{1... | collective-permute-start | bytes 589832 | tf_op jit(solution)/shard_map/ppermute | solution.py:27
  82.9 9.6 %collective-permute-start.10 = (bf16[96,1024]{1,0:T(8,128)(2,1)S(1)}, bf16[96,1024]{1,0:T(8,128)(2,1)S(1)}, u32[]{:S(2)}, u32[]{:S(2)}) collective-permute-start(bf16[96,1024]{1,0:T(8,128)(2,1)S(1)} %slice.69), channel_id=1, source_target_pairs={{0,112},{16,0},{32,16},{48,32},{64,48},{80,64},{96,80},{112,96},{1... | collective-permute-start | bytes 589832 | tf_op jit(solution)/shard_map/ppermute | solution.py:27
  87.2 11.5 %collective-permute-start.17 = (bf16[192,1024]{1,0:T(8,128)(2,1)S(1)}, bf16[192,1024]{1,0:T(8,128)(2,1)S(1)}, u32[]{:S(2)}, u32[]{:S(2)}) collective-permute-start(bf16[192,1024]{1,0:T(8,128)(2,1)S(1)} %collective-permute-done.15), channel_id=1, source_target_pairs={{0,16},{16,32},{32,48},{48,64},{64,80},{80,96},{96,112},{112,0},{1... | collective-permute-start | bytes 1179656 | tf_op jit(solution)/shard_map/ppermute | solution.py:27
  89.4 12.3 %collective-permute-start.18 = (bf16[192,1024]{1,0:T(8,128)(2,1)S(1)}, bf16[192,1024]{1,0:T(8,128)(2,1)S(1)}, u32[]{:S(2)}, u32[]{:S(2)}) collective-permute-start(bf16[192,1024]{1,0:T(8,128)(2,1)S(1)} %collective-permute-done.16), channel_id=1, source_target_pairs={{0,112},{16,0},{32,16},{48,32},{64,48},{80,64},{96,80},{112,96},{1... | collective-permute-start | bytes 1179656 | tf_op jit(solution)/shard_map/ppermute | solution.py:27
  98.7 6.4 %collective-permute-start.19 = (bf16[96,1024]{1,0:T(8,128)(2,1)S(1)}, bf16[96,1024]{1,0:T(8,128)(2,1)S(1)}, u32[]{:S(2)}, u32[]{:S(2)}) collective-permute-start(bf16[96,1024]{1,0:T(8,128)(2,1)S(1)} %slice.70), channel_id=1, source_target_pairs={{0,16},{16,32},{32,48},{48,64},{64,80},{80,96},{96,112},{112,0},{1... | collective-permute-start | bytes 589832 | tf_op jit(solution)/shard_map/ppermute | solution.py:27
  101.7 7.6 %collective-permute-start.20 = (bf16[96,1024]{1,0:T(8,128)(2,1)S(1)}, bf16[96,1024]{1,0:T(8,128)(2,1)S(1)}, u32[]{:S(2)}, u32[]{:S(2)}) collective-permute-start(bf16[96,1024]{1,0:T(8,128)(2,1)S(1)} %slice.71), channel_id=1, source_target_pairs={{0,112},{16,0},{32,16},{48,32},{64,48},{80,64},{96,80},{112,96},{1... | collective-permute-start | bytes 589832 | tf_op jit(solution)/shard_map/ppermute | solution.py:27
  109.4 2.6 %copy-start = (bf16[2,2,8,96,1024]{4,3,2,1,0:T(8,128)(2,1)}, bf16[2,2,8,96,1024]{4,3,2,1,0:T(8,128)(2,1)S(1)}, u32[]{:S(2)}) copy-start(bf16[2,2,8,96,1024]{4,3,2,1,0:T(8,128)(2,1)S(1)} %bitcast_dynamic-update-slice_fusion) | copy-start | bytes 18874372
  109.4 9.2 %copy-start.4 = (f32[128]{0:T(128)S(1)}, f32[128]{0:T(128)}, u32[]{:S(2)}) copy-start(f32[128]{0:T(128)} %param.9) | copy-start | bytes 1540
  112.1 6.5 %collective-permute-start.22 = (f32[8,128]{1,0:T(8,128)S(1)}, f32[8,128]{1,0:T(8,128)S(1)}, u32[]{:S(2)}, u32[]{:S(2)}) collective-permute-start(f32[8,128]{1,0:T(8,128)S(1)} %reshape.130), channel_id=1, source_target_pairs={{0,256},{16,272},{32,288},{48,304},{64,320},{80,336},{96,352},{112... | collective-permute-start | bytes 12296 | tf_op jit(solution)/shard_map/ppermute | solution.py:22
  136.8 2.8 %copy-start.1 = (bf16[2,2,8,96,1024]{4,3,2,1,0:T(8,128)(2,1)S(1)}, bf16[2,2,8,96,1024]{4,3,2,1,0:T(8,128)(2,1)}, u32[]{:S(2)}) copy-start(bf16[2,2,8,96,1024]{4,3,2,1,0:T(8,128)(2,1)} %copy-done) | copy-start | bytes 18874372
  139.6 6.6 %copy-start.2 = (bf16[2,2,8,96,1024]{4,3,2,1,0:T(8,128)(2,1)S(1)}, bf16[2,2,8,96,1024]{4,3,2,1,0:T(8,128)(2,1)}, u32[]{:S(2)}) copy-start(bf16[2,2,8,96,1024]{4,3,2,1,0:T(8,128)(2,1)} %copy-done) | copy-start | bytes 18874372
  142.1 6.1 %collective-permute-start.23 = (bf16[2,1536,128]{2,1,0:T(8,128)(2,1)S(1)}, bf16[2,1536,128]{2,1,0:T(8,128)(2,1)S(1)}, u32[]{:S(2)}, u32[]{:S(2)}) collective-permute-start(bf16[2,1536,128]{2,1,0:T(8,128)(2,1)S(1)} %get-tuple-element.9), channel_id=1, source_target_pairs={{0,256},{16,272},{32,288},{48,304},{64,320},{80,336},{96,352},{112... | collective-permute-start | bytes 2359304 | tf_op jit(solution)/shard_map/ppermute | solution.py:22
  149.3 27.5 %all-to-all-start.1 = ((bf16[32,96,128]{2,1,0:T(8,128)(2,1)}), bf16[32,96,128]{2,1,0:T(8,128)(2,1)S(1)}, u32[]{:S(2)}, u32[]{:S(2)}) async-start(bf16[32,96,128]{2,1,0:T(8,128)(2,1)} %bitcast.51), calls=%async_computation.1 | async-start | bytes 1572864 | tf_op jit(solution)/shard_map/all_to_all | solution.py:37

commit v8 on v3

--- a/solution.py
+++ b/solution.py
@@ -1,6 +1,8 @@
 import jax
 import jax.numpy as jnp
 from jax import lax
+from jax.experimental import pallas as pl
+from jax.experimental.pallas import tpu as pltpu
 from jax.sharding import PartitionSpec as P
 
 GROUP = 128
@@ -66,6 +68,50 @@
     return parts
 
 
+TILE = 256
+
+
+def tile_grads(w_ref, logit_grad, g_ref):
+    g = lax.dot_general(
+        w_ref[0], logit_grad, (((1,), (1,)), ((), ())), preferred_element_type=jnp.float32
+    ).astype(g_ref.dtype)
+    tok = g_ref.shape[2]
+    for z in range(NZH):
+        g_ref[z] = g[:, z * tok : (z + 1) * tok]
+
+
+def first_grads_kernel(s_ref, t_ref, row_ref, w_ref, lg_ref, g_ref):
+    @pl.when(pl.program_id(0) == 0)
+    def _():
+        student_lse, teacher_lse, weight = row_ref[:, 0:1], row_ref[:, 1:2], row_ref[:, 2:3]
+        student = jnp.exp(s_ref[...] - student_lse)
+        teacher = jnp.exp(t_ref[...].astype(jnp.float32) - teacher_lse)
+        lg_ref[...] = (weight * TEMP * (student - teacher)).astype(jnp.bfloat16)
+
+    tile_grads(w_ref, lg_ref[...], g_ref)
+
+
+def second_grads_kernel(lg_ref, w_ref, g_ref):
+    tile_grads(w_ref, lg_ref[...], g_ref)
+
+
+def over_tiles(kernel, section, ins, weights, whole_outs, grads):
+    whole = pl.BlockSpec(memory_space=pltpu.VMEM)
+    width = weights.shape[2]
+    zs, feats, tok = grads.shape
+    return pl.pallas_call(
+        kernel,
+        grid=(feats // TILE,),
+        in_specs=[whole] * len(ins) + [pl.BlockSpec((1, TILE, width), lambda k: (section, k, 0))],
+        out_specs=[whole] * len(whole_outs) + [pl.BlockSpec((zs, TILE, tok), lambda k: (0, k, 0))],
+        out_shape=[*whole_outs, grads],
+        compiler_params=pltpu.CompilerParams(vmem_limit_bytes=16 * 2**20),
+        cost_estimate=pl.CostEstimate(
+            flops=10**9, bytes_accessed=5 * 10**6, transcendentals=5 * 10**5
+        ),
+    )(*ins, weights)
+
+
 def on_device(hidden, head, codes, exponents, loss_weight):
     s = lax.axis_index("section")
     dp = lax.axis_index("dp")
@@ -106,18 +152,19 @@
     h_all = jnp.concatenate([h_sec, flip(h_sec, 1, 0)], axis=1)
     teacher = teacher_half(codes, exponents)
     t_send = after(columns(teacher, 0, 1), near_parts[3][2])
-    scaled_t = both(columns(teacher, 0, 0), flip(t_send, 0, 1)).astype(jnp.float32)
+    scaled_t = both(columns(teacher, 0, 0), flip(t_send, 0, 1))
 
     logits = jnp.dot(h_all, weights, preferred_element_type=jnp.float32)
     scaled_s = logits / TEMP
     m = jnp.max(scaled_s, axis=1)
-    t_exp = jnp.exp(scaled_t)
+    t_wide = scaled_t.astype(jnp.float32)
+    t_exp = jnp.exp(t_wide)
     stats = jnp.stack(
         [
             m,
             jnp.sum(jnp.exp(scaled_s - m[:, None]), axis=1),
             jnp.sum(t_exp, axis=1),
-            jnp.sum(t_exp * (scaled_t - scaled_s), axis=1),
+            jnp.sum(t_exp * (t_wide - scaled_s), axis=1),
         ]
     ).reshape(8, tok)
 
@@ -146,18 +193,28 @@
     kl_loss = TEMP * TEMP * kl_loss
 
     student_lse, teacher_lse = student_lse.reshape(2 * tok), teacher_lse.reshape(2 * tok)
-    logit_grad = (
-        weight[:, None]
-        * TEMP
-        * (jnp.exp(scaled_s - student_lse[:, None]) - jnp.exp(scaled_t - teacher_lse[:, None]))
-    ).astype(jnp.bfloat16)
-
-    g = lax.dot_general(
-        weights, logit_grad, (((1,), (1,)), ((), ())), preferred_element_type=jnp.float32
-    ).reshape(2, NQ, rows, 2 * tok)
-    g = g[0] + flip(g[1].astype(jnp.bfloat16), 1, 0).astype(jnp.float32)
-    g = g.astype(jnp.bfloat16).reshape(NQ, rows, 2, tok)
-    g = g.transpose(2, 0, 1, 3).reshape(NZH * NQ, rows, tok)
+    per_row = jnp.stack([student_lse, teacher_lse, weight], axis=1)
+    w = weights.reshape(2, -1, width)
+    feats = w.shape[1]
+    logit_grad, g = over_tiles(
+        first_grads_kernel,
+        1,
+        (scaled_s, scaled_t, per_row),
+        w,
+        [jax.ShapeDtypeStruct(scaled_s.shape, jnp.bfloat16)],
+        jax.ShapeDtypeStruct((NZH, feats, tok), jnp.bfloat16),
+    )
+    theirs = flip(g, 1, 0)
+    (mine,) = over_tiles(
+        second_grads_kernel,
+        0,
+        (logit_grad,),
+        w,
+        [],
+        jax.ShapeDtypeStruct((NZH, feats, tok), jnp.float32),
+    )
+    g = (mine + theirs.astype(jnp.float32)).astype(jnp.bfloat16)
+    g = g.reshape(NZH * NQ, rows, tok)
     g = exchange(g)
     g = jnp.sum(g.astype(jnp.float32), axis=0)
     return (kl_loss, g.T.astype(jnp.bfloat16))

time: 180 us -> 179 us (level)
  matrix products: 7.09 us -> 2 us
  Pallas kernels: 0 us -> 4.69 us
    dot_general x1 -> x0, matrix products: 5.08 us -> none  [on_device(): lax.dot_general(weights, logit_grad, (((1,), (1,)), ((), ())), preferred_...]
    pallas_call x0 -> x2, Pallas kernels: none -> 4.69 us  [over_tiles(): pl.pallas_call(kernel, grid=(feats // TILE,), in_specs=[whole] * len(ins)...]
    unnamed x6 -> x10, local copies, waits for them, and re-layouts: 0.07 us -> 2.82 us
  transfers between devices with their start and end apart: 25 -> 25, of which waited for: 8 -> 7; matrix products, arithmetic and copies ran while one was open for 6% -> 5% of each run, Pallas kernels for 0% -> 1%
where the time goes in v8:
time: 179 us; the launch traced here: 178 us
  starting transfers between devices  99.6 us (56%)
  waiting for transfers between devices  37.5 us (21%)
  blocking collectives  17.8 us (10%)
  local copies, waits for them, and re-layouts  7.43 us (4%)
  other arithmetic  7.04 us (4%)
  Pallas kernels  4.69 us (3%)
  matrix products  2 us (1%)
    ppermute x16, starting transfers between devices, along_y(): return lax.ppermute(x, 'dp', perm)  49.2 us
    ppermute x8, starting transfers between devices, flip(): return lax.ppermute(x, ('section', 'dp'), perm)  46.4 us
    all_to_all x1, waiting for transfers between devices, exchange(): lax.all_to_all(x, ('section', 'dp', 'vocab'), split_axis=0, concat_axis=0...  23 us
    all_to_all x1, blocking collectives, exchange(): lax.all_to_all(x, ('section', 'dp', 'vocab'), split_axis=0, concat_axis=0...  17.8 us
    ppermute x16, waiting for transfers between devices, along_y(): return lax.ppermute(x, 'dp', perm)  13.7 us
    pallas_call x2, Pallas kernels, over_tiles(): pl.pallas_call(kernel, grid=(feats // TILE,), in_specs=[whole] * len(ins)...  4.69 us
    all_to_all x1, starting transfers between devices, exchange(): lax.all_to_all(x, ('section', 'dp', 'vocab'), split_axis=0, concat_axis=0...  3.91 us
  transfers between devices with their start and end apart: 25, of which 7 were waited for; matrix products, arithmetic and copies ran while one was open for 5% of the time, Pallas kernels for 1%

profile of v8, /device:TPU:25, one launch (start us, length us, event | category | flops | bytes accessed | tf_op | source)
XLA Modules:
  0.0 177.6 jit_solution(2679470506329872819)
XLA Ops:
  0.7 1.1 constant_dynamic-slice_fusion.9
  1.8 2.6 %collective-permute-start = (bf16[96,1024]{1,0:T(8,128)(2,1)S(1)}, bf16[96,1024]{1,0:T(8,128)(2,1)S(1)}, u32[]{:S(2)}, u32[]{:S(2)}) collective-permute-start(bf16[96,1024]{1,0:T(8,128)(2,1)S(1)} %get-tuple-element.19), channel_id=1, source_target_pairs={{0,256},{16,272},{32,288},{48,304},{64,320},{80,336},{96,352},{112... | collective-permute-start | bytes 589832 | tf_op jit(solution)/shard_map/ppermute | solution.py:22
  4.4 1.0 constant_dynamic-slice_fusion.7
  5.4 10.6 %collective-permute-start.11 = (bf16[96,2048]{1,0:T(8,128)(2,1)S(1)}, bf16[96,2048]{1,0:T(8,128)(2,1)S(1)}, u32[]{:S(2)}, u32[]{:S(2)}) collective-permute-start(bf16[96,2048]{1,0:T(8,128)(2,1)S(1)} %constant_dynamic-slice_fusion.7), channel_id=1, source_target_pairs={{0,128},{16,144},{32,160},{48,176},{64,192},{80,208},{96,224},{112... | collective-permute-start | bytes 1179656 | tf_op jit(solution)/shard_map/ppermute | solution.py:22
  16.0 0.7 exponential_multiply_fusion
  16.9 4.4 %collective-permute-start.1 = (bf16[192,1024]{1,0:T(8,128)(2,1)S(1)}, bf16[192,1024]{1,0:T(8,128)(2,1)S(1)}, u32[]{:S(2)}, u32[]{:S(2)}) collective-permute-start(bf16[192,1024]{1,0:T(8,128)(2,1)S(1)} %pad_maximum_fusion), channel_id=1, source_target_pairs={{0,16},{16,32},{32,48},{48,64},{64,80},{80,96},{96,112},{112,0},{1... | collective-permute-start | bytes 1179656 | tf_op jit(solution)/shard_map/ppermute | solution.py:27
  21.3 1.9 %collective-permute-start.4 = (bf16[192,1024]{1,0:T(8,128)(2,1)S(1)}, bf16[192,1024]{1,0:T(8,128)(2,1)S(1)}, u32[]{:S(2)}, u32[]{:S(2)}) collective-permute-start(bf16[192,1024]{1,0:T(8,128)(2,1)S(1)} %pad_maximum_fusion), channel_id=1, source_target_pairs={{0,112},{16,0},{32,16},{48,32},{64,48},{80,64},{96,80},{112,96},{1... | collective-permute-start | bytes 1179656 | tf_op jit(solution)/shard_map/ppermute | solution.py:27
  23.3 0.6 mul.60
  23.9 2.9 %fusion = bf16[128,4096]{1,0:T(8,128)(2,1)S(1)} fusion(f32[16,8,32,128]{3,2,1,0:T(8,128)S(1)} %bitcast.103, s32[128,4096]{1,0:T(8,128)} %param.7), kind=kLoop, calls=%fused_computation.1 | loop fusion | flops 1572864 | bytes 5242880 | tf_op jit(solution)/shard_map/convert_element_type | solution.py:51
  27.0 2.5 %collective-permute-start.12 = (bf16[96,1024]{1,0:T(8,128)(2,1)S(1)}, bf16[96,1024]{1,0:T(8,128)(2,1)S(1)}, u32[]{:S(2)}, u32[]{:S(2)}) collective-permute-start(bf16[96,1024]{1,0:T(8,128)(2,1)S(1)} %get-tuple-element.21), channel_id=1, source_target_pairs={{0,256},{16,272},{32,288},{48,304},{64,320},{80,336},{96,352},{112... | collective-permute-start | bytes 589832 | tf_op jit(solution)/shard_map/ppermute | solution.py:22
  29.6 14.2 %collective-permute-start.2 = (bf16[128,1536]{1,0:T(8,128)(2,1)S(1)}, bf16[128,1536]{1,0:T(8,128)(2,1)S(1)}, u32[]{:S(2)}, u32[]{:S(2)}) collective-permute-start(bf16[128,1536]{1,0:T(8,128)(2,1)S(1)} %copy-done.3), channel_id=1, source_target_pairs={{0,128},{16,144},{32,160},{48,176},{64,192},{80,208},{96,224},{112... | collective-permute-start | bytes 1179656 | tf_op jit(solution)/shard_map/ppermute | solution.py:22
  43.8 4.4 %collective-permute-start.5 = (bf16[192,1024]{1,0:T(8,128)(2,1)S(1)}, bf16[192,1024]{1,0:T(8,128)(2,1)S(1)}, u32[]{:S(2)}, u32[]{:S(2)}) collective-permute-start(bf16[192,1024]{1,0:T(8,128)(2,1)S(1)} %collective-permute-done.1), channel_id=1, source_target_pairs={{0,16},{16,32},{32,48},{48,64},{64,80},{80,96},{96,112},{112,0},{1... | collective-permute-start | bytes 1179656 | tf_op jit(solution)/shard_map/ppermute | solution.py:27
  48.3 1.9 %collective-permute-start.6 = (bf16[192,1024]{1,0:T(8,128)(2,1)S(1)}, bf16[192,1024]{1,0:T(8,128)(2,1)S(1)}, u32[]{:S(2)}, u32[]{:S(2)}) collective-permute-start(bf16[192,1024]{1,0:T(8,128)(2,1)S(1)} %collective-permute-done.4), channel_id=1, source_target_pairs={{0,112},{16,0},{32,16},{48,32},{64,48},{80,64},{96,80},{112,96},{1... | collective-permute-start | bytes 1179656 | tf_op jit(solution)/shard_map/ppermute | solution.py:27
  50.2 0.8 broadcast_in_dim.6
  51.1 4.6 %collective-permute-start.13 = (bf16[192,1024]{1,0:T(8,128)(2,1)S(1)}, bf16[192,1024]{1,0:T(8,128)(2,1)S(1)}, u32[]{:S(2)}, u32[]{:S(2)}) collective-permute-start(bf16[192,1024]{1,0:T(8,128)(2,1)S(1)} %pad_maximum_fusion.1), channel_id=1, source_target_pairs={{0,16},{16,32},{32,48},{48,64},{64,80},{80,96},{96,112},{112,0},{1... | collective-permute-start | bytes 1179656 | tf_op jit(solution)/shard_map/ppermute | solution.py:27
  55.7 1.9 %collective-permute-start.14 = (bf16[192,1024]{1,0:T(8,128)(2,1)S(1)}, bf16[192,1024]{1,0:T(8,128)(2,1)S(1)}, u32[]{:S(2)}, u32[]{:S(2)}) collective-permute-start(bf16[192,1024]{1,0:T(8,128)(2,1)S(1)} %pad_maximum_fusion.1), channel_id=1, source_target_pairs={{0,112},{16,0},{32,16},{48,32},{64,48},{80,64},{96,80},{112,96},{1... | collective-permute-start | bytes 1179656 | tf_op jit(solution)/shard_map/ppermute | solution.py:27
  57.7 4.6 %collective-permute-start.7 = (bf16[192,1024]{1,0:T(8,128)(2,1)S(1)}, bf16[192,1024]{1,0:T(8,128)(2,1)S(1)}, u32[]{:S(2)}, u32[]{:S(2)}) collective-permute-start(bf16[192,1024]{1,0:T(8,128)(2,1)S(1)} %collective-permute-done.5), channel_id=1, source_target_pairs={{0,16},{16,32},{32,48},{48,64},{64,80},{80,96},{96,112},{112,0},{1... | collective-permute-start | bytes 1179656 | tf_op jit(solution)/shard_map/ppermute | solution.py:27
  62.3 1.9 %collective-permute-start.8 = (bf16[192,1024]{1,0:T(8,128)(2,1)S(1)}, bf16[192,1024]{1,0:T(8,128)(2,1)S(1)}, u32[]{:S(2)}, u32[]{:S(2)}) collective-permute-start(bf16[192,1024]{1,0:T(8,128)(2,1)S(1)} %collective-permute-done.6), channel_id=1, source_target_pairs={{0,112},{16,0},{32,16},{48,32},{64,48},{80,64},{96,80},{112,96},{1... | collective-permute-start | bytes 1179656 | tf_op jit(solution)/shard_map/ppermute | solution.py:27
  64.2 0.2 maximum_select_fusion
  64.4 3.6 %collective-permute-start.3 = (bf16[256,1536]{1,0:T(8,128)(2,1)S(1)}, bf16[256,1536]{1,0:T(8,128)(2,1)S(1)}, u32[]{:S(2)}, u32[]{:S(2)}) collective-permute-start(bf16[256,1536]{1,0:T(8,128)(2,1)S(1)} %maximum_select_fusion), channel_id=1, source_target_pairs={{0,256},{16,272},{32,288},{48,304},{64,320},{80,336},{96,352},{112... | collective-permute-start | bytes 2359304 | tf_op jit(solution)/shard_map/ppermute | solution.py:22
  68.0 4.9 %collective-permute-start.15 = (bf16[192,1024]{1,0:T(8,128)(2,1)S(1)}, bf16[192,1024]{1,0:T(8,128)(2,1)S(1)}, u32[]{:S(2)}, u32[]{:S(2)}) collective-permute-start(bf16[192,1024]{1,0:T(8,128)(2,1)S(1)} %collective-permute-done.13), channel_id=1, source_target_pairs={{0,16},{16,32},{32,48},{48,64},{64,80},{80,96},{96,112},{112,0},{1... | collective-permute-start | bytes 1179656 | tf_op jit(solution)/shard_map/ppermute | solution.py:27
  72.9 1.9 %collective-permute-start.16 = (bf16[192,1024]{1,0:T(8,128)(2,1)S(1)}, bf16[192,1024]{1,0:T(8,128)(2,1)S(1)}, u32[]{:S(2)}, u32[]{:S(2)}) collective-permute-start(bf16[192,1024]{1,0:T(8,128)(2,1)S(1)} %collective-permute-done.14), channel_id=1, source_target_pairs={{0,112},{16,0},{32,16},{48,32},{64,48},{80,64},{96,80},{112,96},{1... | collective-permute-start | bytes 1179656 | tf_op jit(solution)/shard_map/ppermute | solution.py:27
  74.9 3.2 %collective-permute-start.21 = (bf16[128,1024]{1,0:T(8,128)(2,1)S(1)}, bf16[128,1024]{1,0:T(8,128)(2,1)S(1)}, u32[]{:S(2)}, u32[]{:S(2)}) collective-permute-start(bf16[128,1024]{1,0:T(8,128)(2,1)S(1)} %get-tuple-element.7), channel_id=1, source_target_pairs={{0,128},{16,144},{32,160},{48,176},{64,192},{80,208},{96,224},{112... | collective-permute-start | bytes 786440 | tf_op jit(solution)/shard_map/ppermute | solution.py:22
  78.2 0.2 collective-permute-done.8
  78.4 4.3 %collective-permute-start.9 = (bf16[96,1024]{1,0:T(8,128)(2,1)S(1)}, bf16[96,1024]{1,0:T(8,128)(2,1)S(1)}, u32[]{:S(2)}, u32[]{:S(2)}) collective-permute-start(bf16[96,1024]{1,0:T(8,128)(2,1)S(1)} %slice.68), channel_id=1, source_target_pairs={{0,16},{16,32},{32,48},{48,64},{64,80},{80,96},{96,112},{112,0},{1... | collective-permute-start | bytes 589832 | tf_op jit(solution)/shard_map/ppermute | solution.py:27
  82.9 1.9 %collective-permute-start.10 = (bf16[96,1024]{1,0:T(8,128)(2,1)S(1)}, bf16[96,1024]{1,0:T(8,128)(2,1)S(1)}, u32[]{:S(2)}, u32[]{:S(2)}) collective-permute-start(bf16[96,1024]{1,0:T(8,128)(2,1)S(1)} %slice.69), channel_id=1, source_target_pairs={{0,112},{16,0},{32,16},{48,32},{64,48},{80,64},{96,80},{112,96},{1... | collective-permute-start | bytes 589832 | tf_op jit(solution)/shard_map/ppermute | solution.py:27
  84.8 2.4 %collective-permute-done.16 = bf16[192,1024]{1,0:T(8,128)(2,1)S(1)} collective-permute-done((bf16[192,1024]{1,0:T(8,128)(2,1)S(1)}, bf16[192,1024]{1,0:T(8,128)(2,1)S(1)}, u32[]{:S(2)}, u32[]{:S(2)}) %collective-permute-start.16) | collective-permute-done | bytes 393248 | tf_op jit(solution)/shard_map/ppermute | solution.py:27
  87.2 2.2 %collective-permute-start.17 = (bf16[192,1024]{1,0:T(8,128)(2,1)S(1)}, bf16[192,1024]{1,0:T(8,128)(2,1)S(1)}, u32[]{:S(2)}, u32[]{:S(2)}) collective-permute-start(bf16[192,1024]{1,0:T(8,128)(2,1)S(1)} %collective-permute-done.15), channel_id=1, source_target_pairs={{0,16},{16,32},{32,48},{48,64},{64,80},{80,96},{96,112},{112,0},{1... | collective-permute-start | bytes 1179656 | tf_op jit(solution)/shard_map/ppermute | solution.py:27
  89.4 3.1 %collective-permute-start.18 = (bf16[192,1024]{1,0:T(8,128)(2,1)S(1)}, bf16[192,1024]{1,0:T(8,128)(2,1)S(1)}, u32[]{:S(2)}, u32[]{:S(2)}) collective-permute-start(bf16[192,1024]{1,0:T(8,128)(2,1)S(1)} %collective-permute-done.16), channel_id=1, source_target_pairs={{0,112},{16,0},{32,16},{48,32},{64,48},{80,64},{96,80},{112,96},{1... | collective-permute-start | bytes 1179656 | tf_op jit(solution)/shard_map/ppermute | solution.py:27
  92.8 5.9 %collective-permute-done.17 = bf16[192,1024]{1,0:T(8,128)(2,1)S(1)} collective-permute-done((bf16[192,1024]{1,0:T(8,128)(2,1)S(1)}, bf16[192,1024]{1,0:T(8,128)(2,1)S(1)}, u32[]{:S(2)}, u32[]{:S(2)}) %collective-permute-start.17) | collective-permute-done | bytes 393248 | tf_op jit(solution)/shard_map/ppermute | solution.py:27
  98.7 3.0 %collective-permute-start.19 = (bf16[96,1024]{1,0:T(8,128)(2,1)S(1)}, bf16[96,1024]{1,0:T(8,128)(2,1)S(1)}, u32[]{:S(2)}, u32[]{:S(2)}) collective-permute-start(bf16[96,1024]{1,0:T(8,128)(2,1)S(1)} %slice.70), channel_id=1, source_target_pairs={{0,16},{16,32},{32,48},{48,64},{64,80},{80,96},{96,112},{112,0},{1... | collective-permute-start | bytes 589832 | tf_op jit(solution)/shard_map/ppermute | solution.py:27
  101.7 2.3 %collective-permute-start.20 = (bf16[96,1024]{1,0:T(8,128)(2,1)S(1)}, bf16[96,1024]{1,0:T(8,128)(2,1)S(1)}, u32[]{:S(2)}, u32[]{:S(2)}) collective-permute-start(bf16[96,1024]{1,0:T(8,128)(2,1)S(1)} %slice.71), channel_id=1, source_target_pairs={{0,112},{16,0},{32,16},{48,32},{64,48},{80,64},{96,80},{112,96},{1... | collective-permute-start | bytes 589832 | tf_op jit(solution)/shard_map/ppermute | solution.py:27
  104.2 1.0 collective-permute-done.19
  105.2 4.2 %collective-permute-done.20 = bf16[96,1024]{1,0:T(8,128)(2,1)S(1)} collective-permute-done((bf16[96,1024]{1,0:T(8,128)(2,1)S(1)}, bf16[96,1024]{1,0:T(8,128)(2,1)S(1)}, u32[]{:S(2)}, u32[]{:S(2)}) %collective-permute-start.20) | collective-permute-done | bytes 196640 | tf_op jit(solution)/shard_map/ppermute | solution.py:27
  109.4 2.0 %fusion.23 = (f32[256]{0:T(256)S(1)}, f32[256,1024]{1,0:T(8,128)S(1)}) fusion(bf16[3072,1024]{1,0:T(8,128)(2,1)S(1)} %bitcast.100, bf16[256,1536]{1,0:T(8,128)(2,1)S(1)} %collective-permute-done.3, bf16[256,1536]{1,0:T(8,128)(2,1)S(1)} %maximum_select_fusion), kind=kOutput, calls=%fused_computation.74 | convolution fusion | flops 1614282496 | bytes 8913920 | tf_op jit(solution)/shard_map/dot_general | solution.py:157
  111.4 0.6 exponential_reduce_fusion
  112.1 5.7 %collective-permute-start.22 = (f32[8,128]{1,0:T(8,128)S(1)}, f32[8,128]{1,0:T(8,128)S(1)}, u32[]{:S(2)}, u32[]{:S(2)}) collective-permute-start(f32[8,128]{1,0:T(8,128)S(1)} %reshape.130), channel_id=1, source_target_pairs={{0,256},{16,272},{32,288},{48,304},{64,320},{80,336},{96,352},{112... | collective-permute-start | bytes 12296 | tf_op jit(solution)/shard_map/ppermute | solution.py:22
  117.7 0.8 collective-permute-done.22
  118.7 17.8 %all_to_all.10 = f32[32,8,128]{2,1,0:T(8,128)S(1)} all-to-all(f32[32,8,128]{2,1,0:T(8,128)S(1)} %bitcast.110), channel_id=1, replica_groups={{0,1,2,3,4,5,6,7,8,9,10,11,12,13,14,15,128,129,130,131,132,133,134,135,..., dimensions={0} | all-to-all | bytes 262144 | tf_op jit(solution)/shard_map/all_to_all | solution.py:37
  136.8 2.8 %copy-done.1 = bf16[2,2,8,96,1024]{4,3,2,1,0:T(8,128)(2,1)S(1)} copy-done((bf16[2,2,8,96,1024]{4,3,2,1,0:T(8,128)(2,1)S(1)}, bf16[2,2,8,96,1024]{4,3,2,1,0:T(8,128)(2,1)}, u32[]{:S(2)}) %copy-start.1) | copy-done | bytes 6291480
  139.6 2.6 %shard_map.68 = (bf16[256,1024]{1,0:T(8,128)(2,1)S(1)}, bf16[2,1536,128]{2,1,0:T(8,128)(2,1)S(1)}) custom-call(f32[256,1024]{1,0:T(8,128)S(1)} %get-tuple-element.25.s_ref, bf16[256,1024]{1,0:T(8,128)(2,1)S(1)} %get-tuple-element.15.t_ref, f32[256,3]{1,0:T(8,128)S(1)} %copy.71.row_ref, bf16[2,1536,1024]{2,1,0:T(8,128)(2,1)S(1)} %bitcast.101), custom_call_target="tpu_custom_call" | custom-call | flops 1000000000 | bytes 5000000 | tf_op jit(solution)/shard_map/pallas_call | solution.py:102
  142.2 4.0 %collective-permute-start.23 = (bf16[2,1536,128]{2,1,0:T(8,128)(2,1)S(1)}, bf16[2,1536,128]{2,1,0:T(8,128)(2,1)S(1)}, u32[]{:S(2)}, u32[]{:S(2)}) collective-permute-start(bf16[2,1536,128]{2,1,0:T(8,128)(2,1)S(1)} %get-tuple-element.9), channel_id=1, source_target_pairs={{0,256},{16,272},{32,288},{48,304},{64,320},{80,336},{96,352},{112... | collective-permute-start | bytes 2359304 | tf_op jit(solution)/shard_map/ppermute | solution.py:22
  146.2 2.1 %shard_map.69 = f32[2,1536,128]{2,1,0:T(8,128)S(1)} custom-call(bf16[256,1024]{1,0:T(8,128)(2,1)S(1)} %get-tuple-element.8.lg_ref, bf16[2,1536,1024]{2,1,0:T(8,128)(2,1)S(1)} %bitcast.102), custom_call_target="tpu_custom_call" | custom-call | flops 1000000000 | bytes 5000000 | tf_op jit(solution)/shard_map/pallas_call | solution.py:102
  148.4 1.1 add_convert_fusion
  149.4 3.9 %all-to-all-start.1 = ((bf16[32,96,128]{2,1,0:T(8,128)(2,1)}), bf16[32,96,128]{2,1,0:T(8,128)(2,1)S(1)}, u32[]{:S(2)}, u32[]{:S(2)}) async-start(bf16[32,96,128]{2,1,0:T(8,128)(2,1)} %bitcast.51), calls=%async_computation.1 | async-start | bytes 1572864 | tf_op jit(solution)/shard_map/all_to_all | solution.py:37
  153.4 0.5 fusion.20
  153.9 23.0 %all-to-all-done.1 = bf16[32,96,128]{2,1,0:T(8,128)(2,1)S(1)} async-done(((bf16[32,96,128]{2,1,0:T(8,128)(2,1)}), bf16[32,96,128]{2,1,0:T(8,128)(2,1)S(1)}, u32[]{:S(2)}, u32[]{:S(2)}) %all-to-all-start.1) | async-done | bytes 786464 | tf_op jit(solution)/shard_map/all_to_all | solution.py:37
  176.9 0.7 reduce_sum.92
  (75 shorter events, 1.5 us)
Async XLA Ops:
  0.6 29.0 %copy-start.3 = (bf16[128,1536]{1,0:T(8,128)(2,1)S(1)}, bf16[128,1536]{1,0:T(8,128)(2,1)}, u32[]{:S(2)}) copy-start(bf16[128,1536]{1,0:T(8,128)(2,1)} %param.5) | copy-start | bytes 1179652
  1.8 15.1 %collective-permute-start = (bf16[96,1024]{1,0:T(8,128)(2,1)S(1)}, bf16[96,1024]{1,0:T(8,128)(2,1)S(1)}, u32[]{:S(2)}, u32[]{:S(2)}) collective-permute-start(bf16[96,1024]{1,0:T(8,128)(2,1)S(1)} %get-tuple-element.19), channel_id=1, source_target_pairs={{0,256},{16,272},{32,288},{48,304},{64,320},{80,336},{96,352},{112... | collective-permute-start | bytes 589832 | tf_op jit(solution)/shard_map/ppermute | solution.py:22
  5.4 21.6 %collective-permute-start.11 = (bf16[96,2048]{1,0:T(8,128)(2,1)S(1)}, bf16[96,2048]{1,0:T(8,128)(2,1)S(1)}, u32[]{:S(2)}, u32[]{:S(2)}) collective-permute-start(bf16[96,2048]{1,0:T(8,128)(2,1)S(1)} %constant_dynamic-slice_fusion.7), channel_id=1, source_target_pairs={{0,128},{16,144},{32,160},{48,176},{64,192},{80,208},{96,224},{112... | collective-permute-start | bytes 1179656 | tf_op jit(solution)/shard_map/ppermute | solution.py:22
  16.9 12.7 %collective-permute-start.1 = (bf16[192,1024]{1,0:T(8,128)(2,1)S(1)}, bf16[192,1024]{1,0:T(8,128)(2,1)S(1)}, u32[]{:S(2)}, u32[]{:S(2)}) collective-permute-start(bf16[192,1024]{1,0:T(8,128)(2,1)S(1)} %pad_maximum_fusion), channel_id=1, source_target_pairs={{0,16},{16,32},{32,48},{48,64},{64,80},{80,96},{96,112},{112,0},{1... | collective-permute-start | bytes 1179656 | tf_op jit(solution)/shard_map/ppermute | solution.py:27
  21.3 26.9 %collective-permute-start.4 = (bf16[192,1024]{1,0:T(8,128)(2,1)S(1)}, bf16[192,1024]{1,0:T(8,128)(2,1)S(1)}, u32[]{:S(2)}, u32[]{:S(2)}) collective-permute-start(bf16[192,1024]{1,0:T(8,128)(2,1)S(1)} %pad_maximum_fusion), channel_id=1, source_target_pairs={{0,112},{16,0},{32,16},{48,32},{64,48},{80,64},{96,80},{112,96},{1... | collective-permute-start | bytes 1179656 | tf_op jit(solution)/shard_map/ppermute | solution.py:27
  27.0 24.0 %collective-permute-start.12 = (bf16[96,1024]{1,0:T(8,128)(2,1)S(1)}, bf16[96,1024]{1,0:T(8,128)(2,1)S(1)}, u32[]{:S(2)}, u32[]{:S(2)}) collective-permute-start(bf16[96,1024]{1,0:T(8,128)(2,1)S(1)} %get-tuple-element.21), channel_id=1, source_target_pairs={{0,256},{16,272},{32,288},{48,304},{64,320},{80,336},{96,352},{112... | collective-permute-start | bytes 589832 | tf_op jit(solution)/shard_map/ppermute | solution.py:22
  29.6 34.6 %collective-permute-start.2 = (bf16[128,1536]{1,0:T(8,128)(2,1)S(1)}, bf16[128,1536]{1,0:T(8,128)(2,1)S(1)}, u32[]{:S(2)}, u32[]{:S(2)}) collective-permute-start(bf16[128,1536]{1,0:T(8,128)(2,1)S(1)} %copy-done.3), channel_id=1, source_target_pairs={{0,128},{16,144},{32,160},{48,176},{64,192},{80,208},{96,224},{112... | collective-permute-start | bytes 1179656 | tf_op jit(solution)/shard_map/ppermute | solution.py:22
  43.8 13.9 %collective-permute-start.5 = (bf16[192,1024]{1,0:T(8,128)(2,1)S(1)}, bf16[192,1024]{1,0:T(8,128)(2,1)S(1)}, u32[]{:S(2)}, u32[]{:S(2)}) collective-permute-start(bf16[192,1024]{1,0:T(8,128)(2,1)S(1)} %collective-permute-done.1), channel_id=1, source_target_pairs={{0,16},{16,32},{32,48},{48,64},{64,80},{80,96},{96,112},{112,0},{1... | collective-permute-start | bytes 1179656 | tf_op jit(solution)/shard_map/ppermute | solution.py:27
  48.3 14.0 %collective-permute-start.6 = (bf16[192,1024]{1,0:T(8,128)(2,1)S(1)}, bf16[192,1024]{1,0:T(8,128)(2,1)S(1)}, u32[]{:S(2)}, u32[]{:S(2)}) collective-permute-start(bf16[192,1024]{1,0:T(8,128)(2,1)S(1)} %collective-permute-done.4), channel_id=1, source_target_pairs={{0,112},{16,0},{32,16},{48,32},{64,48},{80,64},{96,80},{112,96},{1... | collective-permute-start | bytes 1179656 | tf_op jit(solution)/shard_map/ppermute | solution.py:27
  51.1 16.9 %collective-permute-start.13 = (bf16[192,1024]{1,0:T(8,128)(2,1)S(1)}, bf16[192,1024]{1,0:T(8,128)(2,1)S(1)}, u32[]{:S(2)}, u32[]{:S(2)}) collective-permute-start(bf16[192,1024]{1,0:T(8,128)(2,1)S(1)} %pad_maximum_fusion.1), channel_id=1, source_target_pairs={{0,16},{16,32},{32,48},{48,64},{64,80},{80,96},{96,112},{112,0},{1... | collective-permute-start | bytes 1179656 | tf_op jit(solution)/shard_map/ppermute | solution.py:27
  55.7 17.2 %collective-permute-start.14 = (bf16[192,1024]{1,0:T(8,128)(2,1)S(1)}, bf16[192,1024]{1,0:T(8,128)(2,1)S(1)}, u32[]{:S(2)}, u32[]{:S(2)}) collective-permute-start(bf16[192,1024]{1,0:T(8,128)(2,1)S(1)} %pad_maximum_fusion.1), channel_id=1, source_target_pairs={{0,112},{16,0},{32,16},{48,32},{64,48},{80,64},{96,80},{112,96},{1... | collective-permute-start | bytes 1179656 | tf_op jit(solution)/shard_map/ppermute | solution.py:27
  57.7 17.2 %collective-permute-start.7 = (bf16[192,1024]{1,0:T(8,128)(2,1)S(1)}, bf16[192,1024]{1,0:T(8,128)(2,1)S(1)}, u32[]{:S(2)}, u32[]{:S(2)}) collective-permute-start(bf16[192,1024]{1,0:T(8,128)(2,1)S(1)} %collective-permute-done.5), channel_id=1, source_target_pairs={{0,16},{16,32},{32,48},{48,64},{64,80},{80,96},{96,112},{112,0},{1... | collective-permute-start | bytes 1179656 | tf_op jit(solution)/shard_map/ppermute | solution.py:27
  62.3 16.1 %collective-permute-start.8 = (bf16[192,1024]{1,0:T(8,128)(2,1)S(1)}, bf16[192,1024]{1,0:T(8,128)(2,1)S(1)}, u32[]{:S(2)}, u32[]{:S(2)}) collective-permute-start(bf16[192,1024]{1,0:T(8,128)(2,1)S(1)} %collective-permute-done.6), channel_id=1, source_target_pairs={{0,112},{16,0},{32,16},{48,32},{64,48},{80,64},{96,80},{112,96},{1... | collective-permute-start | bytes 1179656 | tf_op jit(solution)/shard_map/ppermute | solution.py:27
  64.4 45.0 %collective-permute-start.3 = (bf16[256,1536]{1,0:T(8,128)(2,1)S(1)}, bf16[256,1536]{1,0:T(8,128)(2,1)S(1)}, u32[]{:S(2)}, u32[]{:S(2)}) collective-permute-start(bf16[256,1536]{1,0:T(8,128)(2,1)S(1)} %maximum_select_fusion), channel_id=1, source_target_pairs={{0,256},{16,272},{32,288},{48,304},{64,320},{80,336},{96,352},{112... | collective-permute-start | bytes 2359304 | tf_op jit(solution)/shard_map/ppermute | solution.py:22
  68.0 14.8 %collective-permute-start.15 = (bf16[192,1024]{1,0:T(8,128)(2,1)S(1)}, bf16[192,1024]{1,0:T(8,128)(2,1)S(1)}, u32[]{:S(2)}, u32[]{:S(2)}) collective-permute-start(bf16[192,1024]{1,0:T(8,128)(2,1)S(1)} %collective-permute-done.13), channel_id=1, source_target_pairs={{0,16},{16,32},{32,48},{48,64},{64,80},{80,96},{96,112},{112,0},{1... | collective-permute-start | bytes 1179656 | tf_op jit(solution)/shard_map/ppermute | solution.py:27
  72.9 14.3 %collective-permute-start.16 = (bf16[192,1024]{1,0:T(8,128)(2,1)S(1)}, bf16[192,1024]{1,0:T(8,128)(2,1)S(1)}, u32[]{:S(2)}, u32[]{:S(2)}) collective-permute-start(bf16[192,1024]{1,0:T(8,128)(2,1)S(1)} %collective-permute-done.14), channel_id=1, source_target_pairs={{0,112},{16,0},{32,16},{48,32},{64,48},{80,64},{96,80},{112,96},{1... | collective-permute-start | bytes 1179656 | tf_op jit(solution)/shard_map/ppermute | solution.py:27
  74.9 36.5 %collective-permute-start.21 = (bf16[128,1024]{1,0:T(8,128)(2,1)S(1)}, bf16[128,1024]{1,0:T(8,128)(2,1)S(1)}, u32[]{:S(2)}, u32[]{:S(2)}) collective-permute-start(bf16[128,1024]{1,0:T(8,128)(2,1)S(1)} %get-tuple-element.7), channel_id=1, source_target_pairs={{0,128},{16,144},{32,160},{48,176},{64,192},{80,208},{96,224},{112... | collective-permute-start | bytes 786440 | tf_op jit(solution)/shard_map/ppermute | solution.py:22
  78.4 11.0 %collective-permute-start.9 = (bf16[96,1024]{1,0:T(8,128)(2,1)S(1)}, bf16[96,1024]{1,0:T(8,128)(2,1)S(1)}, u32[]{:S(2)}, u32[]{:S(2)}) collective-permute-start(bf16[96,1024]{1,0:T(8,128)(2,1)S(1)} %slice.68), channel_id=1, source_target_pairs={{0,16},{16,32},{32,48},{48,64},{64,80},{80,96},{96,112},{112,0},{1... | collective-permute-start | bytes 589832 | tf_op jit(solution)/shard_map/ppermute | solution.py:27
  82.9 9.6 %collective-permute-start.10 = (bf16[96,1024]{1,0:T(8,128)(2,1)S(1)}, bf16[96,1024]{1,0:T(8,128)(2,1)S(1)}, u32[]{:S(2)}, u32[]{:S(2)}) collective-permute-start(bf16[96,1024]{1,0:T(8,128)(2,1)S(1)} %slice.69), channel_id=1, source_target_pairs={{0,112},{16,0},{32,16},{48,32},{64,48},{80,64},{96,80},{112,96},{1... | collective-permute-start | bytes 589832 | tf_op jit(solution)/shard_map/ppermute | solution.py:27
  87.2 11.5 %collective-permute-start.17 = (bf16[192,1024]{1,0:T(8,128)(2,1)S(1)}, bf16[192,1024]{1,0:T(8,128)(2,1)S(1)}, u32[]{:S(2)}, u32[]{:S(2)}) collective-permute-start(bf16[192,1024]{1,0:T(8,128)(2,1)S(1)} %collective-permute-done.15), channel_id=1, source_target_pairs={{0,16},{16,32},{32,48},{48,64},{64,80},{80,96},{96,112},{112,0},{1... | collective-permute-start | bytes 1179656 | tf_op jit(solution)/shard_map/ppermute | solution.py:27
  89.4 12.3 %collective-permute-start.18 = (bf16[192,1024]{1,0:T(8,128)(2,1)S(1)}, bf16[192,1024]{1,0:T(8,128)(2,1)S(1)}, u32[]{:S(2)}, u32[]{:S(2)}) collective-permute-start(bf16[192,1024]{1,0:T(8,128)(2,1)S(1)} %collective-permute-done.16), channel_id=1, source_target_pairs={{0,112},{16,0},{32,16},{48,32},{64,48},{80,64},{96,80},{112,96},{1... | collective-permute-start | bytes 1179656 | tf_op jit(solution)/shard_map/ppermute | solution.py:27
  98.7 6.4 %collective-permute-start.19 = (bf16[96,1024]{1,0:T(8,128)(2,1)S(1)}, bf16[96,1024]{1,0:T(8,128)(2,1)S(1)}, u32[]{:S(2)}, u32[]{:S(2)}) collective-permute-start(bf16[96,1024]{1,0:T(8,128)(2,1)S(1)} %slice.70), channel_id=1, source_target_pairs={{0,16},{16,32},{32,48},{48,64},{64,80},{80,96},{96,112},{112,0},{1... | collective-permute-start | bytes 589832 | tf_op jit(solution)/shard_map/ppermute | solution.py:27
  101.7 7.6 %collective-permute-start.20 = (bf16[96,1024]{1,0:T(8,128)(2,1)S(1)}, bf16[96,1024]{1,0:T(8,128)(2,1)S(1)}, u32[]{:S(2)}, u32[]{:S(2)}) collective-permute-start(bf16[96,1024]{1,0:T(8,128)(2,1)S(1)} %slice.71), channel_id=1, source_target_pairs={{0,112},{16,0},{32,16},{48,32},{64,48},{80,64},{96,80},{112,96},{1... | collective-permute-start | bytes 589832 | tf_op jit(solution)/shard_map/ppermute | solution.py:27
  109.4 2.6 %copy-start = (bf16[2,2,8,96,1024]{4,3,2,1,0:T(8,128)(2,1)}, bf16[2,2,8,96,1024]{4,3,2,1,0:T(8,128)(2,1)S(1)}, u32[]{:S(2)}) copy-start(bf16[2,2,8,96,1024]{4,3,2,1,0:T(8,128)(2,1)S(1)} %bitcast_dynamic-update-slice_fusion) | copy-start | bytes 18874372
  109.4 9.2 %copy-start.4 = (f32[128]{0:T(128)S(1)}, f32[128]{0:T(128)}, u32[]{:S(2)}) copy-start(f32[128]{0:T(128)} %param.9) | copy-start | bytes 1540
  112.1 6.5 %collective-permute-start.22 = (f32[8,128]{1,0:T(8,128)S(1)}, f32[8,128]{1,0:T(8,128)S(1)}, u32[]{:S(2)}, u32[]{:S(2)}) collective-permute-start(f32[8,128]{1,0:T(8,128)S(1)} %reshape.130), channel_id=1, source_target_pairs={{0,256},{16,272},{32,288},{48,304},{64,320},{80,336},{96,352},{112... | collective-permute-start | bytes 12296 | tf_op jit(solution)/shard_map/ppermute | solution.py:22
  136.8 2.8 %copy-start.1 = (bf16[2,2,8,96,1024]{4,3,2,1,0:T(8,128)(2,1)S(1)}, bf16[2,2,8,96,1024]{4,3,2,1,0:T(8,128)(2,1)}, u32[]{:S(2)}) copy-start(bf16[2,2,8,96,1024]{4,3,2,1,0:T(8,128)(2,1)} %copy-done) | copy-start | bytes 18874372
  139.6 6.6 %copy-start.2 = (bf16[2,2,8,96,1024]{4,3,2,1,0:T(8,128)(2,1)S(1)}, bf16[2,2,8,96,1024]{4,3,2,1,0:T(8,128)(2,1)}, u32[]{:S(2)}) copy-start(bf16[2,2,8,96,1024]{4,3,2,1,0:T(8,128)(2,1)} %copy-done) | copy-start | bytes 18874372
  142.2 6.2 %collective-permute-start.23 = (bf16[2,1536,128]{2,1,0:T(8,128)(2,1)S(1)}, bf16[2,1536,128]{2,1,0:T(8,128)(2,1)S(1)}, u32[]{:S(2)}, u32[]{:S(2)}) collective-permute-start(bf16[2,1536,128]{2,1,0:T(8,128)(2,1)S(1)} %get-tuple-element.9), channel_id=1, source_target_pairs={{0,256},{16,272},{32,288},{48,304},{64,320},{80,336},{96,352},{112... | collective-permute-start | bytes 2359304 | tf_op jit(solution)/shard_map/ppermute | solution.py:22
  149.4 27.5 %all-to-all-start.1 = ((bf16[32,96,128]{2,1,0:T(8,128)(2,1)}), bf16[32,96,128]{2,1,0:T(8,128)(2,1)S(1)}, u32[]{:S(2)}, u32[]{:S(2)}) async-start(bf16[32,96,128]{2,1,0:T(8,128)(2,1)} %bitcast.51), calls=%async_computation.1 | async-start | bytes 1572864 | tf_op jit(solution)/shard_map/all_to_all | solution.py:37

commit v9 on v8

--- a/solution.py
+++ b/solution.py
@@ -105,7 +105,7 @@
         in_specs=[whole] * len(ins) + [pl.BlockSpec((1, TILE, width), lambda k: (section, k, 0))],
         out_specs=[whole] * len(whole_outs) + [pl.BlockSpec((zs, TILE, tok), lambda k: (0, k, 0))],
         out_shape=[*whole_outs, grads],
-        compiler_params=pltpu.CompilerParams(vmem_limit_bytes=16 * 2**20),
+        compiler_params=pltpu.CompilerParams(vmem_limit_bytes=58 * 2**20),
         cost_estimate=pl.CostEstimate(
             flops=10**9, bytes_accessed=5 * 10**6, transcendentals=5 * 10**5
         ),

time: 179 us -> 186 us (1.039)
  Pallas kernels: 4.69 us -> 12.5 us
  local copies, waits for them, and re-layouts: 7.43 us -> 5.29 us
  other arithmetic: 7.04 us -> 9.07 us
    pallas_call x2, Pallas kernels: 4.69 us -> 12.5 us  [over_tiles(): pl.pallas_call(kernel, grid=(feats // TILE,), in_specs=[whole] * len(ins)...]
    unnamed x10 -> x8, local copies, waits for them, and re-layouts: 2.82 us -> 0.02 us
  transfers between devices with their start and end apart: 25 -> 25, of which waited for: 7 -> 7; matrix products, arithmetic and copies ran while one was open for 5% -> 5% of each run, Pallas kernels for 1% -> 3%
where the time goes in v9:
time: 186 us; the launch traced here: 185 us
  starting transfers between devices  99.5 us (53%)
  waiting for transfers between devices  37.4 us (20%)
  blocking collectives  17.8 us (10%)
  Pallas kernels  12.5 us (7%)
  other arithmetic  9.07 us (5%)
  local copies, waits for them, and re-layouts  5.29 us (3%)
  matrix products  2 us (1%)
    ppermute x16, starting transfers between devices, along_y(): return lax.ppermute(x, 'dp', perm)  49.2 us
    ppermute x8, starting transfers between devices, flip(): return lax.ppermute(x, ('section', 'dp'), perm)  46.4 us
    all_to_all x1, waiting for transfers between devices, exchange(): lax.all_to_all(x, ('section', 'dp', 'vocab'), split_axis=0, concat_axis=0...  22.9 us
    all_to_all x1, blocking collectives, exchange(): lax.all_to_all(x, ('section', 'dp', 'vocab'), split_axis=0, concat_axis=0...  17.8 us
    ppermute x16, waiting for transfers between devices, along_y(): return lax.ppermute(x, 'dp', perm)  13.7 us
    pallas_call x2, Pallas kernels, over_tiles(): pl.pallas_call(kernel, grid=(feats // TILE,), in_specs=[whole] * len(ins)...  12.5 us
    all_to_all x1, starting transfers between devices, exchange(): lax.all_to_all(x, ('section', 'dp', 'vocab'), split_axis=0, concat_axis=0...  3.91 us
  transfers between devices with their start and end apart: 25, of which 7 were waited for; matrix products, arithmetic and copies ran while one was open for 5% of the time, Pallas kernels for 3%

profile of v9, /device:TPU:25, one launch (start us, length us, event | category | flops | bytes accessed | tf_op | source)
XLA Modules:
  0.0 185.2 jit_solution(16204187484558539765)
XLA Ops:
  0.7 1.1 constant_dynamic-slice_fusion.9
  1.8 2.6 %collective-permute-start = (bf16[96,1024]{1,0:T(8,128)(2,1)S(1)}, bf16[96,1024]{1,0:T(8,128)(2,1)S(1)}, u32[]{:S(2)}, u32[]{:S(2)}) collective-permute-start(bf16[96,1024]{1,0:T(8,128)(2,1)S(1)} %get-tuple-element.19), channel_id=1, source_target_pairs={{0,256},{16,272},{32,288},{48,304},{64,320},{80,336},{96,352},{112... | collective-permute-start | bytes 589832 | tf_op jit(solution)/shard_map/ppermute | solution.py:22
  4.4 1.0 constant_dynamic-slice_fusion.7
  5.4 10.6 %collective-permute-start.11 = (bf16[96,2048]{1,0:T(8,128)(2,1)S(1)}, bf16[96,2048]{1,0:T(8,128)(2,1)S(1)}, u32[]{:S(2)}, u32[]{:S(2)}) collective-permute-start(bf16[96,2048]{1,0:T(8,128)(2,1)S(1)} %constant_dynamic-slice_fusion.7), channel_id=1, source_target_pairs={{0,128},{16,144},{32,160},{48,176},{64,192},{80,208},{96,224},{112... | collective-permute-start | bytes 1179656 | tf_op jit(solution)/shard_map/ppermute | solution.py:22
  16.0 0.7 exponential_multiply_fusion
  16.9 4.4 %collective-permute-start.1 = (bf16[192,1024]{1,0:T(8,128)(2,1)S(1)}, bf16[192,1024]{1,0:T(8,128)(2,1)S(1)}, u32[]{:S(2)}, u32[]{:S(2)}) collective-permute-start(bf16[192,1024]{1,0:T(8,128)(2,1)S(1)} %pad_maximum_fusion), channel_id=1, source_target_pairs={{0,16},{16,32},{32,48},{48,64},{64,80},{80,96},{96,112},{112,0},{1... | collective-permute-start | bytes 1179656 | tf_op jit(solution)/shard_map/ppermute | solution.py:27
  21.3 1.9 %collective-permute-start.4 = (bf16[192,1024]{1,0:T(8,128)(2,1)S(1)}, bf16[192,1024]{1,0:T(8,128)(2,1)S(1)}, u32[]{:S(2)}, u32[]{:S(2)}) collective-permute-start(bf16[192,1024]{1,0:T(8,128)(2,1)S(1)} %pad_maximum_fusion), channel_id=1, source_target_pairs={{0,112},{16,0},{32,16},{48,32},{64,48},{80,64},{96,80},{112,96},{1... | collective-permute-start | bytes 1179656 | tf_op jit(solution)/shard_map/ppermute | solution.py:27
  23.3 0.6 mul.60
  23.9 2.9 %fusion = bf16[128,4096]{1,0:T(8,128)(2,1)S(1)} fusion(f32[16,8,32,128]{3,2,1,0:T(8,128)S(1)} %bitcast.103, s32[128,4096]{1,0:T(8,128)} %param.7), kind=kLoop, calls=%fused_computation.1 | loop fusion | flops 1572864 | bytes 5242880 | tf_op jit(solution)/shard_map/convert_element_type | solution.py:51
  27.0 2.5 %collective-permute-start.12 = (bf16[96,1024]{1,0:T(8,128)(2,1)S(1)}, bf16[96,1024]{1,0:T(8,128)(2,1)S(1)}, u32[]{:S(2)}, u32[]{:S(2)}) collective-permute-start(bf16[96,1024]{1,0:T(8,128)(2,1)S(1)} %get-tuple-element.21), channel_id=1, source_target_pairs={{0,256},{16,272},{32,288},{48,304},{64,320},{80,336},{96,352},{112... | collective-permute-start | bytes 589832 | tf_op jit(solution)/shard_map/ppermute | solution.py:22
  29.6 14.2 %collective-permute-start.2 = (bf16[128,1536]{1,0:T(8,128)(2,1)S(1)}, bf16[128,1536]{1,0:T(8,128)(2,1)S(1)}, u32[]{:S(2)}, u32[]{:S(2)}) collective-permute-start(bf16[128,1536]{1,0:T(8,128)(2,1)S(1)} %copy-done.2), channel_id=1, source_target_pairs={{0,128},{16,144},{32,160},{48,176},{64,192},{80,208},{96,224},{112... | collective-permute-start | bytes 1179656 | tf_op jit(solution)/shard_map/ppermute | solution.py:22
  43.8 4.4 %collective-permute-start.5 = (bf16[192,1024]{1,0:T(8,128)(2,1)S(1)}, bf16[192,1024]{1,0:T(8,128)(2,1)S(1)}, u32[]{:S(2)}, u32[]{:S(2)}) collective-permute-start(bf16[192,1024]{1,0:T(8,128)(2,1)S(1)} %collective-permute-done.1), channel_id=1, source_target_pairs={{0,16},{16,32},{32,48},{48,64},{64,80},{80,96},{96,112},{112,0},{1... | collective-permute-start | bytes 1179656 | tf_op jit(solution)/shard_map/ppermute | solution.py:27
  48.3 1.9 %collective-permute-start.6 = (bf16[192,1024]{1,0:T(8,128)(2,1)S(1)}, bf16[192,1024]{1,0:T(8,128)(2,1)S(1)}, u32[]{:S(2)}, u32[]{:S(2)}) collective-permute-start(bf16[192,1024]{1,0:T(8,128)(2,1)S(1)} %collective-permute-done.4), channel_id=1, source_target_pairs={{0,112},{16,0},{32,16},{48,32},{64,48},{80,64},{96,80},{112,96},{1... | collective-permute-start | bytes 1179656 | tf_op jit(solution)/shard_map/ppermute | solution.py:27
  50.2 0.8 broadcast_in_dim.6
  51.1 4.6 %collective-permute-start.13 = (bf16[192,1024]{1,0:T(8,128)(2,1)S(1)}, bf16[192,1024]{1,0:T(8,128)(2,1)S(1)}, u32[]{:S(2)}, u32[]{:S(2)}) collective-permute-start(bf16[192,1024]{1,0:T(8,128)(2,1)S(1)} %pad_maximum_fusion.1), channel_id=1, source_target_pairs={{0,16},{16,32},{32,48},{48,64},{64,80},{80,96},{96,112},{112,0},{1... | collective-permute-start | bytes 1179656 | tf_op jit(solution)/shard_map/ppermute | solution.py:27
  55.7 1.9 %collective-permute-start.14 = (bf16[192,1024]{1,0:T(8,128)(2,1)S(1)}, bf16[192,1024]{1,0:T(8,128)(2,1)S(1)}, u32[]{:S(2)}, u32[]{:S(2)}) collective-permute-start(bf16[192,1024]{1,0:T(8,128)(2,1)S(1)} %pad_maximum_fusion.1), channel_id=1, source_target_pairs={{0,112},{16,0},{32,16},{48,32},{64,48},{80,64},{96,80},{112,96},{1... | collective-permute-start | bytes 1179656 | tf_op jit(solution)/shard_map/ppermute | solution.py:27
  57.7 4.6 %collective-permute-start.7 = (bf16[192,1024]{1,0:T(8,128)(2,1)S(1)}, bf16[192,1024]{1,0:T(8,128)(2,1)S(1)}, u32[]{:S(2)}, u32[]{:S(2)}) collective-permute-start(bf16[192,1024]{1,0:T(8,128)(2,1)S(1)} %collective-permute-done.5), channel_id=1, source_target_pairs={{0,16},{16,32},{32,48},{48,64},{64,80},{80,96},{96,112},{112,0},{1... | collective-permute-start | bytes 1179656 | tf_op jit(solution)/shard_map/ppermute | solution.py:27
  62.3 1.9 %collective-permute-start.8 = (bf16[192,1024]{1,0:T(8,128)(2,1)S(1)}, bf16[192,1024]{1,0:T(8,128)(2,1)S(1)}, u32[]{:S(2)}, u32[]{:S(2)}) collective-permute-start(bf16[192,1024]{1,0:T(8,128)(2,1)S(1)} %collective-permute-done.6), channel_id=1, source_target_pairs={{0,112},{16,0},{32,16},{48,32},{64,48},{80,64},{96,80},{112,96},{1... | collective-permute-start | bytes 1179656 | tf_op jit(solution)/shard_map/ppermute | solution.py:27
  64.2 0.2 maximum_select_fusion
  64.4 3.6 %collective-permute-start.3 = (bf16[256,1536]{1,0:T(8,128)(2,1)S(1)}, bf16[256,1536]{1,0:T(8,128)(2,1)S(1)}, u32[]{:S(2)}, u32[]{:S(2)}) collective-permute-start(bf16[256,1536]{1,0:T(8,128)(2,1)S(1)} %maximum_select_fusion), channel_id=1, source_target_pairs={{0,256},{16,272},{32,288},{48,304},{64,320},{80,336},{96,352},{112... | collective-permute-start | bytes 2359304 | tf_op jit(solution)/shard_map/ppermute | solution.py:22
  68.0 4.9 %collective-permute-start.15 = (bf16[192,1024]{1,0:T(8,128)(2,1)S(1)}, bf16[192,1024]{1,0:T(8,128)(2,1)S(1)}, u32[]{:S(2)}, u32[]{:S(2)}) collective-permute-start(bf16[192,1024]{1,0:T(8,128)(2,1)S(1)} %collective-permute-done.13), channel_id=1, source_target_pairs={{0,16},{16,32},{32,48},{48,64},{64,80},{80,96},{96,112},{112,0},{1... | collective-permute-start | bytes 1179656 | tf_op jit(solution)/shard_map/ppermute | solution.py:27
  72.9 1.9 %collective-permute-start.16 = (bf16[192,1024]{1,0:T(8,128)(2,1)S(1)}, bf16[192,1024]{1,0:T(8,128)(2,1)S(1)}, u32[]{:S(2)}, u32[]{:S(2)}) collective-permute-start(bf16[192,1024]{1,0:T(8,128)(2,1)S(1)} %collective-permute-done.14), channel_id=1, source_target_pairs={{0,112},{16,0},{32,16},{48,32},{64,48},{80,64},{96,80},{112,96},{1... | collective-permute-start | bytes 1179656 | tf_op jit(solution)/shard_map/ppermute | solution.py:27
  74.9 3.2 %collective-permute-start.21 = (bf16[128,1024]{1,0:T(8,128)(2,1)S(1)}, bf16[128,1024]{1,0:T(8,128)(2,1)S(1)}, u32[]{:S(2)}, u32[]{:S(2)}) collective-permute-start(bf16[128,1024]{1,0:T(8,128)(2,1)S(1)} %get-tuple-element.7), channel_id=1, source_target_pairs={{0,128},{16,144},{32,160},{48,176},{64,192},{80,208},{96,224},{112... | collective-permute-start | bytes 786440 | tf_op jit(solution)/shard_map/ppermute | solution.py:22
  78.2 0.2 collective-permute-done.8
  78.4 4.3 %collective-permute-start.9 = (bf16[96,1024]{1,0:T(8,128)(2,1)S(1)}, bf16[96,1024]{1,0:T(8,128)(2,1)S(1)}, u32[]{:S(2)}, u32[]{:S(2)}) collective-permute-start(bf16[96,1024]{1,0:T(8,128)(2,1)S(1)} %slice.68), channel_id=1, source_target_pairs={{0,16},{16,32},{32,48},{48,64},{64,80},{80,96},{96,112},{112,0},{1... | collective-permute-start | bytes 589832 | tf_op jit(solution)/shard_map/ppermute | solution.py:27
  82.9 1.9 %collective-permute-start.10 = (bf16[96,1024]{1,0:T(8,128)(2,1)S(1)}, bf16[96,1024]{1,0:T(8,128)(2,1)S(1)}, u32[]{:S(2)}, u32[]{:S(2)}) collective-permute-start(bf16[96,1024]{1,0:T(8,128)(2,1)S(1)} %slice.69), channel_id=1, source_target_pairs={{0,112},{16,0},{32,16},{48,32},{64,48},{80,64},{96,80},{112,96},{1... | collective-permute-start | bytes 589832 | tf_op jit(solution)/shard_map/ppermute | solution.py:27
  84.8 2.4 %collective-permute-done.16 = bf16[192,1024]{1,0:T(8,128)(2,1)S(1)} collective-permute-done((bf16[192,1024]{1,0:T(8,128)(2,1)S(1)}, bf16[192,1024]{1,0:T(8,128)(2,1)S(1)}, u32[]{:S(2)}, u32[]{:S(2)}) %collective-permute-start.16) | collective-permute-done | bytes 393248 | tf_op jit(solution)/shard_map/ppermute | solution.py:27
  87.2 2.2 %collective-permute-start.17 = (bf16[192,1024]{1,0:T(8,128)(2,1)S(1)}, bf16[192,1024]{1,0:T(8,128)(2,1)S(1)}, u32[]{:S(2)}, u32[]{:S(2)}) collective-permute-start(bf16[192,1024]{1,0:T(8,128)(2,1)S(1)} %collective-permute-done.15), channel_id=1, source_target_pairs={{0,16},{16,32},{32,48},{48,64},{64,80},{80,96},{96,112},{112,0},{1... | collective-permute-start | bytes 1179656 | tf_op jit(solution)/shard_map/ppermute | solution.py:27
  89.4 3.1 %collective-permute-start.18 = (bf16[192,1024]{1,0:T(8,128)(2,1)S(1)}, bf16[192,1024]{1,0:T(8,128)(2,1)S(1)}, u32[]{:S(2)}, u32[]{:S(2)}) collective-permute-start(bf16[192,1024]{1,0:T(8,128)(2,1)S(1)} %collective-permute-done.16), channel_id=1, source_target_pairs={{0,112},{16,0},{32,16},{48,32},{64,48},{80,64},{96,80},{112,96},{1... | collective-permute-start | bytes 1179656 | tf_op jit(solution)/shard_map/ppermute | solution.py:27
  92.8 5.9 %collective-permute-done.17 = bf16[192,1024]{1,0:T(8,128)(2,1)S(1)} collective-permute-done((bf16[192,1024]{1,0:T(8,128)(2,1)S(1)}, bf16[192,1024]{1,0:T(8,128)(2,1)S(1)}, u32[]{:S(2)}, u32[]{:S(2)}) %collective-permute-start.17) | collective-permute-done | bytes 393248 | tf_op jit(solution)/shard_map/ppermute | solution.py:27
  98.7 3.0 %collective-permute-start.19 = (bf16[96,1024]{1,0:T(8,128)(2,1)S(1)}, bf16[96,1024]{1,0:T(8,128)(2,1)S(1)}, u32[]{:S(2)}, u32[]{:S(2)}) collective-permute-start(bf16[96,1024]{1,0:T(8,128)(2,1)S(1)} %slice.70), channel_id=1, source_target_pairs={{0,16},{16,32},{32,48},{48,64},{64,80},{80,96},{96,112},{112,0},{1... | collective-permute-start | bytes 589832 | tf_op jit(solution)/shard_map/ppermute | solution.py:27
  101.7 2.3 %collective-permute-start.20 = (bf16[96,1024]{1,0:T(8,128)(2,1)S(1)}, bf16[96,1024]{1,0:T(8,128)(2,1)S(1)}, u32[]{:S(2)}, u32[]{:S(2)}) collective-permute-start(bf16[96,1024]{1,0:T(8,128)(2,1)S(1)} %slice.71), channel_id=1, source_target_pairs={{0,112},{16,0},{32,16},{48,32},{64,48},{80,64},{96,80},{112,96},{1... | collective-permute-start | bytes 589832 | tf_op jit(solution)/shard_map/ppermute | solution.py:27
  104.2 1.0 collective-permute-done.19
  105.2 4.2 %collective-permute-done.20 = bf16[96,1024]{1,0:T(8,128)(2,1)S(1)} collective-permute-done((bf16[96,1024]{1,0:T(8,128)(2,1)S(1)}, bf16[96,1024]{1,0:T(8,128)(2,1)S(1)}, u32[]{:S(2)}, u32[]{:S(2)}) %collective-permute-start.20) | collective-permute-done | bytes 196640 | tf_op jit(solution)/shard_map/ppermute | solution.py:27
  109.4 2.0 %fusion.23 = (f32[256]{0:T(256)S(1)}, f32[256,1024]{1,0:T(8,128)S(1)}) fusion(bf16[3072,1024]{1,0:T(8,128)(2,1)S(1)} %bitcast.100, bf16[256,1536]{1,0:T(8,128)(2,1)S(1)} %collective-permute-done.3, bf16[256,1536]{1,0:T(8,128)(2,1)S(1)} %maximum_select_fusion), kind=kOutput, calls=%fused_computation.74 | convolution fusion | flops 1614282496 | bytes 8913920 | tf_op jit(solution)/shard_map/dot_general | solution.py:157
  111.4 1.3 exponential_reduce_fusion
  112.7 5.7 %collective-permute-start.22 = (f32[8,128]{1,0:T(8,128)S(1)}, f32[8,128]{1,0:T(8,128)S(1)}, u32[]{:S(2)}, u32[]{:S(2)}) collective-permute-start(f32[8,128]{1,0:T(8,128)S(1)} %reshape.130), channel_id=1, source_target_pairs={{0,256},{16,272},{32,288},{48,304},{64,320},{80,336},{96,352},{112... | collective-permute-start | bytes 12296 | tf_op jit(solution)/shard_map/ppermute | solution.py:22
  118.4 0.8 collective-permute-done.22
  119.3 17.8 %all_to_all.10 = f32[32,8,128]{2,1,0:T(8,128)S(1)} all-to-all(f32[32,8,128]{2,1,0:T(8,128)S(1)} %bitcast.110), channel_id=1, replica_groups={{0,1,2,3,4,5,6,7,8,9,10,11,12,13,14,15,128,129,130,131,132,133,134,135,..., dimensions={0} | all-to-all | bytes 262144 | tf_op jit(solution)/shard_map/all_to_all | solution.py:37
  137.3 0.8 copy.71.row_ref
  138.1 6.6 %shard_map.68 = (bf16[256,1024]{1,0:T(8,128)(2,1)}, bf16[2,1536,128]{2,1,0:T(8,128)(2,1)}) custom-call(f32[256,1024]{1,0:T(8,128)} %copy-done.1, bf16[256,1024]{1,0:T(8,128)(2,1)} %get-tuple-element.15.t_ref, f32[256,3]{1,0:T(8,128)} %copy.71.row_ref, bf16[2,1536,1024]{2,1,0:T(8,128)(2,1)} %bitcast.101), custom_call_target="tpu_custom_call" | custom-call | flops 1000000000 | bytes 5000000 | tf_op jit(solution)/shard_map/pallas_call | solution.py:102
  144.7 4.0 %collective-permute-start.23 = (bf16[2,1536,128]{2,1,0:T(8,128)(2,1)}, bf16[2,1536,128]{2,1,0:T(8,128)(2,1)S(1)}, u32[]{:S(2)}, u32[]{:S(2)}) collective-permute-start(bf16[2,1536,128]{2,1,0:T(8,128)(2,1)} %get-tuple-element.9), channel_id=1, source_target_pairs={{0,256},{16,272},{32,288},{48,304},{64,320},{80,336},{96,352},{112... | collective-permute-start | bytes 2359304 | tf_op jit(solution)/shard_map/ppermute | solution.py:22
  148.7 5.9 %shard_map.69 = f32[2,1536,128]{2,1,0:T(8,128)} custom-call(bf16[256,1024]{1,0:T(8,128)(2,1)} %get-tuple-element.8.lg_ref, bf16[2,1536,1024]{2,1,0:T(8,128)(2,1)} %bitcast.102), custom_call_target="tpu_custom_call" | custom-call | flops 1000000000 | bytes 5000000 | tf_op jit(solution)/shard_map/pallas_call | solution.py:102
  154.6 2.5 %add_convert_fusion = bf16[2,1536,128]{2,1,0:T(8,128)(2,1)} fusion(f32[2,1536,128]{2,1,0:T(8,128)} %shard_map.69, bf16[2,1536,128]{2,1,0:T(8,128)(2,1)S(1)} %collective-permute-done.23), kind=kLoop, calls=%fused_computation.6 | loop fusion | flops 1179648 | bytes 3145728 | tf_op jit(solution)/shard_map/convert_element_type | solution.py:216
  157.1 3.9 %all-to-all-start.1 = ((bf16[32,96,128]{2,1,0:T(8,128)(2,1)}), bf16[32,96,128]{2,1,0:T(8,128)(2,1)S(1)}, u32[]{:S(2)}, u32[]{:S(2)}) async-start(bf16[32,96,128]{2,1,0:T(8,128)(2,1)} %bitcast.51), calls=%async_computation.1 | async-start | bytes 1572864 | tf_op jit(solution)/shard_map/all_to_all | solution.py:37
  161.0 0.5 fusion.20
  161.6 22.9 %all-to-all-done.1 = bf16[32,96,128]{2,1,0:T(8,128)(2,1)S(1)} async-done(((bf16[32,96,128]{2,1,0:T(8,128)(2,1)}), bf16[32,96,128]{2,1,0:T(8,128)(2,1)S(1)}, u32[]{:S(2)}, u32[]{:S(2)}) %all-to-all-start.1) | async-done | bytes 786464 | tf_op jit(solution)/shard_map/all_to_all | solution.py:37
  184.4 0.7 reduce_sum.92
  (73 shorter events, 1.3 us)
Async XLA Ops:
  0.6 29.0 %copy-start.2 = (bf16[128,1536]{1,0:T(8,128)(2,1)S(1)}, bf16[128,1536]{1,0:T(8,128)(2,1)}, u32[]{:S(2)}) copy-start(bf16[128,1536]{1,0:T(8,128)(2,1)} %param.5) | copy-start | bytes 1179652
  1.8 15.1 %collective-permute-start = (bf16[96,1024]{1,0:T(8,128)(2,1)S(1)}, bf16[96,1024]{1,0:T(8,128)(2,1)S(1)}, u32[]{:S(2)}, u32[]{:S(2)}) collective-permute-start(bf16[96,1024]{1,0:T(8,128)(2,1)S(1)} %get-tuple-element.19), channel_id=1, source_target_pairs={{0,256},{16,272},{32,288},{48,304},{64,320},{80,336},{96,352},{112... | collective-permute-start | bytes 589832 | tf_op jit(solution)/shard_map/ppermute | solution.py:22
  5.4 21.6 %collective-permute-start.11 = (bf16[96,2048]{1,0:T(8,128)(2,1)S(1)}, bf16[96,2048]{1,0:T(8,128)(2,1)S(1)}, u32[]{:S(2)}, u32[]{:S(2)}) collective-permute-start(bf16[96,2048]{1,0:T(8,128)(2,1)S(1)} %constant_dynamic-slice_fusion.7), channel_id=1, source_target_pairs={{0,128},{16,144},{32,160},{48,176},{64,192},{80,208},{96,224},{112... | collective-permute-start | bytes 1179656 | tf_op jit(solution)/shard_map/ppermute | solution.py:22
  16.9 12.7 %collective-permute-start.1 = (bf16[192,1024]{1,0:T(8,128)(2,1)S(1)}, bf16[192,1024]{1,0:T(8,128)(2,1)S(1)}, u32[]{:S(2)}, u32[]{:S(2)}) collective-permute-start(bf16[192,1024]{1,0:T(8,128)(2,1)S(1)} %pad_maximum_fusion), channel_id=1, source_target_pairs={{0,16},{16,32},{32,48},{48,64},{64,80},{80,96},{96,112},{112,0},{1... | collective-permute-start | bytes 1179656 | tf_op jit(solution)/shard_map/ppermute | solution.py:27
  21.3 26.9 %collective-permute-start.4 = (bf16[192,1024]{1,0:T(8,128)(2,1)S(1)}, bf16[192,1024]{1,0:T(8,128)(2,1)S(1)}, u32[]{:S(2)}, u32[]{:S(2)}) collective-permute-start(bf16[192,1024]{1,0:T(8,128)(2,1)S(1)} %pad_maximum_fusion), channel_id=1, source_target_pairs={{0,112},{16,0},{32,16},{48,32},{64,48},{80,64},{96,80},{112,96},{1... | collective-permute-start | bytes 1179656 | tf_op jit(solution)/shard_map/ppermute | solution.py:27
  27.0 24.0 %collective-permute-start.12 = (bf16[96,1024]{1,0:T(8,128)(2,1)S(1)}, bf16[96,1024]{1,0:T(8,128)(2,1)S(1)}, u32[]{:S(2)}, u32[]{:S(2)}) collective-permute-start(bf16[96,1024]{1,0:T(8,128)(2,1)S(1)} %get-tuple-element.21), channel_id=1, source_target_pairs={{0,256},{16,272},{32,288},{48,304},{64,320},{80,336},{96,352},{112... | collective-permute-start | bytes 589832 | tf_op jit(solution)/shard_map/ppermute | solution.py:22
  29.6 34.6 %collective-permute-start.2 = (bf16[128,1536]{1,0:T(8,128)(2,1)S(1)}, bf16[128,1536]{1,0:T(8,128)(2,1)S(1)}, u32[]{:S(2)}, u32[]{:S(2)}) collective-permute-start(bf16[128,1536]{1,0:T(8,128)(2,1)S(1)} %copy-done.2), channel_id=1, source_target_pairs={{0,128},{16,144},{32,160},{48,176},{64,192},{80,208},{96,224},{112... | collective-permute-start | bytes 1179656 | tf_op jit(solution)/shard_map/ppermute | solution.py:22
  43.8 13.9 %collective-permute-start.5 = (bf16[192,1024]{1,0:T(8,128)(2,1)S(1)}, bf16[192,1024]{1,0:T(8,128)(2,1)S(1)}, u32[]{:S(2)}, u32[]{:S(2)}) collective-permute-start(bf16[192,1024]{1,0:T(8,128)(2,1)S(1)} %collective-permute-done.1), channel_id=1, source_target_pairs={{0,16},{16,32},{32,48},{48,64},{64,80},{80,96},{96,112},{112,0},{1... | collective-permute-start | bytes 1179656 | tf_op jit(solution)/shard_map/ppermute | solution.py:27
  48.3 14.0 %collective-permute-start.6 = (bf16[192,1024]{1,0:T(8,128)(2,1)S(1)}, bf16[192,1024]{1,0:T(8,128)(2,1)S(1)}, u32[]{:S(2)}, u32[]{:S(2)}) collective-permute-start(bf16[192,1024]{1,0:T(8,128)(2,1)S(1)} %collective-permute-done.4), channel_id=1, source_target_pairs={{0,112},{16,0},{32,16},{48,32},{64,48},{80,64},{96,80},{112,96},{1... | collective-permute-start | bytes 1179656 | tf_op jit(solution)/shard_map/ppermute | solution.py:27
  51.1 16.9 %collective-permute-start.13 = (bf16[192,1024]{1,0:T(8,128)(2,1)S(1)}, bf16[192,1024]{1,0:T(8,128)(2,1)S(1)}, u32[]{:S(2)}, u32[]{:S(2)}) collective-permute-start(bf16[192,1024]{1,0:T(8,128)(2,1)S(1)} %pad_maximum_fusion.1), channel_id=1, source_target_pairs={{0,16},{16,32},{32,48},{48,64},{64,80},{80,96},{96,112},{112,0},{1... | collective-permute-start | bytes 1179656 | tf_op jit(solution)/shard_map/ppermute | solution.py:27
  55.7 17.2 %collective-permute-start.14 = (bf16[192,1024]{1,0:T(8,128)(2,1)S(1)}, bf16[192,1024]{1,0:T(8,128)(2,1)S(1)}, u32[]{:S(2)}, u32[]{:S(2)}) collective-permute-start(bf16[192,1024]{1,0:T(8,128)(2,1)S(1)} %pad_maximum_fusion.1), channel_id=1, source_target_pairs={{0,112},{16,0},{32,16},{48,32},{64,48},{80,64},{96,80},{112,96},{1... | collective-permute-start | bytes 1179656 | tf_op jit(solution)/shard_map/ppermute | solution.py:27
  57.7 17.2 %collective-permute-start.7 = (bf16[192,1024]{1,0:T(8,128)(2,1)S(1)}, bf16[192,1024]{1,0:T(8,128)(2,1)S(1)}, u32[]{:S(2)}, u32[]{:S(2)}) collective-permute-start(bf16[192,1024]{1,0:T(8,128)(2,1)S(1)} %collective-permute-done.5), channel_id=1, source_target_pairs={{0,16},{16,32},{32,48},{48,64},{64,80},{80,96},{96,112},{112,0},{1... | collective-permute-start | bytes 1179656 | tf_op jit(solution)/shard_map/ppermute | solution.py:27
  62.3 16.1 %collective-permute-start.8 = (bf16[192,1024]{1,0:T(8,128)(2,1)S(1)}, bf16[192,1024]{1,0:T(8,128)(2,1)S(1)}, u32[]{:S(2)}, u32[]{:S(2)}) collective-permute-start(bf16[192,1024]{1,0:T(8,128)(2,1)S(1)} %collective-permute-done.6), channel_id=1, source_target_pairs={{0,112},{16,0},{32,16},{48,32},{64,48},{80,64},{96,80},{112,96},{1... | collective-permute-start | bytes 1179656 | tf_op jit(solution)/shard_map/ppermute | solution.py:27
  64.4 45.0 %collective-permute-start.3 = (bf16[256,1536]{1,0:T(8,128)(2,1)S(1)}, bf16[256,1536]{1,0:T(8,128)(2,1)S(1)}, u32[]{:S(2)}, u32[]{:S(2)}) collective-permute-start(bf16[256,1536]{1,0:T(8,128)(2,1)S(1)} %maximum_select_fusion), channel_id=1, source_target_pairs={{0,256},{16,272},{32,288},{48,304},{64,320},{80,336},{96,352},{112... | collective-permute-start | bytes 2359304 | tf_op jit(solution)/shard_map/ppermute | solution.py:22
  68.0 14.8 %collective-permute-start.15 = (bf16[192,1024]{1,0:T(8,128)(2,1)S(1)}, bf16[192,1024]{1,0:T(8,128)(2,1)S(1)}, u32[]{:S(2)}, u32[]{:S(2)}) collective-permute-start(bf16[192,1024]{1,0:T(8,128)(2,1)S(1)} %collective-permute-done.13), channel_id=1, source_target_pairs={{0,16},{16,32},{32,48},{48,64},{64,80},{80,96},{96,112},{112,0},{1... | collective-permute-start | bytes 1179656 | tf_op jit(solution)/shard_map/ppermute | solution.py:27
  72.9 14.3 %collective-permute-start.16 = (bf16[192,1024]{1,0:T(8,128)(2,1)S(1)}, bf16[192,1024]{1,0:T(8,128)(2,1)S(1)}, u32[]{:S(2)}, u32[]{:S(2)}) collective-permute-start(bf16[192,1024]{1,0:T(8,128)(2,1)S(1)} %collective-permute-done.14), channel_id=1, source_target_pairs={{0,112},{16,0},{32,16},{48,32},{64,48},{80,64},{96,80},{112,96},{1... | collective-permute-start | bytes 1179656 | tf_op jit(solution)/shard_map/ppermute | solution.py:27
  74.9 36.5 %collective-permute-start.21 = (bf16[128,1024]{1,0:T(8,128)(2,1)S(1)}, bf16[128,1024]{1,0:T(8,128)(2,1)S(1)}, u32[]{:S(2)}, u32[]{:S(2)}) collective-permute-start(bf16[128,1024]{1,0:T(8,128)(2,1)S(1)} %get-tuple-element.7), channel_id=1, source_target_pairs={{0,128},{16,144},{32,160},{48,176},{64,192},{80,208},{96,224},{112... | collective-permute-start | bytes 786440 | tf_op jit(solution)/shard_map/ppermute | solution.py:22
  78.4 11.0 %collective-permute-start.9 = (bf16[96,1024]{1,0:T(8,128)(2,1)S(1)}, bf16[96,1024]{1,0:T(8,128)(2,1)S(1)}, u32[]{:S(2)}, u32[]{:S(2)}) collective-permute-start(bf16[96,1024]{1,0:T(8,128)(2,1)S(1)} %slice.68), channel_id=1, source_target_pairs={{0,16},{16,32},{32,48},{48,64},{64,80},{80,96},{96,112},{112,0},{1... | collective-permute-start | bytes 589832 | tf_op jit(solution)/shard_map/ppermute | solution.py:27
  82.9 9.6 %collective-permute-start.10 = (bf16[96,1024]{1,0:T(8,128)(2,1)S(1)}, bf16[96,1024]{1,0:T(8,128)(2,1)S(1)}, u32[]{:S(2)}, u32[]{:S(2)}) collective-permute-start(bf16[96,1024]{1,0:T(8,128)(2,1)S(1)} %slice.69), channel_id=1, source_target_pairs={{0,112},{16,0},{32,16},{48,32},{64,48},{80,64},{96,80},{112,96},{1... | collective-permute-start | bytes 589832 | tf_op jit(solution)/shard_map/ppermute | solution.py:27
  87.2 11.5 %collective-permute-start.17 = (bf16[192,1024]{1,0:T(8,128)(2,1)S(1)}, bf16[192,1024]{1,0:T(8,128)(2,1)S(1)}, u32[]{:S(2)}, u32[]{:S(2)}) collective-permute-start(bf16[192,1024]{1,0:T(8,128)(2,1)S(1)} %collective-permute-done.15), channel_id=1, source_target_pairs={{0,16},{16,32},{32,48},{48,64},{64,80},{80,96},{96,112},{112,0},{1... | collective-permute-start | bytes 1179656 | tf_op jit(solution)/shard_map/ppermute | solution.py:27
  89.4 12.3 %collective-permute-start.18 = (bf16[192,1024]{1,0:T(8,128)(2,1)S(1)}, bf16[192,1024]{1,0:T(8,128)(2,1)S(1)}, u32[]{:S(2)}, u32[]{:S(2)}) collective-permute-start(bf16[192,1024]{1,0:T(8,128)(2,1)S(1)} %collective-permute-done.16), channel_id=1, source_target_pairs={{0,112},{16,0},{32,16},{48,32},{64,48},{80,64},{96,80},{112,96},{1... | collective-permute-start | bytes 1179656 | tf_op jit(solution)/shard_map/ppermute | solution.py:27
  98.7 6.4 %collective-permute-start.19 = (bf16[96,1024]{1,0:T(8,128)(2,1)S(1)}, bf16[96,1024]{1,0:T(8,128)(2,1)S(1)}, u32[]{:S(2)}, u32[]{:S(2)}) collective-permute-start(bf16[96,1024]{1,0:T(8,128)(2,1)S(1)} %slice.70), channel_id=1, source_target_pairs={{0,16},{16,32},{32,48},{48,64},{64,80},{80,96},{96,112},{112,0},{1... | collective-permute-start | bytes 589832 | tf_op jit(solution)/shard_map/ppermute | solution.py:27
  101.7 7.6 %collective-permute-start.20 = (bf16[96,1024]{1,0:T(8,128)(2,1)S(1)}, bf16[96,1024]{1,0:T(8,128)(2,1)S(1)}, u32[]{:S(2)}, u32[]{:S(2)}) collective-permute-start(bf16[96,1024]{1,0:T(8,128)(2,1)S(1)} %slice.71), channel_id=1, source_target_pairs={{0,112},{16,0},{32,16},{48,32},{64,48},{80,64},{96,80},{112,96},{1... | collective-permute-start | bytes 589832 | tf_op jit(solution)/shard_map/ppermute | solution.py:27
  109.4 3.3 %copy-start = (bf16[2,2,8,96,1024]{4,3,2,1,0:T(8,128)(2,1)}, bf16[2,2,8,96,1024]{4,3,2,1,0:T(8,128)(2,1)S(1)}, u32[]{:S(2)}) copy-start(bf16[2,2,8,96,1024]{4,3,2,1,0:T(8,128)(2,1)S(1)} %bitcast_dynamic-update-slice_fusion) | copy-start | bytes 18874372
  109.4 9.9 %copy-start.3 = (f32[128]{0:T(128)S(1)}, f32[128]{0:T(128)}, u32[]{:S(2)}) copy-start(f32[128]{0:T(128)} %param.9) | copy-start | bytes 1540
  111.4 26.7 %copy-start.1 = (f32[256,1024]{1,0:T(8,128)}, f32[256,1024]{1,0:T(8,128)S(1)}, u32[]{:S(2)}) copy-start(f32[256,1024]{1,0:T(8,128)S(1)} %get-tuple-element.25.s_ref) | copy-start | bytes 3145732
  112.7 6.5 %collective-permute-start.22 = (f32[8,128]{1,0:T(8,128)S(1)}, f32[8,128]{1,0:T(8,128)S(1)}, u32[]{:S(2)}, u32[]{:S(2)}) collective-permute-start(f32[8,128]{1,0:T(8,128)S(1)} %reshape.130), channel_id=1, source_target_pairs={{0,256},{16,272},{32,288},{48,304},{64,320},{80,336},{96,352},{112... | collective-permute-start | bytes 12296 | tf_op jit(solution)/shard_map/ppermute | solution.py:22
  144.7 9.9 %collective-permute-start.23 = (bf16[2,1536,128]{2,1,0:T(8,128)(2,1)}, bf16[2,1536,128]{2,1,0:T(8,128)(2,1)S(1)}, u32[]{:S(2)}, u32[]{:S(2)}) collective-permute-start(bf16[2,1536,128]{2,1,0:T(8,128)(2,1)} %get-tuple-element.9), channel_id=1, source_target_pairs={{0,256},{16,272},{32,288},{48,304},{64,320},{80,336},{96,352},{112... | collective-permute-start | bytes 2359304 | tf_op jit(solution)/shard_map/ppermute | solution.py:22
  157.1 27.4 %all-to-all-start.1 = ((bf16[32,96,128]{2,1,0:T(8,128)(2,1)}), bf16[32,96,128]{2,1,0:T(8,128)(2,1)S(1)}, u32[]{:S(2)}, u32[]{:S(2)}) async-start(bf16[32,96,128]{2,1,0:T(8,128)(2,1)} %bitcast.51), calls=%async_computation.1 | async-start | bytes 1572864 | tf_op jit(solution)/shard_map/all_to_all | solution.py:37

commit v10 on v8

--- a/solution.py
+++ b/solution.py
@@ -80,13 +80,32 @@
         g_ref[z] = g[:, z * tok : (z + 1) * tok]
 
 
-def first_grads_kernel(s_ref, t_ref, row_ref, w_ref, lg_ref, g_ref):
+def exps_kernel(s_ref, t_ref, m_ref, es_ref, et_ref):
+    es_ref[...] = jnp.exp(s_ref[...] - m_ref[...])
+    et_ref[...] = jnp.exp(t_ref[...].astype(jnp.float32))
+
+
+def exps(scaled_s, scaled_t, m):
+    whole = pl.BlockSpec(memory_space=pltpu.VMEM)
+    out = jax.ShapeDtypeStruct(scaled_s.shape, jnp.float32)
+    return pl.pallas_call(
+        exps_kernel,
+        in_specs=[whole] * 3,
+        out_specs=[whole] * 2,
+        out_shape=[out, out],
+        compiler_params=pltpu.CompilerParams(vmem_limit_bytes=16 * 2**20),
+        cost_estimate=pl.CostEstimate(
+            flops=10**6, bytes_accessed=4 * 10**6, transcendentals=5 * 10**5
+        ),
+    )(scaled_s, scaled_t, m)
+
+
+def first_grads_kernel(es_ref, et_ref, row_ref, w_ref, lg_ref, g_ref):
     @pl.when(pl.program_id(0) == 0)
     def _():
-        student_lse, teacher_lse, weight = row_ref[:, 0:1], row_ref[:, 1:2], row_ref[:, 2:3]
-        student = jnp.exp(s_ref[...] - student_lse)
-        teacher = jnp.exp(t_ref[...].astype(jnp.float32) - teacher_lse)
-        lg_ref[...] = (weight * TEMP * (student - teacher)).astype(jnp.bfloat16)
+        student, teacher, weight = row_ref[:, 0:1], row_ref[:, 1:2], row_ref[:, 2:3]
+        grad = es_ref[...] * student - et_ref[...] * teacher
+        lg_ref[...] = (weight * TEMP * grad).astype(jnp.bfloat16)
 
     tile_grads(w_ref, lg_ref[...], g_ref)
 
@@ -177,7 +196,9 @@
         for z in range(NZH)
     ]
     parts = jnp.broadcast_to(jnp.stack(tiles)[:, None], (NZH, NQ, 8, tok))
-    parts = exchange(parts.reshape(NZH * NQ, 8, tok))
+    parts = parts.reshape(NZH * NQ, 8, tok)
+    e_student, e_teacher = exps(after(scaled_s, parts), scaled_t, m[:, None])
+    parts = exchange(parts)
     top = jnp.max(parts[:, 0:2], axis=0)
     s_sum = jnp.sum(parts[:, 2:4] * jnp.exp(parts[:, 0:2] - top), axis=0)
     t_sum = jnp.sum(parts[:, 4:6], axis=0)
@@ -193,13 +214,13 @@
     kl_loss = TEMP * TEMP * kl_loss
 
     student_lse, teacher_lse = student_lse.reshape(2 * tok), teacher_lse.reshape(2 * tok)
-    per_row = jnp.stack([student_lse, teacher_lse, weight], axis=1)
+    per_row = jnp.stack([jnp.exp(m - student_lse), jnp.exp(-teacher_lse), weight], axis=1)
     w = weights.reshape(2, -1, width)
     feats = w.shape[1]
     logit_grad, g = over_tiles(
         first_grads_kernel,
         1,
-        (scaled_s, scaled_t, per_row),
+        (e_student, e_teacher, per_row),
         w,
         [jax.ShapeDtypeStruct(scaled_s.shape, jnp.bfloat16)],
         jax.ShapeDtypeStruct((NZH, feats, tok), jnp.bfloat16),

time: 179 us -> 181 us (1.011)
  blocking collectives: 17.8 us -> 0 us
  starting transfers between devices: 99.6 us -> 108 us
  waiting for transfers between devices: 37.5 us -> 45.9 us
  local copies, waits for them, and re-layouts: 7.43 us -> 10.4 us
    all_to_all x1 -> x0, blocking collectives: 17.8 us -> none  [exchange(): lax.all_to_all(x, ('section', 'dp', 'vocab'), split_axis=0, concat_axis=0...]
    all_to_all x1 -> x2, waiting for transfers between devices: 23 us -> 31.3 us  [exchange(): lax.all_to_all(x, ('section', 'dp', 'vocab'), split_axis=0, concat_axis=0...]
    all_to_all x1 -> x2, starting transfers between devices: 3.91 us -> 12.1 us  [exchange(): lax.all_to_all(x, ('section', 'dp', 'vocab'), split_axis=0, concat_axis=0...]
    unnamed x10 -> x14, local copies, waits for them, and re-layouts: 2.82 us -> 5.05 us
  transfers between devices with their start and end apart: 25 -> 26, of which waited for: 7 -> 8; matrix products, arithmetic and copies ran while one was open for 5% -> 6% of each run, Pallas kernels for 1% -> 1%
where the time goes in v10:
time: 181 us; the launch traced here: 180 us
  starting transfers between devices  108 us (60%)
  waiting for transfers between devices  45.9 us (25%)
  local copies, waits for them, and re-layouts  10.4 us (6%)
  other arithmetic  7.04 us (4%)
  Pallas kernels  4.91 us (3%)
  matrix products  2 us (1%)
    ppermute x16, starting transfers between devices, along_y(): return lax.ppermute(x, 'dp', perm)  49.2 us
    ppermute x8, starting transfers between devices, flip(): return lax.ppermute(x, ('section', 'dp'), perm)  46.4 us
    all_to_all x2, waiting for transfers between devices, exchange(): lax.all_to_all(x, ('section', 'dp', 'vocab'), split_axis=0, concat_axis=0...  31.3 us
    ppermute x16, waiting for transfers between devices, along_y(): return lax.ppermute(x, 'dp', perm)  13.7 us
    all_to_all x2, starting transfers between devices, exchange(): lax.all_to_all(x, ('section', 'dp', 'vocab'), split_axis=0, concat_axis=0...  12.1 us
    unnamed x14, local copies, waits for them, and re-layouts  5.05 us
    pallas_call x2, Pallas kernels, over_tiles(): pl.pallas_call(kernel, grid=(feats // TILE,), in_specs=[whole] * len(ins)...  4.56 us
  transfers between devices with their start and end apart: 26, of which 8 were waited for; matrix products, arithmetic and copies ran while one was open for 6% of the time, Pallas kernels for 1%

profile of v10, /device:TPU:25, one launch (start us, length us, event | category | flops | bytes accessed | tf_op | source)
XLA Modules:
  0.0 179.6 jit_solution(15791476674822110982)
XLA Ops:
  0.7 1.1 constant_dynamic-slice_fusion.9
  1.8 2.6 %collective-permute-start = (bf16[96,1024]{1,0:T(8,128)(2,1)S(1)}, bf16[96,1024]{1,0:T(8,128)(2,1)S(1)}, u32[]{:S(2)}, u32[]{:S(2)}) collective-permute-start(bf16[96,1024]{1,0:T(8,128)(2,1)S(1)} %get-tuple-element.25), channel_id=1, source_target_pairs={{0,256},{16,272},{32,288},{48,304},{64,320},{80,336},{96,352},{112... | collective-permute-start | bytes 589832 | tf_op jit(solution)/shard_map/ppermute | solution.py:22
  4.4 1.0 constant_dynamic-slice_fusion.7
  5.4 10.6 %collective-permute-start.11 = (bf16[96,2048]{1,0:T(8,128)(2,1)S(1)}, bf16[96,2048]{1,0:T(8,128)(2,1)S(1)}, u32[]{:S(2)}, u32[]{:S(2)}) collective-permute-start(bf16[96,2048]{1,0:T(8,128)(2,1)S(1)} %constant_dynamic-slice_fusion.7), channel_id=1, source_target_pairs={{0,128},{16,144},{32,160},{48,176},{64,192},{80,208},{96,224},{112... | collective-permute-start | bytes 1179656 | tf_op jit(solution)/shard_map/ppermute | solution.py:22
  16.0 0.7 exponential_multiply_fusion
  16.9 4.4 %collective-permute-start.1 = (bf16[192,1024]{1,0:T(8,128)(2,1)S(1)}, bf16[192,1024]{1,0:T(8,128)(2,1)S(1)}, u32[]{:S(2)}, u32[]{:S(2)}) collective-permute-start(bf16[192,1024]{1,0:T(8,128)(2,1)S(1)} %pad_maximum_fusion), channel_id=1, source_target_pairs={{0,16},{16,32},{32,48},{48,64},{64,80},{80,96},{96,112},{112,0},{1... | collective-permute-start | bytes 1179656 | tf_op jit(solution)/shard_map/ppermute | solution.py:27
  21.3 1.9 %collective-permute-start.4 = (bf16[192,1024]{1,0:T(8,128)(2,1)S(1)}, bf16[192,1024]{1,0:T(8,128)(2,1)S(1)}, u32[]{:S(2)}, u32[]{:S(2)}) collective-permute-start(bf16[192,1024]{1,0:T(8,128)(2,1)S(1)} %pad_maximum_fusion), channel_id=1, source_target_pairs={{0,112},{16,0},{32,16},{48,32},{64,48},{80,64},{96,80},{112,96},{1... | collective-permute-start | bytes 1179656 | tf_op jit(solution)/shard_map/ppermute | solution.py:27
  23.3 0.6 mul.60
  23.9 2.9 %fusion = bf16[128,4096]{1,0:T(8,128)(2,1)S(1)} fusion(f32[16,8,32,128]{3,2,1,0:T(8,128)S(1)} %bitcast.104, s32[128,4096]{1,0:T(8,128)} %param.7), kind=kLoop, calls=%fused_computation.1 | loop fusion | flops 1572864 | bytes 5242880 | tf_op jit(solution)/shard_map/convert_element_type | solution.py:51
  27.0 2.5 %collective-permute-start.12 = (bf16[96,1024]{1,0:T(8,128)(2,1)S(1)}, bf16[96,1024]{1,0:T(8,128)(2,1)S(1)}, u32[]{:S(2)}, u32[]{:S(2)}) collective-permute-start(bf16[96,1024]{1,0:T(8,128)(2,1)S(1)} %get-tuple-element.27), channel_id=1, source_target_pairs={{0,256},{16,272},{32,288},{48,304},{64,320},{80,336},{96,352},{112... | collective-permute-start | bytes 589832 | tf_op jit(solution)/shard_map/ppermute | solution.py:22
  29.6 14.2 %collective-permute-start.2 = (bf16[128,1536]{1,0:T(8,128)(2,1)S(1)}, bf16[128,1536]{1,0:T(8,128)(2,1)S(1)}, u32[]{:S(2)}, u32[]{:S(2)}) collective-permute-start(bf16[128,1536]{1,0:T(8,128)(2,1)S(1)} %copy-done.5), channel_id=1, source_target_pairs={{0,128},{16,144},{32,160},{48,176},{64,192},{80,208},{96,224},{112... | collective-permute-start | bytes 1179656 | tf_op jit(solution)/shard_map/ppermute | solution.py:22
  43.8 4.4 %collective-permute-start.5 = (bf16[192,1024]{1,0:T(8,128)(2,1)S(1)}, bf16[192,1024]{1,0:T(8,128)(2,1)S(1)}, u32[]{:S(2)}, u32[]{:S(2)}) collective-permute-start(bf16[192,1024]{1,0:T(8,128)(2,1)S(1)} %collective-permute-done.1), channel_id=1, source_target_pairs={{0,16},{16,32},{32,48},{48,64},{64,80},{80,96},{96,112},{112,0},{1... | collective-permute-start | bytes 1179656 | tf_op jit(solution)/shard_map/ppermute | solution.py:27
  48.3 1.9 %collective-permute-start.6 = (bf16[192,1024]{1,0:T(8,128)(2,1)S(1)}, bf16[192,1024]{1,0:T(8,128)(2,1)S(1)}, u32[]{:S(2)}, u32[]{:S(2)}) collective-permute-start(bf16[192,1024]{1,0:T(8,128)(2,1)S(1)} %collective-permute-done.4), channel_id=1, source_target_pairs={{0,112},{16,0},{32,16},{48,32},{64,48},{80,64},{96,80},{112,96},{1... | collective-permute-start | bytes 1179656 | tf_op jit(solution)/shard_map/ppermute | solution.py:27
  50.2 0.8 broadcast_in_dim.8
  51.1 4.6 %collective-permute-start.13 = (bf16[192,1024]{1,0:T(8,128)(2,1)S(1)}, bf16[192,1024]{1,0:T(8,128)(2,1)S(1)}, u32[]{:S(2)}, u32[]{:S(2)}) collective-permute-start(bf16[192,1024]{1,0:T(8,128)(2,1)S(1)} %pad_maximum_fusion.1), channel_id=1, source_target_pairs={{0,16},{16,32},{32,48},{48,64},{64,80},{80,96},{96,112},{112,0},{1... | collective-permute-start | bytes 1179656 | tf_op jit(solution)/shard_map/ppermute | solution.py:27
  55.7 1.9 %collective-permute-start.14 = (bf16[192,1024]{1,0:T(8,128)(2,1)S(1)}, bf16[192,1024]{1,0:T(8,128)(2,1)S(1)}, u32[]{:S(2)}, u32[]{:S(2)}) collective-permute-start(bf16[192,1024]{1,0:T(8,128)(2,1)S(1)} %pad_maximum_fusion.1), channel_id=1, source_target_pairs={{0,112},{16,0},{32,16},{48,32},{64,48},{80,64},{96,80},{112,96},{1... | collective-permute-start | bytes 1179656 | tf_op jit(solution)/shard_map/ppermute | solution.py:27
  57.7 4.6 %collective-permute-start.7 = (bf16[192,1024]{1,0:T(8,128)(2,1)S(1)}, bf16[192,1024]{1,0:T(8,128)(2,1)S(1)}, u32[]{:S(2)}, u32[]{:S(2)}) collective-permute-start(bf16[192,1024]{1,0:T(8,128)(2,1)S(1)} %collective-permute-done.5), channel_id=1, source_target_pairs={{0,16},{16,32},{32,48},{48,64},{64,80},{80,96},{96,112},{112,0},{1... | collective-permute-start | bytes 1179656 | tf_op jit(solution)/shard_map/ppermute | solution.py:27
  62.3 1.9 %collective-permute-start.8 = (bf16[192,1024]{1,0:T(8,128)(2,1)S(1)}, bf16[192,1024]{1,0:T(8,128)(2,1)S(1)}, u32[]{:S(2)}, u32[]{:S(2)}) collective-permute-start(bf16[192,1024]{1,0:T(8,128)(2,1)S(1)} %collective-permute-done.6), channel_id=1, source_target_pairs={{0,112},{16,0},{32,16},{48,32},{64,48},{80,64},{96,80},{112,96},{1... | collective-permute-start | bytes 1179656 | tf_op jit(solution)/shard_map/ppermute | solution.py:27
  64.4 3.6 %collective-permute-start.3 = (bf16[256,1536]{1,0:T(8,128)(2,1)S(1)}, bf16[256,1536]{1,0:T(8,128)(2,1)S(1)}, u32[]{:S(2)}, u32[]{:S(2)}) collective-permute-start(bf16[256,1536]{1,0:T(8,128)(2,1)S(1)} %maximum_select_fusion), channel_id=1, source_target_pairs={{0,256},{16,272},{32,288},{48,304},{64,320},{80,336},{96,352},{112... | collective-permute-start | bytes 2359304 | tf_op jit(solution)/shard_map/ppermute | solution.py:22
  68.0 4.9 %collective-permute-start.15 = (bf16[192,1024]{1,0:T(8,128)(2,1)S(1)}, bf16[192,1024]{1,0:T(8,128)(2,1)S(1)}, u32[]{:S(2)}, u32[]{:S(2)}) collective-permute-start(bf16[192,1024]{1,0:T(8,128)(2,1)S(1)} %collective-permute-done.13), channel_id=1, source_target_pairs={{0,16},{16,32},{32,48},{48,64},{64,80},{80,96},{96,112},{112,0},{1... | collective-permute-start | bytes 1179656 | tf_op jit(solution)/shard_map/ppermute | solution.py:27
  72.9 1.9 %collective-permute-start.16 = (bf16[192,1024]{1,0:T(8,128)(2,1)S(1)}, bf16[192,1024]{1,0:T(8,128)(2,1)S(1)}, u32[]{:S(2)}, u32[]{:S(2)}) collective-permute-start(bf16[192,1024]{1,0:T(8,128)(2,1)S(1)} %collective-permute-done.14), channel_id=1, source_target_pairs={{0,112},{16,0},{32,16},{48,32},{64,48},{80,64},{96,80},{112,96},{1... | collective-permute-start | bytes 1179656 | tf_op jit(solution)/shard_map/ppermute | solution.py:27
  74.9 3.2 %collective-permute-start.21 = (bf16[128,1024]{1,0:T(8,128)(2,1)S(1)}, bf16[128,1024]{1,0:T(8,128)(2,1)S(1)}, u32[]{:S(2)}, u32[]{:S(2)}) collective-permute-start(bf16[128,1024]{1,0:T(8,128)(2,1)S(1)} %get-tuple-element.10), channel_id=1, source_target_pairs={{0,128},{16,144},{32,160},{48,176},{64,192},{80,208},{96,224},{112... | collective-permute-start | bytes 786440 | tf_op jit(solution)/shard_map/ppermute | solution.py:22
  78.4 4.3 %collective-permute-start.9 = (bf16[96,1024]{1,0:T(8,128)(2,1)S(1)}, bf16[96,1024]{1,0:T(8,128)(2,1)S(1)}, u32[]{:S(2)}, u32[]{:S(2)}) collective-permute-start(bf16[96,1024]{1,0:T(8,128)(2,1)S(1)} %slice.68), channel_id=1, source_target_pairs={{0,16},{16,32},{32,48},{48,64},{64,80},{80,96},{96,112},{112,0},{1... | collective-permute-start | bytes 589832 | tf_op jit(solution)/shard_map/ppermute | solution.py:27
  82.9 1.9 %collective-permute-start.10 = (bf16[96,1024]{1,0:T(8,128)(2,1)S(1)}, bf16[96,1024]{1,0:T(8,128)(2,1)S(1)}, u32[]{:S(2)}, u32[]{:S(2)}) collective-permute-start(bf16[96,1024]{1,0:T(8,128)(2,1)S(1)} %slice.69), channel_id=1, source_target_pairs={{0,112},{16,0},{32,16},{48,32},{64,48},{80,64},{96,80},{112,96},{1... | collective-permute-start | bytes 589832 | tf_op jit(solution)/shard_map/ppermute | solution.py:27
  84.8 2.4 %collective-permute-done.16 = bf16[192,1024]{1,0:T(8,128)(2,1)S(1)} collective-permute-done((bf16[192,1024]{1,0:T(8,128)(2,1)S(1)}, bf16[192,1024]{1,0:T(8,128)(2,1)S(1)}, u32[]{:S(2)}, u32[]{:S(2)}) %collective-permute-start.16) | collective-permute-done | bytes 393248 | tf_op jit(solution)/shard_map/ppermute | solution.py:27
  87.2 2.2 %collective-permute-start.17 = (bf16[192,1024]{1,0:T(8,128)(2,1)S(1)}, bf16[192,1024]{1,0:T(8,128)(2,1)S(1)}, u32[]{:S(2)}, u32[]{:S(2)}) collective-permute-start(bf16[192,1024]{1,0:T(8,128)(2,1)S(1)} %collective-permute-done.15), channel_id=1, source_target_pairs={{0,16},{16,32},{32,48},{48,64},{64,80},{80,96},{96,112},{112,0},{1... | collective-permute-start | bytes 1179656 | tf_op jit(solution)/shard_map/ppermute | solution.py:27
  89.4 3.1 %collective-permute-start.18 = (bf16[192,1024]{1,0:T(8,128)(2,1)S(1)}, bf16[192,1024]{1,0:T(8,128)(2,1)S(1)}, u32[]{:S(2)}, u32[]{:S(2)}) collective-permute-start(bf16[192,1024]{1,0:T(8,128)(2,1)S(1)} %collective-permute-done.16), channel_id=1, source_target_pairs={{0,112},{16,0},{32,16},{48,32},{64,48},{80,64},{96,80},{112,96},{1... | collective-permute-start | bytes 1179656 | tf_op jit(solution)/shard_map/ppermute | solution.py:27
  92.8 5.9 %collective-permute-done.17 = bf16[192,1024]{1,0:T(8,128)(2,1)S(1)} collective-permute-done((bf16[192,1024]{1,0:T(8,128)(2,1)S(1)}, bf16[192,1024]{1,0:T(8,128)(2,1)S(1)}, u32[]{:S(2)}, u32[]{:S(2)}) %collective-permute-start.17) | collective-permute-done | bytes 393248 | tf_op jit(solution)/shard_map/ppermute | solution.py:27
  98.7 3.0 %collective-permute-start.19 = (bf16[96,1024]{1,0:T(8,128)(2,1)S(1)}, bf16[96,1024]{1,0:T(8,128)(2,1)S(1)}, u32[]{:S(2)}, u32[]{:S(2)}) collective-permute-start(bf16[96,1024]{1,0:T(8,128)(2,1)S(1)} %slice.70), channel_id=1, source_target_pairs={{0,16},{16,32},{32,48},{48,64},{64,80},{80,96},{96,112},{112,0},{1... | collective-permute-start | bytes 589832 | tf_op jit(solution)/shard_map/ppermute | solution.py:27
  101.7 2.3 %collective-permute-start.20 = (bf16[96,1024]{1,0:T(8,128)(2,1)S(1)}, bf16[96,1024]{1,0:T(8,128)(2,1)S(1)}, u32[]{:S(2)}, u32[]{:S(2)}) collective-permute-start(bf16[96,1024]{1,0:T(8,128)(2,1)S(1)} %slice.71), channel_id=1, source_target_pairs={{0,112},{16,0},{32,16},{48,32},{64,48},{80,64},{96,80},{112,96},{1... | collective-permute-start | bytes 589832 | tf_op jit(solution)/shard_map/ppermute | solution.py:27
  104.2 1.0 collective-permute-done.19
  105.2 4.2 %collective-permute-done.20 = bf16[96,1024]{1,0:T(8,128)(2,1)S(1)} collective-permute-done((bf16[96,1024]{1,0:T(8,128)(2,1)S(1)}, bf16[96,1024]{1,0:T(8,128)(2,1)S(1)}, u32[]{:S(2)}, u32[]{:S(2)}) %collective-permute-start.20) | collective-permute-done | bytes 196640 | tf_op jit(solution)/shard_map/ppermute | solution.py:27
  109.4 2.0 %fusion.23 = (f32[256]{0:T(256)S(1)}, f32[256,1024]{1,0:T(8,128)S(1)}) fusion(bf16[3072,1024]{1,0:T(8,128)(2,1)S(1)} %bitcast.101, bf16[256,1536]{1,0:T(8,128)(2,1)S(1)} %collective-permute-done.3, bf16[256,1536]{1,0:T(8,128)(2,1)S(1)} %maximum_select_fusion), kind=kOutput, calls=%fused_computation.76 | convolution fusion | flops 1614282496 | bytes 8913920 | tf_op jit(solution)/shard_map/dot_general | solution.py:176
  112.1 5.7 %collective-permute-start.22 = (f32[8,128]{1,0:T(8,128)S(1)}, f32[8,128]{1,0:T(8,128)S(1)}, u32[]{:S(2)}, u32[]{:S(2)}) collective-permute-start(f32[8,128]{1,0:T(8,128)S(1)} %reshape.153), channel_id=1, source_target_pairs={{0,256},{16,272},{32,288},{48,304},{64,320},{80,336},{96,352},{112... | collective-permute-start | bytes 12296 | tf_op jit(solution)/shard_map/ppermute | solution.py:22
  117.8 0.8 collective-permute-done.22
  118.7 0.7 broadcast_in_dim.10
  119.3 8.2 %all-to-all-start = ((f32[32,8,128]{2,1,0:T(8,128)}), f32[32,8,128]{2,1,0:T(8,128)S(1)}, u32[]{:S(2)}, u32[]{:S(2)}) async-start(f32[32,8,128]{2,1,0:T(8,128)} %bitcast.41), calls=%async_computation | async-start | bytes 262144 | tf_op jit(solution)/shard_map/all_to_all | solution.py:37
  128.1 1.0 copy-done.3
  129.0 8.3 %all-to-all-done = f32[32,8,128]{2,1,0:T(8,128)S(1)} async-done(((f32[32,8,128]{2,1,0:T(8,128)}), f32[32,8,128]{2,1,0:T(8,128)S(1)}, u32[]{:S(2)}, u32[]{:S(2)}) %all-to-all-start) | async-done | bytes 131104 | tf_op jit(solution)/shard_map/all_to_all | solution.py:37
  137.7 2.8 %copy-done.1 = bf16[2,2,8,96,1024]{4,3,2,1,0:T(8,128)(2,1)S(1)} copy-done((bf16[2,2,8,96,1024]{4,3,2,1,0:T(8,128)(2,1)S(1)}, bf16[2,2,8,96,1024]{4,3,2,1,0:T(8,128)(2,1)}, u32[]{:S(2)}) %copy-start.1) | copy-done | bytes 6291480
  140.5 1.2 copy-done.4
  141.7 2.4 %shard_map.69 = (bf16[256,1024]{1,0:T(8,128)(2,1)S(1)}, bf16[2,1536,128]{2,1,0:T(8,128)(2,1)S(1)}) custom-call(f32[256,1024]{1,0:T(8,128)S(1)} %get-tuple-element.12.es_ref, f32[256,1024]{1,0:T(8,128)S(1)} %copy-done.4, f32[256,3]{1,0:T(8,128)S(1)} %copy.75.row_ref, bf16[2,1536,1024]{2,1,0:T(8,128)(2,1)S(1)} %bitcast.102), custom_call_target="tpu_custom_call" | custom-call | flops 1000000000 | bytes 5000000 | tf_op jit(solution)/shard_map/pallas_call | solution.py:121
  144.1 4.0 %collective-permute-start.23 = (bf16[2,1536,128]{2,1,0:T(8,128)(2,1)S(1)}, bf16[2,1536,128]{2,1,0:T(8,128)(2,1)S(1)}, u32[]{:S(2)}, u32[]{:S(2)}) collective-permute-start(bf16[2,1536,128]{2,1,0:T(8,128)(2,1)S(1)} %get-tuple-element.15), channel_id=1, source_target_pairs={{0,256},{16,272},{32,288},{48,304},{64,320},{80,336},{96,352},{112... | collective-permute-start | bytes 2359304 | tf_op jit(solution)/shard_map/ppermute | solution.py:22
  148.2 2.1 %shard_map.70 = f32[2,1536,128]{2,1,0:T(8,128)S(1)} custom-call(bf16[256,1024]{1,0:T(8,128)(2,1)S(1)} %get-tuple-element.14.lg_ref, bf16[2,1536,1024]{2,1,0:T(8,128)(2,1)S(1)} %bitcast.103), custom_call_target="tpu_custom_call" | custom-call | flops 1000000000 | bytes 5000000 | tf_op jit(solution)/shard_map/pallas_call | solution.py:121
  150.3 1.1 add_convert_fusion
  151.4 3.9 %all-to-all-start.1 = ((bf16[32,96,128]{2,1,0:T(8,128)(2,1)}), bf16[32,96,128]{2,1,0:T(8,128)(2,1)S(1)}, u32[]{:S(2)}, u32[]{:S(2)}) async-start(bf16[32,96,128]{2,1,0:T(8,128)(2,1)} %bitcast.52), calls=%async_computation.1 | async-start | bytes 1572864 | tf_op jit(solution)/shard_map/all_to_all | solution.py:37
  155.9 23.0 %all-to-all-done.1 = bf16[32,96,128]{2,1,0:T(8,128)(2,1)S(1)} async-done(((bf16[32,96,128]{2,1,0:T(8,128)(2,1)}), bf16[32,96,128]{2,1,0:T(8,128)(2,1)S(1)}, u32[]{:S(2)}, u32[]{:S(2)}) %all-to-all-start.1) | async-done | bytes 786464 | tf_op jit(solution)/shard_map/all_to_all | solution.py:37
  178.9 0.7 reduce_sum.92
  (82 shorter events, 3.5 us)
Async XLA Ops:
  0.6 29.0 %copy-start.5 = (bf16[128,1536]{1,0:T(8,128)(2,1)S(1)}, bf16[128,1536]{1,0:T(8,128)(2,1)}, u32[]{:S(2)}) copy-start(bf16[128,1536]{1,0:T(8,128)(2,1)} %param.5) | copy-start | bytes 1179652
  1.8 15.1 %collective-permute-start = (bf16[96,1024]{1,0:T(8,128)(2,1)S(1)}, bf16[96,1024]{1,0:T(8,128)(2,1)S(1)}, u32[]{:S(2)}, u32[]{:S(2)}) collective-permute-start(bf16[96,1024]{1,0:T(8,128)(2,1)S(1)} %get-tuple-element.25), channel_id=1, source_target_pairs={{0,256},{16,272},{32,288},{48,304},{64,320},{80,336},{96,352},{112... | collective-permute-start | bytes 589832 | tf_op jit(solution)/shard_map/ppermute | solution.py:22
  5.4 21.6 %collective-permute-start.11 = (bf16[96,2048]{1,0:T(8,128)(2,1)S(1)}, bf16[96,2048]{1,0:T(8,128)(2,1)S(1)}, u32[]{:S(2)}, u32[]{:S(2)}) collective-permute-start(bf16[96,2048]{1,0:T(8,128)(2,1)S(1)} %constant_dynamic-slice_fusion.7), channel_id=1, source_target_pairs={{0,128},{16,144},{32,160},{48,176},{64,192},{80,208},{96,224},{112... | collective-permute-start | bytes 1179656 | tf_op jit(solution)/shard_map/ppermute | solution.py:22
  16.9 12.7 %collective-permute-start.1 = (bf16[192,1024]{1,0:T(8,128)(2,1)S(1)}, bf16[192,1024]{1,0:T(8,128)(2,1)S(1)}, u32[]{:S(2)}, u32[]{:S(2)}) collective-permute-start(bf16[192,1024]{1,0:T(8,128)(2,1)S(1)} %pad_maximum_fusion), channel_id=1, source_target_pairs={{0,16},{16,32},{32,48},{48,64},{64,80},{80,96},{96,112},{112,0},{1... | collective-permute-start | bytes 1179656 | tf_op jit(solution)/shard_map/ppermute | solution.py:27
  21.3 26.9 %collective-permute-start.4 = (bf16[192,1024]{1,0:T(8,128)(2,1)S(1)}, bf16[192,1024]{1,0:T(8,128)(2,1)S(1)}, u32[]{:S(2)}, u32[]{:S(2)}) collective-permute-start(bf16[192,1024]{1,0:T(8,128)(2,1)S(1)} %pad_maximum_fusion), channel_id=1, source_target_pairs={{0,112},{16,0},{32,16},{48,32},{64,48},{80,64},{96,80},{112,96},{1... | collective-permute-start | bytes 1179656 | tf_op jit(solution)/shard_map/ppermute | solution.py:27
  27.0 24.0 %collective-permute-start.12 = (bf16[96,1024]{1,0:T(8,128)(2,1)S(1)}, bf16[96,1024]{1,0:T(8,128)(2,1)S(1)}, u32[]{:S(2)}, u32[]{:S(2)}) collective-permute-start(bf16[96,1024]{1,0:T(8,128)(2,1)S(1)} %get-tuple-element.27), channel_id=1, source_target_pairs={{0,256},{16,272},{32,288},{48,304},{64,320},{80,336},{96,352},{112... | collective-permute-start | bytes 589832 | tf_op jit(solution)/shard_map/ppermute | solution.py:22
  29.6 34.6 %collective-permute-start.2 = (bf16[128,1536]{1,0:T(8,128)(2,1)S(1)}, bf16[128,1536]{1,0:T(8,128)(2,1)S(1)}, u32[]{:S(2)}, u32[]{:S(2)}) collective-permute-start(bf16[128,1536]{1,0:T(8,128)(2,1)S(1)} %copy-done.5), channel_id=1, source_target_pairs={{0,128},{16,144},{32,160},{48,176},{64,192},{80,208},{96,224},{112... | collective-permute-start | bytes 1179656 | tf_op jit(solution)/shard_map/ppermute | solution.py:22
  43.8 13.9 %collective-permute-start.5 = (bf16[192,1024]{1,0:T(8,128)(2,1)S(1)}, bf16[192,1024]{1,0:T(8,128)(2,1)S(1)}, u32[]{:S(2)}, u32[]{:S(2)}) collective-permute-start(bf16[192,1024]{1,0:T(8,128)(2,1)S(1)} %collective-permute-done.1), channel_id=1, source_target_pairs={{0,16},{16,32},{32,48},{48,64},{64,80},{80,96},{96,112},{112,0},{1... | collective-permute-start | bytes 1179656 | tf_op jit(solution)/shard_map/ppermute | solution.py:27
  48.3 14.0 %collective-permute-start.6 = (bf16[192,1024]{1,0:T(8,128)(2,1)S(1)}, bf16[192,1024]{1,0:T(8,128)(2,1)S(1)}, u32[]{:S(2)}, u32[]{:S(2)}) collective-permute-start(bf16[192,1024]{1,0:T(8,128)(2,1)S(1)} %collective-permute-done.4), channel_id=1, source_target_pairs={{0,112},{16,0},{32,16},{48,32},{64,48},{80,64},{96,80},{112,96},{1... | collective-permute-start | bytes 1179656 | tf_op jit(solution)/shard_map/ppermute | solution.py:27
  51.1 16.9 %collective-permute-start.13 = (bf16[192,1024]{1,0:T(8,128)(2,1)S(1)}, bf16[192,1024]{1,0:T(8,128)(2,1)S(1)}, u32[]{:S(2)}, u32[]{:S(2)}) collective-permute-start(bf16[192,1024]{1,0:T(8,128)(2,1)S(1)} %pad_maximum_fusion.1), channel_id=1, source_target_pairs={{0,16},{16,32},{32,48},{48,64},{64,80},{80,96},{96,112},{112,0},{1... | collective-permute-start | bytes 1179656 | tf_op jit(solution)/shard_map/ppermute | solution.py:27
  55.7 17.2 %collective-permute-start.14 = (bf16[192,1024]{1,0:T(8,128)(2,1)S(1)}, bf16[192,1024]{1,0:T(8,128)(2,1)S(1)}, u32[]{:S(2)}, u32[]{:S(2)}) collective-permute-start(bf16[192,1024]{1,0:T(8,128)(2,1)S(1)} %pad_maximum_fusion.1), channel_id=1, source_target_pairs={{0,112},{16,0},{32,16},{48,32},{64,48},{80,64},{96,80},{112,96},{1... | collective-permute-start | bytes 1179656 | tf_op jit(solution)/shard_map/ppermute | solution.py:27
  57.7 17.2 %collective-permute-start.7 = (bf16[192,1024]{1,0:T(8,128)(2,1)S(1)}, bf16[192,1024]{1,0:T(8,128)(2,1)S(1)}, u32[]{:S(2)}, u32[]{:S(2)}) collective-permute-start(bf16[192,1024]{1,0:T(8,128)(2,1)S(1)} %collective-permute-done.5), channel_id=1, source_target_pairs={{0,16},{16,32},{32,48},{48,64},{64,80},{80,96},{96,112},{112,0},{1... | collective-permute-start | bytes 1179656 | tf_op jit(solution)/shard_map/ppermute | solution.py:27
  62.3 16.1 %collective-permute-start.8 = (bf16[192,1024]{1,0:T(8,128)(2,1)S(1)}, bf16[192,1024]{1,0:T(8,128)(2,1)S(1)}, u32[]{:S(2)}, u32[]{:S(2)}) collective-permute-start(bf16[192,1024]{1,0:T(8,128)(2,1)S(1)} %collective-permute-done.6), channel_id=1, source_target_pairs={{0,112},{16,0},{32,16},{48,32},{64,48},{80,64},{96,80},{112,96},{1... | collective-permute-start | bytes 1179656 | tf_op jit(solution)/shard_map/ppermute | solution.py:27
  64.4 45.0 %collective-permute-start.3 = (bf16[256,1536]{1,0:T(8,128)(2,1)S(1)}, bf16[256,1536]{1,0:T(8,128)(2,1)S(1)}, u32[]{:S(2)}, u32[]{:S(2)}) collective-permute-start(bf16[256,1536]{1,0:T(8,128)(2,1)S(1)} %maximum_select_fusion), channel_id=1, source_target_pairs={{0,256},{16,272},{32,288},{48,304},{64,320},{80,336},{96,352},{112... | collective-permute-start | bytes 2359304 | tf_op jit(solution)/shard_map/ppermute | solution.py:22
  68.0 14.8 %collective-permute-start.15 = (bf16[192,1024]{1,0:T(8,128)(2,1)S(1)}, bf16[192,1024]{1,0:T(8,128)(2,1)S(1)}, u32[]{:S(2)}, u32[]{:S(2)}) collective-permute-start(bf16[192,1024]{1,0:T(8,128)(2,1)S(1)} %collective-permute-done.13), channel_id=1, source_target_pairs={{0,16},{16,32},{32,48},{48,64},{64,80},{80,96},{96,112},{112,0},{1... | collective-permute-start | bytes 1179656 | tf_op jit(solution)/shard_map/ppermute | solution.py:27
  72.9 14.3 %collective-permute-start.16 = (bf16[192,1024]{1,0:T(8,128)(2,1)S(1)}, bf16[192,1024]{1,0:T(8,128)(2,1)S(1)}, u32[]{:S(2)}, u32[]{:S(2)}) collective-permute-start(bf16[192,1024]{1,0:T(8,128)(2,1)S(1)} %collective-permute-done.14), channel_id=1, source_target_pairs={{0,112},{16,0},{32,16},{48,32},{64,48},{80,64},{96,80},{112,96},{1... | collective-permute-start | bytes 1179656 | tf_op jit(solution)/shard_map/ppermute | solution.py:27
  74.9 36.5 %collective-permute-start.21 = (bf16[128,1024]{1,0:T(8,128)(2,1)S(1)}, bf16[128,1024]{1,0:T(8,128)(2,1)S(1)}, u32[]{:S(2)}, u32[]{:S(2)}) collective-permute-start(bf16[128,1024]{1,0:T(8,128)(2,1)S(1)} %get-tuple-element.10), channel_id=1, source_target_pairs={{0,128},{16,144},{32,160},{48,176},{64,192},{80,208},{96,224},{112... | collective-permute-start | bytes 786440 | tf_op jit(solution)/shard_map/ppermute | solution.py:22
  78.4 11.0 %collective-permute-start.9 = (bf16[96,1024]{1,0:T(8,128)(2,1)S(1)}, bf16[96,1024]{1,0:T(8,128)(2,1)S(1)}, u32[]{:S(2)}, u32[]{:S(2)}) collective-permute-start(bf16[96,1024]{1,0:T(8,128)(2,1)S(1)} %slice.68), channel_id=1, source_target_pairs={{0,16},{16,32},{32,48},{48,64},{64,80},{80,96},{96,112},{112,0},{1... | collective-permute-start | bytes 589832 | tf_op jit(solution)/shard_map/ppermute | solution.py:27
  82.9 9.6 %collective-permute-start.10 = (bf16[96,1024]{1,0:T(8,128)(2,1)S(1)}, bf16[96,1024]{1,0:T(8,128)(2,1)S(1)}, u32[]{:S(2)}, u32[]{:S(2)}) collective-permute-start(bf16[96,1024]{1,0:T(8,128)(2,1)S(1)} %slice.69), channel_id=1, source_target_pairs={{0,112},{16,0},{32,16},{48,32},{64,48},{80,64},{96,80},{112,96},{1... | collective-permute-start | bytes 589832 | tf_op jit(solution)/shard_map/ppermute | solution.py:27
  87.2 11.5 %collective-permute-start.17 = (bf16[192,1024]{1,0:T(8,128)(2,1)S(1)}, bf16[192,1024]{1,0:T(8,128)(2,1)S(1)}, u32[]{:S(2)}, u32[]{:S(2)}) collective-permute-start(bf16[192,1024]{1,0:T(8,128)(2,1)S(1)} %collective-permute-done.15), channel_id=1, source_target_pairs={{0,16},{16,32},{32,48},{48,64},{64,80},{80,96},{96,112},{112,0},{1... | collective-permute-start | bytes 1179656 | tf_op jit(solution)/shard_map/ppermute | solution.py:27
  89.4 12.3 %collective-permute-start.18 = (bf16[192,1024]{1,0:T(8,128)(2,1)S(1)}, bf16[192,1024]{1,0:T(8,128)(2,1)S(1)}, u32[]{:S(2)}, u32[]{:S(2)}) collective-permute-start(bf16[192,1024]{1,0:T(8,128)(2,1)S(1)} %collective-permute-done.16), channel_id=1, source_target_pairs={{0,112},{16,0},{32,16},{48,32},{64,48},{80,64},{96,80},{112,96},{1... | collective-permute-start | bytes 1179656 | tf_op jit(solution)/shard_map/ppermute | solution.py:27
  98.7 6.4 %collective-permute-start.19 = (bf16[96,1024]{1,0:T(8,128)(2,1)S(1)}, bf16[96,1024]{1,0:T(8,128)(2,1)S(1)}, u32[]{:S(2)}, u32[]{:S(2)}) collective-permute-start(bf16[96,1024]{1,0:T(8,128)(2,1)S(1)} %slice.70), channel_id=1, source_target_pairs={{0,16},{16,32},{32,48},{48,64},{64,80},{80,96},{96,112},{112,0},{1... | collective-permute-start | bytes 589832 | tf_op jit(solution)/shard_map/ppermute | solution.py:27
  101.7 7.6 %collective-permute-start.20 = (bf16[96,1024]{1,0:T(8,128)(2,1)S(1)}, bf16[96,1024]{1,0:T(8,128)(2,1)S(1)}, u32[]{:S(2)}, u32[]{:S(2)}) collective-permute-start(bf16[96,1024]{1,0:T(8,128)(2,1)S(1)} %slice.71), channel_id=1, source_target_pairs={{0,112},{16,0},{32,16},{48,32},{64,48},{80,64},{96,80},{112,96},{1... | collective-permute-start | bytes 589832 | tf_op jit(solution)/shard_map/ppermute | solution.py:27
  109.4 2.7 %copy-start = (bf16[2,2,8,96,1024]{4,3,2,1,0:T(8,128)(2,1)}, bf16[2,2,8,96,1024]{4,3,2,1,0:T(8,128)(2,1)S(1)}, u32[]{:S(2)}) copy-start(bf16[2,2,8,96,1024]{4,3,2,1,0:T(8,128)(2,1)S(1)} %bitcast_dynamic-update-slice_fusion) | copy-start | bytes 18874372
  109.4 9.2 %copy-start.6 = (f32[128]{0:T(128)S(1)}, f32[128]{0:T(128)}, u32[]{:S(2)}) copy-start(f32[128]{0:T(128)} %param.9) | copy-start | bytes 1540
  112.1 6.5 %collective-permute-start.22 = (f32[8,128]{1,0:T(8,128)S(1)}, f32[8,128]{1,0:T(8,128)S(1)}, u32[]{:S(2)}, u32[]{:S(2)}) collective-permute-start(f32[8,128]{1,0:T(8,128)S(1)} %reshape.153), channel_id=1, source_target_pairs={{0,256},{16,272},{32,288},{48,304},{64,320},{80,336},{96,352},{112... | collective-permute-start | bytes 12296 | tf_op jit(solution)/shard_map/ppermute | solution.py:22
  119.3 18.0 %all-to-all-start = ((f32[32,8,128]{2,1,0:T(8,128)}), f32[32,8,128]{2,1,0:T(8,128)S(1)}, u32[]{:S(2)}, u32[]{:S(2)}) async-start(f32[32,8,128]{2,1,0:T(8,128)} %bitcast.41), calls=%async_computation | async-start | bytes 262144 | tf_op jit(solution)/shard_map/all_to_all | solution.py:37
  128.0 1.0 copy-start.3
  137.7 2.8 %copy-start.1 = (bf16[2,2,8,96,1024]{4,3,2,1,0:T(8,128)(2,1)S(1)}, bf16[2,2,8,96,1024]{4,3,2,1,0:T(8,128)(2,1)}, u32[]{:S(2)}) copy-start(bf16[2,2,8,96,1024]{4,3,2,1,0:T(8,128)(2,1)} %copy-done) | copy-start | bytes 18874372
  140.5 1.2 copy-start.4
  141.7 6.5 %copy-start.2 = (bf16[2,2,8,96,1024]{4,3,2,1,0:T(8,128)(2,1)S(1)}, bf16[2,2,8,96,1024]{4,3,2,1,0:T(8,128)(2,1)}, u32[]{:S(2)}) copy-start(bf16[2,2,8,96,1024]{4,3,2,1,0:T(8,128)(2,1)} %copy-done) | copy-start | bytes 18874372
  144.1 6.2 %collective-permute-start.23 = (bf16[2,1536,128]{2,1,0:T(8,128)(2,1)S(1)}, bf16[2,1536,128]{2,1,0:T(8,128)(2,1)S(1)}, u32[]{:S(2)}, u32[]{:S(2)}) collective-permute-start(bf16[2,1536,128]{2,1,0:T(8,128)(2,1)S(1)} %get-tuple-element.15), channel_id=1, source_target_pairs={{0,256},{16,272},{32,288},{48,304},{64,320},{80,336},{96,352},{112... | collective-permute-start | bytes 2359304 | tf_op jit(solution)/shard_map/ppermute | solution.py:22
  151.4 27.5 %all-to-all-start.1 = ((bf16[32,96,128]{2,1,0:T(8,128)(2,1)}), bf16[32,96,128]{2,1,0:T(8,128)(2,1)S(1)}, u32[]{:S(2)}, u32[]{:S(2)}) async-start(bf16[32,96,128]{2,1,0:T(8,128)(2,1)} %bitcast.52), calls=%async_computation.1 | async-start | bytes 1572864 | tf_op jit(solution)/shard_map/all_to_all | solution.py:37

commit v11 on v8

--- a/solution.py
+++ b/solution.py
@@ -129,9 +129,10 @@
             zh == 0, jnp.concatenate([mine, other]), jnp.concatenate([other, mine])
         )
 
-    near = jnp.concatenate([columns(head, 0, 0), flip(columns(head, 1, 0), 1, 0)], axis=0)
+    away = lax.dynamic_slice_in_dim(head, (zh ^ 1) * 2 * width, 2 * width, axis=1)
+    first = after(head, away)
+    near = jnp.concatenate([columns(first, 0, 0), flip(columns(first, 1, 0), 1, 0)], axis=0)
     near_parts = ring(near)
-    away = lax.dynamic_slice_in_dim(head, (zh ^ 1) * 2 * width, 2 * width, axis=1)
     came = flip(away, 0, 1)
     came_mine = lax.dynamic_slice_in_dim(came, s * width, width, axis=1)
     came_send = lax.dynamic_slice_in_dim(came, (s ^ 1) * width, width, axis=1)

time: 179 us -> 175 us (0.978)
  starting transfers between devices: 99.6 us -> 95.7 us
    ppermute x8, starting transfers between devices: 46.4 us -> 42.5 us  [flip(): return lax.ppermute(x, ('section', 'dp'), perm)]
  transfers between devices with their start and end apart: 25 -> 25, of which waited for: 7 -> 8; matrix products, arithmetic and copies ran while one was open for 5% -> 6% of each run, Pallas kernels for 1% -> 1%
where the time goes in v11:
time: 175 us; the launch traced here: 174 us
  starting transfers between devices  95.7 us (55%)
  waiting for transfers between devices  37.8 us (22%)
  blocking collectives  17.8 us (10%)
  local copies, waits for them, and re-layouts  7.43 us (4%)
  other arithmetic  7.04 us (4%)
  Pallas kernels  4.68 us (3%)
  matrix products  2 us (1%)
    ppermute x16, starting transfers between devices, along_y(): return lax.ppermute(x, 'dp', perm)  49.2 us
    ppermute x8, starting transfers between devices, flip(): return lax.ppermute(x, ('section', 'dp'), perm)  42.5 us
    all_to_all x1, waiting for transfers between devices, exchange(): lax.all_to_all(x, ('section', 'dp', 'vocab'), split_axis=0, concat_axis=0...  23 us
    all_to_all x1, blocking collectives, exchange(): lax.all_to_all(x, ('section', 'dp', 'vocab'), split_axis=0, concat_axis=0...  17.8 us
    ppermute x16, waiting for transfers between devices, along_y(): return lax.ppermute(x, 'dp', perm)  13.7 us
    pallas_call x2, Pallas kernels, over_tiles(): pl.pallas_call(kernel, grid=(feats // TILE,), in_specs=[whole] * len(ins)...  4.68 us
    all_to_all x1, starting transfers between devices, exchange(): lax.all_to_all(x, ('section', 'dp', 'vocab'), split_axis=0, concat_axis=0...  3.91 us
  transfers between devices with their start and end apart: 25, of which 8 were waited for; matrix products, arithmetic and copies ran while one was open for 6% of the time, Pallas kernels for 1%

profile of v11, /device:TPU:25, one launch (start us, length us, event | category | flops | bytes accessed | tf_op | source)
XLA Modules:
  0.0 174.0 jit_solution(1070971464077232588)
XLA Ops:
  0.7 1.1 constant_dynamic-slice_fusion.9
  1.7 10.6 %collective-permute-start.11 = (bf16[96,2048]{1,0:T(8,128)(2,1)S(1)}, bf16[96,2048]{1,0:T(8,128)(2,1)S(1)}, u32[]{:S(2)}, u32[]{:S(2)}) collective-permute-start(bf16[96,2048]{1,0:T(8,128)(2,1)S(1)} %constant_dynamic-slice_fusion.9), channel_id=1, source_target_pairs={{0,128},{16,144},{32,160},{48,176},{64,192},{80,208},{96,224},{112... | collective-permute-start | bytes 1179656 | tf_op jit(solution)/shard_map/ppermute | solution.py:22
  12.4 1.1 constant_dynamic-slice_fusion.8
  13.5 2.9 %collective-permute-start = (bf16[96,1024]{1,0:T(8,128)(2,1)S(1)}, bf16[96,1024]{1,0:T(8,128)(2,1)S(1)}, u32[]{:S(2)}, u32[]{:S(2)}) collective-permute-start(bf16[96,1024]{1,0:T(8,128)(2,1)S(1)} %get-tuple-element.21), channel_id=1, source_target_pairs={{0,256},{16,272},{32,288},{48,304},{64,320},{80,336},{96,352},{112... | collective-permute-start | bytes 589832 | tf_op jit(solution)/shard_map/ppermute | solution.py:22
  16.3 0.7 exponential_multiply_fusion
  17.2 0.2 collective-permute-done
  17.4 4.4 %collective-permute-start.1 = (bf16[192,1024]{1,0:T(8,128)(2,1)S(1)}, bf16[192,1024]{1,0:T(8,128)(2,1)S(1)}, u32[]{:S(2)}, u32[]{:S(2)}) collective-permute-start(bf16[192,1024]{1,0:T(8,128)(2,1)S(1)} %pad_maximum_fusion), channel_id=1, source_target_pairs={{0,16},{16,32},{32,48},{48,64},{64,80},{80,96},{96,112},{112,0},{1... | collective-permute-start | bytes 1179656 | tf_op jit(solution)/shard_map/ppermute | solution.py:27
  21.8 1.9 %collective-permute-start.4 = (bf16[192,1024]{1,0:T(8,128)(2,1)S(1)}, bf16[192,1024]{1,0:T(8,128)(2,1)S(1)}, u32[]{:S(2)}, u32[]{:S(2)}) collective-permute-start(bf16[192,1024]{1,0:T(8,128)(2,1)S(1)} %pad_maximum_fusion), channel_id=1, source_target_pairs={{0,112},{16,0},{32,16},{48,32},{64,48},{80,64},{96,80},{112,96},{1... | collective-permute-start | bytes 1179656 | tf_op jit(solution)/shard_map/ppermute | solution.py:27
  23.8 0.6 mul.60
  24.4 2.9 %fusion = bf16[128,4096]{1,0:T(8,128)(2,1)S(1)} fusion(f32[16,8,32,128]{3,2,1,0:T(8,128)S(1)} %bitcast.103, s32[128,4096]{1,0:T(8,128)} %param.7), kind=kLoop, calls=%fused_computation.1 | loop fusion | flops 1572864 | bytes 5242880 | tf_op jit(solution)/shard_map/convert_element_type | solution.py:51
  27.5 2.6 %collective-permute-start.12 = (bf16[96,1024]{1,0:T(8,128)(2,1)S(1)}, bf16[96,1024]{1,0:T(8,128)(2,1)S(1)}, u32[]{:S(2)}, u32[]{:S(2)}) collective-permute-start(bf16[96,1024]{1,0:T(8,128)(2,1)S(1)} %get-tuple-element.23), channel_id=1, source_target_pairs={{0,256},{16,272},{32,288},{48,304},{64,320},{80,336},{96,352},{112... | collective-permute-start | bytes 589832 | tf_op jit(solution)/shard_map/ppermute | solution.py:22
  30.2 10.0 %collective-permute-start.2 = (bf16[128,1536]{1,0:T(8,128)(2,1)S(1)}, bf16[128,1536]{1,0:T(8,128)(2,1)S(1)}, u32[]{:S(2)}, u32[]{:S(2)}) collective-permute-start(bf16[128,1536]{1,0:T(8,128)(2,1)S(1)} %copy-done.3), channel_id=1, source_target_pairs={{0,128},{16,144},{32,160},{48,176},{64,192},{80,208},{96,224},{112... | collective-permute-start | bytes 1179656 | tf_op jit(solution)/shard_map/ppermute | solution.py:22
  40.2 4.4 %collective-permute-start.5 = (bf16[192,1024]{1,0:T(8,128)(2,1)S(1)}, bf16[192,1024]{1,0:T(8,128)(2,1)S(1)}, u32[]{:S(2)}, u32[]{:S(2)}) collective-permute-start(bf16[192,1024]{1,0:T(8,128)(2,1)S(1)} %collective-permute-done.1), channel_id=1, source_target_pairs={{0,16},{16,32},{32,48},{48,64},{64,80},{80,96},{96,112},{112,0},{1... | collective-permute-start | bytes 1179656 | tf_op jit(solution)/shard_map/ppermute | solution.py:27
  44.6 1.9 %collective-permute-start.6 = (bf16[192,1024]{1,0:T(8,128)(2,1)S(1)}, bf16[192,1024]{1,0:T(8,128)(2,1)S(1)}, u32[]{:S(2)}, u32[]{:S(2)}) collective-permute-start(bf16[192,1024]{1,0:T(8,128)(2,1)S(1)} %collective-permute-done.4), channel_id=1, source_target_pairs={{0,112},{16,0},{32,16},{48,32},{64,48},{80,64},{96,80},{112,96},{1... | collective-permute-start | bytes 1179656 | tf_op jit(solution)/shard_map/ppermute | solution.py:27
  46.5 0.8 broadcast_in_dim.6
  47.4 4.6 %collective-permute-start.13 = (bf16[192,1024]{1,0:T(8,128)(2,1)S(1)}, bf16[192,1024]{1,0:T(8,128)(2,1)S(1)}, u32[]{:S(2)}, u32[]{:S(2)}) collective-permute-start(bf16[192,1024]{1,0:T(8,128)(2,1)S(1)} %pad_maximum_fusion.1), channel_id=1, source_target_pairs={{0,16},{16,32},{32,48},{48,64},{64,80},{80,96},{96,112},{112,0},{1... | collective-permute-start | bytes 1179656 | tf_op jit(solution)/shard_map/ppermute | solution.py:27
  52.0 1.9 %collective-permute-start.14 = (bf16[192,1024]{1,0:T(8,128)(2,1)S(1)}, bf16[192,1024]{1,0:T(8,128)(2,1)S(1)}, u32[]{:S(2)}, u32[]{:S(2)}) collective-permute-start(bf16[192,1024]{1,0:T(8,128)(2,1)S(1)} %pad_maximum_fusion.1), channel_id=1, source_target_pairs={{0,112},{16,0},{32,16},{48,32},{64,48},{80,64},{96,80},{112,96},{1... | collective-permute-start | bytes 1179656 | tf_op jit(solution)/shard_map/ppermute | solution.py:27
  54.0 4.6 %collective-permute-start.7 = (bf16[192,1024]{1,0:T(8,128)(2,1)S(1)}, bf16[192,1024]{1,0:T(8,128)(2,1)S(1)}, u32[]{:S(2)}, u32[]{:S(2)}) collective-permute-start(bf16[192,1024]{1,0:T(8,128)(2,1)S(1)} %collective-permute-done.5), channel_id=1, source_target_pairs={{0,16},{16,32},{32,48},{48,64},{64,80},{80,96},{96,112},{112,0},{1... | collective-permute-start | bytes 1179656 | tf_op jit(solution)/shard_map/ppermute | solution.py:27
  58.6 1.9 %collective-permute-start.8 = (bf16[192,1024]{1,0:T(8,128)(2,1)S(1)}, bf16[192,1024]{1,0:T(8,128)(2,1)S(1)}, u32[]{:S(2)}, u32[]{:S(2)}) collective-permute-start(bf16[192,1024]{1,0:T(8,128)(2,1)S(1)} %collective-permute-done.6), channel_id=1, source_target_pairs={{0,112},{16,0},{32,16},{48,32},{64,48},{80,64},{96,80},{112,96},{1... | collective-permute-start | bytes 1179656 | tf_op jit(solution)/shard_map/ppermute | solution.py:27
  60.7 3.6 %collective-permute-start.3 = (bf16[256,1536]{1,0:T(8,128)(2,1)S(1)}, bf16[256,1536]{1,0:T(8,128)(2,1)S(1)}, u32[]{:S(2)}, u32[]{:S(2)}) collective-permute-start(bf16[256,1536]{1,0:T(8,128)(2,1)S(1)} %maximum_select_fusion), channel_id=1, source_target_pairs={{0,256},{16,272},{32,288},{48,304},{64,320},{80,336},{96,352},{112... | collective-permute-start | bytes 2359304 | tf_op jit(solution)/shard_map/ppermute | solution.py:22
  64.3 4.9 %collective-permute-start.15 = (bf16[192,1024]{1,0:T(8,128)(2,1)S(1)}, bf16[192,1024]{1,0:T(8,128)(2,1)S(1)}, u32[]{:S(2)}, u32[]{:S(2)}) collective-permute-start(bf16[192,1024]{1,0:T(8,128)(2,1)S(1)} %collective-permute-done.13), channel_id=1, source_target_pairs={{0,16},{16,32},{32,48},{48,64},{64,80},{80,96},{96,112},{112,0},{1... | collective-permute-start | bytes 1179656 | tf_op jit(solution)/shard_map/ppermute | solution.py:27
  69.2 1.9 %collective-permute-start.16 = (bf16[192,1024]{1,0:T(8,128)(2,1)S(1)}, bf16[192,1024]{1,0:T(8,128)(2,1)S(1)}, u32[]{:S(2)}, u32[]{:S(2)}) collective-permute-start(bf16[192,1024]{1,0:T(8,128)(2,1)S(1)} %collective-permute-done.14), channel_id=1, source_target_pairs={{0,112},{16,0},{32,16},{48,32},{64,48},{80,64},{96,80},{112,96},{1... | collective-permute-start | bytes 1179656 | tf_op jit(solution)/shard_map/ppermute | solution.py:27
  71.3 3.2 %collective-permute-start.21 = (bf16[128,1024]{1,0:T(8,128)(2,1)S(1)}, bf16[128,1024]{1,0:T(8,128)(2,1)S(1)}, u32[]{:S(2)}, u32[]{:S(2)}) collective-permute-start(bf16[128,1024]{1,0:T(8,128)(2,1)S(1)} %get-tuple-element.9), channel_id=1, source_target_pairs={{0,128},{16,144},{32,160},{48,176},{64,192},{80,208},{96,224},{112... | collective-permute-start | bytes 786440 | tf_op jit(solution)/shard_map/ppermute | solution.py:22
  74.5 0.2 collective-permute-done.8
  74.7 4.3 %collective-permute-start.9 = (bf16[96,1024]{1,0:T(8,128)(2,1)S(1)}, bf16[96,1024]{1,0:T(8,128)(2,1)S(1)}, u32[]{:S(2)}, u32[]{:S(2)}) collective-permute-start(bf16[96,1024]{1,0:T(8,128)(2,1)S(1)} %slice.68), channel_id=1, source_target_pairs={{0,16},{16,32},{32,48},{48,64},{64,80},{80,96},{96,112},{112,0},{1... | collective-permute-start | bytes 589832 | tf_op jit(solution)/shard_map/ppermute | solution.py:27
  79.2 1.9 %collective-permute-start.10 = (bf16[96,1024]{1,0:T(8,128)(2,1)S(1)}, bf16[96,1024]{1,0:T(8,128)(2,1)S(1)}, u32[]{:S(2)}, u32[]{:S(2)}) collective-permute-start(bf16[96,1024]{1,0:T(8,128)(2,1)S(1)} %slice.69), channel_id=1, source_target_pairs={{0,112},{16,0},{32,16},{48,32},{64,48},{80,64},{96,80},{112,96},{1... | collective-permute-start | bytes 589832 | tf_op jit(solution)/shard_map/ppermute | solution.py:27
  81.1 2.4 %collective-permute-done.16 = bf16[192,1024]{1,0:T(8,128)(2,1)S(1)} collective-permute-done((bf16[192,1024]{1,0:T(8,128)(2,1)S(1)}, bf16[192,1024]{1,0:T(8,128)(2,1)S(1)}, u32[]{:S(2)}, u32[]{:S(2)}) %collective-permute-start.16) | collective-permute-done | bytes 393248 | tf_op jit(solution)/shard_map/ppermute | solution.py:27
  83.5 2.2 %collective-permute-start.17 = (bf16[192,1024]{1,0:T(8,128)(2,1)S(1)}, bf16[192,1024]{1,0:T(8,128)(2,1)S(1)}, u32[]{:S(2)}, u32[]{:S(2)}) collective-permute-start(bf16[192,1024]{1,0:T(8,128)(2,1)S(1)} %collective-permute-done.15), channel_id=1, source_target_pairs={{0,16},{16,32},{32,48},{48,64},{64,80},{80,96},{96,112},{112,0},{1... | collective-permute-start | bytes 1179656 | tf_op jit(solution)/shard_map/ppermute | solution.py:27
  85.7 3.1 %collective-permute-start.18 = (bf16[192,1024]{1,0:T(8,128)(2,1)S(1)}, bf16[192,1024]{1,0:T(8,128)(2,1)S(1)}, u32[]{:S(2)}, u32[]{:S(2)}) collective-permute-start(bf16[192,1024]{1,0:T(8,128)(2,1)S(1)} %collective-permute-done.16), channel_id=1, source_target_pairs={{0,112},{16,0},{32,16},{48,32},{64,48},{80,64},{96,80},{112,96},{1... | collective-permute-start | bytes 1179656 | tf_op jit(solution)/shard_map/ppermute | solution.py:27
  89.1 5.9 %collective-permute-done.17 = bf16[192,1024]{1,0:T(8,128)(2,1)S(1)} collective-permute-done((bf16[192,1024]{1,0:T(8,128)(2,1)S(1)}, bf16[192,1024]{1,0:T(8,128)(2,1)S(1)}, u32[]{:S(2)}, u32[]{:S(2)}) %collective-permute-start.17) | collective-permute-done | bytes 393248 | tf_op jit(solution)/shard_map/ppermute | solution.py:27
  95.1 3.0 %collective-permute-start.19 = (bf16[96,1024]{1,0:T(8,128)(2,1)S(1)}, bf16[96,1024]{1,0:T(8,128)(2,1)S(1)}, u32[]{:S(2)}, u32[]{:S(2)}) collective-permute-start(bf16[96,1024]{1,0:T(8,128)(2,1)S(1)} %slice.70), channel_id=1, source_target_pairs={{0,16},{16,32},{32,48},{48,64},{64,80},{80,96},{96,112},{112,0},{1... | collective-permute-start | bytes 589832 | tf_op jit(solution)/shard_map/ppermute | solution.py:27
  98.1 2.3 %collective-permute-start.20 = (bf16[96,1024]{1,0:T(8,128)(2,1)S(1)}, bf16[96,1024]{1,0:T(8,128)(2,1)S(1)}, u32[]{:S(2)}, u32[]{:S(2)}) collective-permute-start(bf16[96,1024]{1,0:T(8,128)(2,1)S(1)} %slice.71), channel_id=1, source_target_pairs={{0,112},{16,0},{32,16},{48,32},{64,48},{80,64},{96,80},{112,96},{1... | collective-permute-start | bytes 589832 | tf_op jit(solution)/shard_map/ppermute | solution.py:27
  100.5 1.0 collective-permute-done.19
  101.5 4.2 %collective-permute-done.20 = bf16[96,1024]{1,0:T(8,128)(2,1)S(1)} collective-permute-done((bf16[96,1024]{1,0:T(8,128)(2,1)S(1)}, bf16[96,1024]{1,0:T(8,128)(2,1)S(1)}, u32[]{:S(2)}, u32[]{:S(2)}) %collective-permute-start.20) | collective-permute-done | bytes 196640 | tf_op jit(solution)/shard_map/ppermute | solution.py:27
  105.8 2.0 %fusion.23 = (f32[256]{0:T(256)S(1)}, f32[256,1024]{1,0:T(8,128)S(1)}) fusion(bf16[3072,1024]{1,0:T(8,128)(2,1)S(1)} %bitcast.100, bf16[256,1536]{1,0:T(8,128)(2,1)S(1)} %collective-permute-done.3, bf16[256,1536]{1,0:T(8,128)(2,1)S(1)} %maximum_select_fusion), kind=kOutput, calls=%fused_computation.74 | convolution fusion | flops 1614282496 | bytes 8913920 | tf_op jit(solution)/shard_map/dot_general | solution.py:158
  107.8 0.6 exponential_reduce_fusion
  108.4 5.7 %collective-permute-start.22 = (f32[8,128]{1,0:T(8,128)S(1)}, f32[8,128]{1,0:T(8,128)S(1)}, u32[]{:S(2)}, u32[]{:S(2)}) collective-permute-start(f32[8,128]{1,0:T(8,128)S(1)} %reshape.130), channel_id=1, source_target_pairs={{0,256},{16,272},{32,288},{48,304},{64,320},{80,336},{96,352},{112... | collective-permute-start | bytes 12296 | tf_op jit(solution)/shard_map/ppermute | solution.py:22
  114.1 0.8 collective-permute-done.22
  115.0 17.8 %all_to_all.10 = f32[32,8,128]{2,1,0:T(8,128)S(1)} all-to-all(f32[32,8,128]{2,1,0:T(8,128)S(1)} %bitcast.110), channel_id=1, replica_groups={{0,1,2,3,4,5,6,7,8,9,10,11,12,13,14,15,128,129,130,131,132,133,134,135,..., dimensions={0} | all-to-all | bytes 262144 | tf_op jit(solution)/shard_map/all_to_all | solution.py:37
  133.2 2.8 %copy-done.1 = bf16[2,2,8,96,1024]{4,3,2,1,0:T(8,128)(2,1)S(1)} copy-done((bf16[2,2,8,96,1024]{4,3,2,1,0:T(8,128)(2,1)S(1)}, bf16[2,2,8,96,1024]{4,3,2,1,0:T(8,128)(2,1)}, u32[]{:S(2)}) %copy-start.1) | copy-done | bytes 6291480
  135.9 2.5 %shard_map.68 = (bf16[256,1024]{1,0:T(8,128)(2,1)S(1)}, bf16[2,1536,128]{2,1,0:T(8,128)(2,1)S(1)}) custom-call(f32[256,1024]{1,0:T(8,128)S(1)} %get-tuple-element.27.s_ref, bf16[256,1024]{1,0:T(8,128)(2,1)S(1)} %get-tuple-element.17.t_ref, f32[256,3]{1,0:T(8,128)S(1)} %copy.71.row_ref, bf16[2,1536,1024]{2,1,0:T(8,128)(2,1)S(1)} %bitcast.101), custom_call_target="tpu_custom_call" | custom-call | flops 1000000000 | bytes 5000000 | tf_op jit(solution)/shard_map/pallas_call | solution.py:102
  138.5 4.0 %collective-permute-start.23 = (bf16[2,1536,128]{2,1,0:T(8,128)(2,1)S(1)}, bf16[2,1536,128]{2,1,0:T(8,128)(2,1)S(1)}, u32[]{:S(2)}, u32[]{:S(2)}) collective-permute-start(bf16[2,1536,128]{2,1,0:T(8,128)(2,1)S(1)} %get-tuple-element.11), channel_id=1, source_target_pairs={{0,256},{16,272},{32,288},{48,304},{64,320},{80,336},{96,352},{112... | collective-permute-start | bytes 2359304 | tf_op jit(solution)/shard_map/ppermute | solution.py:22
  142.5 2.1 %shard_map.69 = f32[2,1536,128]{2,1,0:T(8,128)S(1)} custom-call(bf16[256,1024]{1,0:T(8,128)(2,1)S(1)} %get-tuple-element.10.lg_ref, bf16[2,1536,1024]{2,1,0:T(8,128)(2,1)S(1)} %bitcast.102), custom_call_target="tpu_custom_call" | custom-call | flops 1000000000 | bytes 5000000 | tf_op jit(solution)/shard_map/pallas_call | solution.py:102
  144.7 1.1 add_convert_fusion
  145.8 3.9 %all-to-all-start.1 = ((bf16[32,96,128]{2,1,0:T(8,128)(2,1)}), bf16[32,96,128]{2,1,0:T(8,128)(2,1)S(1)}, u32[]{:S(2)}, u32[]{:S(2)}) async-start(bf16[32,96,128]{2,1,0:T(8,128)(2,1)} %bitcast.51), calls=%async_computation.1 | async-start | bytes 1572864 | tf_op jit(solution)/shard_map/all_to_all | solution.py:37
  149.7 0.5 fusion.20
  150.3 23.0 %all-to-all-done.1 = bf16[32,96,128]{2,1,0:T(8,128)(2,1)S(1)} async-done(((bf16[32,96,128]{2,1,0:T(8,128)(2,1)}), bf16[32,96,128]{2,1,0:T(8,128)(2,1)S(1)}, u32[]{:S(2)}, u32[]{:S(2)}) %all-to-all-start.1) | async-done | bytes 786464 | tf_op jit(solution)/shard_map/all_to_all | solution.py:37
  173.2 0.7 reduce_sum.92
  (75 shorter events, 1.6 us)
Async XLA Ops:
  0.6 29.5 %copy-start.3 = (bf16[128,1536]{1,0:T(8,128)(2,1)S(1)}, bf16[128,1536]{1,0:T(8,128)(2,1)}, u32[]{:S(2)}) copy-start(bf16[128,1536]{1,0:T(8,128)(2,1)} %param.5) | copy-start | bytes 1179652
  1.7 25.8 %collective-permute-start.11 = (bf16[96,2048]{1,0:T(8,128)(2,1)S(1)}, bf16[96,2048]{1,0:T(8,128)(2,1)S(1)}, u32[]{:S(2)}, u32[]{:S(2)}) collective-permute-start(bf16[96,2048]{1,0:T(8,128)(2,1)S(1)} %constant_dynamic-slice_fusion.9), channel_id=1, source_target_pairs={{0,128},{16,144},{32,160},{48,176},{64,192},{80,208},{96,224},{112... | collective-permute-start | bytes 1179656 | tf_op jit(solution)/shard_map/ppermute | solution.py:22
  13.5 3.9 %collective-permute-start = (bf16[96,1024]{1,0:T(8,128)(2,1)S(1)}, bf16[96,1024]{1,0:T(8,128)(2,1)S(1)}, u32[]{:S(2)}, u32[]{:S(2)}) collective-permute-start(bf16[96,1024]{1,0:T(8,128)(2,1)S(1)} %get-tuple-element.21), channel_id=1, source_target_pairs={{0,256},{16,272},{32,288},{48,304},{64,320},{80,336},{96,352},{112... | collective-permute-start | bytes 589832 | tf_op jit(solution)/shard_map/ppermute | solution.py:22
  17.4 12.7 %collective-permute-start.1 = (bf16[192,1024]{1,0:T(8,128)(2,1)S(1)}, bf16[192,1024]{1,0:T(8,128)(2,1)S(1)}, u32[]{:S(2)}, u32[]{:S(2)}) collective-permute-start(bf16[192,1024]{1,0:T(8,128)(2,1)S(1)} %pad_maximum_fusion), channel_id=1, source_target_pairs={{0,16},{16,32},{32,48},{48,64},{64,80},{80,96},{96,112},{112,0},{1... | collective-permute-start | bytes 1179656 | tf_op jit(solution)/shard_map/ppermute | solution.py:27
  21.8 22.8 %collective-permute-start.4 = (bf16[192,1024]{1,0:T(8,128)(2,1)S(1)}, bf16[192,1024]{1,0:T(8,128)(2,1)S(1)}, u32[]{:S(2)}, u32[]{:S(2)}) collective-permute-start(bf16[192,1024]{1,0:T(8,128)(2,1)S(1)} %pad_maximum_fusion), channel_id=1, source_target_pairs={{0,112},{16,0},{32,16},{48,32},{64,48},{80,64},{96,80},{112,96},{1... | collective-permute-start | bytes 1179656 | tf_op jit(solution)/shard_map/ppermute | solution.py:27
  27.5 19.8 %collective-permute-start.12 = (bf16[96,1024]{1,0:T(8,128)(2,1)S(1)}, bf16[96,1024]{1,0:T(8,128)(2,1)S(1)}, u32[]{:S(2)}, u32[]{:S(2)}) collective-permute-start(bf16[96,1024]{1,0:T(8,128)(2,1)S(1)} %get-tuple-element.23), channel_id=1, source_target_pairs={{0,256},{16,272},{32,288},{48,304},{64,320},{80,336},{96,352},{112... | collective-permute-start | bytes 589832 | tf_op jit(solution)/shard_map/ppermute | solution.py:22
  30.2 30.4 %collective-permute-start.2 = (bf16[128,1536]{1,0:T(8,128)(2,1)S(1)}, bf16[128,1536]{1,0:T(8,128)(2,1)S(1)}, u32[]{:S(2)}, u32[]{:S(2)}) collective-permute-start(bf16[128,1536]{1,0:T(8,128)(2,1)S(1)} %copy-done.3), channel_id=1, source_target_pairs={{0,128},{16,144},{32,160},{48,176},{64,192},{80,208},{96,224},{112... | collective-permute-start | bytes 1179656 | tf_op jit(solution)/shard_map/ppermute | solution.py:22
  40.2 13.9 %collective-permute-start.5 = (bf16[192,1024]{1,0:T(8,128)(2,1)S(1)}, bf16[192,1024]{1,0:T(8,128)(2,1)S(1)}, u32[]{:S(2)}, u32[]{:S(2)}) collective-permute-start(bf16[192,1024]{1,0:T(8,128)(2,1)S(1)} %collective-permute-done.1), channel_id=1, source_target_pairs={{0,16},{16,32},{32,48},{48,64},{64,80},{80,96},{96,112},{112,0},{1... | collective-permute-start | bytes 1179656 | tf_op jit(solution)/shard_map/ppermute | solution.py:27
  44.6 14.0 %collective-permute-start.6 = (bf16[192,1024]{1,0:T(8,128)(2,1)S(1)}, bf16[192,1024]{1,0:T(8,128)(2,1)S(1)}, u32[]{:S(2)}, u32[]{:S(2)}) collective-permute-start(bf16[192,1024]{1,0:T(8,128)(2,1)S(1)} %collective-permute-done.4), channel_id=1, source_target_pairs={{0,112},{16,0},{32,16},{48,32},{64,48},{80,64},{96,80},{112,96},{1... | collective-permute-start | bytes 1179656 | tf_op jit(solution)/shard_map/ppermute | solution.py:27
  47.4 16.9 %collective-permute-start.13 = (bf16[192,1024]{1,0:T(8,128)(2,1)S(1)}, bf16[192,1024]{1,0:T(8,128)(2,1)S(1)}, u32[]{:S(2)}, u32[]{:S(2)}) collective-permute-start(bf16[192,1024]{1,0:T(8,128)(2,1)S(1)} %pad_maximum_fusion.1), channel_id=1, source_target_pairs={{0,16},{16,32},{32,48},{48,64},{64,80},{80,96},{96,112},{112,0},{1... | collective-permute-start | bytes 1179656 | tf_op jit(solution)/shard_map/ppermute | solution.py:27
  52.0 17.2 %collective-permute-start.14 = (bf16[192,1024]{1,0:T(8,128)(2,1)S(1)}, bf16[192,1024]{1,0:T(8,128)(2,1)S(1)}, u32[]{:S(2)}, u32[]{:S(2)}) collective-permute-start(bf16[192,1024]{1,0:T(8,128)(2,1)S(1)} %pad_maximum_fusion.1), channel_id=1, source_target_pairs={{0,112},{16,0},{32,16},{48,32},{64,48},{80,64},{96,80},{112,96},{1... | collective-permute-start | bytes 1179656 | tf_op jit(solution)/shard_map/ppermute | solution.py:27
  54.0 17.2 %collective-permute-start.7 = (bf16[192,1024]{1,0:T(8,128)(2,1)S(1)}, bf16[192,1024]{1,0:T(8,128)(2,1)S(1)}, u32[]{:S(2)}, u32[]{:S(2)}) collective-permute-start(bf16[192,1024]{1,0:T(8,128)(2,1)S(1)} %collective-permute-done.5), channel_id=1, source_target_pairs={{0,16},{16,32},{32,48},{48,64},{64,80},{80,96},{96,112},{112,0},{1... | collective-permute-start | bytes 1179656 | tf_op jit(solution)/shard_map/ppermute | solution.py:27
  58.6 16.1 %collective-permute-start.8 = (bf16[192,1024]{1,0:T(8,128)(2,1)S(1)}, bf16[192,1024]{1,0:T(8,128)(2,1)S(1)}, u32[]{:S(2)}, u32[]{:S(2)}) collective-permute-start(bf16[192,1024]{1,0:T(8,128)(2,1)S(1)} %collective-permute-done.6), channel_id=1, source_target_pairs={{0,112},{16,0},{32,16},{48,32},{64,48},{80,64},{96,80},{112,96},{1... | collective-permute-start | bytes 1179656 | tf_op jit(solution)/shard_map/ppermute | solution.py:27
  60.7 45.0 %collective-permute-start.3 = (bf16[256,1536]{1,0:T(8,128)(2,1)S(1)}, bf16[256,1536]{1,0:T(8,128)(2,1)S(1)}, u32[]{:S(2)}, u32[]{:S(2)}) collective-permute-start(bf16[256,1536]{1,0:T(8,128)(2,1)S(1)} %maximum_select_fusion), channel_id=1, source_target_pairs={{0,256},{16,272},{32,288},{48,304},{64,320},{80,336},{96,352},{112... | collective-permute-start | bytes 2359304 | tf_op jit(solution)/shard_map/ppermute | solution.py:22
  64.3 14.8 %collective-permute-start.15 = (bf16[192,1024]{1,0:T(8,128)(2,1)S(1)}, bf16[192,1024]{1,0:T(8,128)(2,1)S(1)}, u32[]{:S(2)}, u32[]{:S(2)}) collective-permute-start(bf16[192,1024]{1,0:T(8,128)(2,1)S(1)} %collective-permute-done.13), channel_id=1, source_target_pairs={{0,16},{16,32},{32,48},{48,64},{64,80},{80,96},{96,112},{112,0},{1... | collective-permute-start | bytes 1179656 | tf_op jit(solution)/shard_map/ppermute | solution.py:27
  69.2 14.3 %collective-permute-start.16 = (bf16[192,1024]{1,0:T(8,128)(2,1)S(1)}, bf16[192,1024]{1,0:T(8,128)(2,1)S(1)}, u32[]{:S(2)}, u32[]{:S(2)}) collective-permute-start(bf16[192,1024]{1,0:T(8,128)(2,1)S(1)} %collective-permute-done.14), channel_id=1, source_target_pairs={{0,112},{16,0},{32,16},{48,32},{64,48},{80,64},{96,80},{112,96},{1... | collective-permute-start | bytes 1179656 | tf_op jit(solution)/shard_map/ppermute | solution.py:27
  71.3 36.5 %collective-permute-start.21 = (bf16[128,1024]{1,0:T(8,128)(2,1)S(1)}, bf16[128,1024]{1,0:T(8,128)(2,1)S(1)}, u32[]{:S(2)}, u32[]{:S(2)}) collective-permute-start(bf16[128,1024]{1,0:T(8,128)(2,1)S(1)} %get-tuple-element.9), channel_id=1, source_target_pairs={{0,128},{16,144},{32,160},{48,176},{64,192},{80,208},{96,224},{112... | collective-permute-start | bytes 786440 | tf_op jit(solution)/shard_map/ppermute | solution.py:22
  74.7 11.0 %collective-permute-start.9 = (bf16[96,1024]{1,0:T(8,128)(2,1)S(1)}, bf16[96,1024]{1,0:T(8,128)(2,1)S(1)}, u32[]{:S(2)}, u32[]{:S(2)}) collective-permute-start(bf16[96,1024]{1,0:T(8,128)(2,1)S(1)} %slice.68), channel_id=1, source_target_pairs={{0,16},{16,32},{32,48},{48,64},{64,80},{80,96},{96,112},{112,0},{1... | collective-permute-start | bytes 589832 | tf_op jit(solution)/shard_map/ppermute | solution.py:27
  79.2 9.6 %collective-permute-start.10 = (bf16[96,1024]{1,0:T(8,128)(2,1)S(1)}, bf16[96,1024]{1,0:T(8,128)(2,1)S(1)}, u32[]{:S(2)}, u32[]{:S(2)}) collective-permute-start(bf16[96,1024]{1,0:T(8,128)(2,1)S(1)} %slice.69), channel_id=1, source_target_pairs={{0,112},{16,0},{32,16},{48,32},{64,48},{80,64},{96,80},{112,96},{1... | collective-permute-start | bytes 589832 | tf_op jit(solution)/shard_map/ppermute | solution.py:27
  83.5 11.5 %collective-permute-start.17 = (bf16[192,1024]{1,0:T(8,128)(2,1)S(1)}, bf16[192,1024]{1,0:T(8,128)(2,1)S(1)}, u32[]{:S(2)}, u32[]{:S(2)}) collective-permute-start(bf16[192,1024]{1,0:T(8,128)(2,1)S(1)} %collective-permute-done.15), channel_id=1, source_target_pairs={{0,16},{16,32},{32,48},{48,64},{64,80},{80,96},{96,112},{112,0},{1... | collective-permute-start | bytes 1179656 | tf_op jit(solution)/shard_map/ppermute | solution.py:27
  85.7 12.3 %collective-permute-start.18 = (bf16[192,1024]{1,0:T(8,128)(2,1)S(1)}, bf16[192,1024]{1,0:T(8,128)(2,1)S(1)}, u32[]{:S(2)}, u32[]{:S(2)}) collective-permute-start(bf16[192,1024]{1,0:T(8,128)(2,1)S(1)} %collective-permute-done.16), channel_id=1, source_target_pairs={{0,112},{16,0},{32,16},{48,32},{64,48},{80,64},{96,80},{112,96},{1... | collective-permute-start | bytes 1179656 | tf_op jit(solution)/shard_map/ppermute | solution.py:27
  95.1 6.4 %collective-permute-start.19 = (bf16[96,1024]{1,0:T(8,128)(2,1)S(1)}, bf16[96,1024]{1,0:T(8,128)(2,1)S(1)}, u32[]{:S(2)}, u32[]{:S(2)}) collective-permute-start(bf16[96,1024]{1,0:T(8,128)(2,1)S(1)} %slice.70), channel_id=1, source_target_pairs={{0,16},{16,32},{32,48},{48,64},{64,80},{80,96},{96,112},{112,0},{1... | collective-permute-start | bytes 589832 | tf_op jit(solution)/shard_map/ppermute | solution.py:27
  98.1 7.6 %collective-permute-start.20 = (bf16[96,1024]{1,0:T(8,128)(2,1)S(1)}, bf16[96,1024]{1,0:T(8,128)(2,1)S(1)}, u32[]{:S(2)}, u32[]{:S(2)}) collective-permute-start(bf16[96,1024]{1,0:T(8,128)(2,1)S(1)} %slice.71), channel_id=1, source_target_pairs={{0,112},{16,0},{32,16},{48,32},{64,48},{80,64},{96,80},{112,96},{1... | collective-permute-start | bytes 589832 | tf_op jit(solution)/shard_map/ppermute | solution.py:27
  105.7 2.6 %copy-start = (bf16[2,2,8,96,1024]{4,3,2,1,0:T(8,128)(2,1)}, bf16[2,2,8,96,1024]{4,3,2,1,0:T(8,128)(2,1)S(1)}, u32[]{:S(2)}) copy-start(bf16[2,2,8,96,1024]{4,3,2,1,0:T(8,128)(2,1)S(1)} %bitcast_dynamic-update-slice_fusion) | copy-start | bytes 18874372
  105.7 9.2 %copy-start.4 = (f32[128]{0:T(128)S(1)}, f32[128]{0:T(128)}, u32[]{:S(2)}) copy-start(f32[128]{0:T(128)} %param.9) | copy-start | bytes 1540
  108.4 6.5 %collective-permute-start.22 = (f32[8,128]{1,0:T(8,128)S(1)}, f32[8,128]{1,0:T(8,128)S(1)}, u32[]{:S(2)}, u32[]{:S(2)}) collective-permute-start(f32[8,128]{1,0:T(8,128)S(1)} %reshape.130), channel_id=1, source_target_pairs={{0,256},{16,272},{32,288},{48,304},{64,320},{80,336},{96,352},{112... | collective-permute-start | bytes 12296 | tf_op jit(solution)/shard_map/ppermute | solution.py:22
  133.1 2.8 %copy-start.1 = (bf16[2,2,8,96,1024]{4,3,2,1,0:T(8,128)(2,1)S(1)}, bf16[2,2,8,96,1024]{4,3,2,1,0:T(8,128)(2,1)}, u32[]{:S(2)}) copy-start(bf16[2,2,8,96,1024]{4,3,2,1,0:T(8,128)(2,1)} %copy-done) | copy-start | bytes 18874372
  135.9 6.6 %copy-start.2 = (bf16[2,2,8,96,1024]{4,3,2,1,0:T(8,128)(2,1)S(1)}, bf16[2,2,8,96,1024]{4,3,2,1,0:T(8,128)(2,1)}, u32[]{:S(2)}) copy-start(bf16[2,2,8,96,1024]{4,3,2,1,0:T(8,128)(2,1)} %copy-done) | copy-start | bytes 18874372
  138.5 6.2 %collective-permute-start.23 = (bf16[2,1536,128]{2,1,0:T(8,128)(2,1)S(1)}, bf16[2,1536,128]{2,1,0:T(8,128)(2,1)S(1)}, u32[]{:S(2)}, u32[]{:S(2)}) collective-permute-start(bf16[2,1536,128]{2,1,0:T(8,128)(2,1)S(1)} %get-tuple-element.11), channel_id=1, source_target_pairs={{0,256},{16,272},{32,288},{48,304},{64,320},{80,336},{96,352},{112... | collective-permute-start | bytes 2359304 | tf_op jit(solution)/shard_map/ppermute | solution.py:22
  145.8 27.5 %all-to-all-start.1 = ((bf16[32,96,128]{2,1,0:T(8,128)(2,1)}), bf16[32,96,128]{2,1,0:T(8,128)(2,1)S(1)}, u32[]{:S(2)}, u32[]{:S(2)}) async-start(bf16[32,96,128]{2,1,0:T(8,128)(2,1)} %bitcast.51), calls=%async_computation.1 | async-start | bytes 1572864 | tf_op jit(solution)/shard_map/all_to_all | solution.py:37

commit v12 on v11

--- a/solution.py
+++ b/solution.py
@@ -134,7 +134,9 @@
     near = jnp.concatenate([columns(first, 0, 0), flip(columns(first, 1, 0), 1, 0)], axis=0)
     near_parts = ring(near)
     came = flip(away, 0, 1)
-    came_mine = lax.dynamic_slice_in_dim(came, s * width, width, axis=1)
+    came_mine = lax.dynamic_slice_in_dim(
+        after(came, near_parts[3][2], near_parts[4][2]), s * width, width, axis=1
+    )
     came_send = lax.dynamic_slice_in_dim(came, (s ^ 1) * width, width, axis=1)
     far = jnp.concatenate([came_mine, flip(came_send, 1, 0)], axis=0)
     far_parts = ring(far)
@@ -149,7 +151,7 @@
     weights = weights.reshape(2 * NZH * NY * rows, width)
 
     hidden = after(hidden, near_parts[1][2])
-    h_sec = both(hidden, flip(hidden, 0, 1))
+    h_sec = both(hidden, after(flip(hidden, 0, 1), far_parts[3][2], far_parts[4][2]))
     h_all = jnp.concatenate([h_sec, flip(h_sec, 1, 0)], axis=1)
     teacher = teacher_half(codes, exponents)
     t_send = after(columns(teacher, 0, 1), near_parts[3][2])

time: 175 us -> 177 us (1.011)
  waiting for transfers between devices: 37.8 us -> 44 us
  starting transfers between devices: 95.7 us -> 92.2 us
    ppermute x16, waiting for transfers between devices: 13.7 us -> 20 us  [along_y(): return lax.ppermute(x, 'dp', perm)]
    ppermute x8, starting transfers between devices: 42.5 us -> 40.3 us  [flip(): return lax.ppermute(x, ('section', 'dp'), perm)]
  transfers between devices with their start and end apart: 25 -> 25, of which waited for: 8 -> 9; matrix products, arithmetic and copies ran while one was open for 6% -> 6% of each run, Pallas kernels for 1% -> 1%
where the time goes in v12:
time: 177 us; the launch traced here: 176 us
  starting transfers between devices  92.2 us (52%)
  waiting for transfers between devices  44 us (25%)
  blocking collectives  16.7 us (9%)
  local copies, waits for them, and re-layouts  7.41 us (4%)
  other arithmetic  7.1 us (4%)
  Pallas kernels  4.69 us (3%)
  matrix products  1.99 us (1%)
    ppermute x16, starting transfers between devices, along_y(): return lax.ppermute(x, 'dp', perm)  48 us
    ppermute x8, starting transfers between devices, flip(): return lax.ppermute(x, ('section', 'dp'), perm)  40.3 us
    all_to_all x1, waiting for transfers between devices, exchange(): lax.all_to_all(x, ('section', 'dp', 'vocab'), split_axis=0, concat_axis=0...  23 us
    ppermute x16, waiting for transfers between devices, along_y(): return lax.ppermute(x, 'dp', perm)  20 us
    all_to_all x1, blocking collectives, exchange(): lax.all_to_all(x, ('section', 'dp', 'vocab'), split_axis=0, concat_axis=0...  16.7 us
    pallas_call x2, Pallas kernels, over_tiles(): pl.pallas_call(kernel, grid=(feats // TILE,), in_specs=[whole] * len(ins)...  4.69 us
    all_to_all x1, starting transfers between devices, exchange(): lax.all_to_all(x, ('section', 'dp', 'vocab'), split_axis=0, concat_axis=0...  3.91 us
  transfers between devices with their start and end apart: 25, of which 9 were waited for; matrix products, arithmetic and copies ran while one was open for 6% of the time, Pallas kernels for 1%

profile of v12, /device:TPU:25, one launch (start us, length us, event | category | flops | bytes accessed | tf_op | source)
XLA Modules:
  0.0 175.7 jit_solution(16149969941972582293)
XLA Ops:
  0.7 1.0 constant_dynamic-slice_fusion.9
  1.7 10.6 %collective-permute-start.3 = (bf16[96,2048]{1,0:T(8,128)(2,1)S(1)}, bf16[96,2048]{1,0:T(8,128)(2,1)S(1)}, u32[]{:S(2)}, u32[]{:S(2)}) collective-permute-start(bf16[96,2048]{1,0:T(8,128)(2,1)S(1)} %constant_dynamic-slice_fusion.9), channel_id=1, source_target_pairs={{0,128},{16,144},{32,160},{48,176},{64,192},{80,208},{96,224},{112... | collective-permute-start | bytes 1179656 | tf_op jit(solution)/shard_map/ppermute | solution.py:22
  12.3 1.1 constant_dynamic-slice_fusion.8
  13.4 2.9 %collective-permute-start = (bf16[96,1024]{1,0:T(8,128)(2,1)S(1)}, bf16[96,1024]{1,0:T(8,128)(2,1)S(1)}, u32[]{:S(2)}, u32[]{:S(2)}) collective-permute-start(bf16[96,1024]{1,0:T(8,128)(2,1)S(1)} %get-tuple-element.25), channel_id=1, source_target_pairs={{0,256},{16,272},{32,288},{48,304},{64,320},{80,336},{96,352},{112... | collective-permute-start | bytes 589832 | tf_op jit(solution)/shard_map/ppermute | solution.py:22
  16.3 0.7 exponential_multiply_fusion
  17.4 4.4 %collective-permute-start.1 = (bf16[192,1024]{1,0:T(8,128)(2,1)S(1)}, bf16[192,1024]{1,0:T(8,128)(2,1)S(1)}, u32[]{:S(2)}, u32[]{:S(2)}) collective-permute-start(bf16[192,1024]{1,0:T(8,128)(2,1)S(1)} %pad_maximum_fusion), channel_id=1, source_target_pairs={{0,16},{16,32},{32,48},{48,64},{64,80},{80,96},{96,112},{112,0},{1... | collective-permute-start | bytes 1179656 | tf_op jit(solution)/shard_map/ppermute | solution.py:27
  21.8 1.9 %collective-permute-start.5 = (bf16[192,1024]{1,0:T(8,128)(2,1)S(1)}, bf16[192,1024]{1,0:T(8,128)(2,1)S(1)}, u32[]{:S(2)}, u32[]{:S(2)}) collective-permute-start(bf16[192,1024]{1,0:T(8,128)(2,1)S(1)} %pad_maximum_fusion), channel_id=1, source_target_pairs={{0,112},{16,0},{32,16},{48,32},{64,48},{80,64},{96,80},{112,96},{1... | collective-permute-start | bytes 1179656 | tf_op jit(solution)/shard_map/ppermute | solution.py:27
  23.7 0.6 mul.60
  24.3 3.0 %fusion = bf16[128,4096]{1,0:T(8,128)(2,1)S(1)} fusion(f32[16,8,32,128]{3,2,1,0:T(8,128)S(1)} %bitcast.103, s32[128,4096]{1,0:T(8,128)} %param.7), kind=kLoop, calls=%fused_computation.1 | loop fusion | flops 1572864 | bytes 5242880 | tf_op jit(solution)/shard_map/convert_element_type | solution.py:51
  27.5 2.3 %collective-permute-done.1 = bf16[192,1024]{1,0:T(8,128)(2,1)S(1)} collective-permute-done((bf16[192,1024]{1,0:T(8,128)(2,1)S(1)}, bf16[192,1024]{1,0:T(8,128)(2,1)S(1)}, u32[]{:S(2)}, u32[]{:S(2)}) %collective-permute-start.1) | collective-permute-done | bytes 393248 | tf_op jit(solution)/shard_map/ppermute | solution.py:27
  29.9 5.3 %collective-permute-start.4 = (bf16[192,1024]{1,0:T(8,128)(2,1)S(1)}, bf16[192,1024]{1,0:T(8,128)(2,1)S(1)}, u32[]{:S(2)}, u32[]{:S(2)}) collective-permute-start(bf16[192,1024]{1,0:T(8,128)(2,1)S(1)} %collective-permute-done.1), channel_id=1, source_target_pairs={{0,16},{16,32},{32,48},{48,64},{64,80},{80,96},{96,112},{112,0},{1... | collective-permute-start | bytes 1179656 | tf_op jit(solution)/shard_map/ppermute | solution.py:27
  35.2 1.9 %collective-permute-start.6 = (bf16[192,1024]{1,0:T(8,128)(2,1)S(1)}, bf16[192,1024]{1,0:T(8,128)(2,1)S(1)}, u32[]{:S(2)}, u32[]{:S(2)}) collective-permute-start(bf16[192,1024]{1,0:T(8,128)(2,1)S(1)} %collective-permute-done.5), channel_id=1, source_target_pairs={{0,112},{16,0},{32,16},{48,32},{64,48},{80,64},{96,80},{112,96},{1... | collective-permute-start | bytes 1179656 | tf_op jit(solution)/shard_map/ppermute | solution.py:27
  37.1 0.8 broadcast_in_dim.6
  38.0 3.4 %collective-permute-start.7 = (bf16[96,1024]{1,0:T(8,128)(2,1)S(1)}, bf16[96,1024]{1,0:T(8,128)(2,1)S(1)}, u32[]{:S(2)}, u32[]{:S(2)}) collective-permute-start(bf16[96,1024]{1,0:T(8,128)(2,1)S(1)} %constant_dynamic-slice_fusion.5), channel_id=1, source_target_pairs={{0,256},{16,272},{32,288},{48,304},{64,320},{80,336},{96,352},{112... | collective-permute-start | bytes 589832 | tf_op jit(solution)/shard_map/ppermute | solution.py:22
  41.4 1.9 %collective-permute-start.2 = (bf16[128,1536]{1,0:T(8,128)(2,1)S(1)}, bf16[128,1536]{1,0:T(8,128)(2,1)S(1)}, u32[]{:S(2)}, u32[]{:S(2)}) collective-permute-start(bf16[128,1536]{1,0:T(8,128)(2,1)S(1)} %copy-done.3), channel_id=1, source_target_pairs={{0,128},{16,144},{32,160},{48,176},{64,192},{80,208},{96,224},{112... | collective-permute-start | bytes 1179656 | tf_op jit(solution)/shard_map/ppermute | solution.py:22
  43.5 4.0 %collective-permute-done.6 = bf16[192,1024]{1,0:T(8,128)(2,1)S(1)} collective-permute-done((bf16[192,1024]{1,0:T(8,128)(2,1)S(1)}, bf16[192,1024]{1,0:T(8,128)(2,1)S(1)}, u32[]{:S(2)}, u32[]{:S(2)}) %collective-permute-start.6) | collective-permute-done | bytes 393248 | tf_op jit(solution)/shard_map/ppermute | solution.py:27
  47.4 1.9 %collective-permute-start.13 = (bf16[192,1024]{1,0:T(8,128)(2,1)S(1)}, bf16[192,1024]{1,0:T(8,128)(2,1)S(1)}, u32[]{:S(2)}, u32[]{:S(2)}) collective-permute-start(bf16[192,1024]{1,0:T(8,128)(2,1)S(1)} %collective-permute-done.4), channel_id=1, source_target_pairs={{0,16},{16,32},{32,48},{48,64},{64,80},{80,96},{96,112},{112,0},{1... | collective-permute-start | bytes 1179656 | tf_op jit(solution)/shard_map/ppermute | solution.py:27
  49.4 3.4 %collective-permute-start.14 = (bf16[192,1024]{1,0:T(8,128)(2,1)S(1)}, bf16[192,1024]{1,0:T(8,128)(2,1)S(1)}, u32[]{:S(2)}, u32[]{:S(2)}) collective-permute-start(bf16[192,1024]{1,0:T(8,128)(2,1)S(1)} %collective-permute-done.6), channel_id=1, source_target_pairs={{0,112},{16,0},{32,16},{48,32},{64,48},{80,64},{96,80},{112,96},{1... | collective-permute-start | bytes 1179656 | tf_op jit(solution)/shard_map/ppermute | solution.py:27
  52.8 3.1 %collective-permute-start.8 = (bf16[192,1024]{1,0:T(8,128)(2,1)S(1)}, bf16[192,1024]{1,0:T(8,128)(2,1)S(1)}, u32[]{:S(2)}, u32[]{:S(2)}) collective-permute-start(bf16[192,1024]{1,0:T(8,128)(2,1)S(1)} %pad_maximum_fusion.1), channel_id=1, source_target_pairs={{0,16},{16,32},{32,48},{48,64},{64,80},{80,96},{96,112},{112,0},{1... | collective-permute-start | bytes 1179656 | tf_op jit(solution)/shard_map/ppermute | solution.py:27
  55.9 2.2 %collective-permute-start.10 = (bf16[192,1024]{1,0:T(8,128)(2,1)S(1)}, bf16[192,1024]{1,0:T(8,128)(2,1)S(1)}, u32[]{:S(2)}, u32[]{:S(2)}) collective-permute-start(bf16[192,1024]{1,0:T(8,128)(2,1)S(1)} %pad_maximum_fusion.1), channel_id=1, source_target_pairs={{0,112},{16,0},{32,16},{48,32},{64,48},{80,64},{96,80},{112,96},{1... | collective-permute-start | bytes 1179656 | tf_op jit(solution)/shard_map/ppermute | solution.py:27
  58.2 6.0 %collective-permute-start.21 = (bf16[128,1024]{1,0:T(8,128)(2,1)S(1)}, bf16[128,1024]{1,0:T(8,128)(2,1)S(1)}, u32[]{:S(2)}, u32[]{:S(2)}) collective-permute-start(bf16[128,1024]{1,0:T(8,128)(2,1)S(1)} %get-tuple-element.13), channel_id=1, source_target_pairs={{0,128},{16,144},{32,160},{48,176},{64,192},{80,208},{96,224},{112... | collective-permute-start | bytes 786440 | tf_op jit(solution)/shard_map/ppermute | solution.py:22
  64.3 4.9 %collective-permute-start.15 = (bf16[96,1024]{1,0:T(8,128)(2,1)S(1)}, bf16[96,1024]{1,0:T(8,128)(2,1)S(1)}, u32[]{:S(2)}, u32[]{:S(2)}) collective-permute-start(bf16[96,1024]{1,0:T(8,128)(2,1)S(1)} %slice.68), channel_id=1, source_target_pairs={{0,16},{16,32},{32,48},{48,64},{64,80},{80,96},{96,112},{112,0},{1... | collective-permute-start | bytes 589832 | tf_op jit(solution)/shard_map/ppermute | solution.py:27
  69.3 1.9 %collective-permute-start.16 = (bf16[96,1024]{1,0:T(8,128)(2,1)S(1)}, bf16[96,1024]{1,0:T(8,128)(2,1)S(1)}, u32[]{:S(2)}, u32[]{:S(2)}) collective-permute-start(bf16[96,1024]{1,0:T(8,128)(2,1)S(1)} %slice.69), channel_id=1, source_target_pairs={{0,112},{16,0},{32,16},{48,32},{64,48},{80,64},{96,80},{112,96},{1... | collective-permute-start | bytes 589832 | tf_op jit(solution)/shard_map/ppermute | solution.py:27
  71.2 4.6 %collective-permute-start.9 = (bf16[192,1024]{1,0:T(8,128)(2,1)S(1)}, bf16[192,1024]{1,0:T(8,128)(2,1)S(1)}, u32[]{:S(2)}, u32[]{:S(2)}) collective-permute-start(bf16[192,1024]{1,0:T(8,128)(2,1)S(1)} %collective-permute-done.8), channel_id=1, source_target_pairs={{0,16},{16,32},{32,48},{48,64},{64,80},{80,96},{96,112},{112,0},{1... | collective-permute-start | bytes 1179656 | tf_op jit(solution)/shard_map/ppermute | solution.py:27
  75.8 1.9 %collective-permute-start.11 = (bf16[192,1024]{1,0:T(8,128)(2,1)S(1)}, bf16[192,1024]{1,0:T(8,128)(2,1)S(1)}, u32[]{:S(2)}, u32[]{:S(2)}) collective-permute-start(bf16[192,1024]{1,0:T(8,128)(2,1)S(1)} %collective-permute-done.10), channel_id=1, source_target_pairs={{0,112},{16,0},{32,16},{48,32},{64,48},{80,64},{96,80},{112,96},{1... | collective-permute-start | bytes 1179656 | tf_op jit(solution)/shard_map/ppermute | solution.py:27
  78.0 3.5 %collective-permute-done.9 = bf16[192,1024]{1,0:T(8,128)(2,1)S(1)} collective-permute-done((bf16[192,1024]{1,0:T(8,128)(2,1)S(1)}, bf16[192,1024]{1,0:T(8,128)(2,1)S(1)}, u32[]{:S(2)}, u32[]{:S(2)}) %collective-permute-start.9) | collective-permute-done | bytes 393248 | tf_op jit(solution)/shard_map/ppermute | solution.py:27
  81.5 5.1 %collective-permute-done.11 = bf16[192,1024]{1,0:T(8,128)(2,1)S(1)} collective-permute-done((bf16[192,1024]{1,0:T(8,128)(2,1)S(1)}, bf16[192,1024]{1,0:T(8,128)(2,1)S(1)}, u32[]{:S(2)}, u32[]{:S(2)}) %collective-permute-start.11) | collective-permute-done | bytes 393248 | tf_op jit(solution)/shard_map/ppermute | solution.py:27
  86.6 1.9 %collective-permute-start.17 = (bf16[192,1024]{1,0:T(8,128)(2,1)S(1)}, bf16[192,1024]{1,0:T(8,128)(2,1)S(1)}, u32[]{:S(2)}, u32[]{:S(2)}) collective-permute-start(bf16[192,1024]{1,0:T(8,128)(2,1)S(1)} %collective-permute-done.9), channel_id=1, source_target_pairs={{0,16},{16,32},{32,48},{48,64},{64,80},{80,96},{96,112},{112,0},{1... | collective-permute-start | bytes 1179656 | tf_op jit(solution)/shard_map/ppermute | solution.py:27
  88.5 3.4 %collective-permute-start.18 = (bf16[192,1024]{1,0:T(8,128)(2,1)S(1)}, bf16[192,1024]{1,0:T(8,128)(2,1)S(1)}, u32[]{:S(2)}, u32[]{:S(2)}) collective-permute-start(bf16[192,1024]{1,0:T(8,128)(2,1)S(1)} %collective-permute-done.11), channel_id=1, source_target_pairs={{0,112},{16,0},{32,16},{48,32},{64,48},{80,64},{96,80},{112,96},{1... | collective-permute-start | bytes 1179656 | tf_op jit(solution)/shard_map/ppermute | solution.py:27
  92.0 6.3 %collective-permute-start.12 = (bf16[256,1536]{1,0:T(8,128)(2,1)S(1)}, bf16[256,1536]{1,0:T(8,128)(2,1)S(1)}, u32[]{:S(2)}, u32[]{:S(2)}) collective-permute-start(bf16[256,1536]{1,0:T(8,128)(2,1)S(1)} %maximum_select_fusion), channel_id=1, source_target_pairs={{0,256},{16,272},{32,288},{48,304},{64,320},{80,336},{96,352},{112... | collective-permute-start | bytes 2359304 | tf_op jit(solution)/shard_map/ppermute | solution.py:22
  98.5 2.9 %collective-permute-start.19 = (bf16[96,1024]{1,0:T(8,128)(2,1)S(1)}, bf16[96,1024]{1,0:T(8,128)(2,1)S(1)}, u32[]{:S(2)}, u32[]{:S(2)}) collective-permute-start(bf16[96,1024]{1,0:T(8,128)(2,1)S(1)} %slice.70), channel_id=1, source_target_pairs={{0,16},{16,32},{32,48},{48,64},{64,80},{80,96},{96,112},{112,0},{1... | collective-permute-start | bytes 589832 | tf_op jit(solution)/shard_map/ppermute | solution.py:27
  101.4 2.4 %collective-permute-start.20 = (bf16[96,1024]{1,0:T(8,128)(2,1)S(1)}, bf16[96,1024]{1,0:T(8,128)(2,1)S(1)}, u32[]{:S(2)}, u32[]{:S(2)}) collective-permute-start(bf16[96,1024]{1,0:T(8,128)(2,1)S(1)} %slice.71), channel_id=1, source_target_pairs={{0,112},{16,0},{32,16},{48,32},{64,48},{80,64},{96,80},{112,96},{1... | collective-permute-start | bytes 589832 | tf_op jit(solution)/shard_map/ppermute | solution.py:27
  103.9 1.0 collective-permute-done.19
  105.0 4.1 %collective-permute-done.20 = bf16[96,1024]{1,0:T(8,128)(2,1)S(1)} collective-permute-done((bf16[96,1024]{1,0:T(8,128)(2,1)S(1)}, bf16[96,1024]{1,0:T(8,128)(2,1)S(1)}, u32[]{:S(2)}, u32[]{:S(2)}) %collective-permute-start.20) | collective-permute-done | bytes 196640 | tf_op jit(solution)/shard_map/ppermute | solution.py:27
  109.1 2.0 %fusion.23 = (f32[256]{0:T(256)S(1)}, f32[256,1024]{1,0:T(8,128)S(1)}) fusion(bf16[3072,1024]{1,0:T(8,128)(2,1)S(1)} %bitcast.100, bf16[256,1536]{1,0:T(8,128)(2,1)S(1)} %collective-permute-done.12, bf16[256,1536]{1,0:T(8,128)(2,1)S(1)} %maximum_select_fusion), kind=kOutput, calls=%fused_computation.74 | convolution fusion | flops 1614282496 | bytes 8913920 | tf_op jit(solution)/shard_map/dot_general | solution.py:160
  111.1 0.6 exponential_reduce_fusion
  111.7 5.1 %collective-permute-start.22 = (f32[8,128]{1,0:T(8,128)S(1)}, f32[8,128]{1,0:T(8,128)S(1)}, u32[]{:S(2)}, u32[]{:S(2)}) collective-permute-start(f32[8,128]{1,0:T(8,128)S(1)} %reshape.130), channel_id=1, source_target_pairs={{0,256},{16,272},{32,288},{48,304},{64,320},{80,336},{96,352},{112... | collective-permute-start | bytes 12296 | tf_op jit(solution)/shard_map/ppermute | solution.py:22
  116.9 0.8 collective-permute-done.22
  117.8 16.7 %all_to_all.10 = f32[32,8,128]{2,1,0:T(8,128)S(1)} all-to-all(f32[32,8,128]{2,1,0:T(8,128)S(1)} %bitcast.110), channel_id=1, replica_groups={{0,1,2,3,4,5,6,7,8,9,10,11,12,13,14,15,128,129,130,131,132,133,134,135,..., dimensions={0} | all-to-all | bytes 262144 | tf_op jit(solution)/shard_map/all_to_all | solution.py:37
  134.9 2.8 %copy-done.1 = bf16[2,2,8,96,1024]{4,3,2,1,0:T(8,128)(2,1)S(1)} copy-done((bf16[2,2,8,96,1024]{4,3,2,1,0:T(8,128)(2,1)S(1)}, bf16[2,2,8,96,1024]{4,3,2,1,0:T(8,128)(2,1)}, u32[]{:S(2)}) %copy-start.1) | copy-done | bytes 6291480
  137.7 2.6 %shard_map.68 = (bf16[256,1024]{1,0:T(8,128)(2,1)S(1)}, bf16[2,1536,128]{2,1,0:T(8,128)(2,1)S(1)}) custom-call(f32[256,1024]{1,0:T(8,128)S(1)} %get-tuple-element.29.s_ref, bf16[256,1024]{1,0:T(8,128)(2,1)S(1)} %get-tuple-element.21.t_ref, f32[256,3]{1,0:T(8,128)S(1)} %copy.71.row_ref, bf16[2,1536,1024]{2,1,0:T(8,128)(2,1)S(1)} %bitcast.101), custom_call_target="tpu_custom_call" | custom-call | flops 1000000000 | bytes 5000000 | tf_op jit(solution)/shard_map/pallas_call | solution.py:102
  140.2 4.0 %collective-permute-start.23 = (bf16[2,1536,128]{2,1,0:T(8,128)(2,1)S(1)}, bf16[2,1536,128]{2,1,0:T(8,128)(2,1)S(1)}, u32[]{:S(2)}, u32[]{:S(2)}) collective-permute-start(bf16[2,1536,128]{2,1,0:T(8,128)(2,1)S(1)} %get-tuple-element.15), channel_id=1, source_target_pairs={{0,256},{16,272},{32,288},{48,304},{64,320},{80,336},{96,352},{112... | collective-permute-start | bytes 2359304 | tf_op jit(solution)/shard_map/ppermute | solution.py:22
  144.2 2.1 %shard_map.69 = f32[2,1536,128]{2,1,0:T(8,128)S(1)} custom-call(bf16[256,1024]{1,0:T(8,128)(2,1)S(1)} %get-tuple-element.14.lg_ref, bf16[2,1536,1024]{2,1,0:T(8,128)(2,1)S(1)} %bitcast.102), custom_call_target="tpu_custom_call" | custom-call | flops 1000000000 | bytes 5000000 | tf_op jit(solution)/shard_map/pallas_call | solution.py:102
  146.4 1.1 add_convert_fusion
  147.5 3.9 %all-to-all-start.1 = ((bf16[32,96,128]{2,1,0:T(8,128)(2,1)}), bf16[32,96,128]{2,1,0:T(8,128)(2,1)S(1)}, u32[]{:S(2)}, u32[]{:S(2)}) async-start(bf16[32,96,128]{2,1,0:T(8,128)(2,1)} %bitcast.51), calls=%async_computation.1 | async-start | bytes 1572864 | tf_op jit(solution)/shard_map/all_to_all | solution.py:37
  151.5 0.5 fusion.20
  152.0 23.0 %all-to-all-done.1 = bf16[32,96,128]{2,1,0:T(8,128)(2,1)S(1)} async-done(((bf16[32,96,128]{2,1,0:T(8,128)(2,1)}), bf16[32,96,128]{2,1,0:T(8,128)(2,1)S(1)}, u32[]{:S(2)}, u32[]{:S(2)}) %all-to-all-start.1) | async-done | bytes 786464 | tf_op jit(solution)/shard_map/all_to_all | solution.py:37
  175.0 0.7 reduce_sum.92
  (76 shorter events, 1.9 us)
Async XLA Ops:
  1.7 36.3 %collective-permute-start.3 = (bf16[96,2048]{1,0:T(8,128)(2,1)S(1)}, bf16[96,2048]{1,0:T(8,128)(2,1)S(1)}, u32[]{:S(2)}, u32[]{:S(2)}) collective-permute-start(bf16[96,2048]{1,0:T(8,128)(2,1)S(1)} %constant_dynamic-slice_fusion.9), channel_id=1, source_target_pairs={{0,128},{16,144},{32,160},{48,176},{64,192},{80,208},{96,224},{112... | collective-permute-start | bytes 1179656 | tf_op jit(solution)/shard_map/ppermute | solution.py:22
  13.4 3.9 %collective-permute-start = (bf16[96,1024]{1,0:T(8,128)(2,1)S(1)}, bf16[96,1024]{1,0:T(8,128)(2,1)S(1)}, u32[]{:S(2)}, u32[]{:S(2)}) collective-permute-start(bf16[96,1024]{1,0:T(8,128)(2,1)S(1)} %get-tuple-element.25), channel_id=1, source_target_pairs={{0,256},{16,272},{32,288},{48,304},{64,320},{80,336},{96,352},{112... | collective-permute-start | bytes 589832 | tf_op jit(solution)/shard_map/ppermute | solution.py:22
  17.4 12.5 %collective-permute-start.1 = (bf16[192,1024]{1,0:T(8,128)(2,1)S(1)}, bf16[192,1024]{1,0:T(8,128)(2,1)S(1)}, u32[]{:S(2)}, u32[]{:S(2)}) collective-permute-start(bf16[192,1024]{1,0:T(8,128)(2,1)S(1)} %pad_maximum_fusion), channel_id=1, source_target_pairs={{0,16},{16,32},{32,48},{48,64},{64,80},{80,96},{96,112},{112,0},{1... | collective-permute-start | bytes 1179656 | tf_op jit(solution)/shard_map/ppermute | solution.py:27
  21.8 13.4 %collective-permute-start.5 = (bf16[192,1024]{1,0:T(8,128)(2,1)S(1)}, bf16[192,1024]{1,0:T(8,128)(2,1)S(1)}, u32[]{:S(2)}, u32[]{:S(2)}) collective-permute-start(bf16[192,1024]{1,0:T(8,128)(2,1)S(1)} %pad_maximum_fusion), channel_id=1, source_target_pairs={{0,112},{16,0},{32,16},{48,32},{64,48},{80,64},{96,80},{112,96},{1... | collective-permute-start | bytes 1179656 | tf_op jit(solution)/shard_map/ppermute | solution.py:27
  24.3 17.1 %copy-start.3 = (bf16[128,1536]{1,0:T(8,128)(2,1)S(1)}, bf16[128,1536]{1,0:T(8,128)(2,1)}, u32[]{:S(2)}) copy-start(bf16[128,1536]{1,0:T(8,128)(2,1)} %param.5) | copy-start | bytes 1179652
  29.9 13.6 %collective-permute-start.4 = (bf16[192,1024]{1,0:T(8,128)(2,1)S(1)}, bf16[192,1024]{1,0:T(8,128)(2,1)S(1)}, u32[]{:S(2)}, u32[]{:S(2)}) collective-permute-start(bf16[192,1024]{1,0:T(8,128)(2,1)S(1)} %collective-permute-done.1), channel_id=1, source_target_pairs={{0,16},{16,32},{32,48},{48,64},{64,80},{80,96},{96,112},{112,0},{1... | collective-permute-start | bytes 1179656 | tf_op jit(solution)/shard_map/ppermute | solution.py:27
  35.2 12.2 %collective-permute-start.6 = (bf16[192,1024]{1,0:T(8,128)(2,1)S(1)}, bf16[192,1024]{1,0:T(8,128)(2,1)S(1)}, u32[]{:S(2)}, u32[]{:S(2)}) collective-permute-start(bf16[192,1024]{1,0:T(8,128)(2,1)S(1)} %collective-permute-done.5), channel_id=1, source_target_pairs={{0,112},{16,0},{32,16},{48,32},{64,48},{80,64},{96,80},{112,96},{1... | collective-permute-start | bytes 1179656 | tf_op jit(solution)/shard_map/ppermute | solution.py:27
  38.0 14.7 %collective-permute-start.7 = (bf16[96,1024]{1,0:T(8,128)(2,1)S(1)}, bf16[96,1024]{1,0:T(8,128)(2,1)S(1)}, u32[]{:S(2)}, u32[]{:S(2)}) collective-permute-start(bf16[96,1024]{1,0:T(8,128)(2,1)S(1)} %constant_dynamic-slice_fusion.5), channel_id=1, source_target_pairs={{0,256},{16,272},{32,288},{48,304},{64,320},{80,336},{96,352},{112... | collective-permute-start | bytes 589832 | tf_op jit(solution)/shard_map/ppermute | solution.py:22
  41.4 36.5 %collective-permute-start.2 = (bf16[128,1536]{1,0:T(8,128)(2,1)S(1)}, bf16[128,1536]{1,0:T(8,128)(2,1)S(1)}, u32[]{:S(2)}, u32[]{:S(2)}) collective-permute-start(bf16[128,1536]{1,0:T(8,128)(2,1)S(1)} %copy-done.3), channel_id=1, source_target_pairs={{0,128},{16,144},{32,160},{48,176},{64,192},{80,208},{96,224},{112... | collective-permute-start | bytes 1179656 | tf_op jit(solution)/shard_map/ppermute | solution.py:22
  47.4 10.8 %collective-permute-start.13 = (bf16[192,1024]{1,0:T(8,128)(2,1)S(1)}, bf16[192,1024]{1,0:T(8,128)(2,1)S(1)}, u32[]{:S(2)}, u32[]{:S(2)}) collective-permute-start(bf16[192,1024]{1,0:T(8,128)(2,1)S(1)} %collective-permute-done.4), channel_id=1, source_target_pairs={{0,16},{16,32},{32,48},{48,64},{64,80},{80,96},{96,112},{112,0},{1... | collective-permute-start | bytes 1179656 | tf_op jit(solution)/shard_map/ppermute | solution.py:27
  49.4 14.9 %collective-permute-start.14 = (bf16[192,1024]{1,0:T(8,128)(2,1)S(1)}, bf16[192,1024]{1,0:T(8,128)(2,1)S(1)}, u32[]{:S(2)}, u32[]{:S(2)}) collective-permute-start(bf16[192,1024]{1,0:T(8,128)(2,1)S(1)} %collective-permute-done.6), channel_id=1, source_target_pairs={{0,112},{16,0},{32,16},{48,32},{64,48},{80,64},{96,80},{112,96},{1... | collective-permute-start | bytes 1179656 | tf_op jit(solution)/shard_map/ppermute | solution.py:27
  52.8 16.5 %collective-permute-start.8 = (bf16[192,1024]{1,0:T(8,128)(2,1)S(1)}, bf16[192,1024]{1,0:T(8,128)(2,1)S(1)}, u32[]{:S(2)}, u32[]{:S(2)}) collective-permute-start(bf16[192,1024]{1,0:T(8,128)(2,1)S(1)} %pad_maximum_fusion.1), channel_id=1, source_target_pairs={{0,16},{16,32},{32,48},{48,64},{64,80},{80,96},{96,112},{112,0},{1... | collective-permute-start | bytes 1179656 | tf_op jit(solution)/shard_map/ppermute | solution.py:27
  55.9 15.3 %collective-permute-start.10 = (bf16[192,1024]{1,0:T(8,128)(2,1)S(1)}, bf16[192,1024]{1,0:T(8,128)(2,1)S(1)}, u32[]{:S(2)}, u32[]{:S(2)}) collective-permute-start(bf16[192,1024]{1,0:T(8,128)(2,1)S(1)} %pad_maximum_fusion.1), channel_id=1, source_target_pairs={{0,112},{16,0},{32,16},{48,32},{64,48},{80,64},{96,80},{112,96},{1... | collective-permute-start | bytes 1179656 | tf_op jit(solution)/shard_map/ppermute | solution.py:27
  58.2 52.9 %collective-permute-start.21 = (bf16[128,1024]{1,0:T(8,128)(2,1)S(1)}, bf16[128,1024]{1,0:T(8,128)(2,1)S(1)}, u32[]{:S(2)}, u32[]{:S(2)}) collective-permute-start(bf16[128,1024]{1,0:T(8,128)(2,1)S(1)} %get-tuple-element.13), channel_id=1, source_target_pairs={{0,128},{16,144},{32,160},{48,176},{64,192},{80,208},{96,224},{112... | collective-permute-start | bytes 786440 | tf_op jit(solution)/shard_map/ppermute | solution.py:22
  64.3 11.5 %collective-permute-start.15 = (bf16[96,1024]{1,0:T(8,128)(2,1)S(1)}, bf16[96,1024]{1,0:T(8,128)(2,1)S(1)}, u32[]{:S(2)}, u32[]{:S(2)}) collective-permute-start(bf16[96,1024]{1,0:T(8,128)(2,1)S(1)} %slice.68), channel_id=1, source_target_pairs={{0,16},{16,32},{32,48},{48,64},{64,80},{80,96},{96,112},{112,0},{1... | collective-permute-start | bytes 589832 | tf_op jit(solution)/shard_map/ppermute | solution.py:27
  69.3 8.5 %collective-permute-start.16 = (bf16[96,1024]{1,0:T(8,128)(2,1)S(1)}, bf16[96,1024]{1,0:T(8,128)(2,1)S(1)}, u32[]{:S(2)}, u32[]{:S(2)}) collective-permute-start(bf16[96,1024]{1,0:T(8,128)(2,1)S(1)} %slice.69), channel_id=1, source_target_pairs={{0,112},{16,0},{32,16},{48,32},{64,48},{80,64},{96,80},{112,96},{1... | collective-permute-start | bytes 589832 | tf_op jit(solution)/shard_map/ppermute | solution.py:27
  71.2 10.3 %collective-permute-start.9 = (bf16[192,1024]{1,0:T(8,128)(2,1)S(1)}, bf16[192,1024]{1,0:T(8,128)(2,1)S(1)}, u32[]{:S(2)}, u32[]{:S(2)}) collective-permute-start(bf16[192,1024]{1,0:T(8,128)(2,1)S(1)} %collective-permute-done.8), channel_id=1, source_target_pairs={{0,16},{16,32},{32,48},{48,64},{64,80},{80,96},{96,112},{112,0},{1... | collective-permute-start | bytes 1179656 | tf_op jit(solution)/shard_map/ppermute | solution.py:27
  75.8 10.8 %collective-permute-start.11 = (bf16[192,1024]{1,0:T(8,128)(2,1)S(1)}, bf16[192,1024]{1,0:T(8,128)(2,1)S(1)}, u32[]{:S(2)}, u32[]{:S(2)}) collective-permute-start(bf16[192,1024]{1,0:T(8,128)(2,1)S(1)} %collective-permute-done.10), channel_id=1, source_target_pairs={{0,112},{16,0},{32,16},{48,32},{64,48},{80,64},{96,80},{112,96},{1... | collective-permute-start | bytes 1179656 | tf_op jit(solution)/shard_map/ppermute | solution.py:27
  86.6 11.9 %collective-permute-start.17 = (bf16[192,1024]{1,0:T(8,128)(2,1)S(1)}, bf16[192,1024]{1,0:T(8,128)(2,1)S(1)}, u32[]{:S(2)}, u32[]{:S(2)}) collective-permute-start(bf16[192,1024]{1,0:T(8,128)(2,1)S(1)} %collective-permute-done.9), channel_id=1, source_target_pairs={{0,16},{16,32},{32,48},{48,64},{64,80},{80,96},{96,112},{112,0},{1... | collective-permute-start | bytes 1179656 | tf_op jit(solution)/shard_map/ppermute | solution.py:27
  88.5 12.9 %collective-permute-start.18 = (bf16[192,1024]{1,0:T(8,128)(2,1)S(1)}, bf16[192,1024]{1,0:T(8,128)(2,1)S(1)}, u32[]{:S(2)}, u32[]{:S(2)}) collective-permute-start(bf16[192,1024]{1,0:T(8,128)(2,1)S(1)} %collective-permute-done.11), channel_id=1, source_target_pairs={{0,112},{16,0},{32,16},{48,32},{64,48},{80,64},{96,80},{112,96},{1... | collective-permute-start | bytes 1179656 | tf_op jit(solution)/shard_map/ppermute | solution.py:27
  92.0 17.0 %collective-permute-start.12 = (bf16[256,1536]{1,0:T(8,128)(2,1)S(1)}, bf16[256,1536]{1,0:T(8,128)(2,1)S(1)}, u32[]{:S(2)}, u32[]{:S(2)}) collective-permute-start(bf16[256,1536]{1,0:T(8,128)(2,1)S(1)} %maximum_select_fusion), channel_id=1, source_target_pairs={{0,256},{16,272},{32,288},{48,304},{64,320},{80,336},{96,352},{112... | collective-permute-start | bytes 2359304 | tf_op jit(solution)/shard_map/ppermute | solution.py:22
  98.5 6.4 %collective-permute-start.19 = (bf16[96,1024]{1,0:T(8,128)(2,1)S(1)}, bf16[96,1024]{1,0:T(8,128)(2,1)S(1)}, u32[]{:S(2)}, u32[]{:S(2)}) collective-permute-start(bf16[96,1024]{1,0:T(8,128)(2,1)S(1)} %slice.70), channel_id=1, source_target_pairs={{0,16},{16,32},{32,48},{48,64},{64,80},{80,96},{96,112},{112,0},{1... | collective-permute-start | bytes 589832 | tf_op jit(solution)/shard_map/ppermute | solution.py:27
  101.4 7.6 %collective-permute-start.20 = (bf16[96,1024]{1,0:T(8,128)(2,1)S(1)}, bf16[96,1024]{1,0:T(8,128)(2,1)S(1)}, u32[]{:S(2)}, u32[]{:S(2)}) collective-permute-start(bf16[96,1024]{1,0:T(8,128)(2,1)S(1)} %slice.71), channel_id=1, source_target_pairs={{0,112},{16,0},{32,16},{48,32},{64,48},{80,64},{96,80},{112,96},{1... | collective-permute-start | bytes 589832 | tf_op jit(solution)/shard_map/ppermute | solution.py:27
  109.1 2.6 %copy-start = (bf16[2,2,8,96,1024]{4,3,2,1,0:T(8,128)(2,1)}, bf16[2,2,8,96,1024]{4,3,2,1,0:T(8,128)(2,1)S(1)}, u32[]{:S(2)}) copy-start(bf16[2,2,8,96,1024]{4,3,2,1,0:T(8,128)(2,1)S(1)} %bitcast_dynamic-update-slice_fusion) | copy-start | bytes 18874372
  109.1 8.6 %copy-start.4 = (f32[128]{0:T(128)S(1)}, f32[128]{0:T(128)}, u32[]{:S(2)}) copy-start(f32[128]{0:T(128)} %param.9) | copy-start | bytes 1540
  111.7 5.9 %collective-permute-start.22 = (f32[8,128]{1,0:T(8,128)S(1)}, f32[8,128]{1,0:T(8,128)S(1)}, u32[]{:S(2)}, u32[]{:S(2)}) collective-permute-start(f32[8,128]{1,0:T(8,128)S(1)} %reshape.130), channel_id=1, source_target_pairs={{0,256},{16,272},{32,288},{48,304},{64,320},{80,336},{96,352},{112... | collective-permute-start | bytes 12296 | tf_op jit(solution)/shard_map/ppermute | solution.py:22
  134.9 2.8 %copy-start.1 = (bf16[2,2,8,96,1024]{4,3,2,1,0:T(8,128)(2,1)S(1)}, bf16[2,2,8,96,1024]{4,3,2,1,0:T(8,128)(2,1)}, u32[]{:S(2)}) copy-start(bf16[2,2,8,96,1024]{4,3,2,1,0:T(8,128)(2,1)} %copy-done) | copy-start | bytes 18874372
  137.7 6.6 %copy-start.2 = (bf16[2,2,8,96,1024]{4,3,2,1,0:T(8,128)(2,1)S(1)}, bf16[2,2,8,96,1024]{4,3,2,1,0:T(8,128)(2,1)}, u32[]{:S(2)}) copy-start(bf16[2,2,8,96,1024]{4,3,2,1,0:T(8,128)(2,1)} %copy-done) | copy-start | bytes 18874372
  140.2 6.2 %collective-permute-start.23 = (bf16[2,1536,128]{2,1,0:T(8,128)(2,1)S(1)}, bf16[2,1536,128]{2,1,0:T(8,128)(2,1)S(1)}, u32[]{:S(2)}, u32[]{:S(2)}) collective-permute-start(bf16[2,1536,128]{2,1,0:T(8,128)(2,1)S(1)} %get-tuple-element.15), channel_id=1, source_target_pairs={{0,256},{16,272},{32,288},{48,304},{64,320},{80,336},{96,352},{112... | collective-permute-start | bytes 2359304 | tf_op jit(solution)/shard_map/ppermute | solution.py:22
  147.5 27.5 %all-to-all-start.1 = ((bf16[32,96,128]{2,1,0:T(8,128)(2,1)}), bf16[32,96,128]{2,1,0:T(8,128)(2,1)S(1)}, u32[]{:S(2)}, u32[]{:S(2)}) async-start(bf16[32,96,128]{2,1,0:T(8,128)(2,1)} %bitcast.51), calls=%async_computation.1 | async-start | bytes 1572864 | tf_op jit(solution)/shard_map/all_to_all | solution.py:37
